TPU v7x, 32 devices: a whole 2x2x4 slice. The times are simulated.
32 devices in a mesh: groups: 2 (over y), expert: 4 (over z), mp: 4 (over x, core).
Axes of the slice: x: 2, y: 2, z: 4, core: 2. Of those that a mesh axis runs over, the one named last changes fastest.
Arguments:
- tokens: bfloat16 [1024, 3584], P(('groups', 'expert'), 'mp'), parts along dimension 0, may hold values from -6 to 6
- route_ids: int32 [1024, 8], P(('groups', 'expert')), parts along dimension 0, may hold values from 0 to 255, all different within a row
- route_weights: float32 [1024, 8], P(('groups', 'expert')), parts along dimension 0, may hold values from 0.2 to 1
- gate_weight: bfloat16 [4, 3584, 1024], P('expert', None, 'mp'), may hold values from -0.09375 to 0.09375
- gate_scale: float32 [4, 28, 8], P('expert', None, 'mp'), may hold values from 0.5 to 2
- up_weight: bfloat16 [4, 3584, 1024], P('expert', None, 'mp'), may hold values from -0.09375 to 0.09375
- up_scale: float32 [4, 28, 8], P('expert', None, 'mp'), may hold values from 0.5 to 2
- down_weight: bfloat16 [4, 1024, 3584], P('expert', 'mp'), may hold values from -0.1875 to 0.1875
- down_scale: float32 [4, 8, 28], P('expert', 'mp'), may hold values from 0.5 to 2
Outputs:
- mixed: bfloat16 [1024, 3584], P(('groups', 'expert'), 'mp'), parts along dimension 0
- hessian: float32 [8, 1024, 1024], P(('groups', 'expert'), 'mp'), parts along dimension 0
There are 2 independent parts, one for each index of `groups`. A program takes and returns all parts, laid end to end along the dimension named above; an argument that names none is the same for every part. Nothing has to cross between parts.
Inputs may be any that keep to these rules, and one draw needn't show every extreme that they name: `route_ids`: each row names 8 different experts of 256, and every expert is named by some row.
All inputs are finite; a program needn't handle non-finite values.
Results may differ from a plain program's by a relative error of at most 0.011.
Values may be sent and summed in bfloat16 or wider, within the bound.
No kernel may reach another device: no remote copies, remote signals or barrier semaphores. Data moves between devices by JAX's collectives and lax.ppermute only.
A program may use at most 64 MiB of HBM per device.

v0:
```python
import jax
import jax.numpy as jnp
from jax import lax
from jax.sharding import PartitionSpec as P

ROUTED_ALL = 256
TOP = 8
QBLK = 128


def dequant(weight, scale):
    row_blocks, col_blocks = scale.shape
    blocks = (
        weight.astype(jnp.float32).reshape(row_blocks, QBLK, col_blocks, QBLK)
        * scale[:, None, :, None]
    )
    return blocks.astype(jnp.bfloat16).reshape(weight.shape)


def route_slots(route_ids, experts, capacity):
    flat = route_ids.reshape(-1)
    onehot = (flat[:, None] == jnp.arange(experts, dtype=jnp.int32)[None, :]).astype(jnp.int32)
    position = jnp.sum((jnp.cumsum(onehot, axis=0) - 1) * onehot, axis=1)
    kept = (flat < experts) & (position < capacity)
    counts = jnp.minimum(jnp.sum(onehot, axis=0), capacity)
    targets = jnp.where(kept, flat * capacity + position, experts * capacity)
    return (targets.reshape(route_ids.shape), counts)


def on_device(
    tokens,
    route_ids,
    route_weights,
    gate_weight,
    gate_scale,
    up_weight,
    up_scale,
    down_weight,
    down_scale,
):
    experts = lax.axis_size("expert")
    capacity = 2 * route_ids.shape[0] * route_ids.shape[1] // ROUTED_ALL
    slot_total = experts * capacity
    targets, counts = route_slots(route_ids, experts, capacity)
    count_column = counts[:, None]
    gate_eff = dequant(gate_weight[0], gate_scale[0])
    up_eff = dequant(up_weight[0], up_scale[0])
    down_eff = dequant(down_weight[0], down_scale[0])
    token_count = route_ids.shape[0]
    source_index = jnp.full((slot_total + 1,), token_count, jnp.int32)
    source_index = source_index.at[targets.reshape(-1)].set(
        jnp.repeat(jnp.arange(token_count, dtype=jnp.int32), TOP)
    )
    source_index = source_index[:slot_total]
    features = lax.all_gather(tokens, "mp", axis=1, tiled=True)
    padded = jnp.concatenate([features, jnp.zeros((1, features.shape[1]), jnp.bfloat16)], axis=0)
    arrived = lax.all_to_all(
        padded[source_index].reshape(experts, capacity, features.shape[1]),
        "expert",
        split_axis=0,
        concat_axis=0,
        tiled=True,
    )
    arrived_counts = lax.all_to_all(count_column, "expert", split_axis=0, concat_axis=0, tiled=True)
    inputs = arrived.reshape(slot_total, features.shape[1])
    gate_proj = jnp.dot(inputs, gate_eff, preferred_element_type=jnp.float32)
    up_proj = jnp.dot(inputs, up_eff, preferred_element_type=jnp.float32)
    hidden = (jax.nn.silu(gate_proj) * up_proj).astype(jnp.bfloat16)
    row_total = jnp.sum(arrived_counts).astype(jnp.float32)
    hessian_rows = lax.dot_general(
        hidden,
        lax.all_gather(hidden, "mp", axis=1, tiled=True),
        (((0,), (0,)), ((), ())),
        preferred_element_type=jnp.float32,
    ) * (2.0 / row_total)
    partial_value = jnp.dot(hidden, down_eff, preferred_element_type=jnp.float32)
    summed = lax.psum_scatter(
        partial_value.astype(jnp.bfloat16), "mp", scatter_dimension=1, tiled=True
    )
    returned = lax.all_to_all(
        summed.reshape(experts, capacity, summed.shape[1]),
        "expert",
        split_axis=0,
        concat_axis=0,
        tiled=True,
    )
    width = returned.shape[2]
    flat_back = jnp.concatenate(
        [returned.reshape(slot_total, width), jnp.zeros((1, width), jnp.bfloat16)], axis=0
    )
    mixed = jnp.zeros((tokens.shape[0], width), jnp.float32)
    for route in range(TOP):
        mixed = mixed + route_weights[:, route : route + 1] * flat_back[targets[:, route]].astype(
            jnp.float32
        )
    return (mixed.astype(jnp.bfloat16), hessian_rows[None])


def solution(mesh):
    placed = (
        P(("groups", "expert"), "mp"),
        P(("groups", "expert"), None),
        P(("groups", "expert"), None),
        P("expert", None, "mp"),
        P("expert", None, "mp"),
        P("expert", None, "mp"),
        P("expert", None, "mp"),
        P("expert", "mp", None),
        P("expert", "mp", None),
    )
    return jax.shard_map(
        on_device,
        mesh=mesh,
        in_specs=placed,
        out_specs=(P(("groups", "expert"), "mp"), P(("groups", "expert"), "mp", None)),
        check_vma=False,
    )
```

profile of v0, /device:TPU:0, one launch (start us, length us, event | category | flops | bytes accessed | tf_op | source)
XLA Modules:
  0.0 115.3 jit_solution(2467194997323305201)
XLA Ops:
  7.2 0.8 copy.29
  8.0 0.1 eq.29
  8.0 0.1 eq.25
  8.1 1.1 reduce-window.6
  9.3 0.2 slice_reduce_fusion
  9.5 0.2 reduce-window.9
  9.7 0.1 add_bitcast_fusion
  9.8 0.1 convert_reduce_fusion
  9.9 0.1 reduce_sum.33
  10.0 0.1 lt.83
  10.1 0.1 mul.163
  10.2 0.1 reshape.239
  10.4 4.3 %scatter_custom_fusion = s32[33]{0:T(128)S(1)} fusion(s32[1024]{0:T(1024)S(1)} %bitcast.90, s32[1024]{0:T(1024)S(1)} %reshape.239, s32[]{:T(128)} %constant.12.clone.1), kind=kCustom, calls=%fused_computation.78 | custom fusion | bytes 136 | tf_op jit(solution)/shard_map/scatter | solution.py:51
  14.7 11.0 %all_gather.6 = bf16[128,3584]{1,0:T(8,128)(2,1)S(1)} all-gather(bf16[128,896]{1,0:T(8,128)(2,1)} %param.9), channel_id=1, replica_groups=mesh['groups'=2,'expert'=4,'mp'=4] {'mp'}, dimensions={1}, use_global_device_ids=true | all-gather | bytes 1146880 | tf_op jit(solution)/shard_map/all_gather | solution.py:55
  25.7 1.4 %gather_fusion = bf16[32,3584]{1,0:T(8,128)(2,1)} fusion(bf16[129,3584]{1,0:T(8,128)(2,1)S(1)} %concatenate.6, s32[1024]{0:T(1024)S(1)} %pad_clamp_fusion.8), kind=kCustom, calls=%fused_computation | custom fusion | bytes 458880 | tf_op jit(solution)/shard_map/gather | solution.py:58
  27.1 4.9 %all-to-all-start = ((bf16[4,8,3584]{2,1,0:T(8,128)(2,1)}), bf16[4,8,3584]{2,1,0:T(8,128)(2,1)S(1)}, u32[]{:S(2)}, u32[]{:S(2)}) async-start(bf16[4,8,3584]{2,1,0:T(8,128)(2,1)} %bitcast.4), calls=%async_computation | async-start | bytes 458752 | tf_op jit(solution)/shard_map/all_to_all | solution.py:57
  32.0 3.1 %reshape.160 = f32[28,128,2,128]{3,2,1,0:T(2,128)} reshape(bf16[1,3584,256]{2,1,0:T(8,128)(2,1)S(1)} %copy-done.1) | data formatting | bytes 5505024 | tf_op jit(solution)/shard_map/convert_element_type | solution.py:14
  35.1 0.1 copy.33
  35.2 4.9 %reshape.161 = f32[28,128,2,128]{3,2,1,0:T(2,128)} reshape(bf16[1,3584,256]{2,1,0:T(8,128)(2,1)} %param.14) | data formatting | bytes 5505024 | tf_op jit(solution)/shard_map/convert_element_type | solution.py:14
  40.1 0.1 copy.34
  40.2 0.7 copy.37
  40.8 0.1 copy.36
  40.9 2.9 %copy.35 = bf16[1,256,3584]{1,2,0:T(8,128)(2,1)S(1)} copy(bf16[1,256,3584]{2,1,0:T(8,128)(2,1)} %param.16) | data formatting | bytes 3670016 | tf_op args[7]
  43.8 5.3 %multiply_convert_fusion.1 = bf16[28,128,2,128]{3,2,1,0:T(2,128)(2,1)} fusion(f32[28,128,2,128]{3,2,1,0:T(2,128)} %reshape.160, f32[28,2]{1,0:T(8,128)S(1)} %copy.33), kind=kLoop, calls=%fused_computation.14 | loop fusion | flops 1835008 | bytes 5505248 | tf_op jit(solution)/shard_map/convert_element_type | solution.py:17
  49.1 3.0 %multiply_convert_fusion = bf16[28,128,2,128]{3,2,1,0:T(2,128)(2,1)} fusion(f32[28,128,2,128]{3,2,1,0:T(2,128)S(1)} %copy-done, f32[28,2]{1,0:T(8,128)S(1)} %copy.34), kind=kLoop, calls=%fused_computation.13 | loop fusion | flops 1835008 | bytes 5505248 | tf_op jit(solution)/shard_map/convert_element_type | solution.py:17
  52.1 0.4 fusion.18
  52.5 5.1 %all-to-all-start.2 = ((s32[4,1,1]{2,1,0:T(1,128)}), s32[4,1,1]{2,1,0:T(1,128)S(1)}, u32[]{:S(2)}, u32[]{:S(2)}) async-start(s32[4,1,1]{2,1,0:T(1,128)} %copy.37), calls=%async_computation.2 | async-start | bytes 4096 | tf_op jit(solution)/shard_map/all_to_all | solution.py:64
  57.6 2.0 %fusion.5 = f32[32,256]{1,0:T(8,128)S(1)} fusion(bf16[448,8,2,128]{3,2,1,0:T(2,128)(2,1)} %bitcast.84, bf16[4,8,3584]{2,1,0:T(8,128)(2,1)S(1)} %all-to-all-done), kind=kOutput, calls=%fused_computation.18 | convolution fusion | flops 58720256 | bytes 2097152 | tf_op jit(solution)/shard_map/dot_general | solution.py:66
  59.7 0.4 fusion.13
  60.1 1.0 mul.173
  61.1 0.7 convolution_convert_fusion
  61.8 1.2 %copy.38 = bf16[32,3584]{0,1:T(8,128)(2,1)} copy(bf16[32,3584]{1,0:T(8,128)(2,1)S(1)} %convolution_convert_fusion) | data formatting | bytes 458752
  63.1 0.6 reduce_sum.35
  64.5 5.2 %all_gather.7 = bf16[32,1024]{1,0:T(8,128)(2,1)S(1)} all-gather(bf16[32,256]{1,0:T(8,128)(2,1)S(1)} %fusion.13), channel_id=1, replica_groups=mesh['groups'=2,'expert'=4,'mp'=4] {'mp'}, dimensions={1}, use_global_device_ids=true | all-gather | bytes 81920 | tf_op jit(solution)/shard_map/all_gather | solution.py:72
  69.7 18.6 %reduce-scatter.4.cloned.1.call-done = bf16[896,32]{1,0:T(8,128)(2,1)} async-done(((bf16[3584,32]{1,0:T(8,128)(2,1)}), bf16[896,32]{1,0:T(8,128)(2,1)}) %reduce-scatter.4.cloned.1.call-update) | async-done | bytes 57360
  88.3 1.7 %copy.39 = bf16[32,896]{1,0:T(8,128)(2,1)} copy(bf16[32,896]{0,1:T(8,128)(2,1)} %bitcast.87) | data formatting | bytes 114688
  90.0 4.6 %all-to-all-start.1 = ((bf16[4,8,896]{2,1,0:T(8,128)(2,1)}), bf16[4,8,896]{2,1,0:T(8,128)(2,1)S(1)}, u32[]{:S(2)}, u32[]{:S(2)}) async-start(bf16[4,8,896]{2,1,0:T(8,128)(2,1)} %bitcast.10), calls=%async_computation.1 | async-start | bytes 114688 | tf_op jit(solution)/shard_map/all_to_all | solution.py:80
  94.6 1.3 %fusion.9 = f32[1,256,1024]{2,1,0:T(8,128)} fusion(bf16[32,256]{1,0:T(8,128)(2,1)S(1)} %fusion.13, bf16[32,1024]{1,0:T(8,128)(2,1)S(1)} %all_gather.7, f32[]{:T(128)S(6)} %div.8), kind=kOutput, calls=%fused_computation.23 | convolution fusion | flops 17039360 | bytes 1130500 | tf_op jit(solution)/shard_map/dot_general | solution.py:70
  95.9 4.4 %all-to-all-done.1 = bf16[4,8,896]{2,1,0:T(8,128)(2,1)S(1)} async-done(((bf16[4,8,896]{2,1,0:T(8,128)(2,1)}), bf16[4,8,896]{2,1,0:T(8,128)(2,1)S(1)}, u32[]{:S(2)}, u32[]{:S(2)}) %all-to-all-start.1) | async-done | bytes 57376 | tf_op jit(solution)/shard_map/all_to_all | solution.py:80
  100.3 0.9 gather_fusion.1
  101.2 0.9 gather_fusion.2
  102.1 0.9 gather_fusion.3
  103.0 0.9 gather_fusion.4
  103.9 0.9 gather_fusion.5
  104.7 0.9 gather_fusion.6
  105.6 0.9 gather_fusion.7
  106.5 0.9 gather_fusion.8
  107.4 1.1 add_convert_fusion
  (32 shorter events, 0.3 us)
Async XLA Ops:
  25.7 6.3 %copy-start.1 = (bf16[1,3584,256]{2,1,0:T(8,128)(2,1)S(1)}, bf16[1,3584,256]{2,1,0:T(8,128)(2,1)}, u32[]{:S(2)}) copy-start(bf16[1,3584,256]{2,1,0:T(8,128)(2,1)} %param.12) | copy-start | bytes 5505028
  27.1 25.4 %all-to-all-start = ((bf16[4,8,3584]{2,1,0:T(8,128)(2,1)}), bf16[4,8,3584]{2,1,0:T(8,128)(2,1)S(1)}, u32[]{:S(2)}, u32[]{:S(2)}) async-start(bf16[4,8,3584]{2,1,0:T(8,128)(2,1)} %bitcast.4), calls=%async_computation | async-start | bytes 458752 | tf_op jit(solution)/shard_map/all_to_all | solution.py:57
  32.0 3.1 %copy-start.4 = (f32[1,28,2]{1,2,0:T(2,128)S(1)}, f32[1,28,2]{1,2,0:T(2,128)}, u32[]{:S(2)}) copy-start(f32[1,28,2]{1,2,0:T(2,128)} %param.13) | copy-start | bytes 676
  35.2 4.9 %copy-start.5 = (f32[1,28,2]{1,2,0:T(2,128)S(1)}, f32[1,28,2]{1,2,0:T(2,128)}, u32[]{:S(2)}) copy-start(f32[1,28,2]{1,2,0:T(2,128)} %param.15) | copy-start | bytes 676
  35.2 5.7 %copy-start.6 = (f32[1,2,28]{2,1,0:T(2,128)S(1)}, f32[1,2,28]{2,1,0:T(2,128)}, u32[]{:S(2)}) copy-start(f32[1,2,28]{2,1,0:T(2,128)} %param.17) | copy-start | bytes 676
  43.8 5.3 %copy-start = (f32[28,128,2,128]{3,2,1,0:T(2,128)S(1)}, f32[28,128,2,128]{3,2,1,0:T(2,128)}, u32[]{:S(2)}) copy-start(f32[28,128,2,128]{3,2,1,0:T(2,128)} %reshape.161) | copy-start | bytes 11010052
  52.5 10.6 %all-to-all-start.2 = ((s32[4,1,1]{2,1,0:T(1,128)}), s32[4,1,1]{2,1,0:T(1,128)S(1)}, u32[]{:S(2)}, u32[]{:S(2)}) async-start(s32[4,1,1]{2,1,0:T(1,128)} %copy.37), calls=%async_computation.2 | async-start | bytes 4096 | tf_op jit(solution)/shard_map/all_to_all | solution.py:64
  57.6 30.8 %reduce-scatter.4.cloned.1.call-start = ((), (), s32[]{:S(2)}) async-start(), calls=%async_computation.4 | async-start | bytes 1146880
  57.6 2.1 %copy-start.2 = (bf16[28,128,2,128]{3,2,1,0:T(2,128)(2,1)S(1)}, bf16[28,128,2,128]{3,2,1,0:T(2,128)(2,1)}, u32[]{:S(2)}) copy-start(bf16[28,128,2,128]{3,2,1,0:T(2,128)(2,1)} %multiply_convert_fusion) | copy-start | bytes 5505028
  61.8 1.3 %copy-start.3 = (f32[128,8]{0,1:T(8,128)S(1)}, f32[128,8]{0,1:T(8,128)}, u32[]{:S(2)}) copy-start(f32[128,8]{0,1:T(8,128)} %param.11) | copy-start | bytes 12292
  90.0 10.3 %all-to-all-start.1 = ((bf16[4,8,896]{2,1,0:T(8,128)(2,1)}), bf16[4,8,896]{2,1,0:T(8,128)(2,1)S(1)}, u32[]{:S(2)}, u32[]{:S(2)}) async-start(bf16[4,8,896]{2,1,0:T(8,128)(2,1)} %bitcast.10), calls=%async_computation.1 | async-start | bytes 114688 | tf_op jit(solution)/shard_map/all_to_all | solution.py:80
Sparse Core Ops, SparseCore 0:
  63.2 25.1 reduce-scatter.3
where the time goes:
time: 116 us; the launch traced here: 115 us
  local copies, waits for them, and re-layouts  30.1 us (26%)
  waiting for transfers between devices  23.1 us (20%)
  blocking collectives  16.2 us (14%)
  between operations  14.9 us (13%)
  starting transfers between devices  14.5 us (12%)
  other arithmetic  12 us (10%)
  matrix products  4.43 us (4%)
    unnamed x2, waiting for transfers between devices  18.6 us
    all_gather x1, blocking collectives, on_device(): features = lax.all_gather(tokens, 'mp', axis=1, tiled=True)  11 us
    convert_element_type x2, other arithmetic, dequant(): return blocks.astype(jnp.bfloat16).reshape(weight.shape)  8.25 us
    convert_element_type x2, local copies, waits for them, and re-layouts, dequant(): weight.astype(jnp.float32).reshape(row_blocks, QBLK, col_blocks, QBLK)  7.98 us
    gather x8, local copies, waits for them, and re-layouts, on_device(): flat_back[targets[:, route]].astype(jnp.float32)  7.04 us
    unnamed x18, local copies, waits for them, and re-layouts  6.62 us
    all_gather x1, blocking collectives, on_device(): lax.all_gather(hidden, 'mp', axis=1, tiled=True)  5.25 us
    all_to_all x1, starting transfers between devices, on_device(): lax.all_to_all(count_column, 'expert', split_axis=0, concat_axis=0, tiled...  5.09 us
  transfers between devices with their start and end apart: 4, of which 2 were waited for; matrix products, arithmetic and copies ran while one was open for 24% of the time, Pallas kernels for 0%

commit v1 on v0

--- a/solution.py
+++ b/solution.py
@@ -1,6 +1,10 @@
+import functools
+
 import jax
 import jax.numpy as jnp
 from jax import lax
+from jax.experimental import pallas as pl
+from jax.experimental.pallas import tpu as pltpu
 from jax.sharding import PartitionSpec as P
 
 ROUTED_ALL = 256
@@ -27,7 +31,7 @@
     return (targets.reshape(route_ids.shape), counts)
 
 
-def on_device(
+def on_device_any_mesh(
     tokens,
     route_ids,
     route_weights,
@@ -96,6 +100,241 @@
     return (mixed.astype(jnp.bfloat16), hessian_rows[None])
 
 
+BOTH = ("expert", "mp")
+VMEM = pl.BlockSpec(memory_space=pltpu.VMEM)
+SMEM = pl.BlockSpec(memory_space=pltpu.SMEM)
+F32 = jnp.float32
+BF16 = jnp.bfloat16
+
+
+def swap_cores(value):
+    return lax.ppermute(value, "mp", [(m, m ^ 1) for m in range(4)])
+
+
+def to_chips(value, k):
+    pairs = [(4 * z + m, 4 * (z ^ k) + (m ^ 2 * (m & 1))) for z in range(4) for m in range(4)]
+    if k == 0:
+        pairs = [(a, b) for a, b in pairs if a != b]
+    return lax.ppermute(value, BOTH, pairs)
+
+
+def across(value):
+    return lax.ppermute(value, "mp", [(m, m ^ 2) for m in range(4)])
+
+
+def route_kernel(capacity, ids_ref, weights_ref, tokens_ref, rows_ref, count_ref, coef_ref):
+    z = lax.axis_index("expert")
+    ids, weights = ids_ref[...], weights_ref[...]
+    rows = ids.shape[1]
+    live, weight = [], []
+    for k in range(4):
+        hit = ids == (z ^ k)
+        live.append(jnp.sum(jnp.where(hit, 1.0, 0.0), axis=0, keepdims=True))
+        weight.append(jnp.sum(jnp.where(hit, weights, 0.0), axis=0, keepdims=True))
+    earlier = lax.broadcasted_iota(jnp.int32, (rows, rows), 0) < lax.broadcasted_iota(jnp.int32, (rows, rows), 1)
+    position = jnp.dot(
+        jnp.concatenate(live, axis=0).astype(BF16),
+        jnp.where(earlier, 1.0, 0.0).astype(BF16),
+        preferred_element_type=F32,
+    )
+    slot = lax.broadcasted_iota(jnp.int32, (capacity, rows), 0).astype(F32)
+    chosen = []
+    for k in range(4):
+        kept = (live[k] > 0.5) & (position[k : k + 1] == slot)
+        one = jnp.where(kept, 1.0, 0.0)
+        chosen.append(one)
+        coef_ref[capacity * k : capacity * (k + 1), :] = one * weight[k]
+        total = jnp.minimum(jnp.sum(live[k], axis=1, keepdims=True), float(capacity))
+        count_ref[k] = jnp.broadcast_to(total, count_ref.shape[1:]).astype(BF16)
+    picked = jnp.dot(
+        jnp.concatenate(chosen, axis=0).astype(BF16), tokens_ref[...], preferred_element_type=F32
+    ).astype(BF16)
+    rows_ref[...] = picked.reshape(rows_ref.shape)
+
+
+def expert_kernel(
+    arrived_ref,
+    swapped_ref,
+    gate_ref,
+    gate_scale_ref,
+    up_ref,
+    up_scale_ref,
+    down_ref,
+    down_scale_ref,
+    keep_ref,
+    send_ref,
+    hidden_ref,
+    scaled_ref,
+):
+    m = lax.axis_index("mp")
+    core = m % 2
+    first = m ^ (2 * core)
+    slots, width = scaled_ref.shape[0] // 4, scaled_ref.shape[1]
+    blocks = width // QBLK
+    half = gate_ref.shape[1] // 2
+    gate = jnp.zeros((2 * slots, 2 * half), F32)
+    up = jnp.zeros((2 * slots, 2 * half), F32)
+    order = (first, first ^ 1, first ^ 3, first ^ 2)
+    for quarter, share in enumerate(order):
+        source = arrived_ref if quarter < 2 else swapped_ref
+        for block in range(blocks):
+            lanes = slice((quarter % 2) * width + block * QBLK, (quarter % 2) * width + (block + 1) * QBLK)
+            x = source[:, :, lanes].reshape(slots, QBLK).astype(F32)
+            at = share * blocks + block
+            into = slice(block * QBLK, (block + 1) * QBLK)
+            scaled_ref[0 * slots : 1 * slots, into] = (x * gate_scale_ref[0, at]).astype(BF16)
+            scaled_ref[1 * slots : 2 * slots, into] = (x * gate_scale_ref[1, at]).astype(BF16)
+            scaled_ref[2 * slots : 3 * slots, into] = (x * up_scale_ref[0, at]).astype(BF16)
+            scaled_ref[3 * slots : 4 * slots, into] = (x * up_scale_ref[1, at]).astype(BF16)
+        depth = pl.ds(pl.multiple_of(share * width, width), width)
+        gate += jnp.dot(scaled_ref[: 2 * slots, :], gate_ref[depth, :], preferred_element_type=F32)
+        up += jnp.dot(scaled_ref[2 * slots :, :], up_ref[depth, :], preferred_element_type=F32)
+    parts = []
+    for i in range(2):
+        g = gate[i * slots : (i + 1) * slots, i * half : (i + 1) * half]
+        u = up[i * slots : (i + 1) * slots, i * half : (i + 1) * half]
+        parts.append((g / (1.0 + jnp.exp(-g)) * u).astype(BF16))
+    hidden_ref[...] = jnp.concatenate(parts, axis=1)
+    send_ref[:, 2 * width :] = hidden_ref[...]
+    none = jnp.zeros_like(parts[0])
+    stacked = jnp.concatenate(
+        [jnp.concatenate([parts[0], none], axis=1), jnp.concatenate([none, parts[1]], axis=1)], axis=0
+    )
+    for out_ref, shares in ((send_ref, (first ^ 3, first ^ 2)), (keep_ref, (first, first ^ 1))):
+        for part, share in enumerate(shares):
+            for block in range(0, blocks, 7):
+                size = min(7, blocks - block)
+                lanes = pl.ds(pl.multiple_of(share * width + block * QBLK, QBLK), size * QBLK)
+                both = jnp.dot(stacked, down_ref[:, lanes], preferred_element_type=F32)
+                for i in range(size):
+                    at = share * blocks + block + i
+                    cut = slice(i * QBLK, (i + 1) * QBLK)
+                    value = both[:slots, cut] * down_scale_ref[0, at] + both[slots:, cut] * down_scale_ref[1, at]
+                    into = part * width + (block + i) * QBLK
+                    out_ref[:, into : into + QBLK] = value.astype(BF16)
+
+
+def hessian_kernel(arrived_ref, near_ref, far_ref, out_ref):
+    m = lax.axis_index("mp")
+    width = out_ref.shape[0]
+    counts = arrived_ref[:, :, arrived_ref.shape[2] - QBLK :].astype(F32)
+    factor = 2.0 / jnp.sum(counts[:, 0, :1], axis=0, keepdims=True)
+    own = near_ref[:, :width]
+    for share, ref, at in ((m, near_ref, 0), (m ^ 1, near_ref, 1), (m ^ 2, far_ref, 0), (m ^ 3, far_ref, 1)):
+        other = ref[:, at * width : (at + 1) * width]
+        block = lax.dot_general(own, other, (((0,), (0,)), ((), ())), preferred_element_type=F32)
+        out_ref[:, pl.ds(pl.multiple_of(share * width, width), width)] = block * factor
+
+
+def combine_kernel(coef_ref, near_ref, far_ref, out_ref):
+    slots, width = coef_ref.shape[0], out_ref.shape[1]
+    result = (near_ref[:, :width].astype(F32) + far_ref[...].astype(F32)).astype(BF16)
+    coef = coef_ref[...]
+    terms = []
+    for _ in range(3):
+        terms.append(coef.astype(BF16))
+        coef = coef - terms[-1].astype(F32)
+    out = lax.dot_general(
+        jnp.concatenate(terms, axis=0),
+        jnp.concatenate([result] * 3, axis=0),
+        (((0,), (0,)), ((), ())),
+        preferred_element_type=F32,
+    )
+    out_ref[...] = out.astype(BF16)
+
+
+def on_device(
+    tokens,
+    route_ids,
+    route_weights,
+    gate_weight,
+    gate_scale,
+    up_weight,
+    up_scale,
+    down_weight,
+    down_scale,
+):
+    rows, width = tokens.shape
+    capacity = 2 * rows * TOP // ROUTED_ALL
+    slots = 4 * capacity
+    hidden_width = gate_weight.shape[2]
+    shape = jax.ShapeDtypeStruct
+    params = pltpu.CompilerParams(vmem_limit_bytes=24 * 1024 * 1024)
+    on_core_one = lax.axis_index("mp") % 2 == 1
+
+    picked, counts, coef = pl.pallas_call(
+        functools.partial(route_kernel, capacity),
+        out_shape=(
+            shape((4, capacity, width), BF16),
+            shape((4, capacity, QBLK), BF16),
+            shape((slots, rows), F32),
+        ),
+        in_specs=[VMEM] * 3,
+        out_specs=(VMEM,) * 3,
+        compiler_params=params,
+        name="route",
+    )(route_ids.T, route_weights.T, tokens)
+
+    message = jnp.concatenate([picked, swap_cores(picked), counts], axis=2)
+    got = [to_chips(message[k], k) for k in range(4)]
+    got[0] = jnp.where(on_core_one, got[0], message[0])
+    arrived = jnp.stack(got)
+    swapped = swap_cores(arrived[:, :, : 2 * width])
+
+    keep, send, hidden = pl.pallas_call(
+        expert_kernel,
+        out_shape=(
+            shape((slots, 2 * width), BF16),
+            shape((slots, 2 * width + hidden_width), BF16),
+            shape((slots, hidden_width), BF16),
+        ),
+        in_specs=[VMEM, VMEM, VMEM, SMEM, VMEM, SMEM, VMEM, SMEM],
+        out_specs=(VMEM,) * 3,
+        scratch_shapes=[pltpu.VMEM((4 * slots, width), BF16)],
+        compiler_params=params,
+        name="expert",
+    )(
+        arrived,
+        swapped,
+        gate_weight[0],
+        gate_scale[0].T,
+        up_weight[0],
+        up_scale[0].T,
+        down_weight[0],
+        down_scale[0],
+    )
+
+    sent = swap_cores(send)
+    summed = (keep.astype(F32) + sent[:, : 2 * width].astype(F32)).astype(BF16).reshape(4, capacity, 2 * width)
+    near = jnp.concatenate([hidden, sent[:, 2 * width :]], axis=1)
+    near_blocks = near.reshape(4, capacity, 2 * hidden_width)
+    message = jnp.concatenate([summed[0]] + [near_blocks[k] for k in range(4)], axis=1)
+    crossed = across(message)
+    far = crossed[:, 2 * width :].reshape(capacity, 4, 2 * hidden_width).swapaxes(0, 1).reshape(slots, 2 * hidden_width)
+    back = [jnp.where(on_core_one, crossed[:, : 2 * width], summed[0])]
+    back += [to_chips(summed[k], k) for k in range(1, 4)]
+    back = jnp.concatenate(back, axis=0)
+
+    hessian = pl.pallas_call(
+        hessian_kernel,
+        out_shape=shape((hidden_width, 4 * hidden_width), F32),
+        in_specs=[VMEM] * 3,
+        out_specs=VMEM,
+        compiler_params=params,
+        name="hessian",
+    )(arrived, near, far)
+
+    mixed = pl.pallas_call(
+        combine_kernel,
+        out_shape=shape((rows, width), BF16),
+        in_specs=[VMEM] * 3,
+        out_specs=VMEM,
+        compiler_params=params,
+        name="combine",
+    )(coef, back, swap_cores(back[:, width:]))
+    return mixed, hessian[None]
+
+
 def solution(mesh):
     placed = (
         P(("groups", "expert"), "mp"),
@@ -108,8 +347,9 @@
         P("expert", "mp", None),
         P("expert", "mp", None),
     )
+    two_level = mesh.shape["expert"] == 4 and mesh.shape["mp"] == 4
     return jax.shard_map(
-        on_device,
+        on_device if two_level else on_device_any_mesh,
         mesh=mesh,
         in_specs=placed,
         out_specs=(P(("groups", "expert"), "mp"), P(("groups", "expert"), "mp", None)),

time: 116 us -> 42.2 us (0.36)
  local copies, waits for them, and re-layouts: 30.1 us -> 8.9 us
  blocking collectives: 16.2 us -> 0 us
  between operations: 14.9 us -> 0.78 us
  other arithmetic: 12 us -> 0.11 us
  waiting for transfers between devices: 23.1 us -> 12.2 us
  matrix products: 4.43 us -> 0 us
  Pallas kernels: 0 us -> 4.3 us
    unnamed x2 -> x0, waiting for transfers between devices: 18.6 us -> none
    all_gather x2 -> x0, blocking collectives: 16.2 us -> none  [the longest x1 11 us: on_device(): features = lax.all_gather(tokens, 'mp', axis=1, tiled=True)]
    ppermute x0 -> x12, starting transfers between devices: none -> 15.6 us  [the longest x7 10.8 us: to_chips(): return lax.ppermute(value, BOTH, pairs)]
    all_to_all x3 -> x0, starting transfers between devices: 14.5 us -> none  [the longest x1 5.09 us: on_device(): lax.all_to_all(count_column, 'expert', split_axis=0, concat_axis=0, tiled...]
    ppermute x0 -> x12, waiting for transfers between devices: none -> 12.2 us  [the longest x7 6.6 us: to_chips(): return lax.ppermute(value, BOTH, pairs)]
    convert_element_type x4 -> x1, other arithmetic: 9.37 us -> 0.03 us  [on_device(): (keep.astype(F32) + sent[:, :2 * width].astype(F32)).astype(BF16)]
    gather x9 -> x0, local copies, waits for them, and re-layouts: 8.42 us -> none  [the longest x8 7.04 us: on_device(): flat_back[targets[:, route]].astype(jnp.float32)]
    convert_element_type x2 -> x0, local copies, waits for them, and re-layouts: 7.98 us -> none  [dequant(): weight.astype(jnp.float32).reshape(row_blocks, QBLK, col_blocks, QBLK)]
  transfers between devices with their start and end apart: 4 -> 12, of which waited for: 2 -> 9; matrix products, arithmetic and copies ran while one was open for 24% -> 0% of each run, Pallas kernels for 0% -> 3%
where the time goes in v1:
time: 42.2 us; the launch traced here: 41.9 us
  starting transfers between devices  15.6 us (37%)
  waiting for transfers between devices  12.2 us (29%)
  local copies, waits for them, and re-layouts  8.9 us (21%)
  Pallas kernels  4.3 us (10%)
  between operations  0.78 us (2%)
    ppermute x7, starting transfers between devices, to_chips(): return lax.ppermute(value, BOTH, pairs)  10.8 us
    unnamed x21, local copies, waits for them, and re-layouts  8.86 us
    ppermute x7, waiting for transfers between devices, to_chips(): return lax.ppermute(value, BOTH, pairs)  6.6 us
    ppermute x4, starting transfers between devices, swap_cores(): return lax.ppermute(value, 'mp', [(m, m ^ 1) for m in range(4)])  3.25 us
    ppermute x4, waiting for transfers between devices, swap_cores(): return lax.ppermute(value, 'mp', [(m, m ^ 1) for m in range(4)])  2.85 us
    ppermute x1, waiting for transfers between devices, across(): return lax.ppermute(value, 'mp', [(m, m ^ 2) for m in range(4)])  2.76 us
    pallas_call x1, Pallas kernels, on_device(): pl.pallas_call(expert_kernel, out_shape=(shape((slots, 2 * width), BF16),...  1.8 us
    ppermute x1, starting transfers between devices, across(): return lax.ppermute(value, 'mp', [(m, m ^ 2) for m in range(4)])  1.57 us
  transfers between devices with their start and end apart: 12, of which 9 were waited for; matrix products, arithmetic and copies ran while one was open for 0% of the time, Pallas kernels for 3%

profile of v1, /device:TPU:0, one launch (start us, length us, event | category | flops | bytes accessed | tf_op | source)
XLA Modules:
  0.0 41.9 jit_solution(12995423734192269456)
XLA Ops:
  0.6 0.0 copy-start.3
  0.6 0.9 %copy-done.3 = bf16[128,896]{1,0:T(8,128)(2,1)S(1)} copy-done((bf16[128,896]{1,0:T(8,128)(2,1)S(1)}, bf16[128,896]{1,0:T(8,128)(2,1)}, u32[]{:S(2)}) %copy-start.3) | copy-done | bytes 229400
  1.6 0.0 copy-start.4
  1.6 0.7 %copy-done.4 = s32[128,8]{0,1:T(8,128)S(1)} copy-done((s32[128,8]{0,1:T(8,128)S(1)}, s32[128,8]{0,1:T(8,128)}, u32[]{:S(2)}) %copy-start.4) | copy-done | bytes 4120
  2.3 0.0 copy-start.5
  2.3 0.7 %copy-done.5 = f32[128,8]{0,1:T(8,128)S(1)} copy-done((f32[128,8]{0,1:T(8,128)S(1)}, f32[128,8]{0,1:T(8,128)}, u32[]{:S(2)}) %copy-start.5) | copy-done | bytes 4120
  2.9 0.3 route.1
  3.2 0.5 %collective-permute-start = (bf16[4,8,896]{2,1,0:T(8,128)(2,1)S(1)}, bf16[4,8,896]{2,1,0:T(8,128)(2,1)S(1)}, u32[]{:S(2)}, u32[]{:S(2)}) collective-permute-start(bf16[4,8,896]{2,1,0:T(8,128)(2,1)S(1)} %get-tuple-element.9), channel_id=1, source_target_pairs={{0,1},{1,0},{2,3},{3,2},{4,5},{5,4},{6,7},{7,6},{8,9},{9,8},{10,11... | collective-permute-start | bytes 172040 | tf_op jit(solution)/shard_map/ppermute | solution.py:111
  3.7 0.9 %collective-permute-done = bf16[4,8,896]{2,1,0:T(8,128)(2,1)S(1)} collective-permute-done((bf16[4,8,896]{2,1,0:T(8,128)(2,1)S(1)}, bf16[4,8,896]{2,1,0:T(8,128)(2,1)S(1)}, u32[]{:S(2)}, u32[]{:S(2)}) %collective-permute-start) | collective-permute-done | bytes 57376 | tf_op jit(solution)/shard_map/ppermute | solution.py:111
  4.7 0.7 %collective-permute-start.1 = (bf16[8,1920]{1,0:T(8,128)(2,1)S(1)}, bf16[8,1920]{1,0:T(8,128)(2,1)S(1)}, u32[]{:S(2)}, u32[]{:S(2)}) collective-permute-start(bf16[8,1920]{1,0:T(8,128)(2,1)S(1)} %get-tuple-element.14), channel_id=1, source_target_pairs={{1,3},{3,1},{5,7},{7,5},{9,11},{11,9},{13,15},{15,13},{17,19},{19,... | collective-permute-start | bytes 92168 | tf_op jit(solution)/shard_map/ppermute | solution.py:118
  5.3 5.0 %collective-permute-start.4 = (bf16[8,1920]{1,0:T(8,128)(2,1)S(1)}, bf16[8,1920]{1,0:T(8,128)(2,1)S(1)}, u32[]{:S(2)}, u32[]{:S(2)}) collective-permute-start(bf16[8,1920]{1,0:T(8,128)(2,1)S(1)} %get-tuple-element.15), channel_id=1, source_target_pairs={{0,12},{1,15},{2,14},{3,13},{4,8},{5,11},{6,10},{7,9},{8,4},{9,7},... | collective-permute-start | bytes 92168 | tf_op jit(solution)/shard_map/ppermute | solution.py:118
  10.4 0.0 collective-permute-start.3
  10.4 0.6 %collective-permute-start.2 = (bf16[8,1920]{1,0:T(8,128)(2,1)S(1)}, bf16[8,1920]{1,0:T(8,128)(2,1)S(1)}, u32[]{:S(2)}, u32[]{:S(2)}) collective-permute-start(bf16[8,1920]{1,0:T(8,128)(2,1)S(1)} %get-tuple-element.17), channel_id=1, source_target_pairs={{0,4},{1,7},{2,6},{3,5},{4,0},{5,3},{6,2},{7,1},{8,12},{9,15},{10,... | collective-permute-start | bytes 92168 | tf_op jit(solution)/shard_map/ppermute | solution.py:118
  11.0 0.0 collective-permute-done.1
  11.0 1.2 %collective-permute-done.4 = bf16[8,1920]{1,0:T(8,128)(2,1)S(1)} collective-permute-done((bf16[8,1920]{1,0:T(8,128)(2,1)S(1)}, bf16[8,1920]{1,0:T(8,128)(2,1)S(1)}, u32[]{:S(2)}, u32[]{:S(2)}) %collective-permute-start.4) | collective-permute-done | bytes 30752 | tf_op jit(solution)/shard_map/ppermute | solution.py:118
  12.2 2.9 %collective-permute-done.3 = bf16[8,1920]{1,0:T(8,128)(2,1)S(1)} collective-permute-done((bf16[8,1920]{1,0:T(8,128)(2,1)S(1)}, bf16[8,1920]{1,0:T(8,128)(2,1)S(1)}, u32[]{:S(2)}, u32[]{:S(2)}) %collective-permute-start.3) | collective-permute-done | bytes 30752 | tf_op jit(solution)/shard_map/ppermute | solution.py:118
  15.2 0.0 collective-permute-done.2
  15.2 2.1 %collective-permute-start.5 = (bf16[4,8,1792]{2,1,0:T(8,128)(2,1)S(1)}, bf16[4,8,1792]{2,1,0:T(8,128)(2,1)S(1)}, u32[]{:S(2)}, u32[]{:S(2)}) collective-permute-start(bf16[4,8,1792]{2,1,0:T(8,128)(2,1)S(1)} %slice.86), channel_id=1, source_target_pairs={{0,1},{1,0},{2,3},{3,2},{4,5},{5,4},{6,7},{7,6},{8,9},{9,8},{10,11... | collective-permute-start | bytes 344072 | tf_op jit(solution)/shard_map/ppermute | solution.py:111
  17.3 1.0 %collective-permute-done.5.swapped_ref = bf16[4,8,1792]{2,1,0:T(8,128)(2,1)S(1)} collective-permute-done((bf16[4,8,1792]{2,1,0:T(8,128)(2,1)S(1)}, bf16[4,8,1792]{2,1,0:T(8,128)(2,1)S(1)}, u32[]{:S(2)}, u32[]{:S(2)}) %collective-permute-start.5) | collective-permute-done | bytes 114720 | tf_op jit(solution)/shard_map/ppermute | solution.py:111
  18.3 0.0 copy-start
  18.3 1.5 %copy-done = bf16[1,3584,256]{2,1,0:T(8,128)(2,1)S(1)} copy-done((bf16[1,3584,256]{2,1,0:T(8,128)(2,1)S(1)}, bf16[1,3584,256]{2,1,0:T(8,128)(2,1)}, u32[]{:S(2)}) %copy-start) | copy-done | bytes 1835032
  19.8 0.0 copy-start.1
  19.8 1.5 %copy-done.1 = bf16[1,3584,256]{2,1,0:T(8,128)(2,1)S(1)} copy-done((bf16[1,3584,256]{2,1,0:T(8,128)(2,1)S(1)}, bf16[1,3584,256]{2,1,0:T(8,128)(2,1)}, u32[]{:S(2)}) %copy-start.1) | copy-done | bytes 1835032
  21.3 0.0 copy-start.2
  21.3 1.5 %copy-done.2 = bf16[1,256,3584]{2,1,0:T(8,128)(2,1)S(1)} copy-done((bf16[1,256,3584]{2,1,0:T(8,128)(2,1)S(1)}, bf16[1,256,3584]{2,1,0:T(8,128)(2,1)}, u32[]{:S(2)}) %copy-start.2) | copy-done | bytes 1835032
  22.8 0.0 copy-start.6
  22.8 0.7 %copy-done.6 = f32[1,28,2]{1,2,0:T(2,128)S(1)} copy-done((f32[1,28,2]{1,2,0:T(2,128)S(1)}, f32[1,28,2]{1,2,0:T(2,128)}, u32[]{:S(2)}) %copy-start.6) | copy-done | bytes 248
  23.5 0.0 copy-start.7
  23.5 0.7 %copy-done.7 = f32[1,28,2]{1,2,0:T(2,128)S(1)} copy-done((f32[1,28,2]{1,2,0:T(2,128)S(1)}, f32[1,28,2]{1,2,0:T(2,128)}, u32[]{:S(2)}) %copy-start.7) | copy-done | bytes 248
  24.1 0.0 copy-start.8
  24.1 0.7 %copy-done.8 = f32[1,2,28]{2,1,0:T(2,128)S(1)} copy-done((f32[1,2,28]{2,1,0:T(2,128)S(1)}, f32[1,2,28]{2,1,0:T(2,128)}, u32[]{:S(2)}) %copy-start.8) | copy-done | bytes 248
  24.8 1.8 %expert.1 = (bf16[32,1792]{1,0:T(8,128)(2,1)S(1)}, bf16[32,2048]{1,0:T(8,128)(2,1)S(1)}, bf16[32,256]{1,0:T(8,128)(2,1)S(1)}) custom-call(bf16[4,8,1920]{2,1,0:T(8,128)(2,1)S(1)} %pad_maximum_fusion.arrived_ref, bf16[4,8,1792]{2,1,0:T(8,128)(2,1)S(1)} %collective-permute-done.5.swapped_ref, bf16[3584,256]{1,0:T(8,128)(2,1)S(1)} %bitcast.33, ...), custom_call_target="tpu_custom_call" | custom-call | tf_op jit(solution)/shard_map/expert/pallas_call | solution.py:284
  26.6 0.4 %collective-permute-start.6 = (bf16[32,2048]{1,0:T(8,128)(2,1)S(1)}, bf16[32,2048]{1,0:T(8,128)(2,1)S(1)}, u32[]{:S(2)}, u32[]{:S(2)}) collective-permute-start(bf16[32,2048]{1,0:T(8,128)(2,1)S(1)} %get-tuple-element.12), channel_id=1, source_target_pairs={{0,1},{1,0},{2,3},{3,2},{4,5},{5,4},{6,7},{7,6},{8,9},{9,8},{10,11... | collective-permute-start | bytes 393224 | tf_op jit(solution)/shard_map/ppermute | solution.py:111
  27.0 1.0 %collective-permute-done.6 = bf16[32,2048]{1,0:T(8,128)(2,1)S(1)} collective-permute-done((bf16[32,2048]{1,0:T(8,128)(2,1)S(1)}, bf16[32,2048]{1,0:T(8,128)(2,1)S(1)}, u32[]{:S(2)}, u32[]{:S(2)}) %collective-permute-start.6) | collective-permute-done | bytes 131104 | tf_op jit(solution)/shard_map/ppermute | solution.py:111
  28.1 1.6 %collective-permute-start.7 = (bf16[8,3840]{1,0:T(8,128)(2,1)S(1)}, bf16[8,3840]{1,0:T(8,128)(2,1)S(1)}, u32[]{:S(2)}, u32[]{:S(2)}) collective-permute-start(bf16[8,3840]{1,0:T(8,128)(2,1)S(1)} %constant_dynamic-update-slice_fusion.3), channel_id=1, source_target_pairs={{0,2},{1,3},{2,0},{3,1},{4,6},{5,7},{6,4},{7,5},{8,10},{9,11},{10,... | collective-permute-start | bytes 184328 | tf_op jit(solution)/shard_map/ppermute | solution.py:122
  29.7 2.8 %collective-permute-done.7 = bf16[8,3840]{1,0:T(8,128)(2,1)S(1)} collective-permute-done((bf16[8,3840]{1,0:T(8,128)(2,1)S(1)}, bf16[8,3840]{1,0:T(8,128)(2,1)S(1)}, u32[]{:S(2)}, u32[]{:S(2)}) %collective-permute-start.7) | collective-permute-done | bytes 61472 | tf_op jit(solution)/shard_map/ppermute | solution.py:122
  32.5 1.7 %collective-permute-start.10 = (bf16[8,1792]{1,0:T(8,128)(2,1)S(1)}, bf16[8,1792]{1,0:T(8,128)(2,1)S(1)}, u32[]{:S(2)}, u32[]{:S(2)}) collective-permute-start(bf16[8,1792]{1,0:T(8,128)(2,1)S(1)} %get-tuple-element.19), channel_id=1, source_target_pairs={{0,12},{1,15},{2,14},{3,13},{4,8},{5,11},{6,10},{7,9},{8,4},{9,7},... | collective-permute-start | bytes 86024 | tf_op jit(solution)/shard_map/ppermute | solution.py:118
  34.2 1.1 %collective-permute-start.9 = (bf16[8,1792]{1,0:T(8,128)(2,1)S(1)}, bf16[8,1792]{1,0:T(8,128)(2,1)S(1)}, u32[]{:S(2)}, u32[]{:S(2)}) collective-permute-start(bf16[8,1792]{1,0:T(8,128)(2,1)S(1)} %get-tuple-element.20), channel_id=1, source_target_pairs={{0,8},{1,11},{2,10},{3,9},{4,12},{5,15},{6,14},{7,13},{8,0},{9,3},... | collective-permute-start | bytes 86024 | tf_op jit(solution)/shard_map/ppermute | solution.py:118
  35.3 1.6 %collective-permute-start.8 = (bf16[8,1792]{1,0:T(8,128)(2,1)S(1)}, bf16[8,1792]{1,0:T(8,128)(2,1)S(1)}, u32[]{:S(2)}, u32[]{:S(2)}) collective-permute-start(bf16[8,1792]{1,0:T(8,128)(2,1)S(1)} %get-tuple-element.21), channel_id=1, source_target_pairs={{0,4},{1,7},{2,6},{3,5},{4,0},{5,3},{6,2},{7,1},{8,12},{9,15},{10,... | collective-permute-start | bytes 86024 | tf_op jit(solution)/shard_map/ppermute | solution.py:118
  36.9 1.4 %collective-permute-done.10 = bf16[8,1792]{1,0:T(8,128)(2,1)S(1)} collective-permute-done((bf16[8,1792]{1,0:T(8,128)(2,1)S(1)}, bf16[8,1792]{1,0:T(8,128)(2,1)S(1)}, u32[]{:S(2)}, u32[]{:S(2)}) %collective-permute-start.10) | collective-permute-done | bytes 28704 | tf_op jit(solution)/shard_map/ppermute | solution.py:118
  38.4 0.6 %collective-permute-done.9 = bf16[8,1792]{1,0:T(8,128)(2,1)S(1)} collective-permute-done((bf16[8,1792]{1,0:T(8,128)(2,1)S(1)}, bf16[8,1792]{1,0:T(8,128)(2,1)S(1)}, u32[]{:S(2)}, u32[]{:S(2)}) %collective-permute-start.9) | collective-permute-done | bytes 28704 | tf_op jit(solution)/shard_map/ppermute | solution.py:118
  39.0 0.4 collective-permute-done.8
  39.4 0.2 collective-permute-start.11
  39.6 1.3 %hessian.1 = f32[256,1024]{1,0:T(8,128)} custom-call(bf16[4,8,1920]{2,1,0:T(8,128)(2,1)S(1)} %pad_maximum_fusion.arrived_ref, bf16[32,512]{1,0:T(8,128)(2,1)S(1)} %pad_maximum_fusion.2.near_ref, bf16[32,512]{1,0:T(8,128)(2,1)S(1)} %bitcast.36), custom_call_target="tpu_custom_call" | custom-call | tf_op jit(solution)/shard_map/hessian/pallas_call | solution.py:318
  40.9 0.0 collective-permute-done.11.far_ref
  40.9 0.9 %combine.1 = bf16[128,896]{1,0:T(8,128)(2,1)} custom-call(f32[32,128]{1,0:T(8,128)S(1)} %get-tuple-element.8.coef_ref, bf16[32,1792]{1,0:T(8,128)(2,1)S(1)} %pad_maximum_fusion.1.near_ref, bf16[32,896]{1,0:T(8,128)(2,1)S(1)} %collective-permute-done.11.far_ref), custom_call_target="tpu_custom_call" | custom-call | tf_op jit(solution)/shard_map/combine/pallas_call | solution.py:327
  (19 shorter events, 0.2 us)
Async XLA Ops:
  0.6 0.9 %copy-start.3 = (bf16[128,896]{1,0:T(8,128)(2,1)S(1)}, bf16[128,896]{1,0:T(8,128)(2,1)}, u32[]{:S(2)}) copy-start(bf16[128,896]{1,0:T(8,128)(2,1)} %tokens_ref.1) | copy-start | bytes 688132
  1.6 0.7 %copy-start.4 = (s32[128,8]{0,1:T(8,128)S(1)}, s32[128,8]{0,1:T(8,128)}, u32[]{:S(2)}) copy-start(s32[128,8]{0,1:T(8,128)} %param.10) | copy-start | bytes 12292
  2.3 0.7 %copy-start.5 = (f32[128,8]{0,1:T(8,128)S(1)}, f32[128,8]{0,1:T(8,128)}, u32[]{:S(2)}) copy-start(f32[128,8]{0,1:T(8,128)} %param.11) | copy-start | bytes 12292
  3.2 1.4 %collective-permute-start = (bf16[4,8,896]{2,1,0:T(8,128)(2,1)S(1)}, bf16[4,8,896]{2,1,0:T(8,128)(2,1)S(1)}, u32[]{:S(2)}, u32[]{:S(2)}) collective-permute-start(bf16[4,8,896]{2,1,0:T(8,128)(2,1)S(1)} %get-tuple-element.9), channel_id=1, source_target_pairs={{0,1},{1,0},{2,3},{3,2},{4,5},{5,4},{6,7},{7,6},{8,9},{9,8},{10,11... | collective-permute-start | bytes 172040 | tf_op jit(solution)/shard_map/ppermute | solution.py:111
  4.7 6.3 %collective-permute-start.1 = (bf16[8,1920]{1,0:T(8,128)(2,1)S(1)}, bf16[8,1920]{1,0:T(8,128)(2,1)S(1)}, u32[]{:S(2)}, u32[]{:S(2)}) collective-permute-start(bf16[8,1920]{1,0:T(8,128)(2,1)S(1)} %get-tuple-element.14), channel_id=1, source_target_pairs={{1,3},{3,1},{5,7},{7,5},{9,11},{11,9},{13,15},{15,13},{17,19},{19,... | collective-permute-start | bytes 92168 | tf_op jit(solution)/shard_map/ppermute | solution.py:118
  5.3 6.9 %collective-permute-start.4 = (bf16[8,1920]{1,0:T(8,128)(2,1)S(1)}, bf16[8,1920]{1,0:T(8,128)(2,1)S(1)}, u32[]{:S(2)}, u32[]{:S(2)}) collective-permute-start(bf16[8,1920]{1,0:T(8,128)(2,1)S(1)} %get-tuple-element.15), channel_id=1, source_target_pairs={{0,12},{1,15},{2,14},{3,13},{4,8},{5,11},{6,10},{7,9},{8,4},{9,7},... | collective-permute-start | bytes 92168 | tf_op jit(solution)/shard_map/ppermute | solution.py:118
  10.4 4.8 %collective-permute-start.3 = (bf16[8,1920]{1,0:T(8,128)(2,1)S(1)}, bf16[8,1920]{1,0:T(8,128)(2,1)S(1)}, u32[]{:S(2)}, u32[]{:S(2)}) collective-permute-start(bf16[8,1920]{1,0:T(8,128)(2,1)S(1)} %get-tuple-element.16), channel_id=1, source_target_pairs={{0,8},{1,11},{2,10},{3,9},{4,12},{5,15},{6,14},{7,13},{8,0},{9,3},... | collective-permute-start | bytes 92168 | tf_op jit(solution)/shard_map/ppermute | solution.py:118
  10.4 4.8 %collective-permute-start.2 = (bf16[8,1920]{1,0:T(8,128)(2,1)S(1)}, bf16[8,1920]{1,0:T(8,128)(2,1)S(1)}, u32[]{:S(2)}, u32[]{:S(2)}) collective-permute-start(bf16[8,1920]{1,0:T(8,128)(2,1)S(1)} %get-tuple-element.17), channel_id=1, source_target_pairs={{0,4},{1,7},{2,6},{3,5},{4,0},{5,3},{6,2},{7,1},{8,12},{9,15},{10,... | collective-permute-start | bytes 92168 | tf_op jit(solution)/shard_map/ppermute | solution.py:118
  15.2 3.1 %collective-permute-start.5 = (bf16[4,8,1792]{2,1,0:T(8,128)(2,1)S(1)}, bf16[4,8,1792]{2,1,0:T(8,128)(2,1)S(1)}, u32[]{:S(2)}, u32[]{:S(2)}) collective-permute-start(bf16[4,8,1792]{2,1,0:T(8,128)(2,1)S(1)} %slice.86), channel_id=1, source_target_pairs={{0,1},{1,0},{2,3},{3,2},{4,5},{5,4},{6,7},{7,6},{8,9},{9,8},{10,11... | collective-permute-start | bytes 344072 | tf_op jit(solution)/shard_map/ppermute | solution.py:111
  18.3 1.5 %copy-start = (bf16[1,3584,256]{2,1,0:T(8,128)(2,1)S(1)}, bf16[1,3584,256]{2,1,0:T(8,128)(2,1)}, u32[]{:S(2)}) copy-start(bf16[1,3584,256]{2,1,0:T(8,128)(2,1)} %param.12) | copy-start | bytes 5505028
  19.8 1.5 %copy-start.1 = (bf16[1,3584,256]{2,1,0:T(8,128)(2,1)S(1)}, bf16[1,3584,256]{2,1,0:T(8,128)(2,1)}, u32[]{:S(2)}) copy-start(bf16[1,3584,256]{2,1,0:T(8,128)(2,1)} %param.14) | copy-start | bytes 5505028
  21.3 1.5 %copy-start.2 = (bf16[1,256,3584]{2,1,0:T(8,128)(2,1)S(1)}, bf16[1,256,3584]{2,1,0:T(8,128)(2,1)}, u32[]{:S(2)}) copy-start(bf16[1,256,3584]{2,1,0:T(8,128)(2,1)} %param.16) | copy-start | bytes 5505028
  22.8 0.7 %copy-start.6 = (f32[1,28,2]{1,2,0:T(2,128)S(1)}, f32[1,28,2]{1,2,0:T(2,128)}, u32[]{:S(2)}) copy-start(f32[1,28,2]{1,2,0:T(2,128)} %param.13) | copy-start | bytes 676
  23.5 0.7 %copy-start.7 = (f32[1,28,2]{1,2,0:T(2,128)S(1)}, f32[1,28,2]{1,2,0:T(2,128)}, u32[]{:S(2)}) copy-start(f32[1,28,2]{1,2,0:T(2,128)} %param.15) | copy-start | bytes 676
  24.1 0.7 %copy-start.8 = (f32[1,2,28]{2,1,0:T(2,128)S(1)}, f32[1,2,28]{2,1,0:T(2,128)}, u32[]{:S(2)}) copy-start(f32[1,2,28]{2,1,0:T(2,128)} %param.17) | copy-start | bytes 676
  26.6 1.4 %collective-permute-start.6 = (bf16[32,2048]{1,0:T(8,128)(2,1)S(1)}, bf16[32,2048]{1,0:T(8,128)(2,1)S(1)}, u32[]{:S(2)}, u32[]{:S(2)}) collective-permute-start(bf16[32,2048]{1,0:T(8,128)(2,1)S(1)} %get-tuple-element.12), channel_id=1, source_target_pairs={{0,1},{1,0},{2,3},{3,2},{4,5},{5,4},{6,7},{7,6},{8,9},{9,8},{10,11... | collective-permute-start | bytes 393224 | tf_op jit(solution)/shard_map/ppermute | solution.py:111
  28.1 4.3 %collective-permute-start.7 = (bf16[8,3840]{1,0:T(8,128)(2,1)S(1)}, bf16[8,3840]{1,0:T(8,128)(2,1)S(1)}, u32[]{:S(2)}, u32[]{:S(2)}) collective-permute-start(bf16[8,3840]{1,0:T(8,128)(2,1)S(1)} %constant_dynamic-update-slice_fusion.3), channel_id=1, source_target_pairs={{0,2},{1,3},{2,0},{3,1},{4,6},{5,7},{6,4},{7,5},{8,10},{9,11},{10,... | collective-permute-start | bytes 184328 | tf_op jit(solution)/shard_map/ppermute | solution.py:122
  32.5 5.9 %collective-permute-start.10 = (bf16[8,1792]{1,0:T(8,128)(2,1)S(1)}, bf16[8,1792]{1,0:T(8,128)(2,1)S(1)}, u32[]{:S(2)}, u32[]{:S(2)}) collective-permute-start(bf16[8,1792]{1,0:T(8,128)(2,1)S(1)} %get-tuple-element.19), channel_id=1, source_target_pairs={{0,12},{1,15},{2,14},{3,13},{4,8},{5,11},{6,10},{7,9},{8,4},{9,7},... | collective-permute-start | bytes 86024 | tf_op jit(solution)/shard_map/ppermute | solution.py:118
  34.2 4.8 %collective-permute-start.9 = (bf16[8,1792]{1,0:T(8,128)(2,1)S(1)}, bf16[8,1792]{1,0:T(8,128)(2,1)S(1)}, u32[]{:S(2)}, u32[]{:S(2)}) collective-permute-start(bf16[8,1792]{1,0:T(8,128)(2,1)S(1)} %get-tuple-element.20), channel_id=1, source_target_pairs={{0,8},{1,11},{2,10},{3,9},{4,12},{5,15},{6,14},{7,13},{8,0},{9,3},... | collective-permute-start | bytes 86024 | tf_op jit(solution)/shard_map/ppermute | solution.py:118
  35.3 4.1 %collective-permute-start.8 = (bf16[8,1792]{1,0:T(8,128)(2,1)S(1)}, bf16[8,1792]{1,0:T(8,128)(2,1)S(1)}, u32[]{:S(2)}, u32[]{:S(2)}) collective-permute-start(bf16[8,1792]{1,0:T(8,128)(2,1)S(1)} %get-tuple-element.21), channel_id=1, source_target_pairs={{0,4},{1,7},{2,6},{3,5},{4,0},{5,3},{6,2},{7,1},{8,12},{9,15},{10,... | collective-permute-start | bytes 86024 | tf_op jit(solution)/shard_map/ppermute | solution.py:118
  39.4 1.5 %collective-permute-start.11 = (bf16[32,896]{1,0:T(8,128)(2,1)S(1)}, bf16[32,896]{1,0:T(8,128)(2,1)S(1)}, u32[]{:S(2)}, u32[]{:S(2)}) collective-permute-start(bf16[32,896]{1,0:T(8,128)(2,1)S(1)} %slice.102), channel_id=1, source_target_pairs={{0,1},{1,0},{2,3},{3,2},{4,5},{5,4},{6,7},{7,6},{8,9},{9,8},{10,11... | collective-permute-start | bytes 172040 | tf_op jit(solution)/shard_map/ppermute | solution.py:111

commit v2 on v1

--- a/solution.py
+++ b/solution.py
@@ -119,10 +119,15 @@
 
 
 def across(value):
-    return lax.ppermute(value, "mp", [(m, m ^ 2) for m in range(4)])
-
-
-def route_kernel(capacity, ids_ref, weights_ref, tokens_ref, rows_ref, count_ref, coef_ref):
+    return lax.ppermute(value, BOTH, [(4 * z + m, 4 * z + (m ^ 2)) for z in range(4) for m in range(4)])
+
+
+def earlier_kernel(out_ref):
+    row, column = (lax.broadcasted_iota(jnp.int32, out_ref.shape, i) for i in range(2))
+    out_ref[...] = jnp.where(row < column, 1.0, 0.0).astype(BF16)
+
+
+def route_kernel(capacity, earlier_ref, ids_ref, weights_ref, tokens_ref, rows_ref, count_ref, coef_ref):
     z = lax.axis_index("expert")
     ids, weights = ids_ref[...], weights_ref[...]
     rows = ids.shape[1]
@@ -131,10 +136,9 @@
         hit = ids == (z ^ k)
         live.append(jnp.sum(jnp.where(hit, 1.0, 0.0), axis=0, keepdims=True))
         weight.append(jnp.sum(jnp.where(hit, weights, 0.0), axis=0, keepdims=True))
-    earlier = lax.broadcasted_iota(jnp.int32, (rows, rows), 0) < lax.broadcasted_iota(jnp.int32, (rows, rows), 1)
     position = jnp.dot(
         jnp.concatenate(live, axis=0).astype(BF16),
-        jnp.where(earlier, 1.0, 0.0).astype(BF16),
+        earlier_ref[...],
         preferred_element_type=F32,
     )
     slot = lax.broadcasted_iota(jnp.int32, (capacity, rows), 0).astype(F32)
@@ -202,26 +206,43 @@
     )
     for out_ref, shares in ((send_ref, (first ^ 3, first ^ 2)), (keep_ref, (first, first ^ 1))):
         for part, share in enumerate(shares):
-            for block in range(0, blocks, 7):
-                size = min(7, blocks - block)
-                lanes = pl.ds(pl.multiple_of(share * width + block * QBLK, QBLK), size * QBLK)
-                both = jnp.dot(stacked, down_ref[:, lanes], preferred_element_type=F32)
-                for i in range(size):
-                    at = share * blocks + block + i
-                    cut = slice(i * QBLK, (i + 1) * QBLK)
-                    value = both[:slots, cut] * down_scale_ref[0, at] + both[slots:, cut] * down_scale_ref[1, at]
-                    into = part * width + (block + i) * QBLK
-                    out_ref[:, into : into + QBLK] = value.astype(BF16)
-
-
-def hessian_kernel(arrived_ref, near_ref, far_ref, out_ref):
+            lanes = pl.ds(pl.multiple_of(share * width, width), width)
+            both = jnp.dot(stacked, down_ref[:, lanes], preferred_element_type=F32)
+            for block in range(blocks):
+                at = share * blocks + block
+                cut = slice(block * QBLK, (block + 1) * QBLK)
+                value = both[:slots, cut] * down_scale_ref[0, at] + both[slots:, cut] * down_scale_ref[1, at]
+                out_ref[:, part * width + block * QBLK : part * width + (block + 1) * QBLK] = value.astype(BF16)
+
+
+def chip_sum_kernel(keep_ref, sent_ref, hidden_ref, message_ref, one_ref, two_ref, three_ref, near_ref):
+    width, hidden_width = keep_ref.shape[1], hidden_ref.shape[1]
+    rows = one_ref.shape[0]
+    for k, out_ref in enumerate((message_ref, one_ref, two_ref, three_ref)):
+        at = slice(k * rows, (k + 1) * rows)
+        both = keep_ref[at, :].astype(F32) + sent_ref[at, :width].astype(F32)
+        out_ref[:, :width] = both.astype(BF16)
+        near = jnp.concatenate([hidden_ref[at, :], sent_ref[at, width:]], axis=1)
+        near_ref[at, :] = near
+        into = width + 2 * k * hidden_width
+        message_ref[:, into : into + 2 * hidden_width] = near
+
+
+def hessian_kernel(arrived_ref, near_ref, crossed_ref, out_ref):
     m = lax.axis_index("mp")
     width = out_ref.shape[0]
     counts = arrived_ref[:, :, arrived_ref.shape[2] - QBLK :].astype(F32)
     factor = 2.0 / jnp.sum(counts[:, 0, :1], axis=0, keepdims=True)
     own = near_ref[:, :width]
-    for share, ref, at in ((m, near_ref, 0), (m ^ 1, near_ref, 1), (m ^ 2, far_ref, 0), (m ^ 3, far_ref, 1)):
-        other = ref[:, at * width : (at + 1) * width]
+    start = crossed_ref.shape[1] - 8 * width
+    far = [crossed_ref[:, start + i * width : start + (i + 1) * width] for i in range(8)]
+    others = (
+        (m, own),
+        (m ^ 1, near_ref[:, width:]),
+        (m ^ 2, jnp.concatenate(far[0::2], axis=0)),
+        (m ^ 3, jnp.concatenate(far[1::2], axis=0)),
+    )
+    for share, other in others:
         block = lax.dot_general(own, other, (((0,), (0,)), ((), ())), preferred_element_type=F32)
         out_ref[:, pl.ds(pl.multiple_of(share * width, width), width)] = block * factor
 
@@ -260,6 +281,15 @@
     hidden_width = gate_weight.shape[2]
     shape = jax.ShapeDtypeStruct
     params = pltpu.CompilerParams(vmem_limit_bytes=24 * 1024 * 1024)
+
+    earlier = pl.pallas_call(
+        earlier_kernel,
+        out_shape=shape((rows, rows), BF16),
+        out_specs=VMEM,
+        compiler_params=params,
+        cost_estimate=pl.CostEstimate(flops=4 * 10**9, bytes_accessed=0, transcendentals=0),
+        name="earlier",
+    )()
     on_core_one = lax.axis_index("mp") % 2 == 1
 
     picked, counts, coef = pl.pallas_call(
@@ -269,13 +299,15 @@
             shape((4, capacity, QBLK), BF16),
             shape((slots, rows), F32),
         ),
-        in_specs=[VMEM] * 3,
+        in_specs=[VMEM] * 4,
         out_specs=(VMEM,) * 3,
         compiler_params=params,
+        cost_estimate=pl.CostEstimate(flops=8 * 10**9, bytes_accessed=0, transcendentals=0),
         name="route",
-    )(route_ids.T, route_weights.T, tokens)
+    )(earlier, route_ids.T, route_weights.T, tokens)
 
     message = jnp.concatenate([picked, swap_cores(picked), counts], axis=2)
+
     got = [to_chips(message[k], k) for k in range(4)]
     got[0] = jnp.where(on_core_one, got[0], message[0])
     arrived = jnp.stack(got)
@@ -304,15 +336,22 @@
         down_scale[0],
     )
 
-    sent = swap_cores(send)
-    summed = (keep.astype(F32) + sent[:, : 2 * width].astype(F32)).astype(BF16).reshape(4, capacity, 2 * width)
-    near = jnp.concatenate([hidden, sent[:, 2 * width :]], axis=1)
-    near_blocks = near.reshape(4, capacity, 2 * hidden_width)
-    message = jnp.concatenate([summed[0]] + [near_blocks[k] for k in range(4)], axis=1)
+    message, *summed, near = pl.pallas_call(
+        chip_sum_kernel,
+        out_shape=(
+            shape((capacity, 2 * width + 8 * hidden_width), BF16),
+            *[shape((capacity, 2 * width), BF16)] * 3,
+            shape((slots, 2 * hidden_width), BF16),
+        ),
+        in_specs=[VMEM] * 3,
+        out_specs=(VMEM,) * 5,
+        compiler_params=params,
+        name="chip_sum",
+    )(keep, swap_cores(send), hidden)
+
     crossed = across(message)
-    far = crossed[:, 2 * width :].reshape(capacity, 4, 2 * hidden_width).swapaxes(0, 1).reshape(slots, 2 * hidden_width)
-    back = [jnp.where(on_core_one, crossed[:, : 2 * width], summed[0])]
-    back += [to_chips(summed[k], k) for k in range(1, 4)]
+    back = [jnp.where(on_core_one, crossed[:, : 2 * width], message[:, : 2 * width])]
+    back += [to_chips(summed[k - 1], k) for k in range(1, 4)]
     back = jnp.concatenate(back, axis=0)
 
     hessian = pl.pallas_call(
@@ -322,7 +361,7 @@
         out_specs=VMEM,
         compiler_params=params,
         name="hessian",
-    )(arrived, near, far)
+    )(arrived, near, crossed)
 
     mixed = pl.pallas_call(
         combine_kernel,

time: 42.2 us -> 35.9 us (0.85)
  local copies, waits for them, and re-layouts: 8.9 us -> 3.99 us
  waiting for transfers between devices: 12.2 us -> 10.7 us
    unnamed x21 -> x20, local copies, waits for them, and re-layouts: 8.86 us -> 3.95 us
    ppermute x1, waiting for transfers between devices: 2.76 us -> 0.01 us  [across(): lax.ppermute(value, BOTH, [(4 * z + m, 4 * z + (m ^ 2)) for z in range(4)...]
    ppermute x7, waiting for transfers between devices: 6.6 us -> 7.9 us  [to_chips(): return lax.ppermute(value, BOTH, pairs)]
    ppermute x4, starting transfers between devices: 3.25 us -> 4.51 us  [swap_cores(): return lax.ppermute(value, 'mp', [(m, m ^ 1) for m in range(4)])]
    ppermute x1, starting transfers between devices: 1.57 us -> 0.62 us  [across(): lax.ppermute(value, BOTH, [(4 * z + m, 4 * z + (m ^ 2)) for z in range(4)...]
  transfers between devices with their start and end apart: 12 -> 12, of which waited for: 9 -> 7; matrix products, arithmetic and copies ran while one was open for 0% -> 0% of each run, Pallas kernels for 3% -> 4%
where the time goes in v2:
time: 35.9 us; the launch traced here: 35.7 us
  starting transfers between devices  15.8 us (44%)
  waiting for transfers between devices  10.7 us (30%)
  Pallas kernels  4.35 us (12%)
  local copies, waits for them, and re-layouts  3.99 us (11%)
  between operations  0.77 us (2%)
    ppermute x7, starting transfers between devices, to_chips(): return lax.ppermute(value, BOTH, pairs)  10.6 us
    ppermute x7, waiting for transfers between devices, to_chips(): return lax.ppermute(value, BOTH, pairs)  7.9 us
    ppermute x4, starting transfers between devices, swap_cores(): return lax.ppermute(value, 'mp', [(m, m ^ 1) for m in range(4)])  4.51 us
    unnamed x20, local copies, waits for them, and re-layouts  3.95 us
    ppermute x4, waiting for transfers between devices, swap_cores(): return lax.ppermute(value, 'mp', [(m, m ^ 1) for m in range(4)])  2.84 us
    pallas_call x1, Pallas kernels, on_device(): pl.pallas_call(expert_kernel, out_shape=(shape((slots, 2 * width), BF16),...  1.79 us
    pallas_call x1, Pallas kernels, on_device(): pl.pallas_call(hessian_kernel, out_shape=shape((hidden_width, 4 * hidden_...  1.31 us
    pallas_call x1, Pallas kernels, on_device(): pl.pallas_call(combine_kernel, out_shape=shape((rows, width), BF16), in_s...  0.94 us
  transfers between devices with their start and end apart: 12, of which 7 were waited for; matrix products, arithmetic and copies ran while one was open for 0% of the time, Pallas kernels for 4%

profile of v2, /device:TPU:0, one launch (start us, length us, event | category | flops | bytes accessed | tf_op | source)
XLA Modules:
  0.0 35.7 jit_solution(10440674605410707887)
XLA Ops:
  0.6 0.0 copy-start.7
  0.6 0.0 copy-start.8
  0.6 0.0 copy-start.6
  0.7 0.6 %copy-done.7 = s32[128,8]{0,1:T(8,128)S(1)} copy-done((s32[128,8]{0,1:T(8,128)S(1)}, s32[128,8]{0,1:T(8,128)}, u32[]{:S(2)}) %copy-start.7) | copy-done | bytes 4120
  1.3 0.0 copy-done.8
  1.3 0.3 copy-done.6
  1.6 0.0 copy-start
  1.6 0.0 copy-start.3
  1.6 0.0 copy-start.4
  1.6 0.0 copy-start.5
  1.6 0.3 route.1
  1.9 0.5 %collective-permute-start = (bf16[4,8,896]{2,1,0:T(8,128)(2,1)S(1)}, bf16[4,8,896]{2,1,0:T(8,128)(2,1)S(1)}, u32[]{:S(2)}, u32[]{:S(2)}) collective-permute-start(bf16[4,8,896]{2,1,0:T(8,128)(2,1)S(1)} %get-tuple-element.14), channel_id=1, source_target_pairs={{0,1},{1,0},{2,3},{3,2},{4,5},{5,4},{6,7},{7,6},{8,9},{9,8},{10,11... | collective-permute-start | bytes 172040 | tf_op jit(solution)/shard_map/ppermute | solution.py:111
  2.4 0.9 %collective-permute-done = bf16[4,8,896]{2,1,0:T(8,128)(2,1)S(1)} collective-permute-done((bf16[4,8,896]{2,1,0:T(8,128)(2,1)S(1)}, bf16[4,8,896]{2,1,0:T(8,128)(2,1)S(1)}, u32[]{:S(2)}, u32[]{:S(2)}) %collective-permute-start) | collective-permute-done | bytes 57376 | tf_op jit(solution)/shard_map/ppermute | solution.py:111
  3.3 0.7 %collective-permute-start.1 = (bf16[8,1920]{1,0:T(8,128)(2,1)S(1)}, bf16[8,1920]{1,0:T(8,128)(2,1)S(1)}, u32[]{:S(2)}, u32[]{:S(2)}) collective-permute-start(bf16[8,1920]{1,0:T(8,128)(2,1)S(1)} %get-tuple-element.24), channel_id=1, source_target_pairs={{1,3},{3,1},{5,7},{7,5},{9,11},{11,9},{13,15},{15,13},{17,19},{19,... | collective-permute-start | bytes 92168 | tf_op jit(solution)/shard_map/ppermute | solution.py:118
  4.0 3.0 %collective-permute-start.2 = (bf16[8,1920]{1,0:T(8,128)(2,1)S(1)}, bf16[8,1920]{1,0:T(8,128)(2,1)S(1)}, u32[]{:S(2)}, u32[]{:S(2)}) collective-permute-start(bf16[8,1920]{1,0:T(8,128)(2,1)S(1)} %get-tuple-element.27), channel_id=1, source_target_pairs={{0,4},{1,7},{2,6},{3,5},{4,0},{5,3},{6,2},{7,1},{8,12},{9,15},{10,... | collective-permute-start | bytes 92168 | tf_op jit(solution)/shard_map/ppermute | solution.py:118
  7.0 2.6 %collective-permute-start.3 = (bf16[8,1920]{1,0:T(8,128)(2,1)S(1)}, bf16[8,1920]{1,0:T(8,128)(2,1)S(1)}, u32[]{:S(2)}, u32[]{:S(2)}) collective-permute-start(bf16[8,1920]{1,0:T(8,128)(2,1)S(1)} %get-tuple-element.26), channel_id=1, source_target_pairs={{0,8},{1,11},{2,10},{3,9},{4,12},{5,15},{6,14},{7,13},{8,0},{9,3},... | collective-permute-start | bytes 92168 | tf_op jit(solution)/shard_map/ppermute | solution.py:118
  9.6 0.0 collective-permute-start.4
  9.6 0.0 collective-permute-done.1
  9.6 0.0 collective-permute-done.2
  9.6 2.4 %collective-permute-done.3 = bf16[8,1920]{1,0:T(8,128)(2,1)S(1)} collective-permute-done((bf16[8,1920]{1,0:T(8,128)(2,1)S(1)}, bf16[8,1920]{1,0:T(8,128)(2,1)S(1)}, u32[]{:S(2)}, u32[]{:S(2)}) %collective-permute-start.3) | collective-permute-done | bytes 30752 | tf_op jit(solution)/shard_map/ppermute | solution.py:118
  12.0 3.3 %collective-permute-done.4 = bf16[8,1920]{1,0:T(8,128)(2,1)S(1)} collective-permute-done((bf16[8,1920]{1,0:T(8,128)(2,1)S(1)}, bf16[8,1920]{1,0:T(8,128)(2,1)S(1)}, u32[]{:S(2)}, u32[]{:S(2)}) %collective-permute-start.4) | collective-permute-done | bytes 30752 | tf_op jit(solution)/shard_map/ppermute | solution.py:118
  15.4 2.7 %collective-permute-start.5 = (bf16[4,8,1792]{2,1,0:T(8,128)(2,1)S(1)}, bf16[4,8,1792]{2,1,0:T(8,128)(2,1)S(1)}, u32[]{:S(2)}, u32[]{:S(2)}) collective-permute-start(bf16[4,8,1792]{2,1,0:T(8,128)(2,1)S(1)} %slice.37), channel_id=1, source_target_pairs={{0,1},{1,0},{2,3},{3,2},{4,5},{5,4},{6,7},{7,6},{8,9},{9,8},{10,11... | collective-permute-start | bytes 344072 | tf_op jit(solution)/shard_map/ppermute | solution.py:111
  18.1 1.0 %collective-permute-done.5.swapped_ref = bf16[4,8,1792]{2,1,0:T(8,128)(2,1)S(1)} collective-permute-done((bf16[4,8,1792]{2,1,0:T(8,128)(2,1)S(1)}, bf16[4,8,1792]{2,1,0:T(8,128)(2,1)S(1)}, u32[]{:S(2)}, u32[]{:S(2)}) %collective-permute-start.5) | collective-permute-done | bytes 114720 | tf_op jit(solution)/shard_map/ppermute | solution.py:111
  19.1 0.0 copy-done
  19.1 0.0 copy-done.3
  19.1 0.0 copy-done.4
  19.1 0.0 copy-done.5
  19.1 0.0 copy-start.1
  19.1 1.5 %copy-done.1 = bf16[1,3584,256]{2,1,0:T(8,128)(2,1)S(1)} copy-done((bf16[1,3584,256]{2,1,0:T(8,128)(2,1)S(1)}, bf16[1,3584,256]{2,1,0:T(8,128)(2,1)}, u32[]{:S(2)}) %copy-start.1) | copy-done | bytes 1835032
  20.6 0.0 copy-start.2
  20.6 1.5 %copy-done.2 = bf16[1,256,3584]{2,1,0:T(8,128)(2,1)S(1)} copy-done((bf16[1,256,3584]{2,1,0:T(8,128)(2,1)S(1)}, bf16[1,256,3584]{2,1,0:T(8,128)(2,1)}, u32[]{:S(2)}) %copy-start.2) | copy-done | bytes 1835032
  22.1 1.8 %expert.1 = (bf16[32,1792]{1,0:T(8,128)(2,1)S(1)}, bf16[32,2048]{1,0:T(8,128)(2,1)S(1)}, bf16[32,256]{1,0:T(8,128)(2,1)S(1)}) custom-call(bf16[4,8,1920]{2,1,0:T(8,128)(2,1)S(1)} %pad_maximum_fusion.arrived_ref, bf16[4,8,1792]{2,1,0:T(8,128)(2,1)S(1)} %collective-permute-done.5.swapped_ref, bf16[3584,256]{1,0:T(8,128)(2,1)S(1)} %bitcast.28, ...), custom_call_target="tpu_custom_call" | custom-call | tf_op jit(solution)/shard_map/expert/pallas_call | solution.py:316
  23.9 0.4 %collective-permute-start.6 = (bf16[32,2048]{1,0:T(8,128)(2,1)S(1)}, bf16[32,2048]{1,0:T(8,128)(2,1)S(1)}, u32[]{:S(2)}, u32[]{:S(2)}) collective-permute-start(bf16[32,2048]{1,0:T(8,128)(2,1)S(1)} %get-tuple-element.17), channel_id=1, source_target_pairs={{0,1},{1,0},{2,3},{3,2},{4,5},{5,4},{6,7},{7,6},{8,9},{9,8},{10,11... | collective-permute-start | bytes 393224 | tf_op jit(solution)/shard_map/ppermute | solution.py:111
  24.3 1.0 %collective-permute-done.6.sent_ref = bf16[32,2048]{1,0:T(8,128)(2,1)S(1)} collective-permute-done((bf16[32,2048]{1,0:T(8,128)(2,1)S(1)}, bf16[32,2048]{1,0:T(8,128)(2,1)S(1)}, u32[]{:S(2)}, u32[]{:S(2)}) %collective-permute-start.6) | collective-permute-done | bytes 131104 | tf_op jit(solution)/shard_map/ppermute | solution.py:111
  25.3 0.6 %collective-permute-start.7 = (bf16[8,3840]{1,0:T(8,128)(2,1)S(1)}, bf16[8,3840]{1,0:T(8,128)(2,1)S(1)}, u32[]{:S(2)}, u32[]{:S(2)}) collective-permute-start(bf16[8,3840]{1,0:T(8,128)(2,1)S(1)} %get-tuple-element.19), channel_id=1, source_target_pairs={{0,2},{1,3},{2,0},{3,1},{4,6},{5,7},{6,4},{7,5},{8,10},{9,11},{10,... | collective-permute-start | bytes 184328 | tf_op jit(solution)/shard_map/ppermute | solution.py:122
  25.9 0.6 %collective-permute-start.10 = (bf16[8,1792]{1,0:T(8,128)(2,1)S(1)}, bf16[8,1792]{1,0:T(8,128)(2,1)S(1)}, u32[]{:S(2)}, u32[]{:S(2)}) collective-permute-start(bf16[8,1792]{1,0:T(8,128)(2,1)S(1)} %get-tuple-element.22), channel_id=1, source_target_pairs={{0,12},{1,15},{2,14},{3,13},{4,8},{5,11},{6,10},{7,9},{8,4},{9,7},... | collective-permute-start | bytes 86024 | tf_op jit(solution)/shard_map/ppermute | solution.py:118
  26.6 0.0 collective-permute-start.8
  26.6 3.7 %collective-permute-start.9 = (bf16[8,1792]{1,0:T(8,128)(2,1)S(1)}, bf16[8,1792]{1,0:T(8,128)(2,1)S(1)}, u32[]{:S(2)}, u32[]{:S(2)}) collective-permute-start(bf16[8,1792]{1,0:T(8,128)(2,1)S(1)} %get-tuple-element.21), channel_id=1, source_target_pairs={{0,8},{1,11},{2,10},{3,9},{4,12},{5,15},{6,14},{7,13},{8,0},{9,3},... | collective-permute-start | bytes 86024 | tf_op jit(solution)/shard_map/ppermute | solution.py:118
  30.3 0.0 collective-permute-done.7.crossed_ref
  30.3 1.6 %collective-permute-done.10 = bf16[8,1792]{1,0:T(8,128)(2,1)S(1)} collective-permute-done((bf16[8,1792]{1,0:T(8,128)(2,1)S(1)}, bf16[8,1792]{1,0:T(8,128)(2,1)S(1)}, u32[]{:S(2)}, u32[]{:S(2)}) %collective-permute-start.10) | collective-permute-done | bytes 28704 | tf_op jit(solution)/shard_map/ppermute | solution.py:118
  31.9 0.0 collective-permute-done.8
  31.9 0.6 %collective-permute-done.9 = bf16[8,1792]{1,0:T(8,128)(2,1)S(1)} collective-permute-done((bf16[8,1792]{1,0:T(8,128)(2,1)S(1)}, bf16[8,1792]{1,0:T(8,128)(2,1)S(1)}, u32[]{:S(2)}, u32[]{:S(2)}) %collective-permute-start.9) | collective-permute-done | bytes 28704 | tf_op jit(solution)/shard_map/ppermute | solution.py:118
  32.6 0.8 %collective-permute-start.11 = (bf16[32,896]{1,0:T(8,128)(2,1)S(1)}, bf16[32,896]{1,0:T(8,128)(2,1)S(1)}, u32[]{:S(2)}, u32[]{:S(2)}) collective-permute-start(bf16[32,896]{1,0:T(8,128)(2,1)S(1)} %slice.39), channel_id=1, source_target_pairs={{0,1},{1,0},{2,3},{3,2},{4,5},{5,4},{6,7},{7,6},{8,9},{9,8},{10,11... | collective-permute-start | bytes 172040 | tf_op jit(solution)/shard_map/ppermute | solution.py:111
  33.4 1.3 %hessian.1 = f32[256,1024]{1,0:T(8,128)} custom-call(bf16[4,8,1920]{2,1,0:T(8,128)(2,1)S(1)} %pad_maximum_fusion.arrived_ref, bf16[32,512]{1,0:T(8,128)(2,1)S(1)} %get-tuple-element.23.near_ref, bf16[8,3840]{1,0:T(8,128)(2,1)S(1)} %collective-permute-done.7.crossed_ref), custom_call_target="tpu_custom_call" | custom-call | tf_op jit(solution)/shard_map/hessian/pallas_call | solution.py:357
  34.7 0.0 collective-permute-done.11.far_ref
  34.7 0.9 %combine.1 = bf16[128,896]{1,0:T(8,128)(2,1)} custom-call(f32[32,128]{1,0:T(8,128)S(1)} %get-tuple-element.13.coef_ref, bf16[32,1792]{1,0:T(8,128)(2,1)S(1)} %pad_maximum_fusion.1.near_ref, bf16[32,896]{1,0:T(8,128)(2,1)S(1)} %collective-permute-done.11.far_ref), custom_call_target="tpu_custom_call" | custom-call | tf_op jit(solution)/shard_map/combine/pallas_call | solution.py:366
  (12 shorter events, 0.1 us)
Async XLA Ops:
  0.6 0.7 %copy-start.7 = (s32[128,8]{0,1:T(8,128)S(1)}, s32[128,8]{0,1:T(8,128)}, u32[]{:S(2)}) copy-start(s32[128,8]{0,1:T(8,128)} %param.10) | copy-start | bytes 12292
  0.6 0.7 %copy-start.8 = (f32[128,8]{0,1:T(8,128)S(1)}, f32[128,8]{0,1:T(8,128)}, u32[]{:S(2)}) copy-start(f32[128,8]{0,1:T(8,128)} %param.11) | copy-start | bytes 12292
  0.6 1.0 %copy-start.6 = (bf16[128,896]{1,0:T(8,128)(2,1)S(1)}, bf16[128,896]{1,0:T(8,128)(2,1)}, u32[]{:S(2)}) copy-start(bf16[128,896]{1,0:T(8,128)(2,1)} %tokens_ref.1) | copy-start | bytes 688132
  1.6 17.5 %copy-start = (bf16[1,3584,256]{2,1,0:T(8,128)(2,1)S(1)}, bf16[1,3584,256]{2,1,0:T(8,128)(2,1)}, u32[]{:S(2)}) copy-start(bf16[1,3584,256]{2,1,0:T(8,128)(2,1)} %param.12) | copy-start | bytes 5505028
  1.6 17.5 %copy-start.3 = (f32[1,28,2]{1,2,0:T(2,128)S(1)}, f32[1,28,2]{1,2,0:T(2,128)}, u32[]{:S(2)}) copy-start(f32[1,28,2]{1,2,0:T(2,128)} %param.13) | copy-start | bytes 676
  1.6 17.5 %copy-start.4 = (f32[1,28,2]{1,2,0:T(2,128)S(1)}, f32[1,28,2]{1,2,0:T(2,128)}, u32[]{:S(2)}) copy-start(f32[1,28,2]{1,2,0:T(2,128)} %param.15) | copy-start | bytes 676
  1.6 17.5 %copy-start.5 = (f32[1,2,28]{2,1,0:T(2,128)S(1)}, f32[1,2,28]{2,1,0:T(2,128)}, u32[]{:S(2)}) copy-start(f32[1,2,28]{2,1,0:T(2,128)} %param.17) | copy-start | bytes 676
  1.9 1.4 %collective-permute-start = (bf16[4,8,896]{2,1,0:T(8,128)(2,1)S(1)}, bf16[4,8,896]{2,1,0:T(8,128)(2,1)S(1)}, u32[]{:S(2)}, u32[]{:S(2)}) collective-permute-start(bf16[4,8,896]{2,1,0:T(8,128)(2,1)S(1)} %get-tuple-element.14), channel_id=1, source_target_pairs={{0,1},{1,0},{2,3},{3,2},{4,5},{5,4},{6,7},{7,6},{8,9},{9,8},{10,11... | collective-permute-start | bytes 172040 | tf_op jit(solution)/shard_map/ppermute | solution.py:111
  3.3 6.3 %collective-permute-start.1 = (bf16[8,1920]{1,0:T(8,128)(2,1)S(1)}, bf16[8,1920]{1,0:T(8,128)(2,1)S(1)}, u32[]{:S(2)}, u32[]{:S(2)}) collective-permute-start(bf16[8,1920]{1,0:T(8,128)(2,1)S(1)} %get-tuple-element.24), channel_id=1, source_target_pairs={{1,3},{3,1},{5,7},{7,5},{9,11},{11,9},{13,15},{15,13},{17,19},{19,... | collective-permute-start | bytes 92168 | tf_op jit(solution)/shard_map/ppermute | solution.py:118
  4.0 5.6 %collective-permute-start.2 = (bf16[8,1920]{1,0:T(8,128)(2,1)S(1)}, bf16[8,1920]{1,0:T(8,128)(2,1)S(1)}, u32[]{:S(2)}, u32[]{:S(2)}) collective-permute-start(bf16[8,1920]{1,0:T(8,128)(2,1)S(1)} %get-tuple-element.27), channel_id=1, source_target_pairs={{0,4},{1,7},{2,6},{3,5},{4,0},{5,3},{6,2},{7,1},{8,12},{9,15},{10,... | collective-permute-start | bytes 92168 | tf_op jit(solution)/shard_map/ppermute | solution.py:118
  7.0 5.0 %collective-permute-start.3 = (bf16[8,1920]{1,0:T(8,128)(2,1)S(1)}, bf16[8,1920]{1,0:T(8,128)(2,1)S(1)}, u32[]{:S(2)}, u32[]{:S(2)}) collective-permute-start(bf16[8,1920]{1,0:T(8,128)(2,1)S(1)} %get-tuple-element.26), channel_id=1, source_target_pairs={{0,8},{1,11},{2,10},{3,9},{4,12},{5,15},{6,14},{7,13},{8,0},{9,3},... | collective-permute-start | bytes 92168 | tf_op jit(solution)/shard_map/ppermute | solution.py:118
  9.6 5.7 %collective-permute-start.4 = (bf16[8,1920]{1,0:T(8,128)(2,1)S(1)}, bf16[8,1920]{1,0:T(8,128)(2,1)S(1)}, u32[]{:S(2)}, u32[]{:S(2)}) collective-permute-start(bf16[8,1920]{1,0:T(8,128)(2,1)S(1)} %get-tuple-element.25), channel_id=1, source_target_pairs={{0,12},{1,15},{2,14},{3,13},{4,8},{5,11},{6,10},{7,9},{8,4},{9,7},... | collective-permute-start | bytes 92168 | tf_op jit(solution)/shard_map/ppermute | solution.py:118
  15.4 3.7 %collective-permute-start.5 = (bf16[4,8,1792]{2,1,0:T(8,128)(2,1)S(1)}, bf16[4,8,1792]{2,1,0:T(8,128)(2,1)S(1)}, u32[]{:S(2)}, u32[]{:S(2)}) collective-permute-start(bf16[4,8,1792]{2,1,0:T(8,128)(2,1)S(1)} %slice.37), channel_id=1, source_target_pairs={{0,1},{1,0},{2,3},{3,2},{4,5},{5,4},{6,7},{7,6},{8,9},{9,8},{10,11... | collective-permute-start | bytes 344072 | tf_op jit(solution)/shard_map/ppermute | solution.py:111
  19.1 1.5 %copy-start.1 = (bf16[1,3584,256]{2,1,0:T(8,128)(2,1)S(1)}, bf16[1,3584,256]{2,1,0:T(8,128)(2,1)}, u32[]{:S(2)}) copy-start(bf16[1,3584,256]{2,1,0:T(8,128)(2,1)} %param.14) | copy-start | bytes 5505028
  20.6 1.5 %copy-start.2 = (bf16[1,256,3584]{2,1,0:T(8,128)(2,1)S(1)}, bf16[1,256,3584]{2,1,0:T(8,128)(2,1)}, u32[]{:S(2)}) copy-start(bf16[1,256,3584]{2,1,0:T(8,128)(2,1)} %param.16) | copy-start | bytes 5505028
  23.9 1.4 %collective-permute-start.6 = (bf16[32,2048]{1,0:T(8,128)(2,1)S(1)}, bf16[32,2048]{1,0:T(8,128)(2,1)S(1)}, u32[]{:S(2)}, u32[]{:S(2)}) collective-permute-start(bf16[32,2048]{1,0:T(8,128)(2,1)S(1)} %get-tuple-element.17), channel_id=1, source_target_pairs={{0,1},{1,0},{2,3},{3,2},{4,5},{5,4},{6,7},{7,6},{8,9},{9,8},{10,11... | collective-permute-start | bytes 393224 | tf_op jit(solution)/shard_map/ppermute | solution.py:111
  25.3 5.0 %collective-permute-start.7 = (bf16[8,3840]{1,0:T(8,128)(2,1)S(1)}, bf16[8,3840]{1,0:T(8,128)(2,1)S(1)}, u32[]{:S(2)}, u32[]{:S(2)}) collective-permute-start(bf16[8,3840]{1,0:T(8,128)(2,1)S(1)} %get-tuple-element.19), channel_id=1, source_target_pairs={{0,2},{1,3},{2,0},{3,1},{4,6},{5,7},{6,4},{7,5},{8,10},{9,11},{10,... | collective-permute-start | bytes 184328 | tf_op jit(solution)/shard_map/ppermute | solution.py:122
  25.9 6.0 %collective-permute-start.10 = (bf16[8,1792]{1,0:T(8,128)(2,1)S(1)}, bf16[8,1792]{1,0:T(8,128)(2,1)S(1)}, u32[]{:S(2)}, u32[]{:S(2)}) collective-permute-start(bf16[8,1792]{1,0:T(8,128)(2,1)S(1)} %get-tuple-element.22), channel_id=1, source_target_pairs={{0,12},{1,15},{2,14},{3,13},{4,8},{5,11},{6,10},{7,9},{8,4},{9,7},... | collective-permute-start | bytes 86024 | tf_op jit(solution)/shard_map/ppermute | solution.py:118
  26.6 5.4 %collective-permute-start.8 = (bf16[8,1792]{1,0:T(8,128)(2,1)S(1)}, bf16[8,1792]{1,0:T(8,128)(2,1)S(1)}, u32[]{:S(2)}, u32[]{:S(2)}) collective-permute-start(bf16[8,1792]{1,0:T(8,128)(2,1)S(1)} %get-tuple-element.20), channel_id=1, source_target_pairs={{0,4},{1,7},{2,6},{3,5},{4,0},{5,3},{6,2},{7,1},{8,12},{9,15},{10,... | collective-permute-start | bytes 86024 | tf_op jit(solution)/shard_map/ppermute | solution.py:118
  26.6 6.0 %collective-permute-start.9 = (bf16[8,1792]{1,0:T(8,128)(2,1)S(1)}, bf16[8,1792]{1,0:T(8,128)(2,1)S(1)}, u32[]{:S(2)}, u32[]{:S(2)}) collective-permute-start(bf16[8,1792]{1,0:T(8,128)(2,1)S(1)} %get-tuple-element.21), channel_id=1, source_target_pairs={{0,8},{1,11},{2,10},{3,9},{4,12},{5,15},{6,14},{7,13},{8,0},{9,3},... | collective-permute-start | bytes 86024 | tf_op jit(solution)/shard_map/ppermute | solution.py:118
  32.6 2.2 %collective-permute-start.11 = (bf16[32,896]{1,0:T(8,128)(2,1)S(1)}, bf16[32,896]{1,0:T(8,128)(2,1)S(1)}, u32[]{:S(2)}, u32[]{:S(2)}) collective-permute-start(bf16[32,896]{1,0:T(8,128)(2,1)S(1)} %slice.39), channel_id=1, source_target_pairs={{0,1},{1,0},{2,3},{3,2},{4,5},{5,4},{6,7},{7,6},{8,9},{9,8},{10,11... | collective-permute-start | bytes 172040 | tf_op jit(solution)/shard_map/ppermute | solution.py:111

commit v3 on v2

--- a/solution.py
+++ b/solution.py
@@ -156,63 +156,95 @@
     rows_ref[...] = picked.reshape(rows_ref.shape)
 
 
-def expert_kernel(
-    arrived_ref,
-    swapped_ref,
+def spread_kernel(*refs):
+    for scale_ref, out_ref in zip(refs[:3], refs[3:]):
+        for at in range(scale_ref.shape[1]):
+            for i in range(2):
+                out_ref[i : i + 1, at * QBLK : (at + 1) * QBLK] = jnp.full((1, QBLK), scale_ref[i, at], F32)
+
+
+def line_up_kernel(own_ref, other_ref, count_ref, *out_refs):
+    for k, out_ref in enumerate(out_refs):
+        out_ref[...] = jnp.concatenate([own_ref[k], other_ref[k], count_ref[k]], axis=1)
+
+
+def collect_kernel(own_ref, three_ref, two_ref, one_ref, zero_ref, _, out_ref, count_ref):
+    rows, width = own_ref.shape[0], out_ref.shape[1]
+    crossed = (lax.axis_index("mp") % 2 == 1).astype(F32)
+    value = own_ref[...].astype(F32) * (1.0 - crossed) + zero_ref[...].astype(F32) * crossed
+    for k, rows_in in enumerate((value.astype(BF16), one_ref[...], two_ref[...], three_ref[...])):
+        out_ref[k * rows : (k + 1) * rows, :] = rows_in[:, :width]
+        count_ref[k * rows : (k + 1) * rows, :] = rows_in[:, width:]
+
+
+def shares_in_order():
+    m = lax.axis_index("mp")
+    first = m ^ (2 * (m % 2))
+    return (first, first ^ 1, first ^ 3, first ^ 2)
+
+
+def project(x_ref, shares, weight_ref, scale_ref):
+    slots, width = x_ref.shape[0], x_ref.shape[1] // len(shares)
+    total = None
+    for part, share in enumerate(shares):
+        depth = pl.ds(pl.multiple_of(share * width, width), width)
+        x = x_ref[:, part * width : (part + 1) * width].astype(F32)
+        scaled = jnp.concatenate([(x * scale_ref[i : i + 1, depth]).astype(BF16) for i in range(2)], axis=0)
+        term = jnp.dot(scaled, weight_ref[depth, :], preferred_element_type=F32)
+        total = term if total is None else total + term
+    return total
+
+
+def project_down(parts, shares, down_ref, scale_ref, out_ref):
+    slots, width = parts[0].shape[0], down_ref.shape[1] // 4
+    none = jnp.zeros_like(parts[0])
+    stacked = jnp.concatenate(
+        [jnp.concatenate([parts[0], none], axis=1), jnp.concatenate([none, parts[1]], axis=1)], axis=0
+    )
+    for part, share in enumerate(shares):
+        lanes = pl.ds(pl.multiple_of(share * width, width), width)
+        both = jnp.dot(stacked, down_ref[:, lanes], preferred_element_type=F32)
+        value = both[:slots] * scale_ref[:1, lanes] + both[slots:] * scale_ref[1:, lanes]
+        out_ref[:, part * width : (part + 1) * width] = value.astype(BF16)
+
+
+def near_kernel(x_ref, gate_ref, up_ref, gate_scale_ref, up_scale_ref, gate_out_ref, up_out_ref):
+    shares = shares_in_order()[:2]
+    gate_out_ref[...] = project(x_ref, shares, gate_ref, gate_scale_ref)
+    up_out_ref[...] = project(x_ref, shares, up_ref, up_scale_ref)
+
+
+def hidden_kernel(
+    x_ref,
+    near_gate_ref,
+    near_up_ref,
     gate_ref,
+    up_ref,
+    down_ref,
     gate_scale_ref,
-    up_ref,
     up_scale_ref,
-    down_ref,
     down_scale_ref,
-    keep_ref,
     send_ref,
     hidden_ref,
-    scaled_ref,
 ):
-    m = lax.axis_index("mp")
-    core = m % 2
-    first = m ^ (2 * core)
-    slots, width = scaled_ref.shape[0] // 4, scaled_ref.shape[1]
-    blocks = width // QBLK
-    half = gate_ref.shape[1] // 2
-    gate = jnp.zeros((2 * slots, 2 * half), F32)
-    up = jnp.zeros((2 * slots, 2 * half), F32)
-    order = (first, first ^ 1, first ^ 3, first ^ 2)
-    for quarter, share in enumerate(order):
-        source = arrived_ref if quarter < 2 else swapped_ref
-        for block in range(blocks):
-            lanes = slice((quarter % 2) * width + block * QBLK, (quarter % 2) * width + (block + 1) * QBLK)
-            x = source[:, :, lanes].reshape(slots, QBLK).astype(F32)
-            at = share * blocks + block
-            into = slice(block * QBLK, (block + 1) * QBLK)
-            scaled_ref[0 * slots : 1 * slots, into] = (x * gate_scale_ref[0, at]).astype(BF16)
-            scaled_ref[1 * slots : 2 * slots, into] = (x * gate_scale_ref[1, at]).astype(BF16)
-            scaled_ref[2 * slots : 3 * slots, into] = (x * up_scale_ref[0, at]).astype(BF16)
-            scaled_ref[3 * slots : 4 * slots, into] = (x * up_scale_ref[1, at]).astype(BF16)
-        depth = pl.ds(pl.multiple_of(share * width, width), width)
-        gate += jnp.dot(scaled_ref[: 2 * slots, :], gate_ref[depth, :], preferred_element_type=F32)
-        up += jnp.dot(scaled_ref[2 * slots :, :], up_ref[depth, :], preferred_element_type=F32)
+    shares = shares_in_order()[2:]
+    gate = near_gate_ref[...] + project(x_ref, shares, gate_ref, gate_scale_ref)
+    up = near_up_ref[...] + project(x_ref, shares, up_ref, up_scale_ref)
+    slots, half = x_ref.shape[0], gate_ref.shape[1] // 2
     parts = []
     for i in range(2):
         g = gate[i * slots : (i + 1) * slots, i * half : (i + 1) * half]
         u = up[i * slots : (i + 1) * slots, i * half : (i + 1) * half]
         parts.append((g / (1.0 + jnp.exp(-g)) * u).astype(BF16))
-    hidden_ref[...] = jnp.concatenate(parts, axis=1)
-    send_ref[:, 2 * width :] = hidden_ref[...]
-    none = jnp.zeros_like(parts[0])
-    stacked = jnp.concatenate(
-        [jnp.concatenate([parts[0], none], axis=1), jnp.concatenate([none, parts[1]], axis=1)], axis=0
-    )
-    for out_ref, shares in ((send_ref, (first ^ 3, first ^ 2)), (keep_ref, (first, first ^ 1))):
-        for part, share in enumerate(shares):
-            lanes = pl.ds(pl.multiple_of(share * width, width), width)
-            both = jnp.dot(stacked, down_ref[:, lanes], preferred_element_type=F32)
-            for block in range(blocks):
-                at = share * blocks + block
-                cut = slice(block * QBLK, (block + 1) * QBLK)
-                value = both[:slots, cut] * down_scale_ref[0, at] + both[slots:, cut] * down_scale_ref[1, at]
-                out_ref[:, part * width + block * QBLK : part * width + (block + 1) * QBLK] = value.astype(BF16)
+        hidden_ref[:, i * half : (i + 1) * half] = parts[i]
+        send_ref[:, x_ref.shape[1] + i * half : x_ref.shape[1] + (i + 1) * half] = parts[i]
+    project_down(parts, shares, down_ref, down_scale_ref, send_ref)
+
+
+def keep_kernel(hidden_ref, down_ref, down_scale_ref, keep_ref):
+    half = hidden_ref.shape[1] // 2
+    parts = (hidden_ref[:, :half], hidden_ref[:, half:])
+    project_down(parts, shares_in_order()[:2], down_ref, down_scale_ref, keep_ref)
 
 
 def chip_sum_kernel(keep_ref, sent_ref, hidden_ref, message_ref, one_ref, two_ref, three_ref, near_ref):
@@ -228,11 +260,12 @@
         message_ref[:, into : into + 2 * hidden_width] = near
 
 
-def hessian_kernel(arrived_ref, near_ref, crossed_ref, out_ref):
+def hessian_kernel(count_ref, near_ref, crossed_ref, out_ref):
     m = lax.axis_index("mp")
     width = out_ref.shape[0]
-    counts = arrived_ref[:, :, arrived_ref.shape[2] - QBLK :].astype(F32)
-    factor = 2.0 / jnp.sum(counts[:, 0, :1], axis=0, keepdims=True)
+    rows = count_ref.shape[0] // 4
+    counts = [count_ref[k * rows : k * rows + 1, :].astype(F32)[:, :1] for k in range(4)]
+    factor = 2.0 / (counts[0] + counts[1] + counts[2] + counts[3])
     own = near_ref[:, :width]
     start = crossed_ref.shape[1] - 8 * width
     far = [crossed_ref[:, start + i * width : start + (i + 1) * width] for i in range(8)]
@@ -247,9 +280,19 @@
         out_ref[:, pl.ds(pl.multiple_of(share * width, width), width)] = block * factor
 
 
+def collect_back_kernel(own_ref, three_ref, two_ref, one_ref, zero_ref, mine_ref, other_ref):
+    rows, width = one_ref.shape[0], mine_ref.shape[1]
+    crossed = (lax.axis_index("mp") % 2 == 1).astype(F32)
+    here = slice(0, 2 * width)
+    value = own_ref[:, here].astype(F32) * (1.0 - crossed) + zero_ref[:, here].astype(F32) * crossed
+    for k, rows_in in enumerate((value.astype(BF16), one_ref[...], two_ref[...], three_ref[...])):
+        mine_ref[k * rows : (k + 1) * rows, :] = rows_in[:, :width]
+        other_ref[k * rows : (k + 1) * rows, :] = rows_in[:, width:]
+
+
 def combine_kernel(coef_ref, near_ref, far_ref, out_ref):
     slots, width = coef_ref.shape[0], out_ref.shape[1]
-    result = (near_ref[:, :width].astype(F32) + far_ref[...].astype(F32)).astype(BF16)
+    result = (near_ref[...].astype(F32) + far_ref[...].astype(F32)).astype(BF16)
     coef = coef_ref[...]
     terms = []
     for _ in range(3):
@@ -280,97 +323,89 @@
     slots = 4 * capacity
     hidden_width = gate_weight.shape[2]
     shape = jax.ShapeDtypeStruct
-    params = pltpu.CompilerParams(vmem_limit_bytes=24 * 1024 * 1024)
-
-    earlier = pl.pallas_call(
-        earlier_kernel,
-        out_shape=shape((rows, rows), BF16),
-        out_specs=VMEM,
-        compiler_params=params,
-        cost_estimate=pl.CostEstimate(flops=4 * 10**9, bytes_accessed=0, transcendentals=0),
-        name="earlier",
-    )()
-    on_core_one = lax.axis_index("mp") % 2 == 1
-
-    picked, counts, coef = pl.pallas_call(
+
+    def call(kernel, name, outs, args, scalars=0, flops=0):
+        single = not isinstance(outs, tuple)
+        return pl.pallas_call(
+            kernel,
+            out_shape=outs,
+            in_specs=[SMEM] * scalars + [VMEM] * (len(args) - scalars),
+            out_specs=VMEM if single else (VMEM,) * len(outs),
+            compiler_params=pltpu.CompilerParams(vmem_limit_bytes=8 * 1024 * 1024),
+            cost_estimate=pl.CostEstimate(flops=flops, bytes_accessed=0, transcendentals=0) if flops else None,
+            name=name,
+        )(*args)
+
+    earlier = call(earlier_kernel, "earlier", shape((rows, rows), BF16), (), flops=4 * 10**9)
+    picked, counts, coef = call(
         functools.partial(route_kernel, capacity),
-        out_shape=(
-            shape((4, capacity, width), BF16),
-            shape((4, capacity, QBLK), BF16),
-            shape((slots, rows), F32),
-        ),
-        in_specs=[VMEM] * 4,
-        out_specs=(VMEM,) * 3,
-        compiler_params=params,
-        cost_estimate=pl.CostEstimate(flops=8 * 10**9, bytes_accessed=0, transcendentals=0),
-        name="route",
-    )(earlier, route_ids.T, route_weights.T, tokens)
-
-    message = jnp.concatenate([picked, swap_cores(picked), counts], axis=2)
-
-    got = [to_chips(message[k], k) for k in range(4)]
-    got[0] = jnp.where(on_core_one, got[0], message[0])
-    arrived = jnp.stack(got)
-    swapped = swap_cores(arrived[:, :, : 2 * width])
-
-    keep, send, hidden = pl.pallas_call(
-        expert_kernel,
-        out_shape=(
-            shape((slots, 2 * width), BF16),
-            shape((slots, 2 * width + hidden_width), BF16),
-            shape((slots, hidden_width), BF16),
-        ),
-        in_specs=[VMEM, VMEM, VMEM, SMEM, VMEM, SMEM, VMEM, SMEM],
-        out_specs=(VMEM,) * 3,
-        scratch_shapes=[pltpu.VMEM((4 * slots, width), BF16)],
-        compiler_params=params,
-        name="expert",
-    )(
-        arrived,
-        swapped,
-        gate_weight[0],
-        gate_scale[0].T,
-        up_weight[0],
-        up_scale[0].T,
-        down_weight[0],
-        down_scale[0],
-    )
-
-    message, *summed, near = pl.pallas_call(
+        "route",
+        (shape((4, capacity, width), BF16), shape((4, capacity, QBLK), BF16), shape((slots, rows), F32)),
+        (earlier, route_ids.T, route_weights.T, tokens),
+        flops=10**11,
+    )
+    messages = call(
+        line_up_kernel,
+        "line_up",
+        (shape((capacity, 2 * width + QBLK), BF16),) * 4,
+        (picked, swap_cores(picked), counts),
+    )
+    scales = call(
+        spread_kernel,
+        "spread",
+        (shape((2, 4 * width), F32),) * 3,
+        (gate_scale[0].T, up_scale[0].T, down_scale[0]),
+        scalars=3,
+    )
+    gate, up, down = gate_weight[0], up_weight[0], down_weight[0]
+
+    arrived, arrived_counts = call(
+        collect_kernel,
+        "collect",
+        (shape((slots, 2 * width), BF16), shape((slots, QBLK), BF16)),
+        (messages[0], *[to_chips(messages[k], k) for k in (3, 2, 1, 0)], scales[0]),
+    )
+    swapped = swap_cores(arrived)
+    near = call(
+        near_kernel,
+        "near",
+        (shape((2 * slots, hidden_width), F32),) * 2,
+        (arrived, gate, up, *scales[:2]),
+    )
+    send, hidden = call(
+        hidden_kernel,
+        "hidden",
+        (shape((slots, 2 * width + hidden_width), BF16), shape((slots, hidden_width), BF16)),
+        (swapped, *near, gate, up, down, *scales),
+    )
+    sent = swap_cores(send)
+    keep = call(keep_kernel, "keep", shape((slots, 2 * width), BF16), (hidden, down, scales[2]))
+
+    message, *summed, chip_hidden = call(
         chip_sum_kernel,
-        out_shape=(
+        "chip_sum",
+        (
             shape((capacity, 2 * width + 8 * hidden_width), BF16),
             *[shape((capacity, 2 * width), BF16)] * 3,
             shape((slots, 2 * hidden_width), BF16),
         ),
-        in_specs=[VMEM] * 3,
-        out_specs=(VMEM,) * 5,
-        compiler_params=params,
-        name="chip_sum",
-    )(keep, swap_cores(send), hidden)
-
+        (keep, sent, hidden),
+    )
     crossed = across(message)
-    back = [jnp.where(on_core_one, crossed[:, : 2 * width], message[:, : 2 * width])]
-    back += [to_chips(summed[k - 1], k) for k in range(1, 4)]
-    back = jnp.concatenate(back, axis=0)
-
-    hessian = pl.pallas_call(
+    back = {k: to_chips(summed[k - 1], k) for k in range(1, 4)}
+    back[0] = crossed
+    hessian = call(
         hessian_kernel,
-        out_shape=shape((hidden_width, 4 * hidden_width), F32),
-        in_specs=[VMEM] * 3,
-        out_specs=VMEM,
-        compiler_params=params,
-        name="hessian",
-    )(arrived, near, crossed)
-
-    mixed = pl.pallas_call(
-        combine_kernel,
-        out_shape=shape((rows, width), BF16),
-        in_specs=[VMEM] * 3,
-        out_specs=VMEM,
-        compiler_params=params,
-        name="combine",
-    )(coef, back, swap_cores(back[:, width:]))
+        "hessian",
+        shape((hidden_width, 4 * hidden_width), F32),
+        (arrived_counts, chip_hidden, crossed),
+    )
+    mine, other = call(
+        collect_back_kernel, "collect_back", (shape((slots, width), BF16),) * 2, (message, *[back[k] for k in (3, 2, 1, 0)])
+    )
+    mixed = call(
+        combine_kernel, "combine", shape((rows, width), BF16), (coef, mine, swap_cores(other))
+    )
     return mixed, hessian[None]
 
 

time: 35.9 us -> 30.3 us (0.84)
  local copies, waits for them, and re-layouts: 3.99 us -> 1.49 us
  starting transfers between devices: 15.8 us -> 14.1 us
  waiting for transfers between devices: 10.7 us -> 9.23 us
    unnamed x20 -> x18, local copies, waits for them, and re-layouts: 3.95 us -> 1.49 us
    ppermute x4, starting transfers between devices: 4.51 us -> 2.63 us  [swap_cores(): return lax.ppermute(value, 'mp', [(m, m ^ 1) for m in range(4)])]
    ppermute x7, waiting for transfers between devices: 7.9 us -> 6.78 us  [to_chips(): return lax.ppermute(value, BOTH, pairs)]
    ppermute x4, waiting for transfers between devices: 2.84 us -> 2.45 us  [swap_cores(): return lax.ppermute(value, 'mp', [(m, m ^ 1) for m in range(4)])]
    pallas_call x6 -> x12, Pallas kernels: 4.35 us -> 4.56 us  [call(): pl.pallas_call(kernel, out_shape=outs, in_specs=[SMEM] * scalars + [VMEM]...]
  transfers between devices with their start and end apart: 12 -> 12, of which waited for: 7 -> 6; matrix products, arithmetic and copies ran while one was open for 0% -> 0% of each run, Pallas kernels for 4% -> 9%
where the time goes in v3:
time: 30.3 us; the launch traced here: 30.1 us
  starting transfers between devices  14.1 us (47%)
  waiting for transfers between devices  9.23 us (30%)
  Pallas kernels  4.56 us (15%)
  local copies, waits for them, and re-layouts  1.49 us (5%)
  between operations  0.78 us (3%)
    ppermute x7, starting transfers between devices, to_chips(): return lax.ppermute(value, BOTH, pairs)  10.7 us
    ppermute x7, waiting for transfers between devices, to_chips(): return lax.ppermute(value, BOTH, pairs)  6.78 us
    pallas_call x12, Pallas kernels, call(): pl.pallas_call(kernel, out_shape=outs, in_specs=[SMEM] * scalars + [VMEM]...  4.56 us
    ppermute x4, starting transfers between devices, swap_cores(): return lax.ppermute(value, 'mp', [(m, m ^ 1) for m in range(4)])  2.63 us
    ppermute x4, waiting for transfers between devices, swap_cores(): return lax.ppermute(value, 'mp', [(m, m ^ 1) for m in range(4)])  2.45 us
    unnamed x18, local copies, waits for them, and re-layouts  1.49 us
    ppermute x1, starting transfers between devices, across(): lax.ppermute(value, BOTH, [(4 * z + m, 4 * z + (m ^ 2)) for z in range(4)...  0.76 us
  transfers between devices with their start and end apart: 12, of which 6 were waited for; matrix products, arithmetic and copies ran while one was open for 0% of the time, Pallas kernels for 9%

profile of v3, /device:TPU:0, one launch (start us, length us, event | category | flops | bytes accessed | tf_op | source)
XLA Modules:
  0.0 30.1 jit_solution(4232701949659480775)
XLA Ops:
  0.6 0.0 copy-start.8
  0.6 0.0 copy-start.7
  0.6 0.0 copy-start.6
  0.7 0.6 %copy-done.8 = f32[128,8]{0,1:T(8,128)S(1)} copy-done((f32[128,8]{0,1:T(8,128)S(1)}, f32[128,8]{0,1:T(8,128)}, u32[]{:S(2)}) %copy-start.8) | copy-done | bytes 4120
  1.3 0.0 copy-done.7
  1.3 0.3 copy-done.6
  1.6 0.0 copy-start.4
  1.6 0.0 copy-start.5
  1.6 0.0 copy-start
  1.6 0.0 copy-start.1
  1.6 0.3 route.1
  1.9 0.5 %collective-permute-start = (bf16[4,8,896]{2,1,0:T(8,128)(2,1)S(1)}, bf16[4,8,896]{2,1,0:T(8,128)(2,1)S(1)}, u32[]{:S(2)}, u32[]{:S(2)}) collective-permute-start(bf16[4,8,896]{2,1,0:T(8,128)(2,1)S(1)} %get-tuple-element.26.own_ref), channel_id=1, source_target_pairs={{0,1},{1,0},{2,3},{3,2},{4,5},{5,4},{6,7},{7,6},{8,9},{9,8},{10,11... | collective-permute-start | bytes 172040 | tf_op jit(solution)/shard_map/ppermute | solution.py:111
  2.4 0.9 %collective-permute-done.other_ref = bf16[4,8,896]{2,1,0:T(8,128)(2,1)S(1)} collective-permute-done((bf16[4,8,896]{2,1,0:T(8,128)(2,1)S(1)}, bf16[4,8,896]{2,1,0:T(8,128)(2,1)S(1)}, u32[]{:S(2)}, u32[]{:S(2)}) %collective-permute-start) | collective-permute-done | bytes 57376 | tf_op jit(solution)/shard_map/ppermute | solution.py:111
  3.3 5.0 %collective-permute-start.1 = (bf16[8,1920]{1,0:T(8,128)(2,1)S(1)}, bf16[8,1920]{1,0:T(8,128)(2,1)S(1)}, u32[]{:S(2)}, u32[]{:S(2)}) collective-permute-start(bf16[8,1920]{1,0:T(8,128)(2,1)S(1)} %get-tuple-element.29), channel_id=1, source_target_pairs={{0,12},{1,15},{2,14},{3,13},{4,8},{5,11},{6,10},{7,9},{8,4},{9,7},... | collective-permute-start | bytes 92168 | tf_op jit(solution)/shard_map/ppermute | solution.py:118
  8.3 0.0 collective-permute-start.2
  8.3 0.6 %collective-permute-start.3 = (bf16[8,1920]{1,0:T(8,128)(2,1)S(1)}, bf16[8,1920]{1,0:T(8,128)(2,1)S(1)}, u32[]{:S(2)}, u32[]{:S(2)}) collective-permute-start(bf16[8,1920]{1,0:T(8,128)(2,1)S(1)} %get-tuple-element.31), channel_id=1, source_target_pairs={{0,4},{1,7},{2,6},{3,5},{4,0},{5,3},{6,2},{7,1},{8,12},{9,15},{10,... | collective-permute-start | bytes 92168 | tf_op jit(solution)/shard_map/ppermute | solution.py:118
  9.0 0.7 %collective-permute-start.4 = (bf16[8,1920]{1,0:T(8,128)(2,1)S(1)}, bf16[8,1920]{1,0:T(8,128)(2,1)S(1)}, u32[]{:S(2)}, u32[]{:S(2)}) collective-permute-start(bf16[8,1920]{1,0:T(8,128)(2,1)S(1)} %get-tuple-element.28.own_ref), channel_id=1, source_target_pairs={{1,3},{3,1},{5,7},{7,5},{9,11},{11,9},{13,15},{15,13},{17,19},{19,... | collective-permute-start | bytes 92168 | tf_op jit(solution)/shard_map/ppermute | solution.py:118
  9.6 0.0 copy-done.3
  9.6 0.0 copy-done.4
  9.7 0.0 copy-done.5
  9.7 0.6 %spread.1 = (f32[2,3584]{1,0:T(2,128)S(1)}, f32[2,3584]{1,0:T(2,128)S(1)}, f32[2,3584]{1,0:T(2,128)S(1)}) custom-call(f32[2,28]{1,0:T(2,128)S(1)} %bitcast.19, f32[2,28]{1,0:T(2,128)S(1)} %bitcast.20, f32[2,28]{1,0:T(2,128)S(1)} %bitcast.21), custom_call_target="tpu_custom_call" | custom-call | tf_op jit(solution)/shard_map/spread/pallas_call | solution.py:329
  10.3 0.0 collective-permute-done.1.three_ref
  10.3 3.0 %collective-permute-done.2.two_ref = bf16[8,1920]{1,0:T(8,128)(2,1)S(1)} collective-permute-done((bf16[8,1920]{1,0:T(8,128)(2,1)S(1)}, bf16[8,1920]{1,0:T(8,128)(2,1)S(1)}, u32[]{:S(2)}, u32[]{:S(2)}) %collective-permute-start.2) | collective-permute-done | bytes 30752 | tf_op jit(solution)/shard_map/ppermute | solution.py:118
  13.3 0.0 collective-permute-done.3.one_ref
  13.3 0.0 collective-permute-done.4.zero_ref
  13.3 1.7 %collective-permute-start.5 = (bf16[32,1792]{1,0:T(8,128)(2,1)S(1)}, bf16[32,1792]{1,0:T(8,128)(2,1)S(1)}, u32[]{:S(2)}, u32[]{:S(2)}) collective-permute-start(bf16[32,1792]{1,0:T(8,128)(2,1)S(1)} %get-tuple-element.33.x_ref), channel_id=1, source_target_pairs={{0,1},{1,0},{2,3},{3,2},{4,5},{5,4},{6,7},{7,6},{8,9},{9,8},{10,11... | collective-permute-start | bytes 344072 | tf_op jit(solution)/shard_map/ppermute | solution.py:111
  15.0 0.0 copy-done
  15.0 0.0 copy-done.1
  15.0 0.0 copy-start.2
  15.0 0.4 %near.1 = (f32[64,256]{1,0:T(8,128)S(1)}, f32[64,256]{1,0:T(8,128)S(1)}) custom-call(bf16[32,1792]{1,0:T(8,128)(2,1)S(1)} %get-tuple-element.33.x_ref, bf16[3584,256]{1,0:T(8,128)(2,1)S(1)} %bitcast.13, bf16[3584,256]{1,0:T(8,128)(2,1)S(1)} %bitcast.15, f32[2,3584]{1,0:T(2,128)S(1)} %get-tuple-element.32._.gate_scale_ref, ...), custom_call_target="tpu_custom_call" | custom-call | tf_op jit(solution)/shard_map/near/pallas_call | solution.py:329
  15.4 0.5 %collective-permute-done.5.x_ref = bf16[32,1792]{1,0:T(8,128)(2,1)S(1)} collective-permute-done((bf16[32,1792]{1,0:T(8,128)(2,1)S(1)}, bf16[32,1792]{1,0:T(8,128)(2,1)S(1)}, u32[]{:S(2)}, u32[]{:S(2)}) %collective-permute-start.5) | collective-permute-done | bytes 114720 | tf_op jit(solution)/shard_map/ppermute | solution.py:111
  15.9 0.5 %copy-done.2 = bf16[1,256,3584]{2,1,0:T(8,128)(2,1)S(1)} copy-done((bf16[1,256,3584]{2,1,0:T(8,128)(2,1)S(1)}, bf16[1,256,3584]{2,1,0:T(8,128)(2,1)}, u32[]{:S(2)}) %copy-start.2) | copy-done | bytes 1835032
  16.5 0.6 %hidden.1 = (bf16[32,2048]{1,0:T(8,128)(2,1)S(1)}, bf16[32,256]{1,0:T(8,128)(2,1)S(1)}) custom-call(bf16[32,1792]{1,0:T(8,128)(2,1)S(1)} %collective-permute-done.5.x_ref, f32[64,256]{1,0:T(8,128)S(1)} %get-tuple-element.35.near_gate_ref, f32[64,256]{1,0:T(8,128)S(1)} %get-tuple-element.36.near_up_ref, bf16[3584,256]{1,0:T(8,128)(2,1)S(1)} %bitcast.14, ...), custom_call_target="tpu_custom_call" | custom-call | tf_op jit(solution)/shard_map/hidden/pallas_call | solution.py:329
  17.1 0.1 collective-permute-start.6
  17.2 0.3 keep.1.keep_ref
  17.5 1.1 %collective-permute-done.6.sent_ref = bf16[32,2048]{1,0:T(8,128)(2,1)S(1)} collective-permute-done((bf16[32,2048]{1,0:T(8,128)(2,1)S(1)}, bf16[32,2048]{1,0:T(8,128)(2,1)S(1)}, u32[]{:S(2)}, u32[]{:S(2)}) %collective-permute-start.6) | collective-permute-done | bytes 131104 | tf_op jit(solution)/shard_map/ppermute | solution.py:111
  18.6 0.8 %collective-permute-start.10 = (bf16[8,3840]{1,0:T(8,128)(2,1)S(1)}, bf16[8,3840]{1,0:T(8,128)(2,1)S(1)}, u32[]{:S(2)}, u32[]{:S(2)}) collective-permute-start(bf16[8,3840]{1,0:T(8,128)(2,1)S(1)} %get-tuple-element.40.own_ref), channel_id=1, source_target_pairs={{0,2},{1,3},{2,0},{3,1},{4,6},{5,7},{6,4},{7,5},{8,10},{9,11},{10,... | collective-permute-start | bytes 184328 | tf_op jit(solution)/shard_map/ppermute | solution.py:122
  19.3 3.4 %collective-permute-start.7 = (bf16[8,1792]{1,0:T(8,128)(2,1)S(1)}, bf16[8,1792]{1,0:T(8,128)(2,1)S(1)}, u32[]{:S(2)}, u32[]{:S(2)}) collective-permute-start(bf16[8,1792]{1,0:T(8,128)(2,1)S(1)} %get-tuple-element.41), channel_id=1, source_target_pairs={{0,12},{1,15},{2,14},{3,13},{4,8},{5,11},{6,10},{7,9},{8,4},{9,7},... | collective-permute-start | bytes 86024 | tf_op jit(solution)/shard_map/ppermute | solution.py:118
  22.8 0.0 collective-permute-start.8
  22.8 0.9 %collective-permute-start.9 = (bf16[8,1792]{1,0:T(8,128)(2,1)S(1)}, bf16[8,1792]{1,0:T(8,128)(2,1)S(1)}, u32[]{:S(2)}, u32[]{:S(2)}) collective-permute-start(bf16[8,1792]{1,0:T(8,128)(2,1)S(1)} %get-tuple-element.43), channel_id=1, source_target_pairs={{0,4},{1,7},{2,6},{3,5},{4,0},{5,3},{6,2},{7,1},{8,12},{9,15},{10,... | collective-permute-start | bytes 86024 | tf_op jit(solution)/shard_map/ppermute | solution.py:118
  23.7 1.3 %collective-permute-done.7.three_ref = bf16[8,1792]{1,0:T(8,128)(2,1)S(1)} collective-permute-done((bf16[8,1792]{1,0:T(8,128)(2,1)S(1)}, bf16[8,1792]{1,0:T(8,128)(2,1)S(1)}, u32[]{:S(2)}, u32[]{:S(2)}) %collective-permute-start.7) | collective-permute-done | bytes 28704 | tf_op jit(solution)/shard_map/ppermute | solution.py:118
  25.0 2.5 %collective-permute-done.8.two_ref = bf16[8,1792]{1,0:T(8,128)(2,1)S(1)} collective-permute-done((bf16[8,1792]{1,0:T(8,128)(2,1)S(1)}, bf16[8,1792]{1,0:T(8,128)(2,1)S(1)}, u32[]{:S(2)}, u32[]{:S(2)}) %collective-permute-start.8) | collective-permute-done | bytes 28704 | tf_op jit(solution)/shard_map/ppermute | solution.py:118
  27.5 0.0 collective-permute-done.9.one_ref
  27.5 0.0 collective-permute-done.10.zero_ref.crossed_ref
  27.6 0.3 %collective-permute-start.11 = (bf16[32,896]{1,0:T(8,128)(2,1)S(1)}, bf16[32,896]{1,0:T(8,128)(2,1)S(1)}, u32[]{:S(2)}, u32[]{:S(2)}) collective-permute-start(bf16[32,896]{1,0:T(8,128)(2,1)S(1)} %get-tuple-element.45), channel_id=1, source_target_pairs={{0,1},{1,0},{2,3},{3,2},{4,5},{5,4},{6,7},{7,6},{8,9},{9,8},{10,11... | collective-permute-start | bytes 172040 | tf_op jit(solution)/shard_map/ppermute | solution.py:111
  27.9 1.3 %hessian.1 = f32[256,1024]{1,0:T(8,128)} custom-call(bf16[32,128]{1,0:T(8,128)(2,1)S(1)} %get-tuple-element.46.count_ref, bf16[32,512]{1,0:T(8,128)(2,1)S(1)} %get-tuple-element.47.near_ref, bf16[8,3840]{1,0:T(8,128)(2,1)S(1)} %collective-permute-done.10.zero_ref.crossed_ref), custom_call_target="tpu_custom_call" | custom-call | tf_op jit(solution)/shard_map/hessian/pallas_call | solution.py:329
  29.2 0.0 collective-permute-done.11.far_ref
  29.2 0.9 %combine.1 = bf16[128,896]{1,0:T(8,128)(2,1)} custom-call(f32[32,128]{1,0:T(8,128)S(1)} %get-tuple-element.25.coef_ref, bf16[32,896]{1,0:T(8,128)(2,1)S(1)} %get-tuple-element.44.near_ref, bf16[32,896]{1,0:T(8,128)(2,1)S(1)} %collective-permute-done.11.far_ref), custom_call_target="tpu_custom_call" | custom-call | tf_op jit(solution)/shard_map/combine/pallas_call | solution.py:329
  (6 shorter events, 0.1 us)
Async XLA Ops:
  0.6 0.7 %copy-start.8 = (f32[128,8]{0,1:T(8,128)S(1)}, f32[128,8]{0,1:T(8,128)}, u32[]{:S(2)}) copy-start(f32[128,8]{0,1:T(8,128)} %param.11) | copy-start | bytes 12292
  0.6 0.7 %copy-start.7 = (s32[128,8]{0,1:T(8,128)S(1)}, s32[128,8]{0,1:T(8,128)}, u32[]{:S(2)}) copy-start(s32[128,8]{0,1:T(8,128)} %param.10) | copy-start | bytes 12292
  0.6 1.0 %copy-start.6 = (bf16[128,896]{1,0:T(8,128)(2,1)S(1)}, bf16[128,896]{1,0:T(8,128)(2,1)}, u32[]{:S(2)}) copy-start(bf16[128,896]{1,0:T(8,128)(2,1)} %tokens_ref.1) | copy-start | bytes 688132
  1.6 8.0 %copy-start.3 = (f32[1,28,2]{1,2,0:T(2,128)S(1)}, f32[1,28,2]{1,2,0:T(2,128)}, u32[]{:S(2)}) copy-start(f32[1,28,2]{1,2,0:T(2,128)} %param.13) | copy-start | bytes 676
  1.6 8.0 %copy-start.4 = (f32[1,28,2]{1,2,0:T(2,128)S(1)}, f32[1,28,2]{1,2,0:T(2,128)}, u32[]{:S(2)}) copy-start(f32[1,28,2]{1,2,0:T(2,128)} %param.15) | copy-start | bytes 676
  1.6 8.0 %copy-start.5 = (f32[1,2,28]{2,1,0:T(2,128)S(1)}, f32[1,2,28]{2,1,0:T(2,128)}, u32[]{:S(2)}) copy-start(f32[1,2,28]{2,1,0:T(2,128)} %param.17) | copy-start | bytes 676
  1.6 13.4 %copy-start = (bf16[1,3584,256]{2,1,0:T(8,128)(2,1)S(1)}, bf16[1,3584,256]{2,1,0:T(8,128)(2,1)}, u32[]{:S(2)}) copy-start(bf16[1,3584,256]{2,1,0:T(8,128)(2,1)} %param.12) | copy-start | bytes 5505028
  1.6 13.4 %copy-start.1 = (bf16[1,3584,256]{2,1,0:T(8,128)(2,1)S(1)}, bf16[1,3584,256]{2,1,0:T(8,128)(2,1)}, u32[]{:S(2)}) copy-start(bf16[1,3584,256]{2,1,0:T(8,128)(2,1)} %param.14) | copy-start | bytes 5505028
  1.9 1.4 %collective-permute-start = (bf16[4,8,896]{2,1,0:T(8,128)(2,1)S(1)}, bf16[4,8,896]{2,1,0:T(8,128)(2,1)S(1)}, u32[]{:S(2)}, u32[]{:S(2)}) collective-permute-start(bf16[4,8,896]{2,1,0:T(8,128)(2,1)S(1)} %get-tuple-element.26.own_ref), channel_id=1, source_target_pairs={{0,1},{1,0},{2,3},{3,2},{4,5},{5,4},{6,7},{7,6},{8,9},{9,8},{10,11... | collective-permute-start | bytes 172040 | tf_op jit(solution)/shard_map/ppermute | solution.py:111
  3.3 7.0 %collective-permute-start.1 = (bf16[8,1920]{1,0:T(8,128)(2,1)S(1)}, bf16[8,1920]{1,0:T(8,128)(2,1)S(1)}, u32[]{:S(2)}, u32[]{:S(2)}) collective-permute-start(bf16[8,1920]{1,0:T(8,128)(2,1)S(1)} %get-tuple-element.29), channel_id=1, source_target_pairs={{0,12},{1,15},{2,14},{3,13},{4,8},{5,11},{6,10},{7,9},{8,4},{9,7},... | collective-permute-start | bytes 92168 | tf_op jit(solution)/shard_map/ppermute | solution.py:118
  8.3 4.9 %collective-permute-start.2 = (bf16[8,1920]{1,0:T(8,128)(2,1)S(1)}, bf16[8,1920]{1,0:T(8,128)(2,1)S(1)}, u32[]{:S(2)}, u32[]{:S(2)}) collective-permute-start(bf16[8,1920]{1,0:T(8,128)(2,1)S(1)} %get-tuple-element.30), channel_id=1, source_target_pairs={{0,8},{1,11},{2,10},{3,9},{4,12},{5,15},{6,14},{7,13},{8,0},{9,3},... | collective-permute-start | bytes 92168 | tf_op jit(solution)/shard_map/ppermute | solution.py:118
  8.3 4.9 %collective-permute-start.3 = (bf16[8,1920]{1,0:T(8,128)(2,1)S(1)}, bf16[8,1920]{1,0:T(8,128)(2,1)S(1)}, u32[]{:S(2)}, u32[]{:S(2)}) collective-permute-start(bf16[8,1920]{1,0:T(8,128)(2,1)S(1)} %get-tuple-element.31), channel_id=1, source_target_pairs={{0,4},{1,7},{2,6},{3,5},{4,0},{5,3},{6,2},{7,1},{8,12},{9,15},{10,... | collective-permute-start | bytes 92168 | tf_op jit(solution)/shard_map/ppermute | solution.py:118
  9.0 4.3 %collective-permute-start.4 = (bf16[8,1920]{1,0:T(8,128)(2,1)S(1)}, bf16[8,1920]{1,0:T(8,128)(2,1)S(1)}, u32[]{:S(2)}, u32[]{:S(2)}) collective-permute-start(bf16[8,1920]{1,0:T(8,128)(2,1)S(1)} %get-tuple-element.28.own_ref), channel_id=1, source_target_pairs={{1,3},{3,1},{5,7},{7,5},{9,11},{11,9},{13,15},{15,13},{17,19},{19,... | collective-permute-start | bytes 92168 | tf_op jit(solution)/shard_map/ppermute | solution.py:118
  13.3 2.7 %collective-permute-start.5 = (bf16[32,1792]{1,0:T(8,128)(2,1)S(1)}, bf16[32,1792]{1,0:T(8,128)(2,1)S(1)}, u32[]{:S(2)}, u32[]{:S(2)}) collective-permute-start(bf16[32,1792]{1,0:T(8,128)(2,1)S(1)} %get-tuple-element.33.x_ref), channel_id=1, source_target_pairs={{0,1},{1,0},{2,3},{3,2},{4,5},{5,4},{6,7},{7,6},{8,9},{9,8},{10,11... | collective-permute-start | bytes 344072 | tf_op jit(solution)/shard_map/ppermute | solution.py:111
  15.0 1.5 %copy-start.2 = (bf16[1,256,3584]{2,1,0:T(8,128)(2,1)S(1)}, bf16[1,256,3584]{2,1,0:T(8,128)(2,1)}, u32[]{:S(2)}) copy-start(bf16[1,256,3584]{2,1,0:T(8,128)(2,1)} %param.16) | copy-start | bytes 5505028
  17.1 1.4 %collective-permute-start.6 = (bf16[32,2048]{1,0:T(8,128)(2,1)S(1)}, bf16[32,2048]{1,0:T(8,128)(2,1)S(1)}, u32[]{:S(2)}, u32[]{:S(2)}) collective-permute-start(bf16[32,2048]{1,0:T(8,128)(2,1)S(1)} %get-tuple-element.39), channel_id=1, source_target_pairs={{0,1},{1,0},{2,3},{3,2},{4,5},{5,4},{6,7},{7,6},{8,9},{9,8},{10,11... | collective-permute-start | bytes 393224 | tf_op jit(solution)/shard_map/ppermute | solution.py:111
  18.6 9.0 %collective-permute-start.10 = (bf16[8,3840]{1,0:T(8,128)(2,1)S(1)}, bf16[8,3840]{1,0:T(8,128)(2,1)S(1)}, u32[]{:S(2)}, u32[]{:S(2)}) collective-permute-start(bf16[8,3840]{1,0:T(8,128)(2,1)S(1)} %get-tuple-element.40.own_ref), channel_id=1, source_target_pairs={{0,2},{1,3},{2,0},{3,1},{4,6},{5,7},{6,4},{7,5},{8,10},{9,11},{10,... | collective-permute-start | bytes 184328 | tf_op jit(solution)/shard_map/ppermute | solution.py:122
  19.3 5.7 %collective-permute-start.7 = (bf16[8,1792]{1,0:T(8,128)(2,1)S(1)}, bf16[8,1792]{1,0:T(8,128)(2,1)S(1)}, u32[]{:S(2)}, u32[]{:S(2)}) collective-permute-start(bf16[8,1792]{1,0:T(8,128)(2,1)S(1)} %get-tuple-element.41), channel_id=1, source_target_pairs={{0,12},{1,15},{2,14},{3,13},{4,8},{5,11},{6,10},{7,9},{8,4},{9,7},... | collective-permute-start | bytes 86024 | tf_op jit(solution)/shard_map/ppermute | solution.py:118
  22.8 4.8 %collective-permute-start.8 = (bf16[8,1792]{1,0:T(8,128)(2,1)S(1)}, bf16[8,1792]{1,0:T(8,128)(2,1)S(1)}, u32[]{:S(2)}, u32[]{:S(2)}) collective-permute-start(bf16[8,1792]{1,0:T(8,128)(2,1)S(1)} %get-tuple-element.42), channel_id=1, source_target_pairs={{0,8},{1,11},{2,10},{3,9},{4,12},{5,15},{6,14},{7,13},{8,0},{9,3},... | collective-permute-start | bytes 86024 | tf_op jit(solution)/shard_map/ppermute | solution.py:118
  22.8 4.8 %collective-permute-start.9 = (bf16[8,1792]{1,0:T(8,128)(2,1)S(1)}, bf16[8,1792]{1,0:T(8,128)(2,1)S(1)}, u32[]{:S(2)}, u32[]{:S(2)}) collective-permute-start(bf16[8,1792]{1,0:T(8,128)(2,1)S(1)} %get-tuple-element.43), channel_id=1, source_target_pairs={{0,4},{1,7},{2,6},{3,5},{4,0},{5,3},{6,2},{7,1},{8,12},{9,15},{10,... | collective-permute-start | bytes 86024 | tf_op jit(solution)/shard_map/ppermute | solution.py:118
  27.6 1.6 %collective-permute-start.11 = (bf16[32,896]{1,0:T(8,128)(2,1)S(1)}, bf16[32,896]{1,0:T(8,128)(2,1)S(1)}, u32[]{:S(2)}, u32[]{:S(2)}) collective-permute-start(bf16[32,896]{1,0:T(8,128)(2,1)S(1)} %get-tuple-element.45), channel_id=1, source_target_pairs={{0,1},{1,0},{2,3},{3,2},{4,5},{5,4},{6,7},{7,6},{8,9},{9,8},{10,11... | collective-permute-start | bytes 172040 | tf_op jit(solution)/shard_map/ppermute | solution.py:111

commit v4 on v3

--- a/solution.py
+++ b/solution.py
@@ -113,8 +113,6 @@
 
 def to_chips(value, k):
     pairs = [(4 * z + m, 4 * (z ^ k) + (m ^ 2 * (m & 1))) for z in range(4) for m in range(4)]
-    if k == 0:
-        pairs = [(a, b) for a, b in pairs if a != b]
     return lax.ppermute(value, BOTH, pairs)
 
 
@@ -127,7 +125,7 @@
     out_ref[...] = jnp.where(row < column, 1.0, 0.0).astype(BF16)
 
 
-def route_kernel(capacity, earlier_ref, ids_ref, weights_ref, tokens_ref, rows_ref, count_ref, coef_ref):
+def route_kernel(capacity, earlier_ref, ids_ref, weights_ref, tokens_ref, rows_ref, cross_ref, count_ref, coef_ref):
     z = lax.axis_index("expert")
     ids, weights = ids_ref[...], weights_ref[...]
     rows = ids.shape[1]
@@ -154,6 +152,8 @@
         jnp.concatenate(chosen, axis=0).astype(BF16), tokens_ref[...], preferred_element_type=F32
     ).astype(BF16)
     rows_ref[...] = picked.reshape(rows_ref.shape)
+    cross_ref[...] = jnp.zeros_like(cross_ref)
+    cross_ref[:, : picked.shape[1]] = picked[:capacity]
 
 
 def spread_kernel(*refs):
@@ -164,17 +164,26 @@
 
 
 def line_up_kernel(own_ref, other_ref, count_ref, *out_refs):
-    for k, out_ref in enumerate(out_refs):
+    for k, out_ref in enumerate(out_refs, 1):
         out_ref[...] = jnp.concatenate([own_ref[k], other_ref[k], count_ref[k]], axis=1)
 
 
-def collect_kernel(own_ref, three_ref, two_ref, one_ref, zero_ref, _, out_ref, count_ref):
-    rows, width = own_ref.shape[0], out_ref.shape[1]
-    crossed = (lax.axis_index("mp") % 2 == 1).astype(F32)
-    value = own_ref[...].astype(F32) * (1.0 - crossed) + zero_ref[...].astype(F32) * crossed
-    for k, rows_in in enumerate((value.astype(BF16), one_ref[...], two_ref[...], three_ref[...])):
-        out_ref[k * rows : (k + 1) * rows, :] = rows_in[:, :width]
-        count_ref[k * rows : (k + 1) * rows, :] = rows_in[:, width:]
+def on_core(core):
+    return (lax.axis_index("mp") % 2 == core).astype(F32)
+
+
+def collect_kernel(own_ref, other_ref, count_ref, crossed_ref, three_ref, two_ref, one_ref, _, out_ref, counts_ref):
+    rows, width = crossed_ref.shape[0], out_ref.shape[1] // 2
+    crossed = crossed_ref[:, :width]
+    zero = on_core(0)
+    out_ref[:rows, :width] = (own_ref[0].astype(F32) * zero + crossed.astype(F32) * (1.0 - zero)).astype(BF16)
+    out_ref[:rows, width:] = (other_ref[0].astype(F32) * zero).astype(BF16)
+    counts_ref[:rows, :] = count_ref[0]
+    for k, ref in enumerate((one_ref, two_ref, three_ref), 1):
+        out_ref[k * rows : (k + 1) * rows, :] = ref[:, : 2 * width]
+        counts_ref[k * rows : (k + 1) * rows, :] = ref[:, 2 * width :]
+    out_ref[4 * rows :, :width] = crossed
+    out_ref[4 * rows :, width:] = jnp.zeros_like(crossed)
 
 
 def shares_in_order():
@@ -183,39 +192,24 @@
     return (first, first ^ 1, first ^ 3, first ^ 2)
 
 
-def project(x_ref, shares, weight_ref, scale_ref):
-    slots, width = x_ref.shape[0], x_ref.shape[1] // len(shares)
-    total = None
-    for part, share in enumerate(shares):
-        depth = pl.ds(pl.multiple_of(share * width, width), width)
-        x = x_ref[:, part * width : (part + 1) * width].astype(F32)
-        scaled = jnp.concatenate([(x * scale_ref[i : i + 1, depth]).astype(BF16) for i in range(2)], axis=0)
-        term = jnp.dot(scaled, weight_ref[depth, :], preferred_element_type=F32)
-        total = term if total is None else total + term
-    return total
-
-
-def project_down(parts, shares, down_ref, scale_ref, out_ref):
-    slots, width = parts[0].shape[0], down_ref.shape[1] // 4
-    none = jnp.zeros_like(parts[0])
-    stacked = jnp.concatenate(
-        [jnp.concatenate([parts[0], none], axis=1), jnp.concatenate([none, parts[1]], axis=1)], axis=0
-    )
-    for part, share in enumerate(shares):
-        lanes = pl.ds(pl.multiple_of(share * width, width), width)
-        both = jnp.dot(stacked, down_ref[:, lanes], preferred_element_type=F32)
-        value = both[:slots] * scale_ref[:1, lanes] + both[slots:] * scale_ref[1:, lanes]
-        out_ref[:, part * width : (part + 1) * width] = value.astype(BF16)
+def project(x, share, weight_ref, scale_ref):
+    width = x.shape[1]
+    depth = pl.ds(pl.multiple_of(share * width, width), width)
+    scaled = jnp.concatenate([(x * scale_ref[i : i + 1, depth]).astype(BF16) for i in range(2)], axis=0)
+    return jnp.dot(scaled, weight_ref[depth, :], preferred_element_type=F32)
 
 
 def near_kernel(x_ref, gate_ref, up_ref, gate_scale_ref, up_scale_ref, gate_out_ref, up_out_ref):
-    shares = shares_in_order()[:2]
-    gate_out_ref[...] = project(x_ref, shares, gate_ref, gate_scale_ref)
-    up_out_ref[...] = project(x_ref, shares, up_ref, up_scale_ref)
+    share = shares_in_order()[0]
+    slots, width = gate_out_ref.shape[0] // 2, x_ref.shape[1] // 2
+    x = x_ref[:slots, :width].astype(F32)
+    gate_out_ref[...] = project(x, share, gate_ref, gate_scale_ref)
+    up_out_ref[...] = project(x, share, up_ref, up_scale_ref)
 
 
 def hidden_kernel(
-    x_ref,
+    arrived_ref,
+    swapped_ref,
     near_gate_ref,
     near_up_ref,
     gate_ref,
@@ -225,67 +219,87 @@
     up_scale_ref,
     down_scale_ref,
     send_ref,
+    keep_ref,
     hidden_ref,
+    cross_ref,
 ):
-    shares = shares_in_order()[2:]
-    gate = near_gate_ref[...] + project(x_ref, shares, gate_ref, gate_scale_ref)
-    up = near_up_ref[...] + project(x_ref, shares, up_ref, up_scale_ref)
-    slots, half = x_ref.shape[0], gate_ref.shape[1] // 2
+    shares = shares_in_order()
+    slots, half = near_gate_ref.shape[0] // 2, gate_ref.shape[1] // 2
+    rows, width = slots // 4, arrived_ref.shape[1] // 2
+    zero = on_core(0)
+    filled = []
+    for ref, lacks, missing_ref in ((arrived_ref, 1.0 - zero, swapped_ref), (swapped_ref, zero, arrived_ref)):
+        first = ref[:rows, width:].astype(F32) + missing_ref[slots:, :width].astype(F32) * lacks
+        filled.append(jnp.concatenate([first, ref[rows:slots, width:].astype(F32)], axis=0))
+    gate, up = near_gate_ref[...], near_up_ref[...]
+    for x, share in ((filled[0], shares[1]), (swapped_ref[:slots, :width].astype(F32), shares[2]), (filled[1], shares[3])):
+        gate += project(x, share, gate_ref, gate_scale_ref)
+        up += project(x, share, up_ref, up_scale_ref)
     parts = []
     for i in range(2):
         g = gate[i * slots : (i + 1) * slots, i * half : (i + 1) * half]
         u = up[i * slots : (i + 1) * slots, i * half : (i + 1) * half]
         parts.append((g / (1.0 + jnp.exp(-g)) * u).astype(BF16))
-        hidden_ref[:, i * half : (i + 1) * half] = parts[i]
-        send_ref[:, x_ref.shape[1] + i * half : x_ref.shape[1] + (i + 1) * half] = parts[i]
-    project_down(parts, shares, down_ref, down_scale_ref, send_ref)
-
-
-def keep_kernel(hidden_ref, down_ref, down_scale_ref, keep_ref):
-    half = hidden_ref.shape[1] // 2
-    parts = (hidden_ref[:, :half], hidden_ref[:, half:])
-    project_down(parts, shares_in_order()[:2], down_ref, down_scale_ref, keep_ref)
-
-
-def chip_sum_kernel(keep_ref, sent_ref, hidden_ref, message_ref, one_ref, two_ref, three_ref, near_ref):
-    width, hidden_width = keep_ref.shape[1], hidden_ref.shape[1]
-    rows = one_ref.shape[0]
-    for k, out_ref in enumerate((message_ref, one_ref, two_ref, three_ref)):
+        lanes = slice(i * half, (i + 1) * half)
+        hidden_ref[:, lanes] = parts[i]
+        send_ref[:, 2 * width + i * half : 2 * width + (i + 1) * half] = parts[i]
+        for k in range(4):
+            into = 2 * width + 2 * k * half + i * half
+            cross_ref[:, into : into + half] = parts[i][k * rows : (k + 1) * rows]
+    none = jnp.zeros_like(parts[0])
+    stacked = jnp.concatenate(
+        [jnp.concatenate([parts[0], none], axis=1), jnp.concatenate([none, parts[1]], axis=1)], axis=0
+    )
+    for out_ref, part, share in (
+        (send_ref, 0, shares[2]),
+        (send_ref, 1, shares[3]),
+        (keep_ref, 0, shares[0]),
+        (keep_ref, 1, shares[1]),
+    ):
+        lanes = pl.ds(pl.multiple_of(share * width, width), width)
+        both = jnp.dot(stacked, down_ref[:, lanes], preferred_element_type=F32)
+        value = both[:slots] * down_scale_ref[:1, lanes] + both[slots:] * down_scale_ref[1:, lanes]
+        out_ref[:, part * width : (part + 1) * width] = value.astype(BF16)
+    for part in range(2):
+        lanes, turned = slice(part * width, (part + 1) * width), slice((1 - part) * width, (2 - part) * width)
+        value = send_ref[:rows, turned].astype(F32) * zero + keep_ref[:rows, lanes].astype(F32) * (1.0 - zero)
+        cross_ref[:, lanes] = value.astype(BF16)
+
+
+def chip_sum_kernel(keep_ref, sent_ref, *out_refs):
+    rows, width = out_refs[0].shape
+    for k, out_ref in enumerate(out_refs):
         at = slice(k * rows, (k + 1) * rows)
-        both = keep_ref[at, :].astype(F32) + sent_ref[at, :width].astype(F32)
-        out_ref[:, :width] = both.astype(BF16)
-        near = jnp.concatenate([hidden_ref[at, :], sent_ref[at, width:]], axis=1)
-        near_ref[at, :] = near
-        into = width + 2 * k * hidden_width
-        message_ref[:, into : into + 2 * hidden_width] = near
-
-
-def hessian_kernel(count_ref, near_ref, crossed_ref, out_ref):
+        out_ref[...] = (keep_ref[at, :].astype(F32) + sent_ref[at, :width].astype(F32)).astype(BF16)
+
+
+def unpack_kernel(crossed_ref, out_ref):
+    width = out_ref.shape[1]
+    rows = out_ref.shape[0] // 4
+    start = crossed_ref.shape[1] - 4 * width
+    for k in range(4):
+        out_ref[k * rows : (k + 1) * rows, :] = crossed_ref[:, start + k * width : start + (k + 1) * width]
+
+
+def hessian_kernel(count_ref, own_ref, sent_ref, far_ref, other_far_ref, out_ref, done_ref):
     m = lax.axis_index("mp")
     width = out_ref.shape[0]
     rows = count_ref.shape[0] // 4
     counts = [count_ref[k * rows : k * rows + 1, :].astype(F32)[:, :1] for k in range(4)]
     factor = 2.0 / (counts[0] + counts[1] + counts[2] + counts[3])
-    own = near_ref[:, :width]
-    start = crossed_ref.shape[1] - 8 * width
-    far = [crossed_ref[:, start + i * width : start + (i + 1) * width] for i in range(8)]
-    others = (
-        (m, own),
-        (m ^ 1, near_ref[:, width:]),
-        (m ^ 2, jnp.concatenate(far[0::2], axis=0)),
-        (m ^ 3, jnp.concatenate(far[1::2], axis=0)),
-    )
+    own = own_ref[...]
+    others = ((m, own), (m ^ 1, sent_ref[:, sent_ref.shape[1] - width :]), (m ^ 2, far_ref[...]), (m ^ 3, other_far_ref[...]))
     for share, other in others:
         block = lax.dot_general(own, other, (((0,), (0,)), ((), ())), preferred_element_type=F32)
         out_ref[:, pl.ds(pl.multiple_of(share * width, width), width)] = block * factor
-
-
-def collect_back_kernel(own_ref, three_ref, two_ref, one_ref, zero_ref, mine_ref, other_ref):
+    done_ref[...] = jnp.zeros_like(done_ref)
+
+
+def collect_back_kernel(summed_ref, crossed_ref, three_ref, two_ref, one_ref, _, mine_ref, other_ref):
     rows, width = one_ref.shape[0], mine_ref.shape[1]
-    crossed = (lax.axis_index("mp") % 2 == 1).astype(F32)
-    here = slice(0, 2 * width)
-    value = own_ref[:, here].astype(F32) * (1.0 - crossed) + zero_ref[:, here].astype(F32) * crossed
-    for k, rows_in in enumerate((value.astype(BF16), one_ref[...], two_ref[...], three_ref[...])):
+    crossed = crossed_ref[:, : 2 * width].astype(F32)
+    value = (crossed + summed_ref[...].astype(F32) * on_core(0)).astype(BF16)
+    for k, rows_in in enumerate((value, one_ref[...], two_ref[...], three_ref[...])):
         mine_ref[k * rows : (k + 1) * rows, :] = rows_in[:, :width]
         other_ref[k * rows : (k + 1) * rows, :] = rows_in[:, width:]
 
@@ -337,18 +351,22 @@
         )(*args)
 
     earlier = call(earlier_kernel, "earlier", shape((rows, rows), BF16), (), flops=4 * 10**9)
-    picked, counts, coef = call(
+    picked, cross, counts, coef = call(
         functools.partial(route_kernel, capacity),
         "route",
-        (shape((4, capacity, width), BF16), shape((4, capacity, QBLK), BF16), shape((slots, rows), F32)),
+        (
+            shape((4, capacity, width), BF16),
+            shape((capacity, 2 * width + 2 * QBLK), BF16),
+            shape((4, capacity, QBLK), BF16),
+            shape((slots, rows), F32),
+        ),
         (earlier, route_ids.T, route_weights.T, tokens),
         flops=10**11,
     )
+    other = swap_cores(picked)
+    crossed = across(cross)
     messages = call(
-        line_up_kernel,
-        "line_up",
-        (shape((capacity, 2 * width + QBLK), BF16),) * 4,
-        (picked, swap_cores(picked), counts),
+        line_up_kernel, "line_up", (shape((capacity, 2 * width + QBLK), BF16),) * 3, (picked, other, counts)
     )
     scales = call(
         spread_kernel,
@@ -362,8 +380,8 @@
     arrived, arrived_counts = call(
         collect_kernel,
         "collect",
-        (shape((slots, 2 * width), BF16), shape((slots, QBLK), BF16)),
-        (messages[0], *[to_chips(messages[k], k) for k in (3, 2, 1, 0)], scales[0]),
+        (shape((slots + capacity, 2 * width), BF16), shape((slots, QBLK), BF16)),
+        (picked, other, counts, crossed, *[to_chips(messages[k - 1], k) for k in (3, 2, 1)], scales[0]),
     )
     swapped = swap_cores(arrived)
     near = call(
@@ -372,36 +390,33 @@
         (shape((2 * slots, hidden_width), F32),) * 2,
         (arrived, gate, up, *scales[:2]),
     )
-    send, hidden = call(
+    send, keep, hidden, cross = call(
         hidden_kernel,
         "hidden",
-        (shape((slots, 2 * width + hidden_width), BF16), shape((slots, hidden_width), BF16)),
-        (swapped, *near, gate, up, down, *scales),
+        (
+            shape((slots, 2 * width + hidden_width), BF16),
+            shape((slots, 2 * width), BF16),
+            shape((slots, hidden_width), BF16),
+            shape((capacity, 2 * width + 4 * hidden_width), BF16),
+        ),
+        (arrived, swapped, *near, gate, up, down, *scales),
     )
     sent = swap_cores(send)
-    keep = call(keep_kernel, "keep", shape((slots, 2 * width), BF16), (hidden, down, scales[2]))
-
-    message, *summed, chip_hidden = call(
-        chip_sum_kernel,
-        "chip_sum",
-        (
-            shape((capacity, 2 * width + 8 * hidden_width), BF16),
-            *[shape((capacity, 2 * width), BF16)] * 3,
-            shape((slots, 2 * hidden_width), BF16),
-        ),
-        (keep, sent, hidden),
-    )
-    crossed = across(message)
-    back = {k: to_chips(summed[k - 1], k) for k in range(1, 4)}
-    back[0] = crossed
-    hessian = call(
+    crossed = across(cross)
+    summed = call(chip_sum_kernel, "chip_sum", (shape((capacity, 2 * width), BF16),) * 4, (keep, sent))
+    back = {k: to_chips(summed[k], k) for k in range(1, 4)}
+    far = call(unpack_kernel, "unpack", shape((slots, hidden_width), BF16), (crossed,))
+    hessian, done = call(
         hessian_kernel,
         "hessian",
-        shape((hidden_width, 4 * hidden_width), F32),
-        (arrived_counts, chip_hidden, crossed),
+        (shape((hidden_width, 4 * hidden_width), F32), shape((8, QBLK), F32)),
+        (arrived_counts, hidden, sent, far, swap_cores(far)),
     )
     mine, other = call(
-        collect_back_kernel, "collect_back", (shape((slots, width), BF16),) * 2, (message, *[back[k] for k in (3, 2, 1, 0)])
+        collect_back_kernel,
+        "collect_back",
+        (shape((slots, width), BF16),) * 2,
+        (summed[0], crossed, *[back[k] for k in (3, 2, 1)], done),
     )
     mixed = call(
         combine_kernel, "combine", shape((rows, width), BF16), (coef, mine, swap_cores(other))

time: 30.3 us -> 27.9 us (0.921)
  waiting for transfers between devices: 9.23 us -> 6.12 us
  starting transfers between devices: 14.1 us -> 15 us
    ppermute x7 -> x6, waiting for transfers between devices: 6.78 us -> 3.51 us  [to_chips(): return lax.ppermute(value, BOTH, pairs)]
    ppermute x1 -> x2, starting transfers between devices: 0.76 us -> 3.71 us  [across(): lax.ppermute(value, BOTH, [(4 * z + m, 4 * z + (m ^ 2)) for z in range(4)...]
    ppermute x7 -> x6, starting transfers between devices: 10.7 us -> 8.9 us  [to_chips(): return lax.ppermute(value, BOTH, pairs)]
    ppermute x4 -> x5, starting transfers between devices: 2.63 us -> 2.41 us  [swap_cores(): return lax.ppermute(value, 'mp', [(m, m ^ 1) for m in range(4)])]
    ppermute x4 -> x5, waiting for transfers between devices: 2.45 us -> 2.61 us  [swap_cores(): return lax.ppermute(value, 'mp', [(m, m ^ 1) for m in range(4)])]
  transfers between devices with their start and end apart: 12 -> 13, of which waited for: 6 -> 5; matrix products, arithmetic and copies ran while one was open for 0% -> 0% of each run, Pallas kernels for 9% -> 8%
where the time goes in v4:
time: 27.9 us; the launch traced here: 27.7 us
  starting transfers between devices  15 us (54%)
  waiting for transfers between devices  6.12 us (22%)
  Pallas kernels  4.5 us (16%)
  local copies, waits for them, and re-layouts  1.29 us (5%)
  between operations  0.75 us (3%)
    ppermute x6, starting transfers between devices, to_chips(): return lax.ppermute(value, BOTH, pairs)  8.9 us
    pallas_call x12, Pallas kernels, call(): pl.pallas_call(kernel, out_shape=outs, in_specs=[SMEM] * scalars + [VMEM]...  4.5 us
    ppermute x2, starting transfers between devices, across(): lax.ppermute(value, BOTH, [(4 * z + m, 4 * z + (m ^ 2)) for z in range(4)...  3.71 us
    ppermute x6, waiting for transfers between devices, to_chips(): return lax.ppermute(value, BOTH, pairs)  3.51 us
    ppermute x5, waiting for transfers between devices, swap_cores(): return lax.ppermute(value, 'mp', [(m, m ^ 1) for m in range(4)])  2.61 us
    ppermute x5, starting transfers between devices, swap_cores(): return lax.ppermute(value, 'mp', [(m, m ^ 1) for m in range(4)])  2.41 us
    unnamed x18, local copies, waits for them, and re-layouts  1.29 us
  transfers between devices with their start and end apart: 13, of which 5 were waited for; matrix products, arithmetic and copies ran while one was open for 0% of the time, Pallas kernels for 8%

profile of v4, /device:TPU:0, one launch (start us, length us, event | category | flops | bytes accessed | tf_op | source)
XLA Modules:
  0.0 27.7 jit_solution(11061908390471587786)
XLA Ops:
  0.6 0.0 copy-start.8
  0.6 0.0 copy-start.7
  0.6 0.0 copy-start.6
  0.7 0.6 %copy-done.8 = f32[128,8]{0,1:T(8,128)S(1)} copy-done((f32[128,8]{0,1:T(8,128)S(1)}, f32[128,8]{0,1:T(8,128)}, u32[]{:S(2)}) %copy-start.8) | copy-done | bytes 4120
  1.3 0.0 copy-done.7
  1.3 0.3 copy-done.6
  1.6 0.0 copy-start.3
  1.6 0.0 copy-start.4
  1.6 0.0 copy-start.5
  1.6 0.0 copy-start.1
  1.6 0.3 route.1
  1.9 0.5 %collective-permute-start = (bf16[4,8,896]{2,1,0:T(8,128)(2,1)S(1)}, bf16[4,8,896]{2,1,0:T(8,128)(2,1)S(1)}, u32[]{:S(2)}, u32[]{:S(2)}) collective-permute-start(bf16[4,8,896]{2,1,0:T(8,128)(2,1)S(1)} %get-tuple-element.29.own_ref), channel_id=1, source_target_pairs={{0,1},{1,0},{2,3},{3,2},{4,5},{5,4},{6,7},{7,6},{8,9},{9,8},{10,11... | collective-permute-start | bytes 172040 | tf_op jit(solution)/shard_map/ppermute | solution.py:111
  2.4 2.6 %collective-permute-start.1 = (bf16[8,2048]{1,0:T(8,128)(2,1)S(1)}, bf16[8,2048]{1,0:T(8,128)(2,1)S(1)}, u32[]{:S(2)}, u32[]{:S(2)}) collective-permute-start(bf16[8,2048]{1,0:T(8,128)(2,1)S(1)} %get-tuple-element.31), channel_id=1, source_target_pairs={{0,2},{1,3},{2,0},{3,1},{4,6},{5,7},{6,4},{7,5},{8,10},{9,11},{10,... | collective-permute-start | bytes 98312 | tf_op jit(solution)/shard_map/ppermute | solution.py:120
  5.0 0.0 collective-permute-done.other_ref
  5.0 3.7 %collective-permute-start.2 = (bf16[8,1920]{1,0:T(8,128)(2,1)S(1)}, bf16[8,1920]{1,0:T(8,128)(2,1)S(1)}, u32[]{:S(2)}, u32[]{:S(2)}) collective-permute-start(bf16[8,1920]{1,0:T(8,128)(2,1)S(1)} %get-tuple-element.32), channel_id=1, source_target_pairs={{0,12},{1,15},{2,14},{3,13},{4,8},{5,11},{6,10},{7,9},{8,4},{9,7},... | collective-permute-start | bytes 92168 | tf_op jit(solution)/shard_map/ppermute | solution.py:116
  8.7 0.0 collective-permute-start.3
  8.7 0.8 %collective-permute-start.4 = (bf16[8,1920]{1,0:T(8,128)(2,1)S(1)}, bf16[8,1920]{1,0:T(8,128)(2,1)S(1)}, u32[]{:S(2)}, u32[]{:S(2)}) collective-permute-start(bf16[8,1920]{1,0:T(8,128)(2,1)S(1)} %get-tuple-element.34), channel_id=1, source_target_pairs={{0,4},{1,7},{2,6},{3,5},{4,0},{5,3},{6,2},{7,1},{8,12},{9,15},{10,... | collective-permute-start | bytes 92168 | tf_op jit(solution)/shard_map/ppermute | solution.py:116
  9.4 0.0 copy-done.3
  9.4 0.0 copy-done.4
  9.5 0.0 copy-done.5
  9.5 0.6 %spread.1 = (f32[2,3584]{1,0:T(2,128)S(1)}, f32[2,3584]{1,0:T(2,128)S(1)}, f32[2,3584]{1,0:T(2,128)S(1)}) custom-call(f32[2,28]{1,0:T(2,128)S(1)} %bitcast.18, f32[2,28]{1,0:T(2,128)S(1)} %bitcast.19, f32[2,28]{1,0:T(2,128)S(1)} %bitcast.20), custom_call_target="tpu_custom_call" | custom-call | tf_op jit(solution)/shard_map/spread/pallas_call | solution.py:343
  10.1 0.0 collective-permute-done.1.crossed_ref
  10.1 0.8 %collective-permute-done.2.three_ref = bf16[8,1920]{1,0:T(8,128)(2,1)S(1)} collective-permute-done((bf16[8,1920]{1,0:T(8,128)(2,1)S(1)}, bf16[8,1920]{1,0:T(8,128)(2,1)S(1)}, u32[]{:S(2)}, u32[]{:S(2)}) %collective-permute-start.2) | collective-permute-done | bytes 30752 | tf_op jit(solution)/shard_map/ppermute | solution.py:116
  10.9 2.7 %collective-permute-done.3.two_ref = bf16[8,1920]{1,0:T(8,128)(2,1)S(1)} collective-permute-done((bf16[8,1920]{1,0:T(8,128)(2,1)S(1)}, bf16[8,1920]{1,0:T(8,128)(2,1)S(1)}, u32[]{:S(2)}, u32[]{:S(2)}) %collective-permute-start.3) | collective-permute-done | bytes 30752 | tf_op jit(solution)/shard_map/ppermute | solution.py:116
  13.6 0.0 collective-permute-done.4.one_ref
  13.6 0.3 collective-permute-start.5
  13.9 0.0 copy-done
  13.9 0.0 copy-done.1
  13.9 0.3 %near.1 = (f32[64,256]{1,0:T(8,128)S(1)}, f32[64,256]{1,0:T(8,128)S(1)}) custom-call(bf16[40,1792]{1,0:T(8,128)(2,1)S(1)} %get-tuple-element.36.x_ref.arrived_ref, bf16[3584,256]{1,0:T(8,128)(2,1)S(1)} %bitcast.13, bf16[3584,256]{1,0:T(8,128)(2,1)S(1)} %bitcast.15, f32[2,3584]{1,0:T(2,128)S(1)} %get-tuple-element.35._.gate_scale_ref, ...), custom_call_target="tpu_custom_call" | custom-call | tf_op jit(solution)/shard_map/near/pallas_call | solution.py:343
  14.2 0.9 %collective-permute-done.5.swapped_ref = bf16[40,1792]{1,0:T(8,128)(2,1)S(1)} collective-permute-done((bf16[40,1792]{1,0:T(8,128)(2,1)S(1)}, bf16[40,1792]{1,0:T(8,128)(2,1)S(1)}, u32[]{:S(2)}, u32[]{:S(2)}) %collective-permute-start.5) | collective-permute-done | bytes 143392 | tf_op jit(solution)/shard_map/ppermute | solution.py:111
  15.1 0.3 %copy-done.2 = bf16[1,256,3584]{2,1,0:T(8,128)(2,1)S(1)} copy-done((bf16[1,256,3584]{2,1,0:T(8,128)(2,1)S(1)}, bf16[1,256,3584]{2,1,0:T(8,128)(2,1)}, u32[]{:S(2)}) %copy-start.2) | copy-done | bytes 1835032
  15.4 1.0 %hidden.1 = (bf16[32,2048]{1,0:T(8,128)(2,1)S(1)}, bf16[32,1792]{1,0:T(8,128)(2,1)S(1)}, bf16[32,256]{1,0:T(8,128)(2,1)S(1)}, bf16[8,2816]{1,0:T(8,128)(2,1)S(1)}) custom-call(bf16[40,1792]{1,0:T(8,128)(2,1)S(1)} %get-tuple-element.36.x_ref.arrived_ref, bf16[40,1792]{1,0:T(8,128)(2,1)S(1)} %collective-permute-done.5.swapped_ref, ...), custom_call_target="tpu_custom_call" | custom-call | tf_op jit(solution)/shard_map/hidden/pallas_call | solution.py:343
  16.4 0.4 %collective-permute-start.6 = (bf16[32,2048]{1,0:T(8,128)(2,1)S(1)}, bf16[32,2048]{1,0:T(8,128)(2,1)S(1)}, u32[]{:S(2)}, u32[]{:S(2)}) collective-permute-start(bf16[32,2048]{1,0:T(8,128)(2,1)S(1)} %get-tuple-element.42), channel_id=1, source_target_pairs={{0,1},{1,0},{2,3},{3,2},{4,5},{5,4},{6,7},{7,6},{8,9},{9,8},{10,11... | collective-permute-start | bytes 393224 | tf_op jit(solution)/shard_map/ppermute | solution.py:111
  16.8 1.1 %collective-permute-start.7 = (bf16[8,2816]{1,0:T(8,128)(2,1)S(1)}, bf16[8,2816]{1,0:T(8,128)(2,1)S(1)}, u32[]{:S(2)}, u32[]{:S(2)}) collective-permute-start(bf16[8,2816]{1,0:T(8,128)(2,1)S(1)} %get-tuple-element.44), channel_id=1, source_target_pairs={{0,2},{1,3},{2,0},{3,1},{4,6},{5,7},{6,4},{7,5},{8,10},{9,11},{10,... | collective-permute-start | bytes 135176 | tf_op jit(solution)/shard_map/ppermute | solution.py:120
  17.9 0.0 collective-permute-done.6.sent_ref
  18.0 1.9 %collective-permute-start.8 = (bf16[8,1792]{1,0:T(8,128)(2,1)S(1)}, bf16[8,1792]{1,0:T(8,128)(2,1)S(1)}, u32[]{:S(2)}, u32[]{:S(2)}) collective-permute-start(bf16[8,1792]{1,0:T(8,128)(2,1)S(1)} %get-tuple-element.45), channel_id=1, source_target_pairs={{0,12},{1,15},{2,14},{3,13},{4,8},{5,11},{6,10},{7,9},{8,4},{9,7},... | collective-permute-start | bytes 86024 | tf_op jit(solution)/shard_map/ppermute | solution.py:116
  19.8 0.3 %collective-permute-start.9 = (bf16[8,1792]{1,0:T(8,128)(2,1)S(1)}, bf16[8,1792]{1,0:T(8,128)(2,1)S(1)}, u32[]{:S(2)}, u32[]{:S(2)}) collective-permute-start(bf16[8,1792]{1,0:T(8,128)(2,1)S(1)} %get-tuple-element.46), channel_id=1, source_target_pairs={{0,8},{1,11},{2,10},{3,9},{4,12},{5,15},{6,14},{7,13},{8,0},{9,3},... | collective-permute-start | bytes 86024 | tf_op jit(solution)/shard_map/ppermute | solution.py:116
  20.2 2.2 %collective-permute-start.10 = (bf16[8,1792]{1,0:T(8,128)(2,1)S(1)}, bf16[8,1792]{1,0:T(8,128)(2,1)S(1)}, u32[]{:S(2)}, u32[]{:S(2)}) collective-permute-start(bf16[8,1792]{1,0:T(8,128)(2,1)S(1)} %get-tuple-element.47), channel_id=1, source_target_pairs={{0,4},{1,7},{2,6},{3,5},{4,0},{5,3},{6,2},{7,1},{8,12},{9,15},{10,... | collective-permute-start | bytes 86024 | tf_op jit(solution)/shard_map/ppermute | solution.py:116
  22.4 0.0 collective-permute-done.7.crossed_ref
  22.4 0.8 %collective-permute-start.11 = (bf16[32,256]{1,0:T(8,128)(2,1)S(1)}, bf16[32,256]{1,0:T(8,128)(2,1)S(1)}, u32[]{:S(2)}, u32[]{:S(2)}) collective-permute-start(bf16[32,256]{1,0:T(8,128)(2,1)S(1)} %unpack.1.far_ref), channel_id=1, source_target_pairs={{0,1},{1,0},{2,3},{3,2},{4,5},{5,4},{6,7},{7,6},{8,9},{9,8},{10,11... | collective-permute-start | bytes 49160 | tf_op jit(solution)/shard_map/ppermute | solution.py:111
  23.3 0.8 %collective-permute-done.11.other_far_ref = bf16[32,256]{1,0:T(8,128)(2,1)S(1)} collective-permute-done((bf16[32,256]{1,0:T(8,128)(2,1)S(1)}, bf16[32,256]{1,0:T(8,128)(2,1)S(1)}, u32[]{:S(2)}, u32[]{:S(2)}) %collective-permute-start.11) | collective-permute-done | bytes 16416 | tf_op jit(solution)/shard_map/ppermute | solution.py:111
  24.1 1.3 %hessian.1 = (f32[256,1024]{1,0:T(8,128)}, f32[8,128]{1,0:T(8,128)S(1)}) custom-call(bf16[32,128]{1,0:T(8,128)(2,1)S(1)} %get-tuple-element.48.count_ref, bf16[32,256]{1,0:T(8,128)(2,1)S(1)} %get-tuple-element.49.own_ref, bf16[32,2048]{1,0:T(8,128)(2,1)S(1)} %collective-permute-done.6.sent_ref, bf16[32,256]{1,0:T(8,128)(2,1)S(1)} %unpack.1.far_ref, ...), custom_call_target="tpu_custom_call" | custom-call | tf_op jit(solution)/shard_map/hessian/pallas_call | solution.py:343
  25.4 0.0 collective-permute-done.8.three_ref
  25.4 0.0 collective-permute-done.9.two_ref
  25.4 0.0 collective-permute-done.10.one_ref
  25.4 0.4 %collective-permute-start.12 = (bf16[32,896]{1,0:T(8,128)(2,1)S(1)}, bf16[32,896]{1,0:T(8,128)(2,1)S(1)}, u32[]{:S(2)}, u32[]{:S(2)}) collective-permute-start(bf16[32,896]{1,0:T(8,128)(2,1)S(1)} %get-tuple-element.52), channel_id=1, source_target_pairs={{0,1},{1,0},{2,3},{3,2},{4,5},{5,4},{6,7},{7,6},{8,9},{9,8},{10,11... | collective-permute-start | bytes 172040 | tf_op jit(solution)/shard_map/ppermute | solution.py:111
  25.8 0.9 %collective-permute-done.12.far_ref = bf16[32,896]{1,0:T(8,128)(2,1)S(1)} collective-permute-done((bf16[32,896]{1,0:T(8,128)(2,1)S(1)}, bf16[32,896]{1,0:T(8,128)(2,1)S(1)}, u32[]{:S(2)}, u32[]{:S(2)}) %collective-permute-start.12) | collective-permute-done | bytes 57376 | tf_op jit(solution)/shard_map/ppermute | solution.py:111
  26.7 0.9 %combine.1 = bf16[128,896]{1,0:T(8,128)(2,1)} custom-call(f32[32,128]{1,0:T(8,128)S(1)} %get-tuple-element.28.coef_ref, bf16[32,896]{1,0:T(8,128)(2,1)S(1)} %get-tuple-element.51.near_ref, bf16[32,896]{1,0:T(8,128)(2,1)S(1)} %collective-permute-done.12.far_ref), custom_call_target="tpu_custom_call" | custom-call | tf_op jit(solution)/shard_map/combine/pallas_call | solution.py:343
  (8 shorter events, 0.1 us)
Async XLA Ops:
  0.6 0.7 %copy-start.8 = (f32[128,8]{0,1:T(8,128)S(1)}, f32[128,8]{0,1:T(8,128)}, u32[]{:S(2)}) copy-start(f32[128,8]{0,1:T(8,128)} %param.11) | copy-start | bytes 12292
  0.6 0.7 %copy-start.7 = (s32[128,8]{0,1:T(8,128)S(1)}, s32[128,8]{0,1:T(8,128)}, u32[]{:S(2)}) copy-start(s32[128,8]{0,1:T(8,128)} %param.10) | copy-start | bytes 12292
  0.6 1.0 %copy-start.6 = (bf16[128,896]{1,0:T(8,128)(2,1)S(1)}, bf16[128,896]{1,0:T(8,128)(2,1)}, u32[]{:S(2)}) copy-start(bf16[128,896]{1,0:T(8,128)(2,1)} %tokens_ref.1) | copy-start | bytes 688132
  1.6 7.8 %copy-start.3 = (f32[1,28,2]{1,2,0:T(2,128)S(1)}, f32[1,28,2]{1,2,0:T(2,128)}, u32[]{:S(2)}) copy-start(f32[1,28,2]{1,2,0:T(2,128)} %param.13) | copy-start | bytes 676
  1.6 7.8 %copy-start.4 = (f32[1,28,2]{1,2,0:T(2,128)S(1)}, f32[1,28,2]{1,2,0:T(2,128)}, u32[]{:S(2)}) copy-start(f32[1,28,2]{1,2,0:T(2,128)} %param.15) | copy-start | bytes 676
  1.6 7.8 %copy-start.5 = (f32[1,2,28]{2,1,0:T(2,128)S(1)}, f32[1,2,28]{2,1,0:T(2,128)}, u32[]{:S(2)}) copy-start(f32[1,2,28]{2,1,0:T(2,128)} %param.17) | copy-start | bytes 676
  1.6 12.3 %copy-start = (bf16[1,3584,256]{2,1,0:T(8,128)(2,1)S(1)}, bf16[1,3584,256]{2,1,0:T(8,128)(2,1)}, u32[]{:S(2)}) copy-start(bf16[1,3584,256]{2,1,0:T(8,128)(2,1)} %param.12) | copy-start | bytes 5505028
  1.6 12.3 %copy-start.1 = (bf16[1,3584,256]{2,1,0:T(8,128)(2,1)S(1)}, bf16[1,3584,256]{2,1,0:T(8,128)(2,1)}, u32[]{:S(2)}) copy-start(bf16[1,3584,256]{2,1,0:T(8,128)(2,1)} %param.14) | copy-start | bytes 5505028
  1.9 3.1 %collective-permute-start = (bf16[4,8,896]{2,1,0:T(8,128)(2,1)S(1)}, bf16[4,8,896]{2,1,0:T(8,128)(2,1)S(1)}, u32[]{:S(2)}, u32[]{:S(2)}) collective-permute-start(bf16[4,8,896]{2,1,0:T(8,128)(2,1)S(1)} %get-tuple-element.29.own_ref), channel_id=1, source_target_pairs={{0,1},{1,0},{2,3},{3,2},{4,5},{5,4},{6,7},{7,6},{8,9},{9,8},{10,11... | collective-permute-start | bytes 172040 | tf_op jit(solution)/shard_map/ppermute | solution.py:111
  2.4 7.7 %collective-permute-start.1 = (bf16[8,2048]{1,0:T(8,128)(2,1)S(1)}, bf16[8,2048]{1,0:T(8,128)(2,1)S(1)}, u32[]{:S(2)}, u32[]{:S(2)}) collective-permute-start(bf16[8,2048]{1,0:T(8,128)(2,1)S(1)} %get-tuple-element.31), channel_id=1, source_target_pairs={{0,2},{1,3},{2,0},{3,1},{4,6},{5,7},{6,4},{7,5},{8,10},{9,11},{10,... | collective-permute-start | bytes 98312 | tf_op jit(solution)/shard_map/ppermute | solution.py:120
  5.0 5.9 %collective-permute-start.2 = (bf16[8,1920]{1,0:T(8,128)(2,1)S(1)}, bf16[8,1920]{1,0:T(8,128)(2,1)S(1)}, u32[]{:S(2)}, u32[]{:S(2)}) collective-permute-start(bf16[8,1920]{1,0:T(8,128)(2,1)S(1)} %get-tuple-element.32), channel_id=1, source_target_pairs={{0,12},{1,15},{2,14},{3,13},{4,8},{5,11},{6,10},{7,9},{8,4},{9,7},... | collective-permute-start | bytes 92168 | tf_op jit(solution)/shard_map/ppermute | solution.py:116
  8.7 4.9 %collective-permute-start.3 = (bf16[8,1920]{1,0:T(8,128)(2,1)S(1)}, bf16[8,1920]{1,0:T(8,128)(2,1)S(1)}, u32[]{:S(2)}, u32[]{:S(2)}) collective-permute-start(bf16[8,1920]{1,0:T(8,128)(2,1)S(1)} %get-tuple-element.33), channel_id=1, source_target_pairs={{0,8},{1,11},{2,10},{3,9},{4,12},{5,15},{6,14},{7,13},{8,0},{9,3},... | collective-permute-start | bytes 92168 | tf_op jit(solution)/shard_map/ppermute | solution.py:116
  8.7 4.9 %collective-permute-start.4 = (bf16[8,1920]{1,0:T(8,128)(2,1)S(1)}, bf16[8,1920]{1,0:T(8,128)(2,1)S(1)}, u32[]{:S(2)}, u32[]{:S(2)}) collective-permute-start(bf16[8,1920]{1,0:T(8,128)(2,1)S(1)} %get-tuple-element.34), channel_id=1, source_target_pairs={{0,4},{1,7},{2,6},{3,5},{4,0},{5,3},{6,2},{7,1},{8,12},{9,15},{10,... | collective-permute-start | bytes 92168 | tf_op jit(solution)/shard_map/ppermute | solution.py:116
  13.6 1.4 %collective-permute-start.5 = (bf16[40,1792]{1,0:T(8,128)(2,1)S(1)}, bf16[40,1792]{1,0:T(8,128)(2,1)S(1)}, u32[]{:S(2)}, u32[]{:S(2)}) collective-permute-start(bf16[40,1792]{1,0:T(8,128)(2,1)S(1)} %get-tuple-element.36.x_ref.arrived_ref), channel_id=1, source_target_pairs={{0,1},{1,0},{2,3},{3,2},{4,5},{5,4},{6,7},{7,6},{8,9},{9,8},{10,11... | collective-permute-start | bytes 430088 | tf_op jit(solution)/shard_map/ppermute | solution.py:111
  13.9 1.5 %copy-start.2 = (bf16[1,256,3584]{2,1,0:T(8,128)(2,1)S(1)}, bf16[1,256,3584]{2,1,0:T(8,128)(2,1)}, u32[]{:S(2)}) copy-start(bf16[1,256,3584]{2,1,0:T(8,128)(2,1)} %param.16) | copy-start | bytes 5505028
  16.4 1.5 %collective-permute-start.6 = (bf16[32,2048]{1,0:T(8,128)(2,1)S(1)}, bf16[32,2048]{1,0:T(8,128)(2,1)S(1)}, u32[]{:S(2)}, u32[]{:S(2)}) collective-permute-start(bf16[32,2048]{1,0:T(8,128)(2,1)S(1)} %get-tuple-element.42), channel_id=1, source_target_pairs={{0,1},{1,0},{2,3},{3,2},{4,5},{5,4},{6,7},{7,6},{8,9},{9,8},{10,11... | collective-permute-start | bytes 393224 | tf_op jit(solution)/shard_map/ppermute | solution.py:111
  16.8 5.6 %collective-permute-start.7 = (bf16[8,2816]{1,0:T(8,128)(2,1)S(1)}, bf16[8,2816]{1,0:T(8,128)(2,1)S(1)}, u32[]{:S(2)}, u32[]{:S(2)}) collective-permute-start(bf16[8,2816]{1,0:T(8,128)(2,1)S(1)} %get-tuple-element.44), channel_id=1, source_target_pairs={{0,2},{1,3},{2,0},{3,1},{4,6},{5,7},{6,4},{7,5},{8,10},{9,11},{10,... | collective-permute-start | bytes 135176 | tf_op jit(solution)/shard_map/ppermute | solution.py:120
  18.0 7.4 %collective-permute-start.8 = (bf16[8,1792]{1,0:T(8,128)(2,1)S(1)}, bf16[8,1792]{1,0:T(8,128)(2,1)S(1)}, u32[]{:S(2)}, u32[]{:S(2)}) collective-permute-start(bf16[8,1792]{1,0:T(8,128)(2,1)S(1)} %get-tuple-element.45), channel_id=1, source_target_pairs={{0,12},{1,15},{2,14},{3,13},{4,8},{5,11},{6,10},{7,9},{8,4},{9,7},... | collective-permute-start | bytes 86024 | tf_op jit(solution)/shard_map/ppermute | solution.py:116
  19.8 5.6 %collective-permute-start.9 = (bf16[8,1792]{1,0:T(8,128)(2,1)S(1)}, bf16[8,1792]{1,0:T(8,128)(2,1)S(1)}, u32[]{:S(2)}, u32[]{:S(2)}) collective-permute-start(bf16[8,1792]{1,0:T(8,128)(2,1)S(1)} %get-tuple-element.46), channel_id=1, source_target_pairs={{0,8},{1,11},{2,10},{3,9},{4,12},{5,15},{6,14},{7,13},{8,0},{9,3},... | collective-permute-start | bytes 86024 | tf_op jit(solution)/shard_map/ppermute | solution.py:116
  20.2 5.3 %collective-permute-start.10 = (bf16[8,1792]{1,0:T(8,128)(2,1)S(1)}, bf16[8,1792]{1,0:T(8,128)(2,1)S(1)}, u32[]{:S(2)}, u32[]{:S(2)}) collective-permute-start(bf16[8,1792]{1,0:T(8,128)(2,1)S(1)} %get-tuple-element.47), channel_id=1, source_target_pairs={{0,4},{1,7},{2,6},{3,5},{4,0},{5,3},{6,2},{7,1},{8,12},{9,15},{10,... | collective-permute-start | bytes 86024 | tf_op jit(solution)/shard_map/ppermute | solution.py:116
  22.4 1.7 %collective-permute-start.11 = (bf16[32,256]{1,0:T(8,128)(2,1)S(1)}, bf16[32,256]{1,0:T(8,128)(2,1)S(1)}, u32[]{:S(2)}, u32[]{:S(2)}) collective-permute-start(bf16[32,256]{1,0:T(8,128)(2,1)S(1)} %unpack.1.far_ref), channel_id=1, source_target_pairs={{0,1},{1,0},{2,3},{3,2},{4,5},{5,4},{6,7},{7,6},{8,9},{9,8},{10,11... | collective-permute-start | bytes 49160 | tf_op jit(solution)/shard_map/ppermute | solution.py:111
  25.4 1.3 %collective-permute-start.12 = (bf16[32,896]{1,0:T(8,128)(2,1)S(1)}, bf16[32,896]{1,0:T(8,128)(2,1)S(1)}, u32[]{:S(2)}, u32[]{:S(2)}) collective-permute-start(bf16[32,896]{1,0:T(8,128)(2,1)S(1)} %get-tuple-element.52), channel_id=1, source_target_pairs={{0,1},{1,0},{2,3},{3,2},{4,5},{5,4},{6,7},{7,6},{8,9},{9,8},{10,11... | collective-permute-start | bytes 172040 | tf_op jit(solution)/shard_map/ppermute | solution.py:111

commit v5 on v4

--- a/solution.py
+++ b/solution.py
@@ -103,6 +103,7 @@
 BOTH = ("expert", "mp")
 VMEM = pl.BlockSpec(memory_space=pltpu.VMEM)
 SMEM = pl.BlockSpec(memory_space=pltpu.SMEM)
+ANY = pl.BlockSpec(memory_space=pl.ANY)
 F32 = jnp.float32
 BF16 = jnp.bfloat16
 
@@ -172,18 +173,16 @@
     return (lax.axis_index("mp") % 2 == core).astype(F32)
 
 
-def collect_kernel(own_ref, other_ref, count_ref, crossed_ref, three_ref, two_ref, one_ref, _, out_ref, counts_ref):
+def collect_kernel(own_ref, other_ref, count_ref, crossed_ref, swapped_ref, three_ref, two_ref, one_ref, _, out_ref, counts_ref):
     rows, width = crossed_ref.shape[0], out_ref.shape[1] // 2
-    crossed = crossed_ref[:, :width]
     zero = on_core(0)
-    out_ref[:rows, :width] = (own_ref[0].astype(F32) * zero + crossed.astype(F32) * (1.0 - zero)).astype(BF16)
-    out_ref[:rows, width:] = (other_ref[0].astype(F32) * zero).astype(BF16)
+    for ref, far_ref, lanes in ((own_ref, crossed_ref, slice(0, width)), (other_ref, swapped_ref, slice(width, 2 * width))):
+        value = ref[0].astype(F32) * zero + far_ref[:, :width].astype(F32) * (1.0 - zero)
+        out_ref[:rows, lanes] = value.astype(BF16)
     counts_ref[:rows, :] = count_ref[0]
     for k, ref in enumerate((one_ref, two_ref, three_ref), 1):
         out_ref[k * rows : (k + 1) * rows, :] = ref[:, : 2 * width]
         counts_ref[k * rows : (k + 1) * rows, :] = ref[:, 2 * width :]
-    out_ref[4 * rows :, :width] = crossed
-    out_ref[4 * rows :, width:] = jnp.zeros_like(crossed)
 
 
 def shares_in_order():
@@ -199,17 +198,19 @@
     return jnp.dot(scaled, weight_ref[depth, :], preferred_element_type=F32)
 
 
-def near_kernel(x_ref, gate_ref, up_ref, gate_scale_ref, up_scale_ref, gate_out_ref, up_out_ref):
-    share = shares_in_order()[0]
-    slots, width = gate_out_ref.shape[0] // 2, x_ref.shape[1] // 2
-    x = x_ref[:slots, :width].astype(F32)
-    gate_out_ref[...] = project(x, share, gate_ref, gate_scale_ref)
-    up_out_ref[...] = project(x, share, up_ref, up_scale_ref)
+def near_kernel(x_ref, gate_ref, up_ref, gate_scale_ref, up_scale_ref, _, gate_out_ref, up_out_ref):
+    width = x_ref.shape[1] // 2
+    gate, up = 0.0, 0.0
+    for part, share in enumerate(shares_in_order()[:2]):
+        x = x_ref[:, part * width : (part + 1) * width].astype(F32)
+        gate += project(x, share, gate_ref, gate_scale_ref)
+        up += project(x, share, up_ref, up_scale_ref)
+    gate_out_ref[...] = gate
+    up_out_ref[...] = up
 
 
 def hidden_kernel(
-    arrived_ref,
-    swapped_ref,
+    x_ref,
     near_gate_ref,
     near_up_ref,
     gate_ref,
@@ -219,20 +220,14 @@
     up_scale_ref,
     down_scale_ref,
     send_ref,
-    keep_ref,
     hidden_ref,
-    cross_ref,
 ):
     shares = shares_in_order()
     slots, half = near_gate_ref.shape[0] // 2, gate_ref.shape[1] // 2
-    rows, width = slots // 4, arrived_ref.shape[1] // 2
-    zero = on_core(0)
-    filled = []
-    for ref, lacks, missing_ref in ((arrived_ref, 1.0 - zero, swapped_ref), (swapped_ref, zero, arrived_ref)):
-        first = ref[:rows, width:].astype(F32) + missing_ref[slots:, :width].astype(F32) * lacks
-        filled.append(jnp.concatenate([first, ref[rows:slots, width:].astype(F32)], axis=0))
+    width = x_ref.shape[1] // 2
     gate, up = near_gate_ref[...], near_up_ref[...]
-    for x, share in ((filled[0], shares[1]), (swapped_ref[:slots, :width].astype(F32), shares[2]), (filled[1], shares[3])):
+    for part, share in enumerate(shares[2:]):
+        x = x_ref[:, part * width : (part + 1) * width].astype(F32)
         gate += project(x, share, gate_ref, gate_scale_ref)
         up += project(x, share, up_ref, up_scale_ref)
     parts = []
@@ -243,27 +238,34 @@
         lanes = slice(i * half, (i + 1) * half)
         hidden_ref[:, lanes] = parts[i]
         send_ref[:, 2 * width + i * half : 2 * width + (i + 1) * half] = parts[i]
-        for k in range(4):
-            into = 2 * width + 2 * k * half + i * half
-            cross_ref[:, into : into + half] = parts[i][k * rows : (k + 1) * rows]
+    project_down(hidden_ref, shares[2:], down_ref, down_scale_ref, send_ref)
+
+
+def project_down(hidden_ref, shares, down_ref, scale_ref, out_ref):
+    slots, half, width = hidden_ref.shape[0], hidden_ref.shape[1] // 2, down_ref.shape[1] // 4
+    parts = (hidden_ref[:, :half], hidden_ref[:, half:])
     none = jnp.zeros_like(parts[0])
     stacked = jnp.concatenate(
         [jnp.concatenate([parts[0], none], axis=1), jnp.concatenate([none, parts[1]], axis=1)], axis=0
     )
-    for out_ref, part, share in (
-        (send_ref, 0, shares[2]),
-        (send_ref, 1, shares[3]),
-        (keep_ref, 0, shares[0]),
-        (keep_ref, 1, shares[1]),
-    ):
+    for part, share in enumerate(shares):
         lanes = pl.ds(pl.multiple_of(share * width, width), width)
         both = jnp.dot(stacked, down_ref[:, lanes], preferred_element_type=F32)
-        value = both[:slots] * down_scale_ref[:1, lanes] + both[slots:] * down_scale_ref[1:, lanes]
+        value = both[:slots] * scale_ref[:1, lanes] + both[slots:] * scale_ref[1:, lanes]
         out_ref[:, part * width : (part + 1) * width] = value.astype(BF16)
+
+
+def keep_kernel(hidden_ref, send_ref, down_ref, down_scale_ref, keep_ref, cross_ref):
+    project_down(hidden_ref, shares_in_order()[:2], down_ref, down_scale_ref, keep_ref)
+    rows, width = cross_ref.shape[0], down_ref.shape[1] // 4
+    zero = on_core(0)
     for part in range(2):
         lanes, turned = slice(part * width, (part + 1) * width), slice((1 - part) * width, (2 - part) * width)
         value = send_ref[:rows, turned].astype(F32) * zero + keep_ref[:rows, lanes].astype(F32) * (1.0 - zero)
         cross_ref[:, lanes] = value.astype(BF16)
+    for k in range(4):
+        into = 2 * width + k * hidden_ref.shape[1]
+        cross_ref[:, into : into + hidden_ref.shape[1]] = hidden_ref[k * rows : (k + 1) * rows, :]
 
 
 def chip_sum_kernel(keep_ref, sent_ref, *out_refs):
@@ -273,40 +275,44 @@
         out_ref[...] = (keep_ref[at, :].astype(F32) + sent_ref[at, :width].astype(F32)).astype(BF16)
 
 
-def unpack_kernel(crossed_ref, out_ref):
-    width = out_ref.shape[1]
-    rows = out_ref.shape[0] // 4
+def hessian_factor(count_ref):
+    rows = count_ref.shape[0] // 4
+    counts = [count_ref[k * rows : k * rows + 1, :].astype(F32)[:, :1] for k in range(4)]
+    return 2.0 / (counts[0] + counts[1] + counts[2] + counts[3])
+
+
+def hessian_block(own_ref, other, factor):
+    return lax.dot_general(own_ref[...], other, (((0,), (0,)), ((), ())), preferred_element_type=F32) * factor
+
+
+def hessian_kernel(count_ref, own_ref, sent_ref, crossed_ref, out_ref, far_ref):
+    m = lax.axis_index("mp")
+    width = out_ref.shape[0]
+    rows = far_ref.shape[0] // 4
     start = crossed_ref.shape[1] - 4 * width
     for k in range(4):
-        out_ref[k * rows : (k + 1) * rows, :] = crossed_ref[:, start + k * width : start + (k + 1) * width]
-
-
-def hessian_kernel(count_ref, own_ref, sent_ref, far_ref, other_far_ref, out_ref, done_ref):
-    m = lax.axis_index("mp")
-    width = out_ref.shape[0]
-    rows = count_ref.shape[0] // 4
-    counts = [count_ref[k * rows : k * rows + 1, :].astype(F32)[:, :1] for k in range(4)]
-    factor = 2.0 / (counts[0] + counts[1] + counts[2] + counts[3])
-    own = own_ref[...]
-    others = ((m, own), (m ^ 1, sent_ref[:, sent_ref.shape[1] - width :]), (m ^ 2, far_ref[...]), (m ^ 3, other_far_ref[...]))
+        far_ref[k * rows : (k + 1) * rows, :] = crossed_ref[:, start + k * width : start + (k + 1) * width]
+    factor = hessian_factor(count_ref)
+    others = ((m, own_ref[...]), (m ^ 1, sent_ref[:, sent_ref.shape[1] - width :]), (m ^ 2, far_ref[...]))
     for share, other in others:
-        block = lax.dot_general(own, other, (((0,), (0,)), ((), ())), preferred_element_type=F32)
-        out_ref[:, pl.ds(pl.multiple_of(share * width, width), width)] = block * factor
-    done_ref[...] = jnp.zeros_like(done_ref)
-
-
-def collect_back_kernel(summed_ref, crossed_ref, three_ref, two_ref, one_ref, _, mine_ref, other_ref):
+        out_ref[:, pl.ds(pl.multiple_of(share * width, width), width)] = hessian_block(own_ref, other, factor)
+
+
+def collect_back_kernel(summed_ref, crossed_ref, three_ref, two_ref, one_ref, far_ref, mine_ref, other_ref):
     rows, width = one_ref.shape[0], mine_ref.shape[1]
     crossed = crossed_ref[:, : 2 * width].astype(F32)
     value = (crossed + summed_ref[...].astype(F32) * on_core(0)).astype(BF16)
     for k, rows_in in enumerate((value, one_ref[...], two_ref[...], three_ref[...])):
         mine_ref[k * rows : (k + 1) * rows, :] = rows_in[:, :width]
-        other_ref[k * rows : (k + 1) * rows, :] = rows_in[:, width:]
-
-
-def combine_kernel(coef_ref, near_ref, far_ref, out_ref):
-    slots, width = coef_ref.shape[0], out_ref.shape[1]
-    result = (near_ref[...].astype(F32) + far_ref[...].astype(F32)).astype(BF16)
+        other_ref[k * rows : (k + 1) * rows, :width] = rows_in[:, width:]
+    other_ref[:, width:] = far_ref[...]
+
+
+def combine_kernel(
+    coef_ref, near_ref, far_ref, count_ref, own_ref, _, mixed_hbm, hessian_hbm, mixed_ref, block_ref, sems
+):
+    width, hidden_width = near_ref.shape[1], block_ref.shape[0]
+    result = (near_ref[...].astype(F32) + far_ref[:, :width].astype(F32)).astype(BF16)
     coef = coef_ref[...]
     terms = []
     for _ in range(3):
@@ -318,7 +324,16 @@
         (((0,), (0,)), ((), ())),
         preferred_element_type=F32,
     )
-    out_ref[...] = out.astype(BF16)
+    mixed_ref[...] = out.astype(BF16)
+    mixed_copy = pltpu.make_async_copy(mixed_ref, mixed_hbm, sems.at[0])
+    mixed_copy.start()
+    block_ref[...] = hessian_block(own_ref, far_ref[:, width:], hessian_factor(count_ref))
+    share = lax.axis_index("mp") ^ 3
+    lanes = pl.ds(pl.multiple_of(share * hidden_width, hidden_width), hidden_width)
+    block_copy = pltpu.make_async_copy(block_ref, hessian_hbm.at[:, lanes], sems.at[1])
+    block_copy.start()
+    mixed_copy.wait()
+    block_copy.wait()
 
 
 def on_device(
@@ -380,47 +395,61 @@
     arrived, arrived_counts = call(
         collect_kernel,
         "collect",
-        (shape((slots + capacity, 2 * width), BF16), shape((slots, QBLK), BF16)),
-        (picked, other, counts, crossed, *[to_chips(messages[k - 1], k) for k in (3, 2, 1)], scales[0]),
+        (shape((slots, 2 * width), BF16), shape((slots, QBLK), BF16)),
+        (picked, other, counts, crossed, swap_cores(crossed[:, :width]), *[to_chips(messages[k - 1], k) for k in (3, 2, 1)], scales[0]),
     )
     swapped = swap_cores(arrived)
     near = call(
         near_kernel,
         "near",
         (shape((2 * slots, hidden_width), F32),) * 2,
-        (arrived, gate, up, *scales[:2]),
-    )
-    send, keep, hidden, cross = call(
+        (arrived, gate, up, *scales[:2], down),
+    )
+    send, hidden = call(
         hidden_kernel,
         "hidden",
         (
             shape((slots, 2 * width + hidden_width), BF16),
-            shape((slots, 2 * width), BF16),
             shape((slots, hidden_width), BF16),
-            shape((capacity, 2 * width + 4 * hidden_width), BF16),
         ),
-        (arrived, swapped, *near, gate, up, down, *scales),
+        (swapped, *near, gate, up, down, *scales),
     )
     sent = swap_cores(send)
+    keep, cross = call(
+        keep_kernel,
+        "keep",
+        (shape((slots, 2 * width), BF16), shape((capacity, 2 * width + 4 * hidden_width), BF16)),
+        (hidden, send, down, scales[2]),
+    )
     crossed = across(cross)
     summed = call(chip_sum_kernel, "chip_sum", (shape((capacity, 2 * width), BF16),) * 4, (keep, sent))
     back = {k: to_chips(summed[k], k) for k in range(1, 4)}
-    far = call(unpack_kernel, "unpack", shape((slots, hidden_width), BF16), (crossed,))
-    hessian, done = call(
+    hessian, far = call(
         hessian_kernel,
         "hessian",
-        (shape((hidden_width, 4 * hidden_width), F32), shape((8, QBLK), F32)),
-        (arrived_counts, hidden, sent, far, swap_cores(far)),
+        (shape((hidden_width, 4 * hidden_width), F32), shape((slots, hidden_width), BF16)),
+        (arrived_counts, hidden, sent, crossed),
     )
     mine, other = call(
         collect_back_kernel,
         "collect_back",
-        (shape((slots, width), BF16),) * 2,
-        (summed[0], crossed, *[back[k] for k in (3, 2, 1)], done),
-    )
-    mixed = call(
-        combine_kernel, "combine", shape((rows, width), BF16), (coef, mine, swap_cores(other))
-    )
+        (shape((slots, width), BF16), shape((slots, width + hidden_width), BF16)),
+        (summed[0], crossed, *[back[k] for k in (3, 2, 1)], far),
+    )
+    mixed, hessian = pl.pallas_call(
+        combine_kernel,
+        out_shape=(shape((rows, width), BF16), shape((hidden_width, 4 * hidden_width), F32)),
+        in_specs=[VMEM] * 5 + [ANY],
+        out_specs=(ANY, ANY),
+        scratch_shapes=[
+            pltpu.VMEM((rows, width), BF16),
+            pltpu.VMEM((hidden_width, hidden_width), F32),
+            pltpu.SemaphoreType.DMA((2,)),
+        ],
+        input_output_aliases={5: 1},
+        compiler_params=pltpu.CompilerParams(vmem_limit_bytes=8 * 1024 * 1024),
+        name="combine",
+    )(coef, mine, swap_cores(other), arrived_counts, hidden, hessian)
     return mixed, hessian[None]
 
 

time: 27.9 us -> 27.4 us (0.982)
  starting transfers between devices: 15 us -> 14.6 us
  local copies, waits for them, and re-layouts: 1.29 us -> 0.96 us
    pallas_call x0 -> x1, Pallas kernels: none -> 1.05 us  [on_device(): pl.pallas_call(combine_kernel, out_shape=(shape((rows, width), BF16), sha...]
    pallas_call x12 -> x11, Pallas kernels: 4.5 us -> 3.67 us  [call(): pl.pallas_call(kernel, out_shape=outs, in_specs=[SMEM] * scalars + [VMEM]...]
    ppermute x6, waiting for transfers between devices: 3.51 us -> 4.05 us  [to_chips(): return lax.ppermute(value, BOTH, pairs)]
    ppermute x5, waiting for transfers between devices: 2.61 us -> 2.11 us  [swap_cores(): return lax.ppermute(value, 'mp', [(m, m ^ 1) for m in range(4)])]
    ppermute x5, starting transfers between devices: 2.41 us -> 1.92 us  [swap_cores(): return lax.ppermute(value, 'mp', [(m, m ^ 1) for m in range(4)])]
    unnamed x18, local copies, waits for them, and re-layouts: 1.29 us -> 0.96 us
  transfers between devices with their start and end apart: 13 -> 13, of which waited for: 5 -> 5; matrix products, arithmetic and copies ran while one was open for 0% -> 0% of each run, Pallas kernels for 8% -> 10%
where the time goes in v5:
time: 27.4 us; the launch traced here: 27.2 us
  starting transfers between devices  14.6 us (53%)
  waiting for transfers between devices  6.17 us (23%)
  Pallas kernels  4.72 us (17%)
  local copies, waits for them, and re-layouts  0.96 us (4%)
  between operations  0.76 us (3%)
    ppermute x6, starting transfers between devices, to_chips(): return lax.ppermute(value, BOTH, pairs)  8.9 us
    ppermute x6, waiting for transfers between devices, to_chips(): return lax.ppermute(value, BOTH, pairs)  4.05 us
    ppermute x2, starting transfers between devices, across(): lax.ppermute(value, BOTH, [(4 * z + m, 4 * z + (m ^ 2)) for z in range(4)...  3.73 us
    pallas_call x11, Pallas kernels, call(): pl.pallas_call(kernel, out_shape=outs, in_specs=[SMEM] * scalars + [VMEM]...  3.67 us
    ppermute x5, waiting for transfers between devices, swap_cores(): return lax.ppermute(value, 'mp', [(m, m ^ 1) for m in range(4)])  2.11 us
    ppermute x5, starting transfers between devices, swap_cores(): return lax.ppermute(value, 'mp', [(m, m ^ 1) for m in range(4)])  1.92 us
    pallas_call x1, Pallas kernels, on_device(): pl.pallas_call(combine_kernel, out_shape=(shape((rows, width), BF16), sha...  1.05 us
    unnamed x18, local copies, waits for them, and re-layouts  0.96 us
  transfers between devices with their start and end apart: 13, of which 5 were waited for; matrix products, arithmetic and copies ran while one was open for 0% of the time, Pallas kernels for 10%

profile of v5, /device:TPU:0, one launch (start us, length us, event | category | flops | bytes accessed | tf_op | source)
XLA Modules:
  0.0 27.2 jit_solution(3425394879622166127)
XLA Ops:
  0.6 0.0 copy-start.8
  0.6 0.0 copy-start.7
  0.6 0.0 copy-start.6
  0.7 0.6 %copy-done.8 = f32[128,8]{0,1:T(8,128)S(1)} copy-done((f32[128,8]{0,1:T(8,128)S(1)}, f32[128,8]{0,1:T(8,128)}, u32[]{:S(2)}) %copy-start.8) | copy-done | bytes 4120
  1.3 0.0 copy-done.7
  1.3 0.3 copy-done.6
  1.6 0.0 copy-start.3
  1.6 0.0 copy-start.1
  1.6 0.0 copy-start.2
  1.6 0.3 route.1
  1.9 0.5 %collective-permute-start = (bf16[4,8,896]{2,1,0:T(8,128)(2,1)S(1)}, bf16[4,8,896]{2,1,0:T(8,128)(2,1)S(1)}, u32[]{:S(2)}, u32[]{:S(2)}) collective-permute-start(bf16[4,8,896]{2,1,0:T(8,128)(2,1)S(1)} %get-tuple-element.31.own_ref), channel_id=1, source_target_pairs={{0,1},{1,0},{2,3},{3,2},{4,5},{5,4},{6,7},{7,6},{8,9},{9,8},{10,11... | collective-permute-start | bytes 172040 | tf_op jit(solution)/shard_map/ppermute | solution.py:112
  2.4 2.6 %collective-permute-start.1 = (bf16[8,2048]{1,0:T(8,128)(2,1)S(1)}, bf16[8,2048]{1,0:T(8,128)(2,1)S(1)}, u32[]{:S(2)}, u32[]{:S(2)}) collective-permute-start(bf16[8,2048]{1,0:T(8,128)(2,1)S(1)} %get-tuple-element.33), channel_id=1, source_target_pairs={{0,2},{1,3},{2,0},{3,1},{4,6},{5,7},{6,4},{7,5},{8,10},{9,11},{10,... | collective-permute-start | bytes 98312 | tf_op jit(solution)/shard_map/ppermute | solution.py:121
  5.0 0.0 collective-permute-done.other_ref
  5.0 3.7 %collective-permute-start.3 = (bf16[8,1920]{1,0:T(8,128)(2,1)S(1)}, bf16[8,1920]{1,0:T(8,128)(2,1)S(1)}, u32[]{:S(2)}, u32[]{:S(2)}) collective-permute-start(bf16[8,1920]{1,0:T(8,128)(2,1)S(1)} %get-tuple-element.34), channel_id=1, source_target_pairs={{0,12},{1,15},{2,14},{3,13},{4,8},{5,11},{6,10},{7,9},{8,4},{9,7},... | collective-permute-start | bytes 92168 | tf_op jit(solution)/shard_map/ppermute | solution.py:117
  8.7 0.0 collective-permute-start.4
  8.7 0.8 %collective-permute-start.5 = (bf16[8,1920]{1,0:T(8,128)(2,1)S(1)}, bf16[8,1920]{1,0:T(8,128)(2,1)S(1)}, u32[]{:S(2)}, u32[]{:S(2)}) collective-permute-start(bf16[8,1920]{1,0:T(8,128)(2,1)S(1)} %get-tuple-element.36), channel_id=1, source_target_pairs={{0,4},{1,7},{2,6},{3,5},{4,0},{5,3},{6,2},{7,1},{8,12},{9,15},{10,... | collective-permute-start | bytes 92168 | tf_op jit(solution)/shard_map/ppermute | solution.py:117
  9.5 0.0 collective-permute-done.1.crossed_ref
  9.5 0.8 %collective-permute-start.2 = (bf16[8,896]{1,0:T(8,128)(2,1)S(1)}, bf16[8,896]{1,0:T(8,128)(2,1)S(1)}, u32[]{:S(2)}, u32[]{:S(2)}) collective-permute-start(bf16[8,896]{1,0:T(8,128)(2,1)S(1)} %slice.4), channel_id=1, source_target_pairs={{0,1},{1,0},{2,3},{3,2},{4,5},{5,4},{6,7},{7,6},{8,9},{9,8},{10,11... | collective-permute-start | bytes 43016 | tf_op jit(solution)/shard_map/ppermute | solution.py:112
  10.3 0.0 copy-done.3
  10.3 0.0 copy-done.4
  10.3 0.0 copy-done.5
  10.3 0.6 %spread.1 = (f32[2,3584]{1,0:T(2,128)S(1)}, f32[2,3584]{1,0:T(2,128)S(1)}, f32[2,3584]{1,0:T(2,128)S(1)}) custom-call(f32[2,28]{1,0:T(2,128)S(1)} %bitcast.20, f32[2,28]{1,0:T(2,128)S(1)} %bitcast.21, f32[2,28]{1,0:T(2,128)S(1)} %bitcast.22), custom_call_target="tpu_custom_call" | custom-call | tf_op jit(solution)/shard_map/spread/pallas_call | solution.py:358
  10.9 0.2 collective-permute-done.2.swapped_ref
  11.1 0.0 collective-permute-done.3.three_ref
  11.1 2.5 %collective-permute-done.4.two_ref = bf16[8,1920]{1,0:T(8,128)(2,1)S(1)} collective-permute-done((bf16[8,1920]{1,0:T(8,128)(2,1)S(1)}, bf16[8,1920]{1,0:T(8,128)(2,1)S(1)}, u32[]{:S(2)}, u32[]{:S(2)}) %collective-permute-start.4) | collective-permute-done | bytes 30752 | tf_op jit(solution)/shard_map/ppermute | solution.py:117
  13.6 0.0 collective-permute-done.5.one_ref
  13.6 0.3 collective-permute-start.6
  13.9 0.0 copy-done
  13.9 0.0 copy-done.1
  13.9 0.0 copy-done.2
  13.9 0.5 %near.1 = (f32[64,256]{1,0:T(8,128)S(1)}, f32[64,256]{1,0:T(8,128)S(1)}) custom-call(bf16[32,1792]{1,0:T(8,128)(2,1)S(1)} %get-tuple-element.38.x_ref, bf16[3584,256]{1,0:T(8,128)(2,1)S(1)} %bitcast.16, bf16[3584,256]{1,0:T(8,128)(2,1)S(1)} %bitcast.18, f32[2,3584]{1,0:T(2,128)S(1)} %get-tuple-element.37._.gate_scale_ref, ...), custom_call_target="tpu_custom_call" | custom-call | tf_op jit(solution)/shard_map/near/pallas_call | solution.py:358
  14.4 0.7 %collective-permute-done.6.x_ref = bf16[32,1792]{1,0:T(8,128)(2,1)S(1)} collective-permute-done((bf16[32,1792]{1,0:T(8,128)(2,1)S(1)}, bf16[32,1792]{1,0:T(8,128)(2,1)S(1)}, u32[]{:S(2)}, u32[]{:S(2)}) %collective-permute-start.6) | collective-permute-done | bytes 114720 | tf_op jit(solution)/shard_map/ppermute | solution.py:112
  15.0 0.7 %hidden.1 = (bf16[32,2048]{1,0:T(8,128)(2,1)S(1)}, bf16[32,256]{1,0:T(8,128)(2,1)S(1)}) custom-call(bf16[32,1792]{1,0:T(8,128)(2,1)S(1)} %collective-permute-done.6.x_ref, f32[64,256]{1,0:T(8,128)S(1)} %get-tuple-element.40.near_gate_ref, f32[64,256]{1,0:T(8,128)S(1)} %get-tuple-element.41.near_up_ref, bf16[3584,256]{1,0:T(8,128)(2,1)S(1)} %bitcast.17, ...), custom_call_target="tpu_custom_call" | custom-call | tf_op jit(solution)/shard_map/hidden/pallas_call | solution.py:358
  15.7 0.3 collective-permute-start.7
  16.0 0.3 keep.1
  16.3 1.2 %collective-permute-start.8 = (bf16[8,2816]{1,0:T(8,128)(2,1)S(1)}, bf16[8,2816]{1,0:T(8,128)(2,1)S(1)}, u32[]{:S(2)}, u32[]{:S(2)}) collective-permute-start(bf16[8,2816]{1,0:T(8,128)(2,1)S(1)} %get-tuple-element.47), channel_id=1, source_target_pairs={{0,2},{1,3},{2,0},{3,1},{4,6},{5,7},{6,4},{7,5},{8,10},{9,11},{10,... | collective-permute-start | bytes 135176 | tf_op jit(solution)/shard_map/ppermute | solution.py:121
  17.4 0.0 collective-permute-done.7.sent_ref
  17.5 1.9 %collective-permute-start.9 = (bf16[8,1792]{1,0:T(8,128)(2,1)S(1)}, bf16[8,1792]{1,0:T(8,128)(2,1)S(1)}, u32[]{:S(2)}, u32[]{:S(2)}) collective-permute-start(bf16[8,1792]{1,0:T(8,128)(2,1)S(1)} %get-tuple-element.48), channel_id=1, source_target_pairs={{0,12},{1,15},{2,14},{3,13},{4,8},{5,11},{6,10},{7,9},{8,4},{9,7},... | collective-permute-start | bytes 86024 | tf_op jit(solution)/shard_map/ppermute | solution.py:117
  19.3 0.5 %collective-permute-start.10 = (bf16[8,1792]{1,0:T(8,128)(2,1)S(1)}, bf16[8,1792]{1,0:T(8,128)(2,1)S(1)}, u32[]{:S(2)}, u32[]{:S(2)}) collective-permute-start(bf16[8,1792]{1,0:T(8,128)(2,1)S(1)} %get-tuple-element.49), channel_id=1, source_target_pairs={{0,8},{1,11},{2,10},{3,9},{4,12},{5,15},{6,14},{7,13},{8,0},{9,3},... | collective-permute-start | bytes 86024 | tf_op jit(solution)/shard_map/ppermute | solution.py:117
  19.8 2.1 %collective-permute-start.11 = (bf16[8,1792]{1,0:T(8,128)(2,1)S(1)}, bf16[8,1792]{1,0:T(8,128)(2,1)S(1)}, u32[]{:S(2)}, u32[]{:S(2)}) collective-permute-start(bf16[8,1792]{1,0:T(8,128)(2,1)S(1)} %get-tuple-element.50), channel_id=1, source_target_pairs={{0,4},{1,7},{2,6},{3,5},{4,0},{5,3},{6,2},{7,1},{8,12},{9,15},{10,... | collective-permute-start | bytes 86024 | tf_op jit(solution)/shard_map/ppermute | solution.py:117
  21.9 0.0 collective-permute-done.8.crossed_ref
  21.9 1.3 %hessian.1 = (f32[256,1024]{1,0:T(8,128)}, bf16[32,256]{1,0:T(8,128)(2,1)S(1)}) custom-call(bf16[32,128]{1,0:T(8,128)(2,1)S(1)} %get-tuple-element.51.count_ref, bf16[32,256]{1,0:T(8,128)(2,1)S(1)} %get-tuple-element.43.hidden_ref.own_ref, bf16[32,2048]{1,0:T(8,128)(2,1)S(1)} %collective-permute-done.7.sent_ref, ...), custom_call_target="tpu_custom_call" | custom-call | tf_op jit(solution)/shard_map/hessian/pallas_call | solution.py:358
  23.2 0.0 collective-permute-done.9.three_ref
  23.2 1.5 %collective-permute-done.10.two_ref = bf16[8,1792]{1,0:T(8,128)(2,1)S(1)} collective-permute-done((bf16[8,1792]{1,0:T(8,128)(2,1)S(1)}, bf16[8,1792]{1,0:T(8,128)(2,1)S(1)}, u32[]{:S(2)}, u32[]{:S(2)}) %collective-permute-start.10) | collective-permute-done | bytes 28704 | tf_op jit(solution)/shard_map/ppermute | solution.py:117
  24.8 0.0 collective-permute-done.11.one_ref
  24.8 0.1 collective-permute-start.12
  24.9 1.3 %collective-permute-done.12.far_ref = bf16[32,1152]{1,0:T(8,128)(2,1)S(1)} collective-permute-done((bf16[32,1152]{1,0:T(8,128)(2,1)S(1)}, bf16[32,1152]{1,0:T(8,128)(2,1)S(1)}, u32[]{:S(2)}, u32[]{:S(2)}) %collective-permute-start.12) | collective-permute-done | bytes 73760 | tf_op jit(solution)/shard_map/ppermute | solution.py:112
  26.1 1.1 %combine.1 = (bf16[128,896]{1,0:T(8,128)(2,1)}, f32[256,1024]{1,0:T(8,128)}) custom-call(f32[32,128]{1,0:T(8,128)S(1)} %get-tuple-element.30.coef_ref, bf16[32,896]{1,0:T(8,128)(2,1)S(1)} %get-tuple-element.53.near_ref, bf16[32,1152]{1,0:T(8,128)(2,1)S(1)} %collective-permute-done.12.far_ref, ...), custom_call_target="tpu_custom_call", output_to_operand_aliasing={{1}: (5, {})} | custom-call | tf_op jit(solution)/shard_map/combine/pallas_call | solution.py:439
  (9 shorter events, 0.1 us)
Async XLA Ops:
  0.6 0.7 %copy-start.8 = (f32[128,8]{0,1:T(8,128)S(1)}, f32[128,8]{0,1:T(8,128)}, u32[]{:S(2)}) copy-start(f32[128,8]{0,1:T(8,128)} %param.11) | copy-start | bytes 12292
  0.6 0.7 %copy-start.7 = (s32[128,8]{0,1:T(8,128)S(1)}, s32[128,8]{0,1:T(8,128)}, u32[]{:S(2)}) copy-start(s32[128,8]{0,1:T(8,128)} %param.10) | copy-start | bytes 12292
  0.6 1.0 %copy-start.6 = (bf16[128,896]{1,0:T(8,128)(2,1)S(1)}, bf16[128,896]{1,0:T(8,128)(2,1)}, u32[]{:S(2)}) copy-start(bf16[128,896]{1,0:T(8,128)(2,1)} %tokens_ref.1) | copy-start | bytes 688132
  1.6 8.7 %copy-start.3 = (f32[1,28,2]{1,2,0:T(2,128)S(1)}, f32[1,28,2]{1,2,0:T(2,128)}, u32[]{:S(2)}) copy-start(f32[1,28,2]{1,2,0:T(2,128)} %param.13) | copy-start | bytes 676
  1.6 8.7 %copy-start.4 = (f32[1,28,2]{1,2,0:T(2,128)S(1)}, f32[1,28,2]{1,2,0:T(2,128)}, u32[]{:S(2)}) copy-start(f32[1,28,2]{1,2,0:T(2,128)} %param.15) | copy-start | bytes 676
  1.6 8.7 %copy-start.5 = (f32[1,2,28]{2,1,0:T(2,128)S(1)}, f32[1,2,28]{2,1,0:T(2,128)}, u32[]{:S(2)}) copy-start(f32[1,2,28]{2,1,0:T(2,128)} %param.17) | copy-start | bytes 676
  1.6 12.3 %copy-start = (bf16[1,256,3584]{2,1,0:T(8,128)(2,1)S(1)}, bf16[1,256,3584]{2,1,0:T(8,128)(2,1)}, u32[]{:S(2)}) copy-start(bf16[1,256,3584]{2,1,0:T(8,128)(2,1)} %param.16) | copy-start | bytes 5505028
  1.6 12.3 %copy-start.1 = (bf16[1,3584,256]{2,1,0:T(8,128)(2,1)S(1)}, bf16[1,3584,256]{2,1,0:T(8,128)(2,1)}, u32[]{:S(2)}) copy-start(bf16[1,3584,256]{2,1,0:T(8,128)(2,1)} %param.12) | copy-start | bytes 5505028
  1.6 12.3 %copy-start.2 = (bf16[1,3584,256]{2,1,0:T(8,128)(2,1)S(1)}, bf16[1,3584,256]{2,1,0:T(8,128)(2,1)}, u32[]{:S(2)}) copy-start(bf16[1,3584,256]{2,1,0:T(8,128)(2,1)} %param.14) | copy-start | bytes 5505028
  1.9 3.1 %collective-permute-start = (bf16[4,8,896]{2,1,0:T(8,128)(2,1)S(1)}, bf16[4,8,896]{2,1,0:T(8,128)(2,1)S(1)}, u32[]{:S(2)}, u32[]{:S(2)}) collective-permute-start(bf16[4,8,896]{2,1,0:T(8,128)(2,1)S(1)} %get-tuple-element.31.own_ref), channel_id=1, source_target_pairs={{0,1},{1,0},{2,3},{3,2},{4,5},{5,4},{6,7},{7,6},{8,9},{9,8},{10,11... | collective-permute-start | bytes 172040 | tf_op jit(solution)/shard_map/ppermute | solution.py:112
  2.4 7.0 %collective-permute-start.1 = (bf16[8,2048]{1,0:T(8,128)(2,1)S(1)}, bf16[8,2048]{1,0:T(8,128)(2,1)S(1)}, u32[]{:S(2)}, u32[]{:S(2)}) collective-permute-start(bf16[8,2048]{1,0:T(8,128)(2,1)S(1)} %get-tuple-element.33), channel_id=1, source_target_pairs={{0,2},{1,3},{2,0},{3,1},{4,6},{5,7},{6,4},{7,5},{8,10},{9,11},{10,... | collective-permute-start | bytes 98312 | tf_op jit(solution)/shard_map/ppermute | solution.py:121
  5.0 6.1 %collective-permute-start.3 = (bf16[8,1920]{1,0:T(8,128)(2,1)S(1)}, bf16[8,1920]{1,0:T(8,128)(2,1)S(1)}, u32[]{:S(2)}, u32[]{:S(2)}) collective-permute-start(bf16[8,1920]{1,0:T(8,128)(2,1)S(1)} %get-tuple-element.34), channel_id=1, source_target_pairs={{0,12},{1,15},{2,14},{3,13},{4,8},{5,11},{6,10},{7,9},{8,4},{9,7},... | collective-permute-start | bytes 92168 | tf_op jit(solution)/shard_map/ppermute | solution.py:117
  8.7 4.9 %collective-permute-start.4 = (bf16[8,1920]{1,0:T(8,128)(2,1)S(1)}, bf16[8,1920]{1,0:T(8,128)(2,1)S(1)}, u32[]{:S(2)}, u32[]{:S(2)}) collective-permute-start(bf16[8,1920]{1,0:T(8,128)(2,1)S(1)} %get-tuple-element.35), channel_id=1, source_target_pairs={{0,8},{1,11},{2,10},{3,9},{4,12},{5,15},{6,14},{7,13},{8,0},{9,3},... | collective-permute-start | bytes 92168 | tf_op jit(solution)/shard_map/ppermute | solution.py:117
  8.7 4.9 %collective-permute-start.5 = (bf16[8,1920]{1,0:T(8,128)(2,1)S(1)}, bf16[8,1920]{1,0:T(8,128)(2,1)S(1)}, u32[]{:S(2)}, u32[]{:S(2)}) collective-permute-start(bf16[8,1920]{1,0:T(8,128)(2,1)S(1)} %get-tuple-element.36), channel_id=1, source_target_pairs={{0,4},{1,7},{2,6},{3,5},{4,0},{5,3},{6,2},{7,1},{8,12},{9,15},{10,... | collective-permute-start | bytes 92168 | tf_op jit(solution)/shard_map/ppermute | solution.py:117
  9.5 1.6 %collective-permute-start.2 = (bf16[8,896]{1,0:T(8,128)(2,1)S(1)}, bf16[8,896]{1,0:T(8,128)(2,1)S(1)}, u32[]{:S(2)}, u32[]{:S(2)}) collective-permute-start(bf16[8,896]{1,0:T(8,128)(2,1)S(1)} %slice.4), channel_id=1, source_target_pairs={{0,1},{1,0},{2,3},{3,2},{4,5},{5,4},{6,7},{7,6},{8,9},{9,8},{10,11... | collective-permute-start | bytes 43016 | tf_op jit(solution)/shard_map/ppermute | solution.py:112
  13.6 1.4 %collective-permute-start.6 = (bf16[32,1792]{1,0:T(8,128)(2,1)S(1)}, bf16[32,1792]{1,0:T(8,128)(2,1)S(1)}, u32[]{:S(2)}, u32[]{:S(2)}) collective-permute-start(bf16[32,1792]{1,0:T(8,128)(2,1)S(1)} %get-tuple-element.38.x_ref), channel_id=1, source_target_pairs={{0,1},{1,0},{2,3},{3,2},{4,5},{5,4},{6,7},{7,6},{8,9},{9,8},{10,11... | collective-permute-start | bytes 344072 | tf_op jit(solution)/shard_map/ppermute | solution.py:112
  15.7 1.7 %collective-permute-start.7 = (bf16[32,2048]{1,0:T(8,128)(2,1)S(1)}, bf16[32,2048]{1,0:T(8,128)(2,1)S(1)}, u32[]{:S(2)}, u32[]{:S(2)}) collective-permute-start(bf16[32,2048]{1,0:T(8,128)(2,1)S(1)} %get-tuple-element.44.send_ref), channel_id=1, source_target_pairs={{0,1},{1,0},{2,3},{3,2},{4,5},{5,4},{6,7},{7,6},{8,9},{9,8},{10,11... | collective-permute-start | bytes 393224 | tf_op jit(solution)/shard_map/ppermute | solution.py:112
  16.3 5.7 %collective-permute-start.8 = (bf16[8,2816]{1,0:T(8,128)(2,1)S(1)}, bf16[8,2816]{1,0:T(8,128)(2,1)S(1)}, u32[]{:S(2)}, u32[]{:S(2)}) collective-permute-start(bf16[8,2816]{1,0:T(8,128)(2,1)S(1)} %get-tuple-element.47), channel_id=1, source_target_pairs={{0,2},{1,3},{2,0},{3,1},{4,6},{5,7},{6,4},{7,5},{8,10},{9,11},{10,... | collective-permute-start | bytes 135176 | tf_op jit(solution)/shard_map/ppermute | solution.py:121
  17.5 5.7 %collective-permute-start.9 = (bf16[8,1792]{1,0:T(8,128)(2,1)S(1)}, bf16[8,1792]{1,0:T(8,128)(2,1)S(1)}, u32[]{:S(2)}, u32[]{:S(2)}) collective-permute-start(bf16[8,1792]{1,0:T(8,128)(2,1)S(1)} %get-tuple-element.48), channel_id=1, source_target_pairs={{0,12},{1,15},{2,14},{3,13},{4,8},{5,11},{6,10},{7,9},{8,4},{9,7},... | collective-permute-start | bytes 86024 | tf_op jit(solution)/shard_map/ppermute | solution.py:117
  19.3 5.4 %collective-permute-start.10 = (bf16[8,1792]{1,0:T(8,128)(2,1)S(1)}, bf16[8,1792]{1,0:T(8,128)(2,1)S(1)}, u32[]{:S(2)}, u32[]{:S(2)}) collective-permute-start(bf16[8,1792]{1,0:T(8,128)(2,1)S(1)} %get-tuple-element.49), channel_id=1, source_target_pairs={{0,8},{1,11},{2,10},{3,9},{4,12},{5,15},{6,14},{7,13},{8,0},{9,3},... | collective-permute-start | bytes 86024 | tf_op jit(solution)/shard_map/ppermute | solution.py:117
  19.8 4.9 %collective-permute-start.11 = (bf16[8,1792]{1,0:T(8,128)(2,1)S(1)}, bf16[8,1792]{1,0:T(8,128)(2,1)S(1)}, u32[]{:S(2)}, u32[]{:S(2)}) collective-permute-start(bf16[8,1792]{1,0:T(8,128)(2,1)S(1)} %get-tuple-element.50), channel_id=1, source_target_pairs={{0,4},{1,7},{2,6},{3,5},{4,0},{5,3},{6,2},{7,1},{8,12},{9,15},{10,... | collective-permute-start | bytes 86024 | tf_op jit(solution)/shard_map/ppermute | solution.py:117
  24.8 1.3 %collective-permute-start.12 = (bf16[32,1152]{1,0:T(8,128)(2,1)S(1)}, bf16[32,1152]{1,0:T(8,128)(2,1)S(1)}, u32[]{:S(2)}, u32[]{:S(2)}) collective-permute-start(bf16[32,1152]{1,0:T(8,128)(2,1)S(1)} %get-tuple-element.54), channel_id=1, source_target_pairs={{0,1},{1,0},{2,3},{3,2},{4,5},{5,4},{6,7},{7,6},{8,9},{9,8},{10,11... | collective-permute-start | bytes 221192 | tf_op jit(solution)/shard_map/ppermute | solution.py:112

commit v6 on v5

--- a/solution.py
+++ b/solution.py
@@ -126,7 +126,11 @@
     out_ref[...] = jnp.where(row < column, 1.0, 0.0).astype(BF16)
 
 
-def route_kernel(capacity, earlier_ref, ids_ref, weights_ref, tokens_ref, rows_ref, cross_ref, count_ref, coef_ref):
+def pick(chosen_ref, tokens_ref):
+    return jnp.dot(chosen_ref[...], tokens_ref[...], preferred_element_type=F32).astype(BF16)
+
+
+def route_kernel(capacity, earlier_ref, ids_ref, weights_ref, tokens_ref, chosen_ref, rows_ref, cross_ref, count_ref, coef_ref):
     z = lax.axis_index("expert")
     ids, weights = ids_ref[...], weights_ref[...]
     rows = ids.shape[1]
@@ -149,9 +153,8 @@
         coef_ref[capacity * k : capacity * (k + 1), :] = one * weight[k]
         total = jnp.minimum(jnp.sum(live[k], axis=1, keepdims=True), float(capacity))
         count_ref[k] = jnp.broadcast_to(total, count_ref.shape[1:]).astype(BF16)
-    picked = jnp.dot(
-        jnp.concatenate(chosen, axis=0).astype(BF16), tokens_ref[...], preferred_element_type=F32
-    ).astype(BF16)
+    chosen_ref[...] = jnp.concatenate(chosen, axis=0).astype(BF16)
+    picked = pick(chosen_ref, tokens_ref)
     rows_ref[...] = picked.reshape(rows_ref.shape)
     cross_ref[...] = jnp.zeros_like(cross_ref)
     cross_ref[:, : picked.shape[1]] = picked[:capacity]
@@ -164,9 +167,12 @@
                 out_ref[i : i + 1, at * QBLK : (at + 1) * QBLK] = jnp.full((1, QBLK), scale_ref[i, at], F32)
 
 
-def line_up_kernel(own_ref, other_ref, count_ref, *out_refs):
+def line_up_kernel(chosen_ref, tokens_ref, own_ref, count_ref, other_ref, *out_refs):
+    rows = other_ref.shape[0]
+    other = pick(chosen_ref, tokens_ref)
+    other_ref[...] = other[:rows]
     for k, out_ref in enumerate(out_refs, 1):
-        out_ref[...] = jnp.concatenate([own_ref[k], other_ref[k], count_ref[k]], axis=1)
+        out_ref[...] = jnp.concatenate([own_ref[k], other[k * rows : (k + 1) * rows], count_ref[k]], axis=1)
 
 
 def on_core(core):
@@ -176,8 +182,11 @@
 def collect_kernel(own_ref, other_ref, count_ref, crossed_ref, swapped_ref, three_ref, two_ref, one_ref, _, out_ref, counts_ref):
     rows, width = crossed_ref.shape[0], out_ref.shape[1] // 2
     zero = on_core(0)
-    for ref, far_ref, lanes in ((own_ref, crossed_ref, slice(0, width)), (other_ref, swapped_ref, slice(width, 2 * width))):
-        value = ref[0].astype(F32) * zero + far_ref[:, :width].astype(F32) * (1.0 - zero)
+    for own, far_ref, lanes in (
+        (own_ref[0], crossed_ref, slice(0, width)),
+        (other_ref[...], swapped_ref, slice(width, 2 * width)),
+    ):
+        value = own.astype(F32) * zero + far_ref[:, :width].astype(F32) * (1.0 - zero)
         out_ref[:rows, lanes] = value.astype(BF16)
     counts_ref[:rows, :] = count_ref[0]
     for k, ref in enumerate((one_ref, two_ref, three_ref), 1):
@@ -366,10 +375,12 @@
         )(*args)
 
     earlier = call(earlier_kernel, "earlier", shape((rows, rows), BF16), (), flops=4 * 10**9)
-    picked, cross, counts, coef = call(
+    other_tokens = swap_cores(tokens)
+    chosen, picked, cross, counts, coef = call(
         functools.partial(route_kernel, capacity),
         "route",
         (
+            shape((slots, rows), BF16),
             shape((4, capacity, width), BF16),
             shape((capacity, 2 * width + 2 * QBLK), BF16),
             shape((4, capacity, QBLK), BF16),
@@ -378,10 +389,12 @@
         (earlier, route_ids.T, route_weights.T, tokens),
         flops=10**11,
     )
-    other = swap_cores(picked)
     crossed = across(cross)
-    messages = call(
-        line_up_kernel, "line_up", (shape((capacity, 2 * width + QBLK), BF16),) * 3, (picked, other, counts)
+    other, *messages = call(
+        line_up_kernel,
+        "line_up",
+        (shape((capacity, width), BF16), *[shape((capacity, 2 * width + QBLK), BF16)] * 3),
+        (chosen, other_tokens, picked, counts),
     )
     scales = call(
         spread_kernel,

time: 27.4 us -> 26.8 us (0.978)
  starting transfers between devices: 14.6 us -> 13.6 us
  waiting for transfers between devices: 6.17 us -> 6.96 us
  local copies, waits for them, and re-layouts: 0.96 us -> 0.42 us
    ppermute x5, starting transfers between devices: 1.92 us -> 1.06 us  [swap_cores(): return lax.ppermute(value, 'mp', [(m, m ^ 1) for m in range(4)])]
    ppermute x5, waiting for transfers between devices: 2.11 us -> 2.73 us  [swap_cores(): return lax.ppermute(value, 'mp', [(m, m ^ 1) for m in range(4)])]
    unnamed x18, local copies, waits for them, and re-layouts: 0.96 us -> 0.42 us
  transfers between devices with their start and end apart: 13 -> 13, of which waited for: 5 -> 7; matrix products, arithmetic and copies ran while one was open for 0% -> 0% of each run, Pallas kernels for 10% -> 12%
where the time goes in v6:
time: 26.8 us; the launch traced here: 26.7 us
  starting transfers between devices  13.6 us (51%)
  waiting for transfers between devices  6.96 us (26%)
  Pallas kernels  4.87 us (18%)
  between operations  0.8 us (3%)
  local copies, waits for them, and re-layouts  0.42 us (2%)
    ppermute x6, starting transfers between devices, to_chips(): return lax.ppermute(value, BOTH, pairs)  8.9 us
    ppermute x6, waiting for transfers between devices, to_chips(): return lax.ppermute(value, BOTH, pairs)  4.23 us
    pallas_call x11, Pallas kernels, call(): pl.pallas_call(kernel, out_shape=outs, in_specs=[SMEM] * scalars + [VMEM]...  3.82 us
    ppermute x2, starting transfers between devices, across(): lax.ppermute(value, BOTH, [(4 * z + m, 4 * z + (m ^ 2)) for z in range(4)...  3.64 us
    ppermute x5, waiting for transfers between devices, swap_cores(): return lax.ppermute(value, 'mp', [(m, m ^ 1) for m in range(4)])  2.73 us
    ppermute x5, starting transfers between devices, swap_cores(): return lax.ppermute(value, 'mp', [(m, m ^ 1) for m in range(4)])  1.06 us
    pallas_call x1, Pallas kernels, on_device(): pl.pallas_call(combine_kernel, out_shape=(shape((rows, width), BF16), sha...  1.05 us
  transfers between devices with their start and end apart: 13, of which 7 were waited for; matrix products, arithmetic and copies ran while one was open for 0% of the time, Pallas kernels for 12%

profile of v6, /device:TPU:0, one launch (start us, length us, event | category | flops | bytes accessed | tf_op | source)
XLA Modules:
  0.0 26.7 jit_solution(2251276246154316651)
XLA Ops:
  0.6 0.0 copy-start.6
  0.6 0.0 copy-start.8
  0.6 0.0 copy-start.7
  0.7 0.5 %collective-permute-start = (bf16[128,896]{1,0:T(8,128)(2,1)}, bf16[128,896]{1,0:T(8,128)(2,1)S(1)}, u32[]{:S(2)}, u32[]{:S(2)}) collective-permute-start(bf16[128,896]{1,0:T(8,128)(2,1)} %tokens_ref.1), channel_id=1, source_target_pairs={{0,1},{1,0},{2,3},{3,2},{4,5},{5,4},{6,7},{7,6},{8,9},{9,8},{10,11... | collective-permute-start | bytes 688136 | tf_op jit(solution)/shard_map/ppermute | solution.py:112
  1.2 0.4 %copy-done.6 = bf16[128,896]{1,0:T(8,128)(2,1)S(1)} copy-done((bf16[128,896]{1,0:T(8,128)(2,1)S(1)}, bf16[128,896]{1,0:T(8,128)(2,1)}, u32[]{:S(2)}) %copy-start.6) | copy-done | bytes 229400
  1.6 0.0 copy-done.8
  1.6 0.0 copy-done.7
  1.6 0.0 copy-start.5
  1.6 0.0 copy-start
  1.6 0.0 copy-start.1
  1.6 0.0 copy-start.2
  1.6 0.3 %route.1 = (bf16[32,128]{1,0:T(8,128)(2,1)S(1)}, bf16[4,8,896]{2,1,0:T(8,128)(2,1)S(1)}, bf16[8,2048]{1,0:T(8,128)(2,1)S(1)}, bf16[4,8,128]{2,1,0:T(8,128)(2,1)S(1)}, f32[32,128]{1,0:T(8,128)S(1)}) custom-call(bf16[128,128]{1,0:T(8,128)(2,1)S(1)} %earlier.1.earlier_ref, s32[8,128]{1,0:T(8,128)S(1)} %bitcast.23, f32[8,128]{1,0:T(8,128)S(1)} %bitcast.24, ...), custom_call_target="tpu_custom_call" | custom-call | flops 99999997952 | tf_op jit(solution)/shard_map/route/pallas_call | solution.py:367
  1.9 3.0 %collective-permute-start.1 = (bf16[8,2048]{1,0:T(8,128)(2,1)S(1)}, bf16[8,2048]{1,0:T(8,128)(2,1)S(1)}, u32[]{:S(2)}, u32[]{:S(2)}) collective-permute-start(bf16[8,2048]{1,0:T(8,128)(2,1)S(1)} %get-tuple-element.37), channel_id=1, source_target_pairs={{0,2},{1,3},{2,0},{3,1},{4,6},{5,7},{6,4},{7,5},{8,10},{9,11},{10,... | collective-permute-start | bytes 98312 | tf_op jit(solution)/shard_map/ppermute | solution.py:121
  4.9 0.0 collective-permute-done.tokens_ref
  4.9 0.1 line_up.1
  5.1 3.7 %collective-permute-start.3 = (bf16[8,1920]{1,0:T(8,128)(2,1)S(1)}, bf16[8,1920]{1,0:T(8,128)(2,1)S(1)}, u32[]{:S(2)}, u32[]{:S(2)}) collective-permute-start(bf16[8,1920]{1,0:T(8,128)(2,1)S(1)} %get-tuple-element.38), channel_id=1, source_target_pairs={{0,12},{1,15},{2,14},{3,13},{4,8},{5,11},{6,10},{7,9},{8,4},{9,7},... | collective-permute-start | bytes 92168 | tf_op jit(solution)/shard_map/ppermute | solution.py:117
  8.7 0.0 collective-permute-start.4
  8.7 0.8 %collective-permute-start.5 = (bf16[8,1920]{1,0:T(8,128)(2,1)S(1)}, bf16[8,1920]{1,0:T(8,128)(2,1)S(1)}, u32[]{:S(2)}, u32[]{:S(2)}) collective-permute-start(bf16[8,1920]{1,0:T(8,128)(2,1)S(1)} %get-tuple-element.40), channel_id=1, source_target_pairs={{0,4},{1,7},{2,6},{3,5},{4,0},{5,3},{6,2},{7,1},{8,12},{9,15},{10,... | collective-permute-start | bytes 92168 | tf_op jit(solution)/shard_map/ppermute | solution.py:117
  9.5 0.0 collective-permute-done.1.crossed_ref
  9.5 0.1 collective-permute-start.2
  9.6 0.0 copy-done.3
  9.6 0.0 copy-done.4
  9.6 0.0 copy-done.5
  9.6 0.6 %spread.1 = (f32[2,3584]{1,0:T(2,128)S(1)}, f32[2,3584]{1,0:T(2,128)S(1)}, f32[2,3584]{1,0:T(2,128)S(1)}) custom-call(f32[2,28]{1,0:T(2,128)S(1)} %bitcast.20, f32[2,28]{1,0:T(2,128)S(1)} %bitcast.21, f32[2,28]{1,0:T(2,128)S(1)} %bitcast.22), custom_call_target="tpu_custom_call" | custom-call | tf_op jit(solution)/shard_map/spread/pallas_call | solution.py:367
  10.2 0.5 %collective-permute-done.2.swapped_ref = bf16[8,896]{1,0:T(8,128)(2,1)S(1)} collective-permute-done((bf16[8,896]{1,0:T(8,128)(2,1)S(1)}, bf16[8,896]{1,0:T(8,128)(2,1)S(1)}, u32[]{:S(2)}, u32[]{:S(2)}) %collective-permute-start.2) | collective-permute-done | bytes 14368 | tf_op jit(solution)/shard_map/ppermute | solution.py:112
  10.7 0.1 collective-permute-done.3.three_ref
  10.8 2.7 %collective-permute-done.4.two_ref = bf16[8,1920]{1,0:T(8,128)(2,1)S(1)} collective-permute-done((bf16[8,1920]{1,0:T(8,128)(2,1)S(1)}, bf16[8,1920]{1,0:T(8,128)(2,1)S(1)}, u32[]{:S(2)}, u32[]{:S(2)}) %collective-permute-start.4) | collective-permute-done | bytes 30752 | tf_op jit(solution)/shard_map/ppermute | solution.py:117
  13.5 0.0 collective-permute-done.5.one_ref
  13.6 0.1 collective-permute-start.6
  13.6 0.0 copy-done
  13.7 0.5 %near.1 = (f32[64,256]{1,0:T(8,128)S(1)}, f32[64,256]{1,0:T(8,128)S(1)}) custom-call(bf16[32,1792]{1,0:T(8,128)(2,1)S(1)} %get-tuple-element.42.x_ref, bf16[3584,256]{1,0:T(8,128)(2,1)S(1)} %bitcast.16, bf16[3584,256]{1,0:T(8,128)(2,1)S(1)} %bitcast.18, f32[2,3584]{1,0:T(2,128)S(1)} %get-tuple-element.41._.gate_scale_ref, ...), custom_call_target="tpu_custom_call" | custom-call | tf_op jit(solution)/shard_map/near/pallas_call | solution.py:367
  14.1 0.8 %collective-permute-done.6.x_ref = bf16[32,1792]{1,0:T(8,128)(2,1)S(1)} collective-permute-done((bf16[32,1792]{1,0:T(8,128)(2,1)S(1)}, bf16[32,1792]{1,0:T(8,128)(2,1)S(1)}, u32[]{:S(2)}, u32[]{:S(2)}) %collective-permute-start.6) | collective-permute-done | bytes 114720 | tf_op jit(solution)/shard_map/ppermute | solution.py:112
  15.0 0.7 %hidden.1 = (bf16[32,2048]{1,0:T(8,128)(2,1)S(1)}, bf16[32,256]{1,0:T(8,128)(2,1)S(1)}) custom-call(bf16[32,1792]{1,0:T(8,128)(2,1)S(1)} %collective-permute-done.6.x_ref, f32[64,256]{1,0:T(8,128)S(1)} %get-tuple-element.44.near_gate_ref, f32[64,256]{1,0:T(8,128)S(1)} %get-tuple-element.45.near_up_ref, bf16[3584,256]{1,0:T(8,128)(2,1)S(1)} %bitcast.17, ...), custom_call_target="tpu_custom_call" | custom-call | tf_op jit(solution)/shard_map/hidden/pallas_call | solution.py:367
  15.7 0.2 collective-permute-start.7
  15.9 0.3 keep.1
  16.1 0.6 %collective-permute-start.8 = (bf16[8,2816]{1,0:T(8,128)(2,1)S(1)}, bf16[8,2816]{1,0:T(8,128)(2,1)S(1)}, u32[]{:S(2)}, u32[]{:S(2)}) collective-permute-start(bf16[8,2816]{1,0:T(8,128)(2,1)S(1)} %get-tuple-element.51), channel_id=1, source_target_pairs={{0,2},{1,3},{2,0},{3,1},{4,6},{5,7},{6,4},{7,5},{8,10},{9,11},{10,... | collective-permute-start | bytes 135176 | tf_op jit(solution)/shard_map/ppermute | solution.py:121
  16.8 0.3 %collective-permute-done.7.sent_ref = bf16[32,2048]{1,0:T(8,128)(2,1)S(1)} collective-permute-done((bf16[32,2048]{1,0:T(8,128)(2,1)S(1)}, bf16[32,2048]{1,0:T(8,128)(2,1)S(1)}, u32[]{:S(2)}, u32[]{:S(2)}) %collective-permute-start.7) | collective-permute-done | bytes 131104 | tf_op jit(solution)/shard_map/ppermute | solution.py:112
  17.1 1.7 %collective-permute-start.9 = (bf16[8,1792]{1,0:T(8,128)(2,1)S(1)}, bf16[8,1792]{1,0:T(8,128)(2,1)S(1)}, u32[]{:S(2)}, u32[]{:S(2)}) collective-permute-start(bf16[8,1792]{1,0:T(8,128)(2,1)S(1)} %get-tuple-element.52), channel_id=1, source_target_pairs={{0,12},{1,15},{2,14},{3,13},{4,8},{5,11},{6,10},{7,9},{8,4},{9,7},... | collective-permute-start | bytes 86024 | tf_op jit(solution)/shard_map/ppermute | solution.py:117
  18.8 0.4 %collective-permute-start.10 = (bf16[8,1792]{1,0:T(8,128)(2,1)S(1)}, bf16[8,1792]{1,0:T(8,128)(2,1)S(1)}, u32[]{:S(2)}, u32[]{:S(2)}) collective-permute-start(bf16[8,1792]{1,0:T(8,128)(2,1)S(1)} %get-tuple-element.53), channel_id=1, source_target_pairs={{0,8},{1,11},{2,10},{3,9},{4,12},{5,15},{6,14},{7,13},{8,0},{9,3},... | collective-permute-start | bytes 86024 | tf_op jit(solution)/shard_map/ppermute | solution.py:117
  19.3 2.3 %collective-permute-start.11 = (bf16[8,1792]{1,0:T(8,128)(2,1)S(1)}, bf16[8,1792]{1,0:T(8,128)(2,1)S(1)}, u32[]{:S(2)}, u32[]{:S(2)}) collective-permute-start(bf16[8,1792]{1,0:T(8,128)(2,1)S(1)} %get-tuple-element.54), channel_id=1, source_target_pairs={{0,4},{1,7},{2,6},{3,5},{4,0},{5,3},{6,2},{7,1},{8,12},{9,15},{10,... | collective-permute-start | bytes 86024 | tf_op jit(solution)/shard_map/ppermute | solution.py:117
  21.6 0.0 collective-permute-done.8.crossed_ref
  21.6 1.3 %hessian.1 = (f32[256,1024]{1,0:T(8,128)}, bf16[32,256]{1,0:T(8,128)(2,1)S(1)}) custom-call(bf16[32,128]{1,0:T(8,128)(2,1)S(1)} %get-tuple-element.55.count_ref, bf16[32,256]{1,0:T(8,128)(2,1)S(1)} %get-tuple-element.47.hidden_ref.own_ref, bf16[32,2048]{1,0:T(8,128)(2,1)S(1)} %collective-permute-done.7.sent_ref, ...), custom_call_target="tpu_custom_call" | custom-call | tf_op jit(solution)/shard_map/hessian/pallas_call | solution.py:367
  22.8 0.0 collective-permute-done.9.three_ref
  22.9 1.4 %collective-permute-done.10.two_ref = bf16[8,1792]{1,0:T(8,128)(2,1)S(1)} collective-permute-done((bf16[8,1792]{1,0:T(8,128)(2,1)S(1)}, bf16[8,1792]{1,0:T(8,128)(2,1)S(1)}, u32[]{:S(2)}, u32[]{:S(2)}) %collective-permute-start.10) | collective-permute-done | bytes 28704 | tf_op jit(solution)/shard_map/ppermute | solution.py:117
  24.2 0.0 collective-permute-done.11.one_ref
  24.3 0.2 collective-permute-start.12
  24.4 1.2 %collective-permute-done.12.far_ref = bf16[32,1152]{1,0:T(8,128)(2,1)S(1)} collective-permute-done((bf16[32,1152]{1,0:T(8,128)(2,1)S(1)}, bf16[32,1152]{1,0:T(8,128)(2,1)S(1)}, u32[]{:S(2)}, u32[]{:S(2)}) %collective-permute-start.12) | collective-permute-done | bytes 73760 | tf_op jit(solution)/shard_map/ppermute | solution.py:112
  25.6 1.0 %combine.1 = (bf16[128,896]{1,0:T(8,128)(2,1)}, f32[256,1024]{1,0:T(8,128)}) custom-call(f32[32,128]{1,0:T(8,128)S(1)} %get-tuple-element.32.coef_ref, bf16[32,896]{1,0:T(8,128)(2,1)S(1)} %get-tuple-element.57.near_ref, bf16[32,1152]{1,0:T(8,128)(2,1)S(1)} %collective-permute-done.12.far_ref, ...), custom_call_target="tpu_custom_call", output_to_operand_aliasing={{1}: (5, {})} | custom-call | tf_op jit(solution)/shard_map/combine/pallas_call | solution.py:452
  (9 shorter events, 0.1 us)
Async XLA Ops:
  0.6 0.9 %copy-start.6 = (bf16[128,896]{1,0:T(8,128)(2,1)S(1)}, bf16[128,896]{1,0:T(8,128)(2,1)}, u32[]{:S(2)}) copy-start(bf16[128,896]{1,0:T(8,128)(2,1)} %tokens_ref.1) | copy-start | bytes 688132
  0.6 0.9 %copy-start.8 = (f32[128,8]{0,1:T(8,128)S(1)}, f32[128,8]{0,1:T(8,128)}, u32[]{:S(2)}) copy-start(f32[128,8]{0,1:T(8,128)} %param.11) | copy-start | bytes 12292
  0.6 0.9 %copy-start.7 = (s32[128,8]{0,1:T(8,128)S(1)}, s32[128,8]{0,1:T(8,128)}, u32[]{:S(2)}) copy-start(s32[128,8]{0,1:T(8,128)} %param.10) | copy-start | bytes 12292
  0.7 4.3 %collective-permute-start = (bf16[128,896]{1,0:T(8,128)(2,1)}, bf16[128,896]{1,0:T(8,128)(2,1)S(1)}, u32[]{:S(2)}, u32[]{:S(2)}) collective-permute-start(bf16[128,896]{1,0:T(8,128)(2,1)} %tokens_ref.1), channel_id=1, source_target_pairs={{0,1},{1,0},{2,3},{3,2},{4,5},{5,4},{6,7},{7,6},{8,9},{9,8},{10,11... | collective-permute-start | bytes 688136 | tf_op jit(solution)/shard_map/ppermute | solution.py:112
  1.6 8.0 %copy-start.3 = (f32[1,28,2]{1,2,0:T(2,128)S(1)}, f32[1,28,2]{1,2,0:T(2,128)}, u32[]{:S(2)}) copy-start(f32[1,28,2]{1,2,0:T(2,128)} %param.13) | copy-start | bytes 676
  1.6 8.0 %copy-start.4 = (f32[1,28,2]{1,2,0:T(2,128)S(1)}, f32[1,28,2]{1,2,0:T(2,128)}, u32[]{:S(2)}) copy-start(f32[1,28,2]{1,2,0:T(2,128)} %param.15) | copy-start | bytes 676
  1.6 8.0 %copy-start.5 = (f32[1,2,28]{2,1,0:T(2,128)S(1)}, f32[1,2,28]{2,1,0:T(2,128)}, u32[]{:S(2)}) copy-start(f32[1,2,28]{2,1,0:T(2,128)} %param.17) | copy-start | bytes 676
  1.6 12.0 %copy-start = (bf16[1,256,3584]{2,1,0:T(8,128)(2,1)S(1)}, bf16[1,256,3584]{2,1,0:T(8,128)(2,1)}, u32[]{:S(2)}) copy-start(bf16[1,256,3584]{2,1,0:T(8,128)(2,1)} %param.16) | copy-start | bytes 5505028
  1.6 12.0 %copy-start.1 = (bf16[1,3584,256]{2,1,0:T(8,128)(2,1)S(1)}, bf16[1,3584,256]{2,1,0:T(8,128)(2,1)}, u32[]{:S(2)}) copy-start(bf16[1,3584,256]{2,1,0:T(8,128)(2,1)} %param.12) | copy-start | bytes 5505028
  1.6 12.0 %copy-start.2 = (bf16[1,3584,256]{2,1,0:T(8,128)(2,1)S(1)}, bf16[1,3584,256]{2,1,0:T(8,128)(2,1)}, u32[]{:S(2)}) copy-start(bf16[1,3584,256]{2,1,0:T(8,128)(2,1)} %param.14) | copy-start | bytes 5505028
  1.9 7.6 %collective-permute-start.1 = (bf16[8,2048]{1,0:T(8,128)(2,1)S(1)}, bf16[8,2048]{1,0:T(8,128)(2,1)S(1)}, u32[]{:S(2)}, u32[]{:S(2)}) collective-permute-start(bf16[8,2048]{1,0:T(8,128)(2,1)S(1)} %get-tuple-element.37), channel_id=1, source_target_pairs={{0,2},{1,3},{2,0},{3,1},{4,6},{5,7},{6,4},{7,5},{8,10},{9,11},{10,... | collective-permute-start | bytes 98312 | tf_op jit(solution)/shard_map/ppermute | solution.py:121
  5.1 5.8 %collective-permute-start.3 = (bf16[8,1920]{1,0:T(8,128)(2,1)S(1)}, bf16[8,1920]{1,0:T(8,128)(2,1)S(1)}, u32[]{:S(2)}, u32[]{:S(2)}) collective-permute-start(bf16[8,1920]{1,0:T(8,128)(2,1)S(1)} %get-tuple-element.38), channel_id=1, source_target_pairs={{0,12},{1,15},{2,14},{3,13},{4,8},{5,11},{6,10},{7,9},{8,4},{9,7},... | collective-permute-start | bytes 92168 | tf_op jit(solution)/shard_map/ppermute | solution.py:117
  8.7 4.8 %collective-permute-start.4 = (bf16[8,1920]{1,0:T(8,128)(2,1)S(1)}, bf16[8,1920]{1,0:T(8,128)(2,1)S(1)}, u32[]{:S(2)}, u32[]{:S(2)}) collective-permute-start(bf16[8,1920]{1,0:T(8,128)(2,1)S(1)} %get-tuple-element.39), channel_id=1, source_target_pairs={{0,8},{1,11},{2,10},{3,9},{4,12},{5,15},{6,14},{7,13},{8,0},{9,3},... | collective-permute-start | bytes 92168 | tf_op jit(solution)/shard_map/ppermute | solution.py:117
  8.7 4.8 %collective-permute-start.5 = (bf16[8,1920]{1,0:T(8,128)(2,1)S(1)}, bf16[8,1920]{1,0:T(8,128)(2,1)S(1)}, u32[]{:S(2)}, u32[]{:S(2)}) collective-permute-start(bf16[8,1920]{1,0:T(8,128)(2,1)S(1)} %get-tuple-element.40), channel_id=1, source_target_pairs={{0,4},{1,7},{2,6},{3,5},{4,0},{5,3},{6,2},{7,1},{8,12},{9,15},{10,... | collective-permute-start | bytes 92168 | tf_op jit(solution)/shard_map/ppermute | solution.py:117
  9.5 1.2 %collective-permute-start.2 = (bf16[8,896]{1,0:T(8,128)(2,1)S(1)}, bf16[8,896]{1,0:T(8,128)(2,1)S(1)}, u32[]{:S(2)}, u32[]{:S(2)}) collective-permute-start(bf16[8,896]{1,0:T(8,128)(2,1)S(1)} %slice.4), channel_id=1, source_target_pairs={{0,1},{1,0},{2,3},{3,2},{4,5},{5,4},{6,7},{7,6},{8,9},{9,8},{10,11... | collective-permute-start | bytes 43016 | tf_op jit(solution)/shard_map/ppermute | solution.py:112
  13.6 1.4 %collective-permute-start.6 = (bf16[32,1792]{1,0:T(8,128)(2,1)S(1)}, bf16[32,1792]{1,0:T(8,128)(2,1)S(1)}, u32[]{:S(2)}, u32[]{:S(2)}) collective-permute-start(bf16[32,1792]{1,0:T(8,128)(2,1)S(1)} %get-tuple-element.42.x_ref), channel_id=1, source_target_pairs={{0,1},{1,0},{2,3},{3,2},{4,5},{5,4},{6,7},{7,6},{8,9},{9,8},{10,11... | collective-permute-start | bytes 344072 | tf_op jit(solution)/shard_map/ppermute | solution.py:112
  15.7 1.4 %collective-permute-start.7 = (bf16[32,2048]{1,0:T(8,128)(2,1)S(1)}, bf16[32,2048]{1,0:T(8,128)(2,1)S(1)}, u32[]{:S(2)}, u32[]{:S(2)}) collective-permute-start(bf16[32,2048]{1,0:T(8,128)(2,1)S(1)} %get-tuple-element.48.send_ref), channel_id=1, source_target_pairs={{0,1},{1,0},{2,3},{3,2},{4,5},{5,4},{6,7},{7,6},{8,9},{9,8},{10,11... | collective-permute-start | bytes 393224 | tf_op jit(solution)/shard_map/ppermute | solution.py:112
  16.1 5.4 %collective-permute-start.8 = (bf16[8,2816]{1,0:T(8,128)(2,1)S(1)}, bf16[8,2816]{1,0:T(8,128)(2,1)S(1)}, u32[]{:S(2)}, u32[]{:S(2)}) collective-permute-start(bf16[8,2816]{1,0:T(8,128)(2,1)S(1)} %get-tuple-element.51), channel_id=1, source_target_pairs={{0,2},{1,3},{2,0},{3,1},{4,6},{5,7},{6,4},{7,5},{8,10},{9,11},{10,... | collective-permute-start | bytes 135176 | tf_op jit(solution)/shard_map/ppermute | solution.py:121
  17.1 5.8 %collective-permute-start.9 = (bf16[8,1792]{1,0:T(8,128)(2,1)S(1)}, bf16[8,1792]{1,0:T(8,128)(2,1)S(1)}, u32[]{:S(2)}, u32[]{:S(2)}) collective-permute-start(bf16[8,1792]{1,0:T(8,128)(2,1)S(1)} %get-tuple-element.52), channel_id=1, source_target_pairs={{0,12},{1,15},{2,14},{3,13},{4,8},{5,11},{6,10},{7,9},{8,4},{9,7},... | collective-permute-start | bytes 86024 | tf_op jit(solution)/shard_map/ppermute | solution.py:117
  18.8 5.4 %collective-permute-start.10 = (bf16[8,1792]{1,0:T(8,128)(2,1)S(1)}, bf16[8,1792]{1,0:T(8,128)(2,1)S(1)}, u32[]{:S(2)}, u32[]{:S(2)}) collective-permute-start(bf16[8,1792]{1,0:T(8,128)(2,1)S(1)} %get-tuple-element.53), channel_id=1, source_target_pairs={{0,8},{1,11},{2,10},{3,9},{4,12},{5,15},{6,14},{7,13},{8,0},{9,3},... | collective-permute-start | bytes 86024 | tf_op jit(solution)/shard_map/ppermute | solution.py:117
  19.3 5.0 %collective-permute-start.11 = (bf16[8,1792]{1,0:T(8,128)(2,1)S(1)}, bf16[8,1792]{1,0:T(8,128)(2,1)S(1)}, u32[]{:S(2)}, u32[]{:S(2)}) collective-permute-start(bf16[8,1792]{1,0:T(8,128)(2,1)S(1)} %get-tuple-element.54), channel_id=1, source_target_pairs={{0,4},{1,7},{2,6},{3,5},{4,0},{5,3},{6,2},{7,1},{8,12},{9,15},{10,... | collective-permute-start | bytes 86024 | tf_op jit(solution)/shard_map/ppermute | solution.py:117
  24.3 1.3 %collective-permute-start.12 = (bf16[32,1152]{1,0:T(8,128)(2,1)S(1)}, bf16[32,1152]{1,0:T(8,128)(2,1)S(1)}, u32[]{:S(2)}, u32[]{:S(2)}) collective-permute-start(bf16[32,1152]{1,0:T(8,128)(2,1)S(1)} %get-tuple-element.58), channel_id=1, source_target_pairs={{0,1},{1,0},{2,3},{3,2},{4,5},{5,4},{6,7},{7,6},{8,9},{9,8},{10,11... | collective-permute-start | bytes 221192 | tf_op jit(solution)/shard_map/ppermute | solution.py:112

commit v7 on v6

--- a/solution.py
+++ b/solution.py
@@ -130,41 +130,53 @@
     return jnp.dot(chosen_ref[...], tokens_ref[...], preferred_element_type=F32).astype(BF16)
 
 
-def route_kernel(capacity, earlier_ref, ids_ref, weights_ref, tokens_ref, chosen_ref, rows_ref, cross_ref, count_ref, coef_ref):
+def route_kernel(capacity, earlier_ref, ids_ref, chosen_ref, count_ref):
     z = lax.axis_index("expert")
-    ids, weights = ids_ref[...], weights_ref[...]
+    ids = ids_ref[...]
     rows = ids.shape[1]
-    live, weight = [], []
-    for k in range(4):
-        hit = ids == (z ^ k)
-        live.append(jnp.sum(jnp.where(hit, 1.0, 0.0), axis=0, keepdims=True))
-        weight.append(jnp.sum(jnp.where(hit, weights, 0.0), axis=0, keepdims=True))
+    live = [jnp.sum(jnp.where(ids == (z ^ k), 1.0, 0.0), axis=0, keepdims=True) for k in range(4)]
     position = jnp.dot(
-        jnp.concatenate(live, axis=0).astype(BF16),
-        earlier_ref[...],
-        preferred_element_type=F32,
+        jnp.concatenate(live, axis=0).astype(BF16), earlier_ref[...], preferred_element_type=F32
     )
     slot = lax.broadcasted_iota(jnp.int32, (capacity, rows), 0).astype(F32)
     chosen = []
     for k in range(4):
         kept = (live[k] > 0.5) & (position[k : k + 1] == slot)
-        one = jnp.where(kept, 1.0, 0.0)
-        chosen.append(one)
-        coef_ref[capacity * k : capacity * (k + 1), :] = one * weight[k]
+        chosen.append(jnp.where(kept, 1.0, 0.0))
         total = jnp.minimum(jnp.sum(live[k], axis=1, keepdims=True), float(capacity))
         count_ref[k] = jnp.broadcast_to(total, count_ref.shape[1:]).astype(BF16)
     chosen_ref[...] = jnp.concatenate(chosen, axis=0).astype(BF16)
+
+
+def own_kernel(chosen_ref, tokens_ref, rows_ref, cross_ref):
     picked = pick(chosen_ref, tokens_ref)
+    rows, width = rows_ref.shape[1:]
     rows_ref[...] = picked.reshape(rows_ref.shape)
-    cross_ref[...] = jnp.zeros_like(cross_ref)
-    cross_ref[:, : picked.shape[1]] = picked[:capacity]
-
-
-def spread_kernel(*refs):
-    for scale_ref, out_ref in zip(refs[:3], refs[3:]):
+    cross_ref[:, :width] = picked[:rows]
+    cross_ref[:, width:] = jnp.zeros((rows, cross_ref.shape[1] - width), BF16)
+
+
+def prepare_kernel(
+    gate_scale_ref, up_scale_ref, down_scale_ref, ids_ref, weights_ref, chosen_ref, gate_out, up_out, down_out, coef_ref
+):
+    for scale_ref, out_ref in ((gate_scale_ref, gate_out), (up_scale_ref, up_out), (down_scale_ref, down_out)):
         for at in range(scale_ref.shape[1]):
             for i in range(2):
                 out_ref[i : i + 1, at * QBLK : (at + 1) * QBLK] = jnp.full((1, QBLK), scale_ref[i, at], F32)
+    z = lax.axis_index("expert")
+    slots = chosen_ref.shape[0]
+    capacity = slots // 4
+    coef = []
+    for k in range(4):
+        weight = jnp.sum(jnp.where(ids_ref[...] == (z ^ k), weights_ref[...], 0.0), axis=0, keepdims=True)
+        coef.append(chosen_ref[k * capacity : (k + 1) * capacity, :].astype(F32) * weight)
+    coef = jnp.concatenate(coef, axis=0)
+    terms = []
+    for _ in range(3):
+        terms.append(coef.astype(BF16).astype(F32))
+        coef = coef - terms[-1]
+    terms.append(jnp.zeros_like(coef))
+    coef_ref[...] = jnp.concatenate(terms, axis=0).T.astype(BF16)
 
 
 def line_up_kernel(chosen_ref, tokens_ref, own_ref, count_ref, other_ref, *out_refs):
@@ -290,11 +302,7 @@
     return 2.0 / (counts[0] + counts[1] + counts[2] + counts[3])
 
 
-def hessian_block(own_ref, other, factor):
-    return lax.dot_general(own_ref[...], other, (((0,), (0,)), ((), ())), preferred_element_type=F32) * factor
-
-
-def hessian_kernel(count_ref, own_ref, sent_ref, crossed_ref, out_ref, far_ref):
+def hessian_kernel(count_ref, own_ref, sent_ref, crossed_ref, out_ref, far_ref, turned_ref):
     m = lax.axis_index("mp")
     width = out_ref.shape[0]
     rows = far_ref.shape[0] // 4
@@ -302,9 +310,11 @@
     for k in range(4):
         far_ref[k * rows : (k + 1) * rows, :] = crossed_ref[:, start + k * width : start + (k + 1) * width]
     factor = hessian_factor(count_ref)
+    turned_ref[...] = own_ref[...].astype(F32).T.astype(BF16)
     others = ((m, own_ref[...]), (m ^ 1, sent_ref[:, sent_ref.shape[1] - width :]), (m ^ 2, far_ref[...]))
     for share, other in others:
-        out_ref[:, pl.ds(pl.multiple_of(share * width, width), width)] = hessian_block(own_ref, other, factor)
+        block = jnp.dot(turned_ref[...], other, preferred_element_type=F32) * factor
+        out_ref[:, pl.ds(pl.multiple_of(share * width, width), width)] = block
 
 
 def collect_back_kernel(summed_ref, crossed_ref, three_ref, two_ref, one_ref, far_ref, mine_ref, other_ref):
@@ -318,31 +328,22 @@
 
 
 def combine_kernel(
-    coef_ref, near_ref, far_ref, count_ref, own_ref, _, mixed_hbm, hessian_hbm, mixed_ref, block_ref, sems
+    coef_ref, near_ref, far_ref, count_ref, turned_ref, _, mixed_hbm, hessian_hbm, mixed_ref, block_ref, sems
 ):
     width, hidden_width = near_ref.shape[1], block_ref.shape[0]
-    result = (near_ref[...].astype(F32) + far_ref[:, :width].astype(F32)).astype(BF16)
-    coef = coef_ref[...]
-    terms = []
-    for _ in range(3):
-        terms.append(coef.astype(BF16))
-        coef = coef - terms[-1].astype(F32)
-    out = lax.dot_general(
-        jnp.concatenate(terms, axis=0),
-        jnp.concatenate([result] * 3, axis=0),
-        (((0,), (0,)), ((), ())),
-        preferred_element_type=F32,
-    )
-    mixed_ref[...] = out.astype(BF16)
-    mixed_copy = pltpu.make_async_copy(mixed_ref, mixed_hbm, sems.at[0])
-    mixed_copy.start()
-    block_ref[...] = hessian_block(own_ref, far_ref[:, width:], hessian_factor(count_ref))
+    block = jnp.dot(turned_ref[...], far_ref[:, width:], preferred_element_type=F32)
+    block_ref[...] = block * hessian_factor(count_ref)
     share = lax.axis_index("mp") ^ 3
     lanes = pl.ds(pl.multiple_of(share * hidden_width, hidden_width), hidden_width)
-    block_copy = pltpu.make_async_copy(block_ref, hessian_hbm.at[:, lanes], sems.at[1])
+    block_copy = pltpu.make_async_copy(block_ref, hessian_hbm.at[:, lanes], sems.at[0])
     block_copy.start()
+    result = (near_ref[...].astype(F32) + far_ref[:, :width].astype(F32)).astype(BF16)
+    out = jnp.dot(coef_ref[...], jnp.concatenate([result] * 4, axis=0), preferred_element_type=F32)
+    mixed_ref[...] = out.astype(BF16)
+    mixed_copy = pltpu.make_async_copy(mixed_ref, mixed_hbm, sems.at[1])
+    mixed_copy.start()
+    block_copy.wait()
     mixed_copy.wait()
-    block_copy.wait()
 
 
 def on_device(
@@ -376,17 +377,17 @@
 
     earlier = call(earlier_kernel, "earlier", shape((rows, rows), BF16), (), flops=4 * 10**9)
     other_tokens = swap_cores(tokens)
-    chosen, picked, cross, counts, coef = call(
+    chosen, counts = call(
         functools.partial(route_kernel, capacity),
         "route",
-        (
-            shape((slots, rows), BF16),
-            shape((4, capacity, width), BF16),
-            shape((capacity, 2 * width + 2 * QBLK), BF16),
-            shape((4, capacity, QBLK), BF16),
-            shape((slots, rows), F32),
-        ),
-        (earlier, route_ids.T, route_weights.T, tokens),
+        (shape((slots, rows), BF16), shape((4, capacity, QBLK), BF16)),
+        (earlier, route_ids.T),
+    )
+    picked, cross = call(
+        own_kernel,
+        "own",
+        (shape((4, capacity, width), BF16), shape((capacity, 2 * width + 2 * QBLK), BF16)),
+        (chosen, tokens),
         flops=10**11,
     )
     crossed = across(cross)
@@ -396,11 +397,11 @@
         (shape((capacity, width), BF16), *[shape((capacity, 2 * width + QBLK), BF16)] * 3),
         (chosen, other_tokens, picked, counts),
     )
-    scales = call(
-        spread_kernel,
-        "spread",
-        (shape((2, 4 * width), F32),) * 3,
-        (gate_scale[0].T, up_scale[0].T, down_scale[0]),
+    *scales, coef = call(
+        prepare_kernel,
+        "prepare",
+        (*[shape((2, 4 * width), F32)] * 3, shape((rows, 4 * slots), BF16)),
+        (gate_scale[0].T, up_scale[0].T, down_scale[0], route_ids.T, route_weights.T, chosen),
         scalars=3,
     )
     gate, up, down = gate_weight[0], up_weight[0], down_weight[0]
@@ -437,10 +438,14 @@
     crossed = across(cross)
     summed = call(chip_sum_kernel, "chip_sum", (shape((capacity, 2 * width), BF16),) * 4, (keep, sent))
     back = {k: to_chips(summed[k], k) for k in range(1, 4)}
-    hessian, far = call(
+    hessian, far, turned = call(
         hessian_kernel,
         "hessian",
-        (shape((hidden_width, 4 * hidden_width), F32), shape((slots, hidden_width), BF16)),
+        (
+            shape((hidden_width, 4 * hidden_width), F32),
+            shape((slots, hidden_width), BF16),
+            shape((hidden_width, slots), BF16),
+        ),
         (arrived_counts, hidden, sent, crossed),
     )
     mine, other = call(
@@ -462,7 +467,7 @@
         input_output_aliases={5: 1},
         compiler_params=pltpu.CompilerParams(vmem_limit_bytes=8 * 1024 * 1024),
         name="combine",
-    )(coef, mine, swap_cores(other), arrived_counts, hidden, hessian)
+    )(coef, mine, swap_cores(other), arrived_counts, turned, hessian)
     return mixed, hessian[None]
 
 

time: 26.8 us -> 26.7 us (level)
  waiting for transfers between devices: 6.96 us -> 6.65 us
    ppermute x5, waiting for transfers between devices: 2.73 us -> 2.42 us  [swap_cores(): return lax.ppermute(value, 'mp', [(m, m ^ 1) for m in range(4)])]
    pallas_call x11 -> x12, Pallas kernels: 3.82 us -> 3.93 us  [call(): pl.pallas_call(kernel, out_shape=outs, in_specs=[SMEM] * scalars + [VMEM]...]
where the time goes in v7:
time: 26.7 us; the launch traced here: 26.5 us
  starting transfers between devices  13.8 us (52%)
  waiting for transfers between devices  6.65 us (25%)
  Pallas kernels  4.92 us (18%)
  between operations  0.78 us (3%)
  local copies, waits for them, and re-layouts  0.31 us (1%)
    ppermute x6, starting transfers between devices, to_chips(): return lax.ppermute(value, BOTH, pairs)  8.9 us
    ppermute x6, waiting for transfers between devices, to_chips(): return lax.ppermute(value, BOTH, pairs)  4.23 us
    pallas_call x12, Pallas kernels, call(): pl.pallas_call(kernel, out_shape=outs, in_specs=[SMEM] * scalars + [VMEM]...  3.93 us
    ppermute x2, starting transfers between devices, across(): lax.ppermute(value, BOTH, [(4 * z + m, 4 * z + (m ^ 2)) for z in range(4)...  3.76 us
    ppermute x5, waiting for transfers between devices, swap_cores(): return lax.ppermute(value, 'mp', [(m, m ^ 1) for m in range(4)])  2.42 us
    ppermute x5, starting transfers between devices, swap_cores(): return lax.ppermute(value, 'mp', [(m, m ^ 1) for m in range(4)])  1.18 us
    pallas_call x1, Pallas kernels, on_device(): pl.pallas_call(combine_kernel, out_shape=(shape((rows, width), BF16), sha...  0.99 us
  transfers between devices with their start and end apart: 13, of which 7 were waited for; matrix products, arithmetic and copies ran while one was open for 0% of the time, Pallas kernels for 12%

profile of v7, /device:TPU:0, one launch (start us, length us, event | category | flops | bytes accessed | tf_op | source)
XLA Modules:
  0.0 26.5 jit_solution(954587160028266271)
XLA Ops:
  0.6 0.0 copy-start.8
  0.6 0.0 copy-start.3
  0.6 0.5 %collective-permute-start = (bf16[128,896]{1,0:T(8,128)(2,1)}, bf16[128,896]{1,0:T(8,128)(2,1)S(1)}, u32[]{:S(2)}, u32[]{:S(2)}) collective-permute-start(bf16[128,896]{1,0:T(8,128)(2,1)} %tokens_ref.1), channel_id=1, source_target_pairs={{0,1},{1,0},{2,3},{3,2},{4,5},{5,4},{6,7},{7,6},{8,9},{9,8},{10,11... | collective-permute-start | bytes 688136 | tf_op jit(solution)/shard_map/ppermute | solution.py:112
  1.2 0.2 copy-done.3
  1.4 0.1 route.1
  1.5 0.1 copy-done.8
  1.6 0.0 copy-start
  1.6 0.0 copy-start.1
  1.6 0.0 copy-start.2
  1.6 0.1 own.1
  1.8 3.0 %collective-permute-start.1 = (bf16[8,2048]{1,0:T(8,128)(2,1)S(1)}, bf16[8,2048]{1,0:T(8,128)(2,1)S(1)}, u32[]{:S(2)}, u32[]{:S(2)}) collective-permute-start(bf16[8,2048]{1,0:T(8,128)(2,1)S(1)} %get-tuple-element.38), channel_id=1, source_target_pairs={{0,2},{1,3},{2,0},{3,1},{4,6},{5,7},{6,4},{7,5},{8,10},{9,11},{10,... | collective-permute-start | bytes 98312 | tf_op jit(solution)/shard_map/ppermute | solution.py:121
  4.8 0.0 collective-permute-done.tokens_ref
  4.8 0.1 line_up.1
  4.9 3.7 %collective-permute-start.3 = (bf16[8,1920]{1,0:T(8,128)(2,1)S(1)}, bf16[8,1920]{1,0:T(8,128)(2,1)S(1)}, u32[]{:S(2)}, u32[]{:S(2)}) collective-permute-start(bf16[8,1920]{1,0:T(8,128)(2,1)S(1)} %get-tuple-element.39), channel_id=1, source_target_pairs={{0,12},{1,15},{2,14},{3,13},{4,8},{5,11},{6,10},{7,9},{8,4},{9,7},... | collective-permute-start | bytes 92168 | tf_op jit(solution)/shard_map/ppermute | solution.py:117
  8.6 0.0 collective-permute-start.4
  8.6 0.8 %collective-permute-start.5 = (bf16[8,1920]{1,0:T(8,128)(2,1)S(1)}, bf16[8,1920]{1,0:T(8,128)(2,1)S(1)}, u32[]{:S(2)}, u32[]{:S(2)}) collective-permute-start(bf16[8,1920]{1,0:T(8,128)(2,1)S(1)} %get-tuple-element.41), channel_id=1, source_target_pairs={{0,4},{1,7},{2,6},{3,5},{4,0},{5,3},{6,2},{7,1},{8,12},{9,15},{10,... | collective-permute-start | bytes 92168 | tf_op jit(solution)/shard_map/ppermute | solution.py:117
  9.4 0.0 collective-permute-done.1.crossed_ref
  9.4 0.2 collective-permute-start.2
  9.6 0.0 copy-done.4
  9.6 0.0 copy-done.5
  9.6 0.0 copy-done.7
  9.6 0.7 %prepare.1 = (f32[2,3584]{1,0:T(2,128)S(1)}, f32[2,3584]{1,0:T(2,128)S(1)}, f32[2,3584]{1,0:T(2,128)S(1)}, bf16[128,128]{1,0:T(8,128)(2,1)S(1)}) custom-call(f32[2,28]{1,0:T(2,128)S(1)} %bitcast.23, f32[2,28]{1,0:T(2,128)S(1)} %bitcast.24, f32[2,28]{1,0:T(2,128)S(1)} %bitcast.25, s32[8,128]{1,0:T(8,128)S(1)} %bitcast.21, f32[8,128]{1,0:T(8,128)S(1)} %bitcast.22, ...), custom_call_target="tpu_custom_call" | custom-call | tf_op jit(solution)/shard_map/prepare/pallas_call | solution.py:368
  10.3 0.3 %collective-permute-done.2.swapped_ref = bf16[8,896]{1,0:T(8,128)(2,1)S(1)} collective-permute-done((bf16[8,896]{1,0:T(8,128)(2,1)S(1)}, bf16[8,896]{1,0:T(8,128)(2,1)S(1)}, u32[]{:S(2)}, u32[]{:S(2)}) %collective-permute-start.2) | collective-permute-done | bytes 14368 | tf_op jit(solution)/shard_map/ppermute | solution.py:112
  10.6 0.1 collective-permute-done.3.three_ref
  10.7 2.7 %collective-permute-done.4.two_ref = bf16[8,1920]{1,0:T(8,128)(2,1)S(1)} collective-permute-done((bf16[8,1920]{1,0:T(8,128)(2,1)S(1)}, bf16[8,1920]{1,0:T(8,128)(2,1)S(1)}, u32[]{:S(2)}, u32[]{:S(2)}) %collective-permute-start.4) | collective-permute-done | bytes 30752 | tf_op jit(solution)/shard_map/ppermute | solution.py:117
  13.4 0.0 collective-permute-done.5.one_ref
  13.4 0.1 collective-permute-start.6
  13.5 0.0 copy-done
  13.5 0.0 copy-done.1
  13.5 0.0 copy-done.2
  13.5 0.5 %near.1 = (f32[64,256]{1,0:T(8,128)S(1)}, f32[64,256]{1,0:T(8,128)S(1)}) custom-call(bf16[32,1792]{1,0:T(8,128)(2,1)S(1)} %get-tuple-element.43.x_ref, bf16[3584,256]{1,0:T(8,128)(2,1)S(1)} %bitcast.16, bf16[3584,256]{1,0:T(8,128)(2,1)S(1)} %bitcast.18, f32[2,3584]{1,0:T(2,128)S(1)} %get-tuple-element.42._.gate_scale_ref, ...), custom_call_target="tpu_custom_call" | custom-call | tf_op jit(solution)/shard_map/near/pallas_call | solution.py:368
  14.0 0.8 %collective-permute-done.6.x_ref = bf16[32,1792]{1,0:T(8,128)(2,1)S(1)} collective-permute-done((bf16[32,1792]{1,0:T(8,128)(2,1)S(1)}, bf16[32,1792]{1,0:T(8,128)(2,1)S(1)}, u32[]{:S(2)}, u32[]{:S(2)}) %collective-permute-start.6) | collective-permute-done | bytes 114720 | tf_op jit(solution)/shard_map/ppermute | solution.py:112
  14.8 0.7 %hidden.1 = (bf16[32,2048]{1,0:T(8,128)(2,1)S(1)}, bf16[32,256]{1,0:T(8,128)(2,1)S(1)}) custom-call(bf16[32,1792]{1,0:T(8,128)(2,1)S(1)} %collective-permute-done.6.x_ref, f32[64,256]{1,0:T(8,128)S(1)} %get-tuple-element.45.near_gate_ref, f32[64,256]{1,0:T(8,128)S(1)} %get-tuple-element.46.near_up_ref, bf16[3584,256]{1,0:T(8,128)(2,1)S(1)} %bitcast.17, ...), custom_call_target="tpu_custom_call" | custom-call | tf_op jit(solution)/shard_map/hidden/pallas_call | solution.py:368
  15.5 0.2 collective-permute-start.7
  15.7 0.3 keep.1
  16.0 0.8 %collective-permute-start.8 = (bf16[8,2816]{1,0:T(8,128)(2,1)S(1)}, bf16[8,2816]{1,0:T(8,128)(2,1)S(1)}, u32[]{:S(2)}, u32[]{:S(2)}) collective-permute-start(bf16[8,2816]{1,0:T(8,128)(2,1)S(1)} %get-tuple-element.52), channel_id=1, source_target_pairs={{0,2},{1,3},{2,0},{3,1},{4,6},{5,7},{6,4},{7,5},{8,10},{9,11},{10,... | collective-permute-start | bytes 135176 | tf_op jit(solution)/shard_map/ppermute | solution.py:121
  16.8 0.2 collective-permute-done.7.sent_ref
  17.0 1.8 %collective-permute-start.9 = (bf16[8,1792]{1,0:T(8,128)(2,1)S(1)}, bf16[8,1792]{1,0:T(8,128)(2,1)S(1)}, u32[]{:S(2)}, u32[]{:S(2)}) collective-permute-start(bf16[8,1792]{1,0:T(8,128)(2,1)S(1)} %get-tuple-element.53), channel_id=1, source_target_pairs={{0,12},{1,15},{2,14},{3,13},{4,8},{5,11},{6,10},{7,9},{8,4},{9,7},... | collective-permute-start | bytes 86024 | tf_op jit(solution)/shard_map/ppermute | solution.py:117
  18.7 0.4 %collective-permute-start.10 = (bf16[8,1792]{1,0:T(8,128)(2,1)S(1)}, bf16[8,1792]{1,0:T(8,128)(2,1)S(1)}, u32[]{:S(2)}, u32[]{:S(2)}) collective-permute-start(bf16[8,1792]{1,0:T(8,128)(2,1)S(1)} %get-tuple-element.54), channel_id=1, source_target_pairs={{0,8},{1,11},{2,10},{3,9},{4,12},{5,15},{6,14},{7,13},{8,0},{9,3},... | collective-permute-start | bytes 86024 | tf_op jit(solution)/shard_map/ppermute | solution.py:117
  19.1 2.3 %collective-permute-start.11 = (bf16[8,1792]{1,0:T(8,128)(2,1)S(1)}, bf16[8,1792]{1,0:T(8,128)(2,1)S(1)}, u32[]{:S(2)}, u32[]{:S(2)}) collective-permute-start(bf16[8,1792]{1,0:T(8,128)(2,1)S(1)} %get-tuple-element.55), channel_id=1, source_target_pairs={{0,4},{1,7},{2,6},{3,5},{4,0},{5,3},{6,2},{7,1},{8,12},{9,15},{10,... | collective-permute-start | bytes 86024 | tf_op jit(solution)/shard_map/ppermute | solution.py:117
  21.4 0.0 collective-permute-done.8.crossed_ref
  21.4 1.3 %hessian.1 = (f32[256,1024]{1,0:T(8,128)}, bf16[32,256]{1,0:T(8,128)(2,1)S(1)}, bf16[256,32]{1,0:T(8,128)(2,1)S(1)}) custom-call(bf16[32,128]{1,0:T(8,128)(2,1)S(1)} %get-tuple-element.56.count_ref, bf16[32,256]{1,0:T(8,128)(2,1)S(1)} %get-tuple-element.48.hidden_ref.own_ref, bf16[32,2048]{1,0:T(8,128)(2,1)S(1)} %collective-permute-done.7.sent_ref, ...), custom_call_target="tpu_custom_call" | custom-call | tf_op jit(solution)/shard_map/hessian/pallas_call | solution.py:368
  22.7 0.0 collective-permute-done.9.three_ref
  22.7 1.4 %collective-permute-done.10.two_ref = bf16[8,1792]{1,0:T(8,128)(2,1)S(1)} collective-permute-done((bf16[8,1792]{1,0:T(8,128)(2,1)S(1)}, bf16[8,1792]{1,0:T(8,128)(2,1)S(1)}, u32[]{:S(2)}, u32[]{:S(2)}) %collective-permute-start.10) | collective-permute-done | bytes 28704 | tf_op jit(solution)/shard_map/ppermute | solution.py:117
  24.1 0.0 collective-permute-done.11.one_ref
  24.2 0.2 collective-permute-start.12
  24.3 1.2 %collective-permute-done.12.far_ref = bf16[32,1152]{1,0:T(8,128)(2,1)S(1)} collective-permute-done((bf16[32,1152]{1,0:T(8,128)(2,1)S(1)}, bf16[32,1152]{1,0:T(8,128)(2,1)S(1)}, u32[]{:S(2)}, u32[]{:S(2)}) %collective-permute-start.12) | collective-permute-done | bytes 73760 | tf_op jit(solution)/shard_map/ppermute | solution.py:112
  25.5 1.0 %combine.1 = (bf16[128,896]{1,0:T(8,128)(2,1)}, f32[256,1024]{1,0:T(8,128)}) custom-call(bf16[128,128]{1,0:T(8,128)(2,1)S(1)} %get-tuple-element.34.coef_ref, bf16[32,896]{1,0:T(8,128)(2,1)S(1)} %get-tuple-element.58.near_ref, bf16[32,1152]{1,0:T(8,128)(2,1)S(1)} %collective-permute-done.12.far_ref, ...), custom_call_target="tpu_custom_call", output_to_operand_aliasing={{1}: (5, {})} | custom-call | tf_op jit(solution)/shard_map/combine/pallas_call | solution.py:457
  (10 shorter events, 0.1 us)
Async XLA Ops:
  0.6 1.0 %copy-start.8 = (bf16[128,896]{1,0:T(8,128)(2,1)S(1)}, bf16[128,896]{1,0:T(8,128)(2,1)}, u32[]{:S(2)}) copy-start(bf16[128,896]{1,0:T(8,128)(2,1)} %tokens_ref.1) | copy-start | bytes 688132
  0.6 0.7 %copy-start.3 = (s32[128,8]{0,1:T(8,128)S(1)}, s32[128,8]{0,1:T(8,128)}, u32[]{:S(2)}) copy-start(s32[128,8]{0,1:T(8,128)} %param.10) | copy-start | bytes 12292
  0.6 4.1 %collective-permute-start = (bf16[128,896]{1,0:T(8,128)(2,1)}, bf16[128,896]{1,0:T(8,128)(2,1)S(1)}, u32[]{:S(2)}, u32[]{:S(2)}) collective-permute-start(bf16[128,896]{1,0:T(8,128)(2,1)} %tokens_ref.1), channel_id=1, source_target_pairs={{0,1},{1,0},{2,3},{3,2},{4,5},{5,4},{6,7},{7,6},{8,9},{9,8},{10,11... | collective-permute-start | bytes 688136 | tf_op jit(solution)/shard_map/ppermute | solution.py:112
  1.6 8.0 %copy-start.4 = (f32[128,8]{0,1:T(8,128)S(1)}, f32[128,8]{0,1:T(8,128)}, u32[]{:S(2)}) copy-start(f32[128,8]{0,1:T(8,128)} %param.11) | copy-start | bytes 12292
  1.6 8.0 %copy-start.5 = (f32[1,28,2]{1,2,0:T(2,128)S(1)}, f32[1,28,2]{1,2,0:T(2,128)}, u32[]{:S(2)}) copy-start(f32[1,28,2]{1,2,0:T(2,128)} %param.13) | copy-start | bytes 676
  1.6 8.0 %copy-start.6 = (f32[1,28,2]{1,2,0:T(2,128)S(1)}, f32[1,28,2]{1,2,0:T(2,128)}, u32[]{:S(2)}) copy-start(f32[1,28,2]{1,2,0:T(2,128)} %param.15) | copy-start | bytes 676
  1.6 8.0 %copy-start.7 = (f32[1,2,28]{2,1,0:T(2,128)S(1)}, f32[1,2,28]{2,1,0:T(2,128)}, u32[]{:S(2)}) copy-start(f32[1,2,28]{2,1,0:T(2,128)} %param.17) | copy-start | bytes 676
  1.6 11.9 %copy-start = (bf16[1,256,3584]{2,1,0:T(8,128)(2,1)S(1)}, bf16[1,256,3584]{2,1,0:T(8,128)(2,1)}, u32[]{:S(2)}) copy-start(bf16[1,256,3584]{2,1,0:T(8,128)(2,1)} %param.16) | copy-start | bytes 5505028
  1.6 11.9 %copy-start.1 = (bf16[1,3584,256]{2,1,0:T(8,128)(2,1)S(1)}, bf16[1,3584,256]{2,1,0:T(8,128)(2,1)}, u32[]{:S(2)}) copy-start(bf16[1,3584,256]{2,1,0:T(8,128)(2,1)} %param.12) | copy-start | bytes 5505028
  1.6 11.9 %copy-start.2 = (bf16[1,3584,256]{2,1,0:T(8,128)(2,1)S(1)}, bf16[1,3584,256]{2,1,0:T(8,128)(2,1)}, u32[]{:S(2)}) copy-start(bf16[1,3584,256]{2,1,0:T(8,128)(2,1)} %param.14) | copy-start | bytes 5505028
  1.8 7.6 %collective-permute-start.1 = (bf16[8,2048]{1,0:T(8,128)(2,1)S(1)}, bf16[8,2048]{1,0:T(8,128)(2,1)S(1)}, u32[]{:S(2)}, u32[]{:S(2)}) collective-permute-start(bf16[8,2048]{1,0:T(8,128)(2,1)S(1)} %get-tuple-element.38), channel_id=1, source_target_pairs={{0,2},{1,3},{2,0},{3,1},{4,6},{5,7},{6,4},{7,5},{8,10},{9,11},{10,... | collective-permute-start | bytes 98312 | tf_op jit(solution)/shard_map/ppermute | solution.py:121
  4.9 5.8 %collective-permute-start.3 = (bf16[8,1920]{1,0:T(8,128)(2,1)S(1)}, bf16[8,1920]{1,0:T(8,128)(2,1)S(1)}, u32[]{:S(2)}, u32[]{:S(2)}) collective-permute-start(bf16[8,1920]{1,0:T(8,128)(2,1)S(1)} %get-tuple-element.39), channel_id=1, source_target_pairs={{0,12},{1,15},{2,14},{3,13},{4,8},{5,11},{6,10},{7,9},{8,4},{9,7},... | collective-permute-start | bytes 92168 | tf_op jit(solution)/shard_map/ppermute | solution.py:117
  8.6 4.8 %collective-permute-start.4 = (bf16[8,1920]{1,0:T(8,128)(2,1)S(1)}, bf16[8,1920]{1,0:T(8,128)(2,1)S(1)}, u32[]{:S(2)}, u32[]{:S(2)}) collective-permute-start(bf16[8,1920]{1,0:T(8,128)(2,1)S(1)} %get-tuple-element.40), channel_id=1, source_target_pairs={{0,8},{1,11},{2,10},{3,9},{4,12},{5,15},{6,14},{7,13},{8,0},{9,3},... | collective-permute-start | bytes 92168 | tf_op jit(solution)/shard_map/ppermute | solution.py:117
  8.6 4.8 %collective-permute-start.5 = (bf16[8,1920]{1,0:T(8,128)(2,1)S(1)}, bf16[8,1920]{1,0:T(8,128)(2,1)S(1)}, u32[]{:S(2)}, u32[]{:S(2)}) collective-permute-start(bf16[8,1920]{1,0:T(8,128)(2,1)S(1)} %get-tuple-element.41), channel_id=1, source_target_pairs={{0,4},{1,7},{2,6},{3,5},{4,0},{5,3},{6,2},{7,1},{8,12},{9,15},{10,... | collective-permute-start | bytes 92168 | tf_op jit(solution)/shard_map/ppermute | solution.py:117
  9.4 1.2 %collective-permute-start.2 = (bf16[8,896]{1,0:T(8,128)(2,1)S(1)}, bf16[8,896]{1,0:T(8,128)(2,1)S(1)}, u32[]{:S(2)}, u32[]{:S(2)}) collective-permute-start(bf16[8,896]{1,0:T(8,128)(2,1)S(1)} %slice.4), channel_id=1, source_target_pairs={{0,1},{1,0},{2,3},{3,2},{4,5},{5,4},{6,7},{7,6},{8,9},{9,8},{10,11... | collective-permute-start | bytes 43016 | tf_op jit(solution)/shard_map/ppermute | solution.py:112
  13.4 1.4 %collective-permute-start.6 = (bf16[32,1792]{1,0:T(8,128)(2,1)S(1)}, bf16[32,1792]{1,0:T(8,128)(2,1)S(1)}, u32[]{:S(2)}, u32[]{:S(2)}) collective-permute-start(bf16[32,1792]{1,0:T(8,128)(2,1)S(1)} %get-tuple-element.43.x_ref), channel_id=1, source_target_pairs={{0,1},{1,0},{2,3},{3,2},{4,5},{5,4},{6,7},{7,6},{8,9},{9,8},{10,11... | collective-permute-start | bytes 344072 | tf_op jit(solution)/shard_map/ppermute | solution.py:112
  15.5 1.4 %collective-permute-start.7 = (bf16[32,2048]{1,0:T(8,128)(2,1)S(1)}, bf16[32,2048]{1,0:T(8,128)(2,1)S(1)}, u32[]{:S(2)}, u32[]{:S(2)}) collective-permute-start(bf16[32,2048]{1,0:T(8,128)(2,1)S(1)} %get-tuple-element.49.send_ref), channel_id=1, source_target_pairs={{0,1},{1,0},{2,3},{3,2},{4,5},{5,4},{6,7},{7,6},{8,9},{9,8},{10,11... | collective-permute-start | bytes 393224 | tf_op jit(solution)/shard_map/ppermute | solution.py:112
  16.0 5.4 %collective-permute-start.8 = (bf16[8,2816]{1,0:T(8,128)(2,1)S(1)}, bf16[8,2816]{1,0:T(8,128)(2,1)S(1)}, u32[]{:S(2)}, u32[]{:S(2)}) collective-permute-start(bf16[8,2816]{1,0:T(8,128)(2,1)S(1)} %get-tuple-element.52), channel_id=1, source_target_pairs={{0,2},{1,3},{2,0},{3,1},{4,6},{5,7},{6,4},{7,5},{8,10},{9,11},{10,... | collective-permute-start | bytes 135176 | tf_op jit(solution)/shard_map/ppermute | solution.py:121
  17.0 5.8 %collective-permute-start.9 = (bf16[8,1792]{1,0:T(8,128)(2,1)S(1)}, bf16[8,1792]{1,0:T(8,128)(2,1)S(1)}, u32[]{:S(2)}, u32[]{:S(2)}) collective-permute-start(bf16[8,1792]{1,0:T(8,128)(2,1)S(1)} %get-tuple-element.53), channel_id=1, source_target_pairs={{0,12},{1,15},{2,14},{3,13},{4,8},{5,11},{6,10},{7,9},{8,4},{9,7},... | collective-permute-start | bytes 86024 | tf_op jit(solution)/shard_map/ppermute | solution.py:117
  18.7 5.4 %collective-permute-start.10 = (bf16[8,1792]{1,0:T(8,128)(2,1)S(1)}, bf16[8,1792]{1,0:T(8,128)(2,1)S(1)}, u32[]{:S(2)}, u32[]{:S(2)}) collective-permute-start(bf16[8,1792]{1,0:T(8,128)(2,1)S(1)} %get-tuple-element.54), channel_id=1, source_target_pairs={{0,8},{1,11},{2,10},{3,9},{4,12},{5,15},{6,14},{7,13},{8,0},{9,3},... | collective-permute-start | bytes 86024 | tf_op jit(solution)/shard_map/ppermute | solution.py:117
  19.1 5.0 %collective-permute-start.11 = (bf16[8,1792]{1,0:T(8,128)(2,1)S(1)}, bf16[8,1792]{1,0:T(8,128)(2,1)S(1)}, u32[]{:S(2)}, u32[]{:S(2)}) collective-permute-start(bf16[8,1792]{1,0:T(8,128)(2,1)S(1)} %get-tuple-element.55), channel_id=1, source_target_pairs={{0,4},{1,7},{2,6},{3,5},{4,0},{5,3},{6,2},{7,1},{8,12},{9,15},{10,... | collective-permute-start | bytes 86024 | tf_op jit(solution)/shard_map/ppermute | solution.py:117
  24.2 1.3 %collective-permute-start.12 = (bf16[32,1152]{1,0:T(8,128)(2,1)S(1)}, bf16[32,1152]{1,0:T(8,128)(2,1)S(1)}, u32[]{:S(2)}, u32[]{:S(2)}) collective-permute-start(bf16[32,1152]{1,0:T(8,128)(2,1)S(1)} %get-tuple-element.59), channel_id=1, source_target_pairs={{0,1},{1,0},{2,3},{3,2},{4,5},{5,4},{6,7},{7,6},{8,9},{9,8},{10,11... | collective-permute-start | bytes 221192 | tf_op jit(solution)/shard_map/ppermute | solution.py:112

commit v8 on v7

--- a/solution.py
+++ b/solution.py
@@ -213,10 +213,15 @@
 
 
 def project(x, share, weight_ref, scale_ref):
-    width = x.shape[1]
+    slots, width = x.shape
     depth = pl.ds(pl.multiple_of(share * width, width), width)
-    scaled = jnp.concatenate([(x * scale_ref[i : i + 1, depth]).astype(BF16) for i in range(2)], axis=0)
-    return jnp.dot(scaled, weight_ref[depth, :], preferred_element_type=F32)
+    terms = []
+    for i in range(2):
+        scaled = x * scale_ref[i : i + 1, depth]
+        terms.append(scaled.astype(BF16))
+        terms.append((scaled - terms[-1].astype(F32)).astype(BF16))
+    out = jnp.dot(jnp.concatenate(terms, axis=0), weight_ref[depth, :], preferred_element_type=F32)
+    return jnp.concatenate([out[:slots] + out[slots : 2 * slots], out[2 * slots : 3 * slots] + out[3 * slots :]], axis=0)
 
 
 def near_kernel(x_ref, gate_ref, up_ref, gate_scale_ref, up_scale_ref, _, gate_out_ref, up_out_ref):

time: 26.7 us -> 26.7 us (level)
  no operation moved by 1% of the time
where the time goes in v8:
time: 26.7 us; the launch traced here: 26.5 us
  starting transfers between devices  13.8 us (52%)
  waiting for transfers between devices  6.66 us (25%)
  Pallas kernels  4.93 us (18%)
  between operations  0.77 us (3%)
  local copies, waits for them, and re-layouts  0.31 us (1%)
    ppermute x6, starting transfers between devices, to_chips(): return lax.ppermute(value, BOTH, pairs)  8.9 us
    ppermute x6, waiting for transfers between devices, to_chips(): return lax.ppermute(value, BOTH, pairs)  4.23 us
    pallas_call x12, Pallas kernels, call(): pl.pallas_call(kernel, out_shape=outs, in_specs=[SMEM] * scalars + [VMEM]...  3.94 us
    ppermute x2, starting transfers between devices, across(): lax.ppermute(value, BOTH, [(4 * z + m, 4 * z + (m ^ 2)) for z in range(4)...  3.76 us
    ppermute x5, waiting for transfers between devices, swap_cores(): return lax.ppermute(value, 'mp', [(m, m ^ 1) for m in range(4)])  2.42 us
    ppermute x5, starting transfers between devices, swap_cores(): return lax.ppermute(value, 'mp', [(m, m ^ 1) for m in range(4)])  1.18 us
    pallas_call x1, Pallas kernels, on_device(): pl.pallas_call(combine_kernel, out_shape=(shape((rows, width), BF16), sha...  0.99 us
  transfers between devices with their start and end apart: 13, of which 7 were waited for; matrix products, arithmetic and copies ran while one was open for 0% of the time, Pallas kernels for 12%

profile of v8, /device:TPU:0, one launch (start us, length us, event | category | flops | bytes accessed | tf_op | source)
XLA Modules:
  0.0 26.5 jit_solution(17164512425743752715)
XLA Ops:
  0.6 0.0 copy-start.8
  0.6 0.0 copy-start.3
  0.6 0.5 %collective-permute-start = (bf16[128,896]{1,0:T(8,128)(2,1)}, bf16[128,896]{1,0:T(8,128)(2,1)S(1)}, u32[]{:S(2)}, u32[]{:S(2)}) collective-permute-start(bf16[128,896]{1,0:T(8,128)(2,1)} %tokens_ref.1), channel_id=1, source_target_pairs={{0,1},{1,0},{2,3},{3,2},{4,5},{5,4},{6,7},{7,6},{8,9},{9,8},{10,11... | collective-permute-start | bytes 688136 | tf_op jit(solution)/shard_map/ppermute | solution.py:112
  1.2 0.2 copy-done.3
  1.4 0.1 route.1
  1.5 0.1 copy-done.8
  1.6 0.0 copy-start
  1.6 0.0 copy-start.1
  1.6 0.0 copy-start.2
  1.6 0.1 own.1
  1.8 3.0 %collective-permute-start.1 = (bf16[8,2048]{1,0:T(8,128)(2,1)S(1)}, bf16[8,2048]{1,0:T(8,128)(2,1)S(1)}, u32[]{:S(2)}, u32[]{:S(2)}) collective-permute-start(bf16[8,2048]{1,0:T(8,128)(2,1)S(1)} %get-tuple-element.38), channel_id=1, source_target_pairs={{0,2},{1,3},{2,0},{3,1},{4,6},{5,7},{6,4},{7,5},{8,10},{9,11},{10,... | collective-permute-start | bytes 98312 | tf_op jit(solution)/shard_map/ppermute | solution.py:121
  4.8 0.0 collective-permute-done.tokens_ref
  4.8 0.1 line_up.1
  4.9 3.7 %collective-permute-start.3 = (bf16[8,1920]{1,0:T(8,128)(2,1)S(1)}, bf16[8,1920]{1,0:T(8,128)(2,1)S(1)}, u32[]{:S(2)}, u32[]{:S(2)}) collective-permute-start(bf16[8,1920]{1,0:T(8,128)(2,1)S(1)} %get-tuple-element.39), channel_id=1, source_target_pairs={{0,12},{1,15},{2,14},{3,13},{4,8},{5,11},{6,10},{7,9},{8,4},{9,7},... | collective-permute-start | bytes 92168 | tf_op jit(solution)/shard_map/ppermute | solution.py:117
  8.6 0.0 collective-permute-start.4
  8.6 0.8 %collective-permute-start.5 = (bf16[8,1920]{1,0:T(8,128)(2,1)S(1)}, bf16[8,1920]{1,0:T(8,128)(2,1)S(1)}, u32[]{:S(2)}, u32[]{:S(2)}) collective-permute-start(bf16[8,1920]{1,0:T(8,128)(2,1)S(1)} %get-tuple-element.41), channel_id=1, source_target_pairs={{0,4},{1,7},{2,6},{3,5},{4,0},{5,3},{6,2},{7,1},{8,12},{9,15},{10,... | collective-permute-start | bytes 92168 | tf_op jit(solution)/shard_map/ppermute | solution.py:117
  9.4 0.0 collective-permute-done.1.crossed_ref
  9.4 0.2 collective-permute-start.2
  9.6 0.0 copy-done.4
  9.6 0.0 copy-done.5
  9.6 0.0 copy-done.6
  9.6 0.0 copy-done.7
  9.6 0.7 %prepare.1 = (f32[2,3584]{1,0:T(2,128)S(1)}, f32[2,3584]{1,0:T(2,128)S(1)}, f32[2,3584]{1,0:T(2,128)S(1)}, bf16[128,128]{1,0:T(8,128)(2,1)S(1)}) custom-call(f32[2,28]{1,0:T(2,128)S(1)} %bitcast.23, f32[2,28]{1,0:T(2,128)S(1)} %bitcast.24, f32[2,28]{1,0:T(2,128)S(1)} %bitcast.25, s32[8,128]{1,0:T(8,128)S(1)} %bitcast.21, f32[8,128]{1,0:T(8,128)S(1)} %bitcast.22, ...), custom_call_target="tpu_custom_call" | custom-call | tf_op jit(solution)/shard_map/prepare/pallas_call | solution.py:373
  10.3 0.3 %collective-permute-done.2.swapped_ref = bf16[8,896]{1,0:T(8,128)(2,1)S(1)} collective-permute-done((bf16[8,896]{1,0:T(8,128)(2,1)S(1)}, bf16[8,896]{1,0:T(8,128)(2,1)S(1)}, u32[]{:S(2)}, u32[]{:S(2)}) %collective-permute-start.2) | collective-permute-done | bytes 14368 | tf_op jit(solution)/shard_map/ppermute | solution.py:112
  10.6 0.1 collective-permute-done.3.three_ref
  10.7 2.7 %collective-permute-done.4.two_ref = bf16[8,1920]{1,0:T(8,128)(2,1)S(1)} collective-permute-done((bf16[8,1920]{1,0:T(8,128)(2,1)S(1)}, bf16[8,1920]{1,0:T(8,128)(2,1)S(1)}, u32[]{:S(2)}, u32[]{:S(2)}) %collective-permute-start.4) | collective-permute-done | bytes 30752 | tf_op jit(solution)/shard_map/ppermute | solution.py:117
  13.4 0.0 collective-permute-done.5.one_ref
  13.4 0.1 collective-permute-start.6
  13.5 0.0 copy-done
  13.5 0.0 copy-done.1
  13.5 0.5 %near.1 = (f32[64,256]{1,0:T(8,128)S(1)}, f32[64,256]{1,0:T(8,128)S(1)}) custom-call(bf16[32,1792]{1,0:T(8,128)(2,1)S(1)} %get-tuple-element.43.x_ref, bf16[3584,256]{1,0:T(8,128)(2,1)S(1)} %bitcast.16, bf16[3584,256]{1,0:T(8,128)(2,1)S(1)} %bitcast.18, f32[2,3584]{1,0:T(2,128)S(1)} %get-tuple-element.42._.gate_scale_ref, ...), custom_call_target="tpu_custom_call" | custom-call | tf_op jit(solution)/shard_map/near/pallas_call | solution.py:373
  14.0 0.8 %collective-permute-done.6.x_ref = bf16[32,1792]{1,0:T(8,128)(2,1)S(1)} collective-permute-done((bf16[32,1792]{1,0:T(8,128)(2,1)S(1)}, bf16[32,1792]{1,0:T(8,128)(2,1)S(1)}, u32[]{:S(2)}, u32[]{:S(2)}) %collective-permute-start.6) | collective-permute-done | bytes 114720 | tf_op jit(solution)/shard_map/ppermute | solution.py:112
  14.8 0.7 %hidden.1 = (bf16[32,2048]{1,0:T(8,128)(2,1)S(1)}, bf16[32,256]{1,0:T(8,128)(2,1)S(1)}) custom-call(bf16[32,1792]{1,0:T(8,128)(2,1)S(1)} %collective-permute-done.6.x_ref, f32[64,256]{1,0:T(8,128)S(1)} %get-tuple-element.45.near_gate_ref, f32[64,256]{1,0:T(8,128)S(1)} %get-tuple-element.46.near_up_ref, bf16[3584,256]{1,0:T(8,128)(2,1)S(1)} %bitcast.17, ...), custom_call_target="tpu_custom_call" | custom-call | tf_op jit(solution)/shard_map/hidden/pallas_call | solution.py:373
  15.5 0.2 collective-permute-start.7
  15.8 0.3 keep.1
  16.0 0.8 %collective-permute-start.8 = (bf16[8,2816]{1,0:T(8,128)(2,1)S(1)}, bf16[8,2816]{1,0:T(8,128)(2,1)S(1)}, u32[]{:S(2)}, u32[]{:S(2)}) collective-permute-start(bf16[8,2816]{1,0:T(8,128)(2,1)S(1)} %get-tuple-element.52), channel_id=1, source_target_pairs={{0,2},{1,3},{2,0},{3,1},{4,6},{5,7},{6,4},{7,5},{8,10},{9,11},{10,... | collective-permute-start | bytes 135176 | tf_op jit(solution)/shard_map/ppermute | solution.py:121
  16.8 0.2 collective-permute-done.7.sent_ref
  17.0 1.8 %collective-permute-start.9 = (bf16[8,1792]{1,0:T(8,128)(2,1)S(1)}, bf16[8,1792]{1,0:T(8,128)(2,1)S(1)}, u32[]{:S(2)}, u32[]{:S(2)}) collective-permute-start(bf16[8,1792]{1,0:T(8,128)(2,1)S(1)} %get-tuple-element.53), channel_id=1, source_target_pairs={{0,12},{1,15},{2,14},{3,13},{4,8},{5,11},{6,10},{7,9},{8,4},{9,7},... | collective-permute-start | bytes 86024 | tf_op jit(solution)/shard_map/ppermute | solution.py:117
  18.8 0.4 %collective-permute-start.10 = (bf16[8,1792]{1,0:T(8,128)(2,1)S(1)}, bf16[8,1792]{1,0:T(8,128)(2,1)S(1)}, u32[]{:S(2)}, u32[]{:S(2)}) collective-permute-start(bf16[8,1792]{1,0:T(8,128)(2,1)S(1)} %get-tuple-element.54), channel_id=1, source_target_pairs={{0,8},{1,11},{2,10},{3,9},{4,12},{5,15},{6,14},{7,13},{8,0},{9,3},... | collective-permute-start | bytes 86024 | tf_op jit(solution)/shard_map/ppermute | solution.py:117
  19.2 2.3 %collective-permute-start.11 = (bf16[8,1792]{1,0:T(8,128)(2,1)S(1)}, bf16[8,1792]{1,0:T(8,128)(2,1)S(1)}, u32[]{:S(2)}, u32[]{:S(2)}) collective-permute-start(bf16[8,1792]{1,0:T(8,128)(2,1)S(1)} %get-tuple-element.55), channel_id=1, source_target_pairs={{0,4},{1,7},{2,6},{3,5},{4,0},{5,3},{6,2},{7,1},{8,12},{9,15},{10,... | collective-permute-start | bytes 86024 | tf_op jit(solution)/shard_map/ppermute | solution.py:117
  21.4 0.0 collective-permute-done.8.crossed_ref
  21.4 1.3 %hessian.1 = (f32[256,1024]{1,0:T(8,128)}, bf16[32,256]{1,0:T(8,128)(2,1)S(1)}, bf16[256,32]{1,0:T(8,128)(2,1)S(1)}) custom-call(bf16[32,128]{1,0:T(8,128)(2,1)S(1)} %get-tuple-element.56.count_ref, bf16[32,256]{1,0:T(8,128)(2,1)S(1)} %get-tuple-element.48.hidden_ref.own_ref, bf16[32,2048]{1,0:T(8,128)(2,1)S(1)} %collective-permute-done.7.sent_ref, ...), custom_call_target="tpu_custom_call" | custom-call | tf_op jit(solution)/shard_map/hessian/pallas_call | solution.py:373
  22.7 0.0 collective-permute-done.9.three_ref
  22.8 1.4 %collective-permute-done.10.two_ref = bf16[8,1792]{1,0:T(8,128)(2,1)S(1)} collective-permute-done((bf16[8,1792]{1,0:T(8,128)(2,1)S(1)}, bf16[8,1792]{1,0:T(8,128)(2,1)S(1)}, u32[]{:S(2)}, u32[]{:S(2)}) %collective-permute-start.10) | collective-permute-done | bytes 28704 | tf_op jit(solution)/shard_map/ppermute | solution.py:117
  24.2 0.0 collective-permute-done.11.one_ref
  24.2 0.2 collective-permute-start.12
  24.4 1.2 %collective-permute-done.12.far_ref = bf16[32,1152]{1,0:T(8,128)(2,1)S(1)} collective-permute-done((bf16[32,1152]{1,0:T(8,128)(2,1)S(1)}, bf16[32,1152]{1,0:T(8,128)(2,1)S(1)}, u32[]{:S(2)}, u32[]{:S(2)}) %collective-permute-start.12) | collective-permute-done | bytes 73760 | tf_op jit(solution)/shard_map/ppermute | solution.py:112
  25.5 1.0 %combine.1 = (bf16[128,896]{1,0:T(8,128)(2,1)}, f32[256,1024]{1,0:T(8,128)}) custom-call(bf16[128,128]{1,0:T(8,128)(2,1)S(1)} %get-tuple-element.34.coef_ref, bf16[32,896]{1,0:T(8,128)(2,1)S(1)} %get-tuple-element.58.near_ref, bf16[32,1152]{1,0:T(8,128)(2,1)S(1)} %collective-permute-done.12.far_ref, ...), custom_call_target="tpu_custom_call", output_to_operand_aliasing={{1}: (5, {})} | custom-call | tf_op jit(solution)/shard_map/combine/pallas_call | solution.py:462
  (10 shorter events, 0.1 us)
Async XLA Ops:
  0.6 1.0 %copy-start.8 = (bf16[128,896]{1,0:T(8,128)(2,1)S(1)}, bf16[128,896]{1,0:T(8,128)(2,1)}, u32[]{:S(2)}) copy-start(bf16[128,896]{1,0:T(8,128)(2,1)} %tokens_ref.1) | copy-start | bytes 688132
  0.6 0.7 %copy-start.3 = (s32[128,8]{0,1:T(8,128)S(1)}, s32[128,8]{0,1:T(8,128)}, u32[]{:S(2)}) copy-start(s32[128,8]{0,1:T(8,128)} %param.10) | copy-start | bytes 12292
  0.6 4.1 %collective-permute-start = (bf16[128,896]{1,0:T(8,128)(2,1)}, bf16[128,896]{1,0:T(8,128)(2,1)S(1)}, u32[]{:S(2)}, u32[]{:S(2)}) collective-permute-start(bf16[128,896]{1,0:T(8,128)(2,1)} %tokens_ref.1), channel_id=1, source_target_pairs={{0,1},{1,0},{2,3},{3,2},{4,5},{5,4},{6,7},{7,6},{8,9},{9,8},{10,11... | collective-permute-start | bytes 688136 | tf_op jit(solution)/shard_map/ppermute | solution.py:112
  1.6 8.0 %copy-start.4 = (f32[128,8]{0,1:T(8,128)S(1)}, f32[128,8]{0,1:T(8,128)}, u32[]{:S(2)}) copy-start(f32[128,8]{0,1:T(8,128)} %param.11) | copy-start | bytes 12292
  1.6 8.0 %copy-start.5 = (f32[1,28,2]{1,2,0:T(2,128)S(1)}, f32[1,28,2]{1,2,0:T(2,128)}, u32[]{:S(2)}) copy-start(f32[1,28,2]{1,2,0:T(2,128)} %param.13) | copy-start | bytes 676
  1.6 8.0 %copy-start.6 = (f32[1,28,2]{1,2,0:T(2,128)S(1)}, f32[1,28,2]{1,2,0:T(2,128)}, u32[]{:S(2)}) copy-start(f32[1,28,2]{1,2,0:T(2,128)} %param.15) | copy-start | bytes 676
  1.6 8.0 %copy-start.7 = (f32[1,2,28]{2,1,0:T(2,128)S(1)}, f32[1,2,28]{2,1,0:T(2,128)}, u32[]{:S(2)}) copy-start(f32[1,2,28]{2,1,0:T(2,128)} %param.17) | copy-start | bytes 676
  1.6 11.9 %copy-start = (bf16[1,256,3584]{2,1,0:T(8,128)(2,1)S(1)}, bf16[1,256,3584]{2,1,0:T(8,128)(2,1)}, u32[]{:S(2)}) copy-start(bf16[1,256,3584]{2,1,0:T(8,128)(2,1)} %param.16) | copy-start | bytes 5505028
  1.6 11.9 %copy-start.1 = (bf16[1,3584,256]{2,1,0:T(8,128)(2,1)S(1)}, bf16[1,3584,256]{2,1,0:T(8,128)(2,1)}, u32[]{:S(2)}) copy-start(bf16[1,3584,256]{2,1,0:T(8,128)(2,1)} %param.12) | copy-start | bytes 5505028
  1.6 11.9 %copy-start.2 = (bf16[1,3584,256]{2,1,0:T(8,128)(2,1)S(1)}, bf16[1,3584,256]{2,1,0:T(8,128)(2,1)}, u32[]{:S(2)}) copy-start(bf16[1,3584,256]{2,1,0:T(8,128)(2,1)} %param.14) | copy-start | bytes 5505028
  1.8 7.6 %collective-permute-start.1 = (bf16[8,2048]{1,0:T(8,128)(2,1)S(1)}, bf16[8,2048]{1,0:T(8,128)(2,1)S(1)}, u32[]{:S(2)}, u32[]{:S(2)}) collective-permute-start(bf16[8,2048]{1,0:T(8,128)(2,1)S(1)} %get-tuple-element.38), channel_id=1, source_target_pairs={{0,2},{1,3},{2,0},{3,1},{4,6},{5,7},{6,4},{7,5},{8,10},{9,11},{10,... | collective-permute-start | bytes 98312 | tf_op jit(solution)/shard_map/ppermute | solution.py:121
  4.9 5.8 %collective-permute-start.3 = (bf16[8,1920]{1,0:T(8,128)(2,1)S(1)}, bf16[8,1920]{1,0:T(8,128)(2,1)S(1)}, u32[]{:S(2)}, u32[]{:S(2)}) collective-permute-start(bf16[8,1920]{1,0:T(8,128)(2,1)S(1)} %get-tuple-element.39), channel_id=1, source_target_pairs={{0,12},{1,15},{2,14},{3,13},{4,8},{5,11},{6,10},{7,9},{8,4},{9,7},... | collective-permute-start | bytes 92168 | tf_op jit(solution)/shard_map/ppermute | solution.py:117
  8.6 4.8 %collective-permute-start.4 = (bf16[8,1920]{1,0:T(8,128)(2,1)S(1)}, bf16[8,1920]{1,0:T(8,128)(2,1)S(1)}, u32[]{:S(2)}, u32[]{:S(2)}) collective-permute-start(bf16[8,1920]{1,0:T(8,128)(2,1)S(1)} %get-tuple-element.40), channel_id=1, source_target_pairs={{0,8},{1,11},{2,10},{3,9},{4,12},{5,15},{6,14},{7,13},{8,0},{9,3},... | collective-permute-start | bytes 92168 | tf_op jit(solution)/shard_map/ppermute | solution.py:117
  8.6 4.8 %collective-permute-start.5 = (bf16[8,1920]{1,0:T(8,128)(2,1)S(1)}, bf16[8,1920]{1,0:T(8,128)(2,1)S(1)}, u32[]{:S(2)}, u32[]{:S(2)}) collective-permute-start(bf16[8,1920]{1,0:T(8,128)(2,1)S(1)} %get-tuple-element.41), channel_id=1, source_target_pairs={{0,4},{1,7},{2,6},{3,5},{4,0},{5,3},{6,2},{7,1},{8,12},{9,15},{10,... | collective-permute-start | bytes 92168 | tf_op jit(solution)/shard_map/ppermute | solution.py:117
  9.4 1.2 %collective-permute-start.2 = (bf16[8,896]{1,0:T(8,128)(2,1)S(1)}, bf16[8,896]{1,0:T(8,128)(2,1)S(1)}, u32[]{:S(2)}, u32[]{:S(2)}) collective-permute-start(bf16[8,896]{1,0:T(8,128)(2,1)S(1)} %slice.4), channel_id=1, source_target_pairs={{0,1},{1,0},{2,3},{3,2},{4,5},{5,4},{6,7},{7,6},{8,9},{9,8},{10,11... | collective-permute-start | bytes 43016 | tf_op jit(solution)/shard_map/ppermute | solution.py:112
  13.4 1.4 %collective-permute-start.6 = (bf16[32,1792]{1,0:T(8,128)(2,1)S(1)}, bf16[32,1792]{1,0:T(8,128)(2,1)S(1)}, u32[]{:S(2)}, u32[]{:S(2)}) collective-permute-start(bf16[32,1792]{1,0:T(8,128)(2,1)S(1)} %get-tuple-element.43.x_ref), channel_id=1, source_target_pairs={{0,1},{1,0},{2,3},{3,2},{4,5},{5,4},{6,7},{7,6},{8,9},{9,8},{10,11... | collective-permute-start | bytes 344072 | tf_op jit(solution)/shard_map/ppermute | solution.py:112
  15.5 1.4 %collective-permute-start.7 = (bf16[32,2048]{1,0:T(8,128)(2,1)S(1)}, bf16[32,2048]{1,0:T(8,128)(2,1)S(1)}, u32[]{:S(2)}, u32[]{:S(2)}) collective-permute-start(bf16[32,2048]{1,0:T(8,128)(2,1)S(1)} %get-tuple-element.49.send_ref), channel_id=1, source_target_pairs={{0,1},{1,0},{2,3},{3,2},{4,5},{5,4},{6,7},{7,6},{8,9},{9,8},{10,11... | collective-permute-start | bytes 393224 | tf_op jit(solution)/shard_map/ppermute | solution.py:112
  16.0 5.4 %collective-permute-start.8 = (bf16[8,2816]{1,0:T(8,128)(2,1)S(1)}, bf16[8,2816]{1,0:T(8,128)(2,1)S(1)}, u32[]{:S(2)}, u32[]{:S(2)}) collective-permute-start(bf16[8,2816]{1,0:T(8,128)(2,1)S(1)} %get-tuple-element.52), channel_id=1, source_target_pairs={{0,2},{1,3},{2,0},{3,1},{4,6},{5,7},{6,4},{7,5},{8,10},{9,11},{10,... | collective-permute-start | bytes 135176 | tf_op jit(solution)/shard_map/ppermute | solution.py:121
  17.0 5.8 %collective-permute-start.9 = (bf16[8,1792]{1,0:T(8,128)(2,1)S(1)}, bf16[8,1792]{1,0:T(8,128)(2,1)S(1)}, u32[]{:S(2)}, u32[]{:S(2)}) collective-permute-start(bf16[8,1792]{1,0:T(8,128)(2,1)S(1)} %get-tuple-element.53), channel_id=1, source_target_pairs={{0,12},{1,15},{2,14},{3,13},{4,8},{5,11},{6,10},{7,9},{8,4},{9,7},... | collective-permute-start | bytes 86024 | tf_op jit(solution)/shard_map/ppermute | solution.py:117
  18.8 5.4 %collective-permute-start.10 = (bf16[8,1792]{1,0:T(8,128)(2,1)S(1)}, bf16[8,1792]{1,0:T(8,128)(2,1)S(1)}, u32[]{:S(2)}, u32[]{:S(2)}) collective-permute-start(bf16[8,1792]{1,0:T(8,128)(2,1)S(1)} %get-tuple-element.54), channel_id=1, source_target_pairs={{0,8},{1,11},{2,10},{3,9},{4,12},{5,15},{6,14},{7,13},{8,0},{9,3},... | collective-permute-start | bytes 86024 | tf_op jit(solution)/shard_map/ppermute | solution.py:117
  19.2 5.0 %collective-permute-start.11 = (bf16[8,1792]{1,0:T(8,128)(2,1)S(1)}, bf16[8,1792]{1,0:T(8,128)(2,1)S(1)}, u32[]{:S(2)}, u32[]{:S(2)}) collective-permute-start(bf16[8,1792]{1,0:T(8,128)(2,1)S(1)} %get-tuple-element.55), channel_id=1, source_target_pairs={{0,4},{1,7},{2,6},{3,5},{4,0},{5,3},{6,2},{7,1},{8,12},{9,15},{10,... | collective-permute-start | bytes 86024 | tf_op jit(solution)/shard_map/ppermute | solution.py:117
  24.2 1.3 %collective-permute-start.12 = (bf16[32,1152]{1,0:T(8,128)(2,1)S(1)}, bf16[32,1152]{1,0:T(8,128)(2,1)S(1)}, u32[]{:S(2)}, u32[]{:S(2)}) collective-permute-start(bf16[32,1152]{1,0:T(8,128)(2,1)S(1)} %get-tuple-element.59), channel_id=1, source_target_pairs={{0,1},{1,0},{2,3},{3,2},{4,5},{5,4},{6,7},{7,6},{8,9},{9,8},{10,11... | collective-permute-start | bytes 221192 | tf_op jit(solution)/shard_map/ppermute | solution.py:112

commit v9 on v8

--- a/solution.py
+++ b/solution.py
@@ -104,6 +104,7 @@
 VMEM = pl.BlockSpec(memory_space=pltpu.VMEM)
 SMEM = pl.BlockSpec(memory_space=pltpu.SMEM)
 ANY = pl.BlockSpec(memory_space=pl.ANY)
+EMPTY = 64.0
 F32 = jnp.float32
 BF16 = jnp.bfloat16
 
@@ -179,12 +180,19 @@
     coef_ref[...] = jnp.concatenate(terms, axis=0).T.astype(BF16)
 
 
-def line_up_kernel(chosen_ref, tokens_ref, own_ref, count_ref, other_ref, *out_refs):
-    rows = other_ref.shape[0]
+def line_up_kernel(chosen_ref, tokens_ref, own_ref, other_ref, *out_refs):
+    rows, width = other_ref.shape
     other = pick(chosen_ref, tokens_ref)
     other_ref[...] = other[:rows]
+    empty = 1.0 - jnp.sum(chosen_ref[...].astype(F32), axis=1, keepdims=True)
+    first = lax.broadcasted_iota(jnp.int32, (rows, QBLK), 1) == 0
     for k, out_ref in enumerate(out_refs, 1):
-        out_ref[...] = jnp.concatenate([own_ref[k], other[k * rows : (k + 1) * rows], count_ref[k]], axis=1)
+        at = slice(k * rows, (k + 1) * rows)
+        own = own_ref[k]
+        mark = jnp.where(first, empty[at] * EMPTY, 0.0)
+        out_ref[:, :QBLK] = (own[:, :QBLK].astype(F32) + mark).astype(BF16)
+        out_ref[:, QBLK:width] = own[:, QBLK:]
+        out_ref[:, width:] = other[at]
 
 
 def on_core(core):
@@ -202,8 +210,13 @@
         out_ref[:rows, lanes] = value.astype(BF16)
     counts_ref[:rows, :] = count_ref[0]
     for k, ref in enumerate((one_ref, two_ref, three_ref), 1):
-        out_ref[k * rows : (k + 1) * rows, :] = ref[:, : 2 * width]
-        counts_ref[k * rows : (k + 1) * rows, :] = ref[:, 2 * width :]
+        at = slice(k * rows, (k + 1) * rows)
+        value = ref[:, :QBLK].astype(F32)
+        empty = value > 0.5 * EMPTY
+        out_ref[at, :QBLK] = jnp.where(empty, 0.0, value).astype(BF16)
+        out_ref[at, QBLK:] = ref[:, QBLK:]
+        kept = rows - jnp.sum(jnp.where(empty[:, :1], 1.0, 0.0), axis=0, keepdims=True)
+        counts_ref[at, :] = jnp.broadcast_to(kept, (rows, QBLK)).astype(BF16)
 
 
 def shares_in_order():
@@ -391,7 +404,7 @@
     picked, cross = call(
         own_kernel,
         "own",
-        (shape((4, capacity, width), BF16), shape((capacity, 2 * width + 2 * QBLK), BF16)),
+        (shape((4, capacity, width), BF16), shape((capacity, 2 * width + QBLK), BF16)),
         (chosen, tokens),
         flops=10**11,
     )
@@ -399,8 +412,8 @@
     other, *messages = call(
         line_up_kernel,
         "line_up",
-        (shape((capacity, width), BF16), *[shape((capacity, 2 * width + QBLK), BF16)] * 3),
-        (chosen, other_tokens, picked, counts),
+        (shape((capacity, width), BF16), *[shape((capacity, 2 * width), BF16)] * 3),
+        (chosen, other_tokens, picked),
     )
     *scales, coef = call(
         prepare_kernel,

time: 26.7 us -> 26.6 us (level)
  no operation moved by 1% of the time
where the time goes in v9:
time: 26.6 us; the launch traced here: 26.4 us
  starting transfers between devices  13.8 us (52%)
  waiting for transfers between devices  6.53 us (25%)
  Pallas kernels  5.01 us (19%)
  between operations  0.76 us (3%)
  local copies, waits for them, and re-layouts  0.31 us (1%)
    ppermute x6, starting transfers between devices, to_chips(): return lax.ppermute(value, BOTH, pairs)  8.9 us
    ppermute x6, waiting for transfers between devices, to_chips(): return lax.ppermute(value, BOTH, pairs)  4.14 us
    pallas_call x12, Pallas kernels, call(): pl.pallas_call(kernel, out_shape=outs, in_specs=[SMEM] * scalars + [VMEM]...  4.02 us
    ppermute x2, starting transfers between devices, across(): lax.ppermute(value, BOTH, [(4 * z + m, 4 * z + (m ^ 2)) for z in range(4)...  3.74 us
    ppermute x5, waiting for transfers between devices, swap_cores(): return lax.ppermute(value, 'mp', [(m, m ^ 1) for m in range(4)])  2.38 us
    ppermute x5, starting transfers between devices, swap_cores(): return lax.ppermute(value, 'mp', [(m, m ^ 1) for m in range(4)])  1.18 us
    pallas_call x1, Pallas kernels, on_device(): pl.pallas_call(combine_kernel, out_shape=(shape((rows, width), BF16), sha...  0.99 us
  transfers between devices with their start and end apart: 13, of which 7 were waited for; matrix products, arithmetic and copies ran while one was open for 0% of the time, Pallas kernels for 12%

profile of v9, /device:TPU:0, one launch (start us, length us, event | category | flops | bytes accessed | tf_op | source)
XLA Modules:
  0.0 26.4 jit_solution(17377698482664793201)
XLA Ops:
  0.6 0.0 copy-start.8
  0.6 0.0 copy-start.3
  0.6 0.5 %collective-permute-start = (bf16[128,896]{1,0:T(8,128)(2,1)}, bf16[128,896]{1,0:T(8,128)(2,1)S(1)}, u32[]{:S(2)}, u32[]{:S(2)}) collective-permute-start(bf16[128,896]{1,0:T(8,128)(2,1)} %tokens_ref.1), channel_id=1, source_target_pairs={{0,1},{1,0},{2,3},{3,2},{4,5},{5,4},{6,7},{7,6},{8,9},{9,8},{10,11... | collective-permute-start | bytes 688136 | tf_op jit(solution)/shard_map/ppermute | solution.py:113
  1.2 0.2 copy-done.3
  1.4 0.1 route.1
  1.5 0.1 copy-done.8
  1.6 0.0 copy-start
  1.6 0.0 copy-start.1
  1.6 0.0 copy-start.2
  1.6 0.1 own.1
  1.8 3.0 %collective-permute-start.1 = (bf16[8,1920]{1,0:T(8,128)(2,1)S(1)}, bf16[8,1920]{1,0:T(8,128)(2,1)S(1)}, u32[]{:S(2)}, u32[]{:S(2)}) collective-permute-start(bf16[8,1920]{1,0:T(8,128)(2,1)S(1)} %get-tuple-element.38), channel_id=1, source_target_pairs={{0,2},{1,3},{2,0},{3,1},{4,6},{5,7},{6,4},{7,5},{8,10},{9,11},{10,... | collective-permute-start | bytes 92168 | tf_op jit(solution)/shard_map/ppermute | solution.py:122
  4.8 0.0 collective-permute-done.tokens_ref
  4.8 0.2 line_up.1
  4.9 3.7 %collective-permute-start.3 = (bf16[8,1792]{1,0:T(8,128)(2,1)S(1)}, bf16[8,1792]{1,0:T(8,128)(2,1)S(1)}, u32[]{:S(2)}, u32[]{:S(2)}) collective-permute-start(bf16[8,1792]{1,0:T(8,128)(2,1)S(1)} %get-tuple-element.39), channel_id=1, source_target_pairs={{0,12},{1,15},{2,14},{3,13},{4,8},{5,11},{6,10},{7,9},{8,4},{9,7},... | collective-permute-start | bytes 86024 | tf_op jit(solution)/shard_map/ppermute | solution.py:118
  8.6 0.0 collective-permute-start.4
  8.6 0.8 %collective-permute-start.5 = (bf16[8,1792]{1,0:T(8,128)(2,1)S(1)}, bf16[8,1792]{1,0:T(8,128)(2,1)S(1)}, u32[]{:S(2)}, u32[]{:S(2)}) collective-permute-start(bf16[8,1792]{1,0:T(8,128)(2,1)S(1)} %get-tuple-element.41), channel_id=1, source_target_pairs={{0,4},{1,7},{2,6},{3,5},{4,0},{5,3},{6,2},{7,1},{8,12},{9,15},{10,... | collective-permute-start | bytes 86024 | tf_op jit(solution)/shard_map/ppermute | solution.py:118
  9.4 0.0 collective-permute-done.1.crossed_ref
  9.4 0.2 collective-permute-start.2
  9.6 0.0 copy-done.4
  9.6 0.0 copy-done.5
  9.6 0.0 copy-done.6
  9.6 0.0 copy-done.7
  9.6 0.7 %prepare.1 = (f32[2,3584]{1,0:T(2,128)S(1)}, f32[2,3584]{1,0:T(2,128)S(1)}, f32[2,3584]{1,0:T(2,128)S(1)}, bf16[128,128]{1,0:T(8,128)(2,1)S(1)}) custom-call(f32[2,28]{1,0:T(2,128)S(1)} %bitcast.23, f32[2,28]{1,0:T(2,128)S(1)} %bitcast.24, f32[2,28]{1,0:T(2,128)S(1)} %bitcast.25, s32[8,128]{1,0:T(8,128)S(1)} %bitcast.21, f32[8,128]{1,0:T(8,128)S(1)} %bitcast.22, ...), custom_call_target="tpu_custom_call" | custom-call | tf_op jit(solution)/shard_map/prepare/pallas_call | solution.py:386
  10.3 0.3 %collective-permute-done.2.swapped_ref = bf16[8,896]{1,0:T(8,128)(2,1)S(1)} collective-permute-done((bf16[8,896]{1,0:T(8,128)(2,1)S(1)}, bf16[8,896]{1,0:T(8,128)(2,1)S(1)}, u32[]{:S(2)}, u32[]{:S(2)}) %collective-permute-start.2) | collective-permute-done | bytes 14368 | tf_op jit(solution)/shard_map/ppermute | solution.py:113
  10.6 0.1 collective-permute-done.3.three_ref
  10.7 2.7 %collective-permute-done.4.two_ref = bf16[8,1792]{1,0:T(8,128)(2,1)S(1)} collective-permute-done((bf16[8,1792]{1,0:T(8,128)(2,1)S(1)}, bf16[8,1792]{1,0:T(8,128)(2,1)S(1)}, u32[]{:S(2)}, u32[]{:S(2)}) %collective-permute-start.4) | collective-permute-done | bytes 28704 | tf_op jit(solution)/shard_map/ppermute | solution.py:118
  13.4 0.0 collective-permute-done.5.one_ref
  13.4 0.1 collect.1
  13.5 0.0 collective-permute-start.6
  13.5 0.0 copy-done
  13.5 0.5 %near.1 = (f32[64,256]{1,0:T(8,128)S(1)}, f32[64,256]{1,0:T(8,128)S(1)}) custom-call(bf16[32,1792]{1,0:T(8,128)(2,1)S(1)} %get-tuple-element.43.x_ref, bf16[3584,256]{1,0:T(8,128)(2,1)S(1)} %bitcast.16, bf16[3584,256]{1,0:T(8,128)(2,1)S(1)} %bitcast.18, f32[2,3584]{1,0:T(2,128)S(1)} %get-tuple-element.42._.gate_scale_ref, ...), custom_call_target="tpu_custom_call" | custom-call | tf_op jit(solution)/shard_map/near/pallas_call | solution.py:386
  14.0 0.8 %collective-permute-done.6.x_ref = bf16[32,1792]{1,0:T(8,128)(2,1)S(1)} collective-permute-done((bf16[32,1792]{1,0:T(8,128)(2,1)S(1)}, bf16[32,1792]{1,0:T(8,128)(2,1)S(1)}, u32[]{:S(2)}, u32[]{:S(2)}) %collective-permute-start.6) | collective-permute-done | bytes 114720 | tf_op jit(solution)/shard_map/ppermute | solution.py:113
  14.8 0.7 %hidden.1 = (bf16[32,2048]{1,0:T(8,128)(2,1)S(1)}, bf16[32,256]{1,0:T(8,128)(2,1)S(1)}) custom-call(bf16[32,1792]{1,0:T(8,128)(2,1)S(1)} %collective-permute-done.6.x_ref, f32[64,256]{1,0:T(8,128)S(1)} %get-tuple-element.45.near_gate_ref, f32[64,256]{1,0:T(8,128)S(1)} %get-tuple-element.46.near_up_ref, bf16[3584,256]{1,0:T(8,128)(2,1)S(1)} %bitcast.17, ...), custom_call_target="tpu_custom_call" | custom-call | tf_op jit(solution)/shard_map/hidden/pallas_call | solution.py:386
  15.5 0.2 collective-permute-start.7
  15.7 0.3 keep.1
  16.0 0.7 %collective-permute-start.8 = (bf16[8,2816]{1,0:T(8,128)(2,1)S(1)}, bf16[8,2816]{1,0:T(8,128)(2,1)S(1)}, u32[]{:S(2)}, u32[]{:S(2)}) collective-permute-start(bf16[8,2816]{1,0:T(8,128)(2,1)S(1)} %get-tuple-element.52), channel_id=1, source_target_pairs={{0,2},{1,3},{2,0},{3,1},{4,6},{5,7},{6,4},{7,5},{8,10},{9,11},{10,... | collective-permute-start | bytes 135176 | tf_op jit(solution)/shard_map/ppermute | solution.py:122
  16.7 0.2 collective-permute-done.7.sent_ref
  17.0 1.7 %collective-permute-start.9 = (bf16[8,1792]{1,0:T(8,128)(2,1)S(1)}, bf16[8,1792]{1,0:T(8,128)(2,1)S(1)}, u32[]{:S(2)}, u32[]{:S(2)}) collective-permute-start(bf16[8,1792]{1,0:T(8,128)(2,1)S(1)} %get-tuple-element.53), channel_id=1, source_target_pairs={{0,12},{1,15},{2,14},{3,13},{4,8},{5,11},{6,10},{7,9},{8,4},{9,7},... | collective-permute-start | bytes 86024 | tf_op jit(solution)/shard_map/ppermute | solution.py:118
  18.6 0.5 %collective-permute-start.10 = (bf16[8,1792]{1,0:T(8,128)(2,1)S(1)}, bf16[8,1792]{1,0:T(8,128)(2,1)S(1)}, u32[]{:S(2)}, u32[]{:S(2)}) collective-permute-start(bf16[8,1792]{1,0:T(8,128)(2,1)S(1)} %get-tuple-element.54), channel_id=1, source_target_pairs={{0,8},{1,11},{2,10},{3,9},{4,12},{5,15},{6,14},{7,13},{8,0},{9,3},... | collective-permute-start | bytes 86024 | tf_op jit(solution)/shard_map/ppermute | solution.py:118
  19.1 2.3 %collective-permute-start.11 = (bf16[8,1792]{1,0:T(8,128)(2,1)S(1)}, bf16[8,1792]{1,0:T(8,128)(2,1)S(1)}, u32[]{:S(2)}, u32[]{:S(2)}) collective-permute-start(bf16[8,1792]{1,0:T(8,128)(2,1)S(1)} %get-tuple-element.55), channel_id=1, source_target_pairs={{0,4},{1,7},{2,6},{3,5},{4,0},{5,3},{6,2},{7,1},{8,12},{9,15},{10,... | collective-permute-start | bytes 86024 | tf_op jit(solution)/shard_map/ppermute | solution.py:118
  21.4 0.0 collective-permute-done.8.crossed_ref
  21.4 1.3 %hessian.1 = (f32[256,1024]{1,0:T(8,128)}, bf16[32,256]{1,0:T(8,128)(2,1)S(1)}, bf16[256,32]{1,0:T(8,128)(2,1)S(1)}) custom-call(bf16[32,128]{1,0:T(8,128)(2,1)S(1)} %get-tuple-element.56.count_ref, bf16[32,256]{1,0:T(8,128)(2,1)S(1)} %get-tuple-element.48.hidden_ref.own_ref, bf16[32,2048]{1,0:T(8,128)(2,1)S(1)} %collective-permute-done.7.sent_ref, ...), custom_call_target="tpu_custom_call" | custom-call | tf_op jit(solution)/shard_map/hessian/pallas_call | solution.py:386
  22.7 0.0 collective-permute-done.9.three_ref
  22.7 1.3 %collective-permute-done.10.two_ref = bf16[8,1792]{1,0:T(8,128)(2,1)S(1)} collective-permute-done((bf16[8,1792]{1,0:T(8,128)(2,1)S(1)}, bf16[8,1792]{1,0:T(8,128)(2,1)S(1)}, u32[]{:S(2)}, u32[]{:S(2)}) %collective-permute-start.10) | collective-permute-done | bytes 28704 | tf_op jit(solution)/shard_map/ppermute | solution.py:118
  24.1 0.0 collective-permute-done.11.one_ref
  24.1 0.2 collective-permute-start.12
  24.3 1.1 %collective-permute-done.12.far_ref = bf16[32,1152]{1,0:T(8,128)(2,1)S(1)} collective-permute-done((bf16[32,1152]{1,0:T(8,128)(2,1)S(1)}, bf16[32,1152]{1,0:T(8,128)(2,1)S(1)}, u32[]{:S(2)}, u32[]{:S(2)}) %collective-permute-start.12) | collective-permute-done | bytes 73760 | tf_op jit(solution)/shard_map/ppermute | solution.py:113
  25.4 1.0 %combine.1 = (bf16[128,896]{1,0:T(8,128)(2,1)}, f32[256,1024]{1,0:T(8,128)}) custom-call(bf16[128,128]{1,0:T(8,128)(2,1)S(1)} %get-tuple-element.34.coef_ref, bf16[32,896]{1,0:T(8,128)(2,1)S(1)} %get-tuple-element.58.near_ref, bf16[32,1152]{1,0:T(8,128)(2,1)S(1)} %collective-permute-done.12.far_ref, ...), custom_call_target="tpu_custom_call", output_to_operand_aliasing={{1}: (5, {})} | custom-call | tf_op jit(solution)/shard_map/combine/pallas_call | solution.py:475
  (10 shorter events, 0.1 us)
Async XLA Ops:
  0.6 1.0 %copy-start.8 = (bf16[128,896]{1,0:T(8,128)(2,1)S(1)}, bf16[128,896]{1,0:T(8,128)(2,1)}, u32[]{:S(2)}) copy-start(bf16[128,896]{1,0:T(8,128)(2,1)} %tokens_ref.1) | copy-start | bytes 688132
  0.6 0.7 %copy-start.3 = (s32[128,8]{0,1:T(8,128)S(1)}, s32[128,8]{0,1:T(8,128)}, u32[]{:S(2)}) copy-start(s32[128,8]{0,1:T(8,128)} %param.10) | copy-start | bytes 12292
  0.6 4.1 %collective-permute-start = (bf16[128,896]{1,0:T(8,128)(2,1)}, bf16[128,896]{1,0:T(8,128)(2,1)S(1)}, u32[]{:S(2)}, u32[]{:S(2)}) collective-permute-start(bf16[128,896]{1,0:T(8,128)(2,1)} %tokens_ref.1), channel_id=1, source_target_pairs={{0,1},{1,0},{2,3},{3,2},{4,5},{5,4},{6,7},{7,6},{8,9},{9,8},{10,11... | collective-permute-start | bytes 688136 | tf_op jit(solution)/shard_map/ppermute | solution.py:113
  1.6 8.0 %copy-start.4 = (f32[128,8]{0,1:T(8,128)S(1)}, f32[128,8]{0,1:T(8,128)}, u32[]{:S(2)}) copy-start(f32[128,8]{0,1:T(8,128)} %param.11) | copy-start | bytes 12292
  1.6 8.0 %copy-start.5 = (f32[1,28,2]{1,2,0:T(2,128)S(1)}, f32[1,28,2]{1,2,0:T(2,128)}, u32[]{:S(2)}) copy-start(f32[1,28,2]{1,2,0:T(2,128)} %param.13) | copy-start | bytes 676
  1.6 8.0 %copy-start.6 = (f32[1,28,2]{1,2,0:T(2,128)S(1)}, f32[1,28,2]{1,2,0:T(2,128)}, u32[]{:S(2)}) copy-start(f32[1,28,2]{1,2,0:T(2,128)} %param.15) | copy-start | bytes 676
  1.6 8.0 %copy-start.7 = (f32[1,2,28]{2,1,0:T(2,128)S(1)}, f32[1,2,28]{2,1,0:T(2,128)}, u32[]{:S(2)}) copy-start(f32[1,2,28]{2,1,0:T(2,128)} %param.17) | copy-start | bytes 676
  1.6 11.9 %copy-start = (bf16[1,256,3584]{2,1,0:T(8,128)(2,1)S(1)}, bf16[1,256,3584]{2,1,0:T(8,128)(2,1)}, u32[]{:S(2)}) copy-start(bf16[1,256,3584]{2,1,0:T(8,128)(2,1)} %param.16) | copy-start | bytes 5505028
  1.6 11.9 %copy-start.1 = (bf16[1,3584,256]{2,1,0:T(8,128)(2,1)S(1)}, bf16[1,3584,256]{2,1,0:T(8,128)(2,1)}, u32[]{:S(2)}) copy-start(bf16[1,3584,256]{2,1,0:T(8,128)(2,1)} %param.12) | copy-start | bytes 5505028
  1.6 11.9 %copy-start.2 = (bf16[1,3584,256]{2,1,0:T(8,128)(2,1)S(1)}, bf16[1,3584,256]{2,1,0:T(8,128)(2,1)}, u32[]{:S(2)}) copy-start(bf16[1,3584,256]{2,1,0:T(8,128)(2,1)} %param.14) | copy-start | bytes 5505028
  1.8 7.6 %collective-permute-start.1 = (bf16[8,1920]{1,0:T(8,128)(2,1)S(1)}, bf16[8,1920]{1,0:T(8,128)(2,1)S(1)}, u32[]{:S(2)}, u32[]{:S(2)}) collective-permute-start(bf16[8,1920]{1,0:T(8,128)(2,1)S(1)} %get-tuple-element.38), channel_id=1, source_target_pairs={{0,2},{1,3},{2,0},{3,1},{4,6},{5,7},{6,4},{7,5},{8,10},{9,11},{10,... | collective-permute-start | bytes 92168 | tf_op jit(solution)/shard_map/ppermute | solution.py:122
  4.9 5.7 %collective-permute-start.3 = (bf16[8,1792]{1,0:T(8,128)(2,1)S(1)}, bf16[8,1792]{1,0:T(8,128)(2,1)S(1)}, u32[]{:S(2)}, u32[]{:S(2)}) collective-permute-start(bf16[8,1792]{1,0:T(8,128)(2,1)S(1)} %get-tuple-element.39), channel_id=1, source_target_pairs={{0,12},{1,15},{2,14},{3,13},{4,8},{5,11},{6,10},{7,9},{8,4},{9,7},... | collective-permute-start | bytes 86024 | tf_op jit(solution)/shard_map/ppermute | solution.py:118
  8.6 4.8 %collective-permute-start.4 = (bf16[8,1792]{1,0:T(8,128)(2,1)S(1)}, bf16[8,1792]{1,0:T(8,128)(2,1)S(1)}, u32[]{:S(2)}, u32[]{:S(2)}) collective-permute-start(bf16[8,1792]{1,0:T(8,128)(2,1)S(1)} %get-tuple-element.40), channel_id=1, source_target_pairs={{0,8},{1,11},{2,10},{3,9},{4,12},{5,15},{6,14},{7,13},{8,0},{9,3},... | collective-permute-start | bytes 86024 | tf_op jit(solution)/shard_map/ppermute | solution.py:118
  8.6 4.8 %collective-permute-start.5 = (bf16[8,1792]{1,0:T(8,128)(2,1)S(1)}, bf16[8,1792]{1,0:T(8,128)(2,1)S(1)}, u32[]{:S(2)}, u32[]{:S(2)}) collective-permute-start(bf16[8,1792]{1,0:T(8,128)(2,1)S(1)} %get-tuple-element.41), channel_id=1, source_target_pairs={{0,4},{1,7},{2,6},{3,5},{4,0},{5,3},{6,2},{7,1},{8,12},{9,15},{10,... | collective-permute-start | bytes 86024 | tf_op jit(solution)/shard_map/ppermute | solution.py:118
  9.4 1.2 %collective-permute-start.2 = (bf16[8,896]{1,0:T(8,128)(2,1)S(1)}, bf16[8,896]{1,0:T(8,128)(2,1)S(1)}, u32[]{:S(2)}, u32[]{:S(2)}) collective-permute-start(bf16[8,896]{1,0:T(8,128)(2,1)S(1)} %slice.4), channel_id=1, source_target_pairs={{0,1},{1,0},{2,3},{3,2},{4,5},{5,4},{6,7},{7,6},{8,9},{9,8},{10,11... | collective-permute-start | bytes 43016 | tf_op jit(solution)/shard_map/ppermute | solution.py:113
  13.5 1.3 %collective-permute-start.6 = (bf16[32,1792]{1,0:T(8,128)(2,1)S(1)}, bf16[32,1792]{1,0:T(8,128)(2,1)S(1)}, u32[]{:S(2)}, u32[]{:S(2)}) collective-permute-start(bf16[32,1792]{1,0:T(8,128)(2,1)S(1)} %get-tuple-element.43.x_ref), channel_id=1, source_target_pairs={{0,1},{1,0},{2,3},{3,2},{4,5},{5,4},{6,7},{7,6},{8,9},{9,8},{10,11... | collective-permute-start | bytes 344072 | tf_op jit(solution)/shard_map/ppermute | solution.py:113
  15.5 1.4 %collective-permute-start.7 = (bf16[32,2048]{1,0:T(8,128)(2,1)S(1)}, bf16[32,2048]{1,0:T(8,128)(2,1)S(1)}, u32[]{:S(2)}, u32[]{:S(2)}) collective-permute-start(bf16[32,2048]{1,0:T(8,128)(2,1)S(1)} %get-tuple-element.49.send_ref), channel_id=1, source_target_pairs={{0,1},{1,0},{2,3},{3,2},{4,5},{5,4},{6,7},{7,6},{8,9},{9,8},{10,11... | collective-permute-start | bytes 393224 | tf_op jit(solution)/shard_map/ppermute | solution.py:113
  16.0 5.4 %collective-permute-start.8 = (bf16[8,2816]{1,0:T(8,128)(2,1)S(1)}, bf16[8,2816]{1,0:T(8,128)(2,1)S(1)}, u32[]{:S(2)}, u32[]{:S(2)}) collective-permute-start(bf16[8,2816]{1,0:T(8,128)(2,1)S(1)} %get-tuple-element.52), channel_id=1, source_target_pairs={{0,2},{1,3},{2,0},{3,1},{4,6},{5,7},{6,4},{7,5},{8,10},{9,11},{10,... | collective-permute-start | bytes 135176 | tf_op jit(solution)/shard_map/ppermute | solution.py:122
  17.0 5.8 %collective-permute-start.9 = (bf16[8,1792]{1,0:T(8,128)(2,1)S(1)}, bf16[8,1792]{1,0:T(8,128)(2,1)S(1)}, u32[]{:S(2)}, u32[]{:S(2)}) collective-permute-start(bf16[8,1792]{1,0:T(8,128)(2,1)S(1)} %get-tuple-element.53), channel_id=1, source_target_pairs={{0,12},{1,15},{2,14},{3,13},{4,8},{5,11},{6,10},{7,9},{8,4},{9,7},... | collective-permute-start | bytes 86024 | tf_op jit(solution)/shard_map/ppermute | solution.py:118
  18.6 5.4 %collective-permute-start.10 = (bf16[8,1792]{1,0:T(8,128)(2,1)S(1)}, bf16[8,1792]{1,0:T(8,128)(2,1)S(1)}, u32[]{:S(2)}, u32[]{:S(2)}) collective-permute-start(bf16[8,1792]{1,0:T(8,128)(2,1)S(1)} %get-tuple-element.54), channel_id=1, source_target_pairs={{0,8},{1,11},{2,10},{3,9},{4,12},{5,15},{6,14},{7,13},{8,0},{9,3},... | collective-permute-start | bytes 86024 | tf_op jit(solution)/shard_map/ppermute | solution.py:118
  19.1 4.9 %collective-permute-start.11 = (bf16[8,1792]{1,0:T(8,128)(2,1)S(1)}, bf16[8,1792]{1,0:T(8,128)(2,1)S(1)}, u32[]{:S(2)}, u32[]{:S(2)}) collective-permute-start(bf16[8,1792]{1,0:T(8,128)(2,1)S(1)} %get-tuple-element.55), channel_id=1, source_target_pairs={{0,4},{1,7},{2,6},{3,5},{4,0},{5,3},{6,2},{7,1},{8,12},{9,15},{10,... | collective-permute-start | bytes 86024 | tf_op jit(solution)/shard_map/ppermute | solution.py:118
  24.1 1.3 %collective-permute-start.12 = (bf16[32,1152]{1,0:T(8,128)(2,1)S(1)}, bf16[32,1152]{1,0:T(8,128)(2,1)S(1)}, u32[]{:S(2)}, u32[]{:S(2)}) collective-permute-start(bf16[32,1152]{1,0:T(8,128)(2,1)S(1)} %get-tuple-element.59), channel_id=1, source_target_pairs={{0,1},{1,0},{2,3},{3,2},{4,5},{5,4},{6,7},{7,6},{8,9},{9,8},{10,11... | collective-permute-start | bytes 221192 | tf_op jit(solution)/shard_map/ppermute | solution.py:113

commit v10 on v9

--- a/solution.py
+++ b/solution.py
@@ -149,12 +149,8 @@
     chosen_ref[...] = jnp.concatenate(chosen, axis=0).astype(BF16)
 
 
-def own_kernel(chosen_ref, tokens_ref, rows_ref, cross_ref):
-    picked = pick(chosen_ref, tokens_ref)
-    rows, width = rows_ref.shape[1:]
-    rows_ref[...] = picked.reshape(rows_ref.shape)
-    cross_ref[:, :width] = picked[:rows]
-    cross_ref[:, width:] = jnp.zeros((rows, cross_ref.shape[1] - width), BF16)
+def own_kernel(chosen_ref, tokens_ref, rows_ref):
+    rows_ref[...] = pick(chosen_ref, tokens_ref).reshape(rows_ref.shape)
 
 
 def prepare_kernel(
@@ -180,34 +176,28 @@
     coef_ref[...] = jnp.concatenate(terms, axis=0).T.astype(BF16)
 
 
-def line_up_kernel(chosen_ref, tokens_ref, own_ref, other_ref, *out_refs):
-    rows, width = other_ref.shape
+def line_up_kernel(chosen_ref, tokens_ref, own_ref, *out_refs):
+    rows, width = own_ref.shape[1:]
     other = pick(chosen_ref, tokens_ref)
-    other_ref[...] = other[:rows]
     empty = 1.0 - jnp.sum(chosen_ref[...].astype(F32), axis=1, keepdims=True)
     first = lax.broadcasted_iota(jnp.int32, (rows, QBLK), 1) == 0
-    for k, out_ref in enumerate(out_refs, 1):
+    for k, out_ref in enumerate(out_refs):
         at = slice(k * rows, (k + 1) * rows)
         own = own_ref[k]
-        mark = jnp.where(first, empty[at] * EMPTY, 0.0)
-        out_ref[:, :QBLK] = (own[:, :QBLK].astype(F32) + mark).astype(BF16)
-        out_ref[:, QBLK:width] = own[:, QBLK:]
+        out_ref[:, :width] = own
         out_ref[:, width:] = other[at]
+        if k:
+            mark = jnp.where(first, empty[at] * EMPTY, 0.0)
+            out_ref[:, :QBLK] = (own[:, :QBLK].astype(F32) + mark).astype(BF16)
 
 
 def on_core(core):
     return (lax.axis_index("mp") % 2 == core).astype(F32)
 
 
-def collect_kernel(own_ref, other_ref, count_ref, crossed_ref, swapped_ref, three_ref, two_ref, one_ref, _, out_ref, counts_ref):
-    rows, width = crossed_ref.shape[0], out_ref.shape[1] // 2
-    zero = on_core(0)
-    for own, far_ref, lanes in (
-        (own_ref[0], crossed_ref, slice(0, width)),
-        (other_ref[...], swapped_ref, slice(width, 2 * width)),
-    ):
-        value = own.astype(F32) * zero + far_ref[:, :width].astype(F32) * (1.0 - zero)
-        out_ref[:rows, lanes] = value.astype(BF16)
+def collect_kernel(own_ref, count_ref, two_ref, three_ref, one_ref, _, out_ref, counts_ref):
+    rows, width = own_ref.shape
+    out_ref[:rows, :] = (own_ref[...].astype(F32) * on_core(0)).astype(BF16)
     counts_ref[:rows, :] = count_ref[0]
     for k, ref in enumerate((one_ref, two_ref, three_ref), 1):
         at = slice(k * rows, (k + 1) * rows)
@@ -217,6 +207,14 @@
         out_ref[at, QBLK:] = ref[:, QBLK:]
         kept = rows - jnp.sum(jnp.where(empty[:, :1], 1.0, 0.0), axis=0, keepdims=True)
         counts_ref[at, :] = jnp.broadcast_to(kept, (rows, QBLK)).astype(BF16)
+
+
+def filled(x_ref, crossed_ref, part, part_of_crossed, lacks):
+    rows, width = crossed_ref.shape[0], crossed_ref.shape[1] // 2
+    lanes, lanes_of_crossed = (slice(i * width, (i + 1) * width) for i in (part, part_of_crossed))
+    x = x_ref[:, lanes].astype(F32)
+    first = x[:rows] + crossed_ref[:, lanes_of_crossed].astype(F32) * lacks
+    return jnp.concatenate([first, x[rows:]], axis=0)
 
 
 def shares_in_order():
@@ -237,11 +235,10 @@
     return jnp.concatenate([out[:slots] + out[slots : 2 * slots], out[2 * slots : 3 * slots] + out[3 * slots :]], axis=0)
 
 
-def near_kernel(x_ref, gate_ref, up_ref, gate_scale_ref, up_scale_ref, _, gate_out_ref, up_out_ref):
-    width = x_ref.shape[1] // 2
+def near_kernel(x_ref, crossed_ref, gate_ref, up_ref, gate_scale_ref, up_scale_ref, _, gate_out_ref, up_out_ref):
     gate, up = 0.0, 0.0
     for part, share in enumerate(shares_in_order()[:2]):
-        x = x_ref[:, part * width : (part + 1) * width].astype(F32)
+        x = filled(x_ref, crossed_ref, part, part, on_core(1))
         gate += project(x, share, gate_ref, gate_scale_ref)
         up += project(x, share, up_ref, up_scale_ref)
     gate_out_ref[...] = gate
@@ -250,6 +247,7 @@
 
 def hidden_kernel(
     x_ref,
+    crossed_ref,
     near_gate_ref,
     near_up_ref,
     gate_ref,
@@ -266,7 +264,7 @@
     width = x_ref.shape[1] // 2
     gate, up = near_gate_ref[...], near_up_ref[...]
     for part, share in enumerate(shares[2:]):
-        x = x_ref[:, part * width : (part + 1) * width].astype(F32)
+        x = filled(x_ref, crossed_ref, part, 1 - part, on_core(0))
         gate += project(x, share, gate_ref, gate_scale_ref)
         up += project(x, share, up_ref, up_scale_ref)
     parts = []
@@ -335,7 +333,7 @@
         out_ref[:, pl.ds(pl.multiple_of(share * width, width), width)] = block
 
 
-def collect_back_kernel(summed_ref, crossed_ref, three_ref, two_ref, one_ref, far_ref, mine_ref, other_ref):
+def collect_back_kernel(summed_ref, crossed_ref, three_ref, one_ref, two_ref, far_ref, mine_ref, other_ref):
     rows, width = one_ref.shape[0], mine_ref.shape[1]
     crossed = crossed_ref[:, : 2 * width].astype(F32)
     value = (crossed + summed_ref[...].astype(F32) * on_core(0)).astype(BF16)
@@ -401,18 +399,17 @@
         (shape((slots, rows), BF16), shape((4, capacity, QBLK), BF16)),
         (earlier, route_ids.T),
     )
-    picked, cross = call(
+    picked = call(
         own_kernel,
         "own",
-        (shape((4, capacity, width), BF16), shape((capacity, 2 * width + QBLK), BF16)),
+        shape((4, capacity, width), BF16),
         (chosen, tokens),
         flops=10**11,
     )
-    crossed = across(cross)
-    other, *messages = call(
+    messages = call(
         line_up_kernel,
         "line_up",
-        (shape((capacity, width), BF16), *[shape((capacity, 2 * width), BF16)] * 3),
+        (shape((capacity, 2 * width), BF16),) * 4,
         (chosen, other_tokens, picked),
     )
     *scales, coef = call(
@@ -428,14 +425,16 @@
         collect_kernel,
         "collect",
         (shape((slots, 2 * width), BF16), shape((slots, QBLK), BF16)),
-        (picked, other, counts, crossed, swap_cores(crossed[:, :width]), *[to_chips(messages[k - 1], k) for k in (3, 2, 1)], scales[0]),
+        (messages[0], counts, *[to_chips(messages[k], k) for k in (2, 3, 1)], scales[0]),
     )
     swapped = swap_cores(arrived)
+    crossed = across(messages[0])
     near = call(
         near_kernel,
         "near",
         (shape((2 * slots, hidden_width), F32),) * 2,
-        (arrived, gate, up, *scales[:2], down),
+        (arrived, crossed, gate, up, *scales[:2], down),
+        flops=10**10,
     )
     send, hidden = call(
         hidden_kernel,
@@ -444,7 +443,7 @@
             shape((slots, 2 * width + hidden_width), BF16),
             shape((slots, hidden_width), BF16),
         ),
-        (swapped, *near, gate, up, down, *scales),
+        (swapped, crossed, *near, gate, up, down, *scales),
     )
     sent = swap_cores(send)
     keep, cross = call(
@@ -470,7 +469,7 @@
         collect_back_kernel,
         "collect_back",
         (shape((slots, width), BF16), shape((slots, width + hidden_width), BF16)),
-        (summed[0], crossed, *[back[k] for k in (3, 2, 1)], far),
+        (summed[0], crossed, *[back[k] for k in (3, 1, 2)], far),
     )
     mixed, hessian = pl.pallas_call(
         combine_kernel,

time: 26.6 us -> 26.3 us (0.989)
  waiting for transfers between devices: 6.53 us -> 5.35 us
  starting transfers between devices: 13.8 us -> 14.7 us
    ppermute x6, starting transfers between devices: 8.9 us -> 10.1 us  [to_chips(): return lax.ppermute(value, BOTH, pairs)]
    ppermute x6, waiting for transfers between devices: 4.14 us -> 3.19 us  [to_chips(): return lax.ppermute(value, BOTH, pairs)]
    ppermute x2, starting transfers between devices: 3.74 us -> 2.82 us  [across(): lax.ppermute(value, BOTH, [(4 * z + m, 4 * z + (m ^ 2)) for z in range(4)...]
    ppermute x5 -> x4, starting transfers between devices: 1.18 us -> 1.82 us  [swap_cores(): return lax.ppermute(value, 'mp', [(m, m ^ 1) for m in range(4)])]
    ppermute x5 -> x4, waiting for transfers between devices: 2.38 us -> 2.16 us  [swap_cores(): return lax.ppermute(value, 'mp', [(m, m ^ 1) for m in range(4)])]
  transfers between devices with their start and end apart: 13 -> 12, of which waited for: 7 -> 7; matrix products, arithmetic and copies ran while one was open for 0% -> 0% of each run, Pallas kernels for 12% -> 12%
where the time goes in v10:
time: 26.3 us; the launch traced here: 26.1 us
  starting transfers between devices  14.7 us (56%)
  waiting for transfers between devices  5.35 us (20%)
  Pallas kernels  5 us (19%)
  between operations  0.74 us (3%)
  local copies, waits for them, and re-layouts  0.3 us (1%)
    ppermute x6, starting transfers between devices, to_chips(): return lax.ppermute(value, BOTH, pairs)  10.1 us
    pallas_call x12, Pallas kernels, call(): pl.pallas_call(kernel, out_shape=outs, in_specs=[SMEM] * scalars + [VMEM]...  4.01 us
    ppermute x6, waiting for transfers between devices, to_chips(): return lax.ppermute(value, BOTH, pairs)  3.19 us
    ppermute x2, starting transfers between devices, across(): lax.ppermute(value, BOTH, [(4 * z + m, 4 * z + (m ^ 2)) for z in range(4)...  2.82 us
    ppermute x4, waiting for transfers between devices, swap_cores(): return lax.ppermute(value, 'mp', [(m, m ^ 1) for m in range(4)])  2.16 us
    ppermute x4, starting transfers between devices, swap_cores(): return lax.ppermute(value, 'mp', [(m, m ^ 1) for m in range(4)])  1.82 us
    pallas_call x1, Pallas kernels, on_device(): pl.pallas_call(combine_kernel, out_shape=(shape((rows, width), BF16), sha...  0.99 us
  transfers between devices with their start and end apart: 12, of which 7 were waited for; matrix products, arithmetic and copies ran while one was open for 0% of the time, Pallas kernels for 12%

profile of v10, /device:TPU:0, one launch (start us, length us, event | category | flops | bytes accessed | tf_op | source)
XLA Modules:
  0.0 26.1 jit_solution(5012432086283344104)
XLA Ops:
  0.6 0.0 copy-start.8
  0.6 0.0 copy-start.3
  0.6 0.5 %collective-permute-start = (bf16[128,896]{1,0:T(8,128)(2,1)}, bf16[128,896]{1,0:T(8,128)(2,1)S(1)}, u32[]{:S(2)}, u32[]{:S(2)}) collective-permute-start(bf16[128,896]{1,0:T(8,128)(2,1)} %tokens_ref.1), channel_id=1, source_target_pairs={{0,1},{1,0},{2,3},{3,2},{4,5},{5,4},{6,7},{7,6},{8,9},{9,8},{10,11... | collective-permute-start | bytes 688136 | tf_op jit(solution)/shard_map/ppermute | solution.py:113
  1.2 0.2 copy-done.3
  1.4 0.1 route.1
  1.5 0.1 copy-done.8
  1.6 0.0 copy-start
  1.6 0.0 copy-start.1
  1.6 0.0 copy-start.2
  1.6 0.1 own.1.own_ref
  1.8 0.7 %collective-permute-done.tokens_ref = bf16[128,896]{1,0:T(8,128)(2,1)S(1)} collective-permute-done((bf16[128,896]{1,0:T(8,128)(2,1)}, bf16[128,896]{1,0:T(8,128)(2,1)S(1)}, u32[]{:S(2)}, u32[]{:S(2)}) %collective-permute-start) | collective-permute-done | bytes 229408 | tf_op jit(solution)/shard_map/ppermute | solution.py:113
  2.5 0.1 line_up.1
  2.6 4.0 %collective-permute-start.1 = (bf16[8,1792]{1,0:T(8,128)(2,1)S(1)}, bf16[8,1792]{1,0:T(8,128)(2,1)S(1)}, u32[]{:S(2)}, u32[]{:S(2)}) collective-permute-start(bf16[8,1792]{1,0:T(8,128)(2,1)S(1)} %get-tuple-element.35), channel_id=1, source_target_pairs={{0,8},{1,11},{2,10},{3,9},{4,12},{5,15},{6,14},{7,13},{8,0},{9,3},... | collective-permute-start | bytes 86024 | tf_op jit(solution)/shard_map/ppermute | solution.py:118
  6.7 1.3 %collective-permute-start.2 = (bf16[8,1792]{1,0:T(8,128)(2,1)S(1)}, bf16[8,1792]{1,0:T(8,128)(2,1)S(1)}, u32[]{:S(2)}, u32[]{:S(2)}) collective-permute-start(bf16[8,1792]{1,0:T(8,128)(2,1)S(1)} %get-tuple-element.36), channel_id=1, source_target_pairs={{0,12},{1,15},{2,14},{3,13},{4,8},{5,11},{6,10},{7,9},{8,4},{9,7},... | collective-permute-start | bytes 86024 | tf_op jit(solution)/shard_map/ppermute | solution.py:118
  8.0 0.2 collective-permute-start.3
  8.2 1.5 %collective-permute-start.5 = (bf16[8,1792]{1,0:T(8,128)(2,1)S(1)}, bf16[8,1792]{1,0:T(8,128)(2,1)S(1)}, u32[]{:S(2)}, u32[]{:S(2)}) collective-permute-start(bf16[8,1792]{1,0:T(8,128)(2,1)S(1)} %get-tuple-element.33.own_ref), channel_id=1, source_target_pairs={{0,2},{1,3},{2,0},{3,1},{4,6},{5,7},{6,4},{7,5},{8,10},{9,11},{10,... | collective-permute-start | bytes 86024 | tf_op jit(solution)/shard_map/ppermute | solution.py:122
  9.7 0.0 copy-done.4
  9.7 0.0 copy-done.5
  9.7 0.0 copy-done.6
  9.7 0.0 copy-done.7
  9.8 0.7 %prepare.1 = (f32[2,3584]{1,0:T(2,128)S(1)}, f32[2,3584]{1,0:T(2,128)S(1)}, f32[2,3584]{1,0:T(2,128)S(1)}, bf16[128,128]{1,0:T(8,128)(2,1)S(1)}) custom-call(f32[2,28]{1,0:T(2,128)S(1)} %bitcast.23, f32[2,28]{1,0:T(2,128)S(1)} %bitcast.24, f32[2,28]{1,0:T(2,128)S(1)} %bitcast.25, s32[8,128]{1,0:T(8,128)S(1)} %bitcast.21, f32[8,128]{1,0:T(8,128)S(1)} %bitcast.22, ...), custom_call_target="tpu_custom_call" | custom-call | tf_op jit(solution)/shard_map/prepare/pallas_call | solution.py:384
  10.4 0.0 collective-permute-done.1.two_ref
  10.5 2.1 %collective-permute-done.2.three_ref = bf16[8,1792]{1,0:T(8,128)(2,1)S(1)} collective-permute-done((bf16[8,1792]{1,0:T(8,128)(2,1)S(1)}, bf16[8,1792]{1,0:T(8,128)(2,1)S(1)}, u32[]{:S(2)}, u32[]{:S(2)}) %collective-permute-start.2) | collective-permute-done | bytes 28704 | tf_op jit(solution)/shard_map/ppermute | solution.py:118
  12.5 0.0 collective-permute-done.3.one_ref
  12.5 0.1 collect.1
  12.6 0.5 %collective-permute-start.4 = (bf16[32,1792]{1,0:T(8,128)(2,1)S(1)}, bf16[32,1792]{1,0:T(8,128)(2,1)S(1)}, u32[]{:S(2)}, u32[]{:S(2)}) collective-permute-start(bf16[32,1792]{1,0:T(8,128)(2,1)S(1)} %get-tuple-element.39.x_ref), channel_id=1, source_target_pairs={{0,1},{1,0},{2,3},{3,2},{4,5},{5,4},{6,7},{7,6},{8,9},{9,8},{10,11... | collective-permute-start | bytes 344072 | tf_op jit(solution)/shard_map/ppermute | solution.py:113
  13.1 0.0 collective-permute-done.5.crossed_ref
  13.1 0.0 copy-done
  13.1 0.0 copy-done.1
  13.1 0.0 copy-done.2
  13.1 0.5 %near.1 = (f32[64,256]{1,0:T(8,128)S(1)}, f32[64,256]{1,0:T(8,128)S(1)}) custom-call(bf16[32,1792]{1,0:T(8,128)(2,1)S(1)} %get-tuple-element.39.x_ref, bf16[8,1792]{1,0:T(8,128)(2,1)S(1)} %collective-permute-done.5.crossed_ref, bf16[3584,256]{1,0:T(8,128)(2,1)S(1)} %bitcast.16, bf16[3584,256]{1,0:T(8,128)(2,1)S(1)} %bitcast.18, ...), custom_call_target="tpu_custom_call" | custom-call | flops 10000000000 | tf_op jit(solution)/shard_map/near/pallas_call | solution.py:384
  13.6 0.5 %collective-permute-done.4.x_ref = bf16[32,1792]{1,0:T(8,128)(2,1)S(1)} collective-permute-done((bf16[32,1792]{1,0:T(8,128)(2,1)S(1)}, bf16[32,1792]{1,0:T(8,128)(2,1)S(1)}, u32[]{:S(2)}, u32[]{:S(2)}) %collective-permute-start.4) | collective-permute-done | bytes 114720 | tf_op jit(solution)/shard_map/ppermute | solution.py:113
  14.1 0.7 %hidden.1 = (bf16[32,2048]{1,0:T(8,128)(2,1)S(1)}, bf16[32,256]{1,0:T(8,128)(2,1)S(1)}) custom-call(bf16[32,1792]{1,0:T(8,128)(2,1)S(1)} %collective-permute-done.4.x_ref, bf16[8,1792]{1,0:T(8,128)(2,1)S(1)} %collective-permute-done.5.crossed_ref, f32[64,256]{1,0:T(8,128)S(1)} %get-tuple-element.41.near_gate_ref, ...), custom_call_target="tpu_custom_call" | custom-call | tf_op jit(solution)/shard_map/hidden/pallas_call | solution.py:384
  14.8 0.4 %collective-permute-start.6 = (bf16[32,2048]{1,0:T(8,128)(2,1)S(1)}, bf16[32,2048]{1,0:T(8,128)(2,1)S(1)}, u32[]{:S(2)}, u32[]{:S(2)}) collective-permute-start(bf16[32,2048]{1,0:T(8,128)(2,1)S(1)} %get-tuple-element.45.send_ref), channel_id=1, source_target_pairs={{0,1},{1,0},{2,3},{3,2},{4,5},{5,4},{6,7},{7,6},{8,9},{9,8},{10,11... | collective-permute-start | bytes 393224 | tf_op jit(solution)/shard_map/ppermute | solution.py:113
  15.2 0.3 %keep.1 = (bf16[32,1792]{1,0:T(8,128)(2,1)S(1)}, bf16[8,2816]{1,0:T(8,128)(2,1)S(1)}) custom-call(bf16[32,256]{1,0:T(8,128)(2,1)S(1)} %get-tuple-element.44.hidden_ref.own_ref, bf16[32,2048]{1,0:T(8,128)(2,1)S(1)} %get-tuple-element.45.send_ref, bf16[256,3584]{1,0:T(8,128)(2,1)S(1)} %bitcast.15, f32[2,3584]{1,0:T(2,128)S(1)} %get-tuple-element.43.down_scale_ref), custom_call_target="tpu_custom_call" | custom-call | tf_op jit(solution)/shard_map/keep/pallas_call | solution.py:384
  15.5 1.3 %collective-permute-start.7 = (bf16[8,2816]{1,0:T(8,128)(2,1)S(1)}, bf16[8,2816]{1,0:T(8,128)(2,1)S(1)}, u32[]{:S(2)}, u32[]{:S(2)}) collective-permute-start(bf16[8,2816]{1,0:T(8,128)(2,1)S(1)} %get-tuple-element.48), channel_id=1, source_target_pairs={{0,2},{1,3},{2,0},{3,1},{4,6},{5,7},{6,4},{7,5},{8,10},{9,11},{10,... | collective-permute-start | bytes 135176 | tf_op jit(solution)/shard_map/ppermute | solution.py:122
  16.8 0.0 collective-permute-done.6.sent_ref
  16.9 1.9 %collective-permute-start.8 = (bf16[8,1792]{1,0:T(8,128)(2,1)S(1)}, bf16[8,1792]{1,0:T(8,128)(2,1)S(1)}, u32[]{:S(2)}, u32[]{:S(2)}) collective-permute-start(bf16[8,1792]{1,0:T(8,128)(2,1)S(1)} %get-tuple-element.49), channel_id=1, source_target_pairs={{0,12},{1,15},{2,14},{3,13},{4,8},{5,11},{6,10},{7,9},{8,4},{9,7},... | collective-permute-start | bytes 86024 | tf_op jit(solution)/shard_map/ppermute | solution.py:118
  18.7 0.0 collective-permute-start.9
  18.7 2.6 %collective-permute-start.10 = (bf16[8,1792]{1,0:T(8,128)(2,1)S(1)}, bf16[8,1792]{1,0:T(8,128)(2,1)S(1)}, u32[]{:S(2)}, u32[]{:S(2)}) collective-permute-start(bf16[8,1792]{1,0:T(8,128)(2,1)S(1)} %get-tuple-element.51), channel_id=1, source_target_pairs={{0,8},{1,11},{2,10},{3,9},{4,12},{5,15},{6,14},{7,13},{8,0},{9,3},... | collective-permute-start | bytes 86024 | tf_op jit(solution)/shard_map/ppermute | solution.py:118
  21.3 0.0 collective-permute-done.7.crossed_ref
  21.3 1.3 %hessian.1 = (f32[256,1024]{1,0:T(8,128)}, bf16[32,256]{1,0:T(8,128)(2,1)S(1)}, bf16[256,32]{1,0:T(8,128)(2,1)S(1)}) custom-call(bf16[32,128]{1,0:T(8,128)(2,1)S(1)} %get-tuple-element.52.count_ref, bf16[32,256]{1,0:T(8,128)(2,1)S(1)} %get-tuple-element.44.hidden_ref.own_ref, bf16[32,2048]{1,0:T(8,128)(2,1)S(1)} %collective-permute-done.6.sent_ref, ...), custom_call_target="tpu_custom_call" | custom-call | tf_op jit(solution)/shard_map/hessian/pallas_call | solution.py:384
  22.6 0.1 collective-permute-done.8.three_ref
  22.7 0.3 %collective-permute-done.9.one_ref = bf16[8,1792]{1,0:T(8,128)(2,1)S(1)} collective-permute-done((bf16[8,1792]{1,0:T(8,128)(2,1)S(1)}, bf16[8,1792]{1,0:T(8,128)(2,1)S(1)}, u32[]{:S(2)}, u32[]{:S(2)}) %collective-permute-start.9) | collective-permute-done | bytes 28704 | tf_op jit(solution)/shard_map/ppermute | solution.py:118
  23.0 0.7 %collective-permute-done.10.two_ref = bf16[8,1792]{1,0:T(8,128)(2,1)S(1)} collective-permute-done((bf16[8,1792]{1,0:T(8,128)(2,1)S(1)}, bf16[8,1792]{1,0:T(8,128)(2,1)S(1)}, u32[]{:S(2)}, u32[]{:S(2)}) %collective-permute-start.10) | collective-permute-done | bytes 28704 | tf_op jit(solution)/shard_map/ppermute | solution.py:118
  23.8 0.4 %collective-permute-start.11 = (bf16[32,1152]{1,0:T(8,128)(2,1)S(1)}, bf16[32,1152]{1,0:T(8,128)(2,1)S(1)}, u32[]{:S(2)}, u32[]{:S(2)}) collective-permute-start(bf16[32,1152]{1,0:T(8,128)(2,1)S(1)} %get-tuple-element.55), channel_id=1, source_target_pairs={{0,1},{1,0},{2,3},{3,2},{4,5},{5,4},{6,7},{7,6},{8,9},{9,8},{10,11... | collective-permute-start | bytes 221192 | tf_op jit(solution)/shard_map/ppermute | solution.py:113
  24.1 1.0 %collective-permute-done.11.far_ref = bf16[32,1152]{1,0:T(8,128)(2,1)S(1)} collective-permute-done((bf16[32,1152]{1,0:T(8,128)(2,1)S(1)}, bf16[32,1152]{1,0:T(8,128)(2,1)S(1)}, u32[]{:S(2)}, u32[]{:S(2)}) %collective-permute-start.11) | collective-permute-done | bytes 73760 | tf_op jit(solution)/shard_map/ppermute | solution.py:113
  25.1 1.0 %combine.1 = (bf16[128,896]{1,0:T(8,128)(2,1)}, f32[256,1024]{1,0:T(8,128)}) custom-call(bf16[128,128]{1,0:T(8,128)(2,1)S(1)} %get-tuple-element.32.coef_ref, bf16[32,896]{1,0:T(8,128)(2,1)S(1)} %get-tuple-element.54.near_ref, bf16[32,1152]{1,0:T(8,128)(2,1)S(1)} %collective-permute-done.11.far_ref, ...), custom_call_target="tpu_custom_call", output_to_operand_aliasing={{1}: (5, {})} | custom-call | tf_op jit(solution)/shard_map/combine/pallas_call | solution.py:474
  (7 shorter events, 0.1 us)
Async XLA Ops:
  0.6 1.0 %copy-start.8 = (bf16[128,896]{1,0:T(8,128)(2,1)S(1)}, bf16[128,896]{1,0:T(8,128)(2,1)}, u32[]{:S(2)}) copy-start(bf16[128,896]{1,0:T(8,128)(2,1)} %tokens_ref.1) | copy-start | bytes 688132
  0.6 0.7 %copy-start.3 = (s32[128,8]{0,1:T(8,128)S(1)}, s32[128,8]{0,1:T(8,128)}, u32[]{:S(2)}) copy-start(s32[128,8]{0,1:T(8,128)} %param.10) | copy-start | bytes 12292
  0.6 1.8 %collective-permute-start = (bf16[128,896]{1,0:T(8,128)(2,1)}, bf16[128,896]{1,0:T(8,128)(2,1)S(1)}, u32[]{:S(2)}, u32[]{:S(2)}) collective-permute-start(bf16[128,896]{1,0:T(8,128)(2,1)} %tokens_ref.1), channel_id=1, source_target_pairs={{0,1},{1,0},{2,3},{3,2},{4,5},{5,4},{6,7},{7,6},{8,9},{9,8},{10,11... | collective-permute-start | bytes 688136 | tf_op jit(solution)/shard_map/ppermute | solution.py:113
  1.6 8.2 %copy-start.4 = (f32[128,8]{0,1:T(8,128)S(1)}, f32[128,8]{0,1:T(8,128)}, u32[]{:S(2)}) copy-start(f32[128,8]{0,1:T(8,128)} %param.11) | copy-start | bytes 12292
  1.6 8.2 %copy-start.5 = (f32[1,28,2]{1,2,0:T(2,128)S(1)}, f32[1,28,2]{1,2,0:T(2,128)}, u32[]{:S(2)}) copy-start(f32[1,28,2]{1,2,0:T(2,128)} %param.13) | copy-start | bytes 676
  1.6 8.2 %copy-start.6 = (f32[1,28,2]{1,2,0:T(2,128)S(1)}, f32[1,28,2]{1,2,0:T(2,128)}, u32[]{:S(2)}) copy-start(f32[1,28,2]{1,2,0:T(2,128)} %param.15) | copy-start | bytes 676
  1.6 8.2 %copy-start.7 = (f32[1,2,28]{2,1,0:T(2,128)S(1)}, f32[1,2,28]{2,1,0:T(2,128)}, u32[]{:S(2)}) copy-start(f32[1,2,28]{2,1,0:T(2,128)} %param.17) | copy-start | bytes 676
  1.6 11.5 %copy-start = (bf16[1,256,3584]{2,1,0:T(8,128)(2,1)S(1)}, bf16[1,256,3584]{2,1,0:T(8,128)(2,1)}, u32[]{:S(2)}) copy-start(bf16[1,256,3584]{2,1,0:T(8,128)(2,1)} %param.16) | copy-start | bytes 5505028
  1.6 11.5 %copy-start.1 = (bf16[1,3584,256]{2,1,0:T(8,128)(2,1)S(1)}, bf16[1,3584,256]{2,1,0:T(8,128)(2,1)}, u32[]{:S(2)}) copy-start(bf16[1,3584,256]{2,1,0:T(8,128)(2,1)} %param.12) | copy-start | bytes 5505028
  1.6 11.5 %copy-start.2 = (bf16[1,3584,256]{2,1,0:T(8,128)(2,1)S(1)}, bf16[1,3584,256]{2,1,0:T(8,128)(2,1)}, u32[]{:S(2)}) copy-start(bf16[1,3584,256]{2,1,0:T(8,128)(2,1)} %param.14) | copy-start | bytes 5505028
  2.6 7.8 %collective-permute-start.1 = (bf16[8,1792]{1,0:T(8,128)(2,1)S(1)}, bf16[8,1792]{1,0:T(8,128)(2,1)S(1)}, u32[]{:S(2)}, u32[]{:S(2)}) collective-permute-start(bf16[8,1792]{1,0:T(8,128)(2,1)S(1)} %get-tuple-element.35), channel_id=1, source_target_pairs={{0,8},{1,11},{2,10},{3,9},{4,12},{5,15},{6,14},{7,13},{8,0},{9,3},... | collective-permute-start | bytes 86024 | tf_op jit(solution)/shard_map/ppermute | solution.py:118
  6.7 5.9 %collective-permute-start.2 = (bf16[8,1792]{1,0:T(8,128)(2,1)S(1)}, bf16[8,1792]{1,0:T(8,128)(2,1)S(1)}, u32[]{:S(2)}, u32[]{:S(2)}) collective-permute-start(bf16[8,1792]{1,0:T(8,128)(2,1)S(1)} %get-tuple-element.36), channel_id=1, source_target_pairs={{0,12},{1,15},{2,14},{3,13},{4,8},{5,11},{6,10},{7,9},{8,4},{9,7},... | collective-permute-start | bytes 86024 | tf_op jit(solution)/shard_map/ppermute | solution.py:118
  8.0 4.5 %collective-permute-start.3 = (bf16[8,1792]{1,0:T(8,128)(2,1)S(1)}, bf16[8,1792]{1,0:T(8,128)(2,1)S(1)}, u32[]{:S(2)}, u32[]{:S(2)}) collective-permute-start(bf16[8,1792]{1,0:T(8,128)(2,1)S(1)} %get-tuple-element.37), channel_id=1, source_target_pairs={{0,4},{1,7},{2,6},{3,5},{4,0},{5,3},{6,2},{7,1},{8,12},{9,15},{10,... | collective-permute-start | bytes 86024 | tf_op jit(solution)/shard_map/ppermute | solution.py:118
  8.2 4.9 %collective-permute-start.5 = (bf16[8,1792]{1,0:T(8,128)(2,1)S(1)}, bf16[8,1792]{1,0:T(8,128)(2,1)S(1)}, u32[]{:S(2)}, u32[]{:S(2)}) collective-permute-start(bf16[8,1792]{1,0:T(8,128)(2,1)S(1)} %get-tuple-element.33.own_ref), channel_id=1, source_target_pairs={{0,2},{1,3},{2,0},{3,1},{4,6},{5,7},{6,4},{7,5},{8,10},{9,11},{10,... | collective-permute-start | bytes 86024 | tf_op jit(solution)/shard_map/ppermute | solution.py:122
  12.6 1.5 %collective-permute-start.4 = (bf16[32,1792]{1,0:T(8,128)(2,1)S(1)}, bf16[32,1792]{1,0:T(8,128)(2,1)S(1)}, u32[]{:S(2)}, u32[]{:S(2)}) collective-permute-start(bf16[32,1792]{1,0:T(8,128)(2,1)S(1)} %get-tuple-element.39.x_ref), channel_id=1, source_target_pairs={{0,1},{1,0},{2,3},{3,2},{4,5},{5,4},{6,7},{7,6},{8,9},{9,8},{10,11... | collective-permute-start | bytes 344072 | tf_op jit(solution)/shard_map/ppermute | solution.py:113
  14.8 2.0 %collective-permute-start.6 = (bf16[32,2048]{1,0:T(8,128)(2,1)S(1)}, bf16[32,2048]{1,0:T(8,128)(2,1)S(1)}, u32[]{:S(2)}, u32[]{:S(2)}) collective-permute-start(bf16[32,2048]{1,0:T(8,128)(2,1)S(1)} %get-tuple-element.45.send_ref), channel_id=1, source_target_pairs={{0,1},{1,0},{2,3},{3,2},{4,5},{5,4},{6,7},{7,6},{8,9},{9,8},{10,11... | collective-permute-start | bytes 393224 | tf_op jit(solution)/shard_map/ppermute | solution.py:113
  15.5 5.8 %collective-permute-start.7 = (bf16[8,2816]{1,0:T(8,128)(2,1)S(1)}, bf16[8,2816]{1,0:T(8,128)(2,1)S(1)}, u32[]{:S(2)}, u32[]{:S(2)}) collective-permute-start(bf16[8,2816]{1,0:T(8,128)(2,1)S(1)} %get-tuple-element.48), channel_id=1, source_target_pairs={{0,2},{1,3},{2,0},{3,1},{4,6},{5,7},{6,4},{7,5},{8,10},{9,11},{10,... | collective-permute-start | bytes 135176 | tf_op jit(solution)/shard_map/ppermute | solution.py:122
  16.9 5.8 %collective-permute-start.8 = (bf16[8,1792]{1,0:T(8,128)(2,1)S(1)}, bf16[8,1792]{1,0:T(8,128)(2,1)S(1)}, u32[]{:S(2)}, u32[]{:S(2)}) collective-permute-start(bf16[8,1792]{1,0:T(8,128)(2,1)S(1)} %get-tuple-element.49), channel_id=1, source_target_pairs={{0,12},{1,15},{2,14},{3,13},{4,8},{5,11},{6,10},{7,9},{8,4},{9,7},... | collective-permute-start | bytes 86024 | tf_op jit(solution)/shard_map/ppermute | solution.py:118
  18.7 4.3 %collective-permute-start.9 = (bf16[8,1792]{1,0:T(8,128)(2,1)S(1)}, bf16[8,1792]{1,0:T(8,128)(2,1)S(1)}, u32[]{:S(2)}, u32[]{:S(2)}) collective-permute-start(bf16[8,1792]{1,0:T(8,128)(2,1)S(1)} %get-tuple-element.50), channel_id=1, source_target_pairs={{0,4},{1,7},{2,6},{3,5},{4,0},{5,3},{6,2},{7,1},{8,12},{9,15},{10,... | collective-permute-start | bytes 86024 | tf_op jit(solution)/shard_map/ppermute | solution.py:118
  18.7 5.0 %collective-permute-start.10 = (bf16[8,1792]{1,0:T(8,128)(2,1)S(1)}, bf16[8,1792]{1,0:T(8,128)(2,1)S(1)}, u32[]{:S(2)}, u32[]{:S(2)}) collective-permute-start(bf16[8,1792]{1,0:T(8,128)(2,1)S(1)} %get-tuple-element.51), channel_id=1, source_target_pairs={{0,8},{1,11},{2,10},{3,9},{4,12},{5,15},{6,14},{7,13},{8,0},{9,3},... | collective-permute-start | bytes 86024 | tf_op jit(solution)/shard_map/ppermute | solution.py:118
  23.8 1.3 %collective-permute-start.11 = (bf16[32,1152]{1,0:T(8,128)(2,1)S(1)}, bf16[32,1152]{1,0:T(8,128)(2,1)S(1)}, u32[]{:S(2)}, u32[]{:S(2)}) collective-permute-start(bf16[32,1152]{1,0:T(8,128)(2,1)S(1)} %get-tuple-element.55), channel_id=1, source_target_pairs={{0,1},{1,0},{2,3},{3,2},{4,5},{5,4},{6,7},{7,6},{8,9},{9,8},{10,11... | collective-permute-start | bytes 221192 | tf_op jit(solution)/shard_map/ppermute | solution.py:113

commit v11 on v10

--- a/solution.py
+++ b/solution.py
@@ -279,16 +279,13 @@
 
 
 def project_down(hidden_ref, shares, down_ref, scale_ref, out_ref):
-    slots, half, width = hidden_ref.shape[0], hidden_ref.shape[1] // 2, down_ref.shape[1] // 4
+    half, width = hidden_ref.shape[1] // 2, down_ref.shape[1] // 4
     parts = (hidden_ref[:, :half], hidden_ref[:, half:])
-    none = jnp.zeros_like(parts[0])
-    stacked = jnp.concatenate(
-        [jnp.concatenate([parts[0], none], axis=1), jnp.concatenate([none, parts[1]], axis=1)], axis=0
-    )
     for part, share in enumerate(shares):
         lanes = pl.ds(pl.multiple_of(share * width, width), width)
-        both = jnp.dot(stacked, down_ref[:, lanes], preferred_element_type=F32)
-        value = both[:slots] * scale_ref[:1, lanes] + both[slots:] * scale_ref[1:, lanes]
+        upper = jnp.dot(parts[0], down_ref[:half, lanes], preferred_element_type=F32)
+        lower = jnp.dot(parts[1], down_ref[half:, lanes], preferred_element_type=F32)
+        value = upper * scale_ref[:1, lanes] + lower * scale_ref[1:, lanes]
         out_ref[:, part * width : (part + 1) * width] = value.astype(BF16)
 
 

time: 26.3 us -> 26.3 us (level)
  no operation moved by 1% of the time
where the time goes in v11:
time: 26.3 us; the launch traced here: 26.1 us
  starting transfers between devices  14.7 us (56%)
  waiting for transfers between devices  5.35 us (20%)
  Pallas kernels  5 us (19%)
  between operations  0.74 us (3%)
  local copies, waits for them, and re-layouts  0.3 us (1%)
    ppermute x6, starting transfers between devices, to_chips(): return lax.ppermute(value, BOTH, pairs)  10.1 us
    pallas_call x12, Pallas kernels, call(): pl.pallas_call(kernel, out_shape=outs, in_specs=[SMEM] * scalars + [VMEM]...  4.01 us
    ppermute x6, waiting for transfers between devices, to_chips(): return lax.ppermute(value, BOTH, pairs)  3.19 us
    ppermute x2, starting transfers between devices, across(): lax.ppermute(value, BOTH, [(4 * z + m, 4 * z + (m ^ 2)) for z in range(4)...  2.82 us
    ppermute x4, waiting for transfers between devices, swap_cores(): return lax.ppermute(value, 'mp', [(m, m ^ 1) for m in range(4)])  2.16 us
    ppermute x4, starting transfers between devices, swap_cores(): return lax.ppermute(value, 'mp', [(m, m ^ 1) for m in range(4)])  1.82 us
    pallas_call x1, Pallas kernels, on_device(): pl.pallas_call(combine_kernel, out_shape=(shape((rows, width), BF16), sha...  0.99 us
  transfers between devices with their start and end apart: 12, of which 7 were waited for; matrix products, arithmetic and copies ran while one was open for 0% of the time, Pallas kernels for 12%

profile of v11, /device:TPU:0, one launch (start us, length us, event | category | flops | bytes accessed | tf_op | source)
XLA Modules:
  0.0 26.1 jit_solution(15884680337864260285)
XLA Ops:
  0.6 0.0 copy-start.8
  0.6 0.0 copy-start.3
  0.6 0.5 %collective-permute-start = (bf16[128,896]{1,0:T(8,128)(2,1)}, bf16[128,896]{1,0:T(8,128)(2,1)S(1)}, u32[]{:S(2)}, u32[]{:S(2)}) collective-permute-start(bf16[128,896]{1,0:T(8,128)(2,1)} %tokens_ref.1), channel_id=1, source_target_pairs={{0,1},{1,0},{2,3},{3,2},{4,5},{5,4},{6,7},{7,6},{8,9},{9,8},{10,11... | collective-permute-start | bytes 688136 | tf_op jit(solution)/shard_map/ppermute | solution.py:113
  1.2 0.2 copy-done.3
  1.4 0.1 route.1
  1.5 0.1 copy-done.8
  1.6 0.0 copy-start
  1.6 0.0 copy-start.1
  1.6 0.0 copy-start.2
  1.6 0.1 own.1.own_ref
  1.8 0.7 %collective-permute-done.tokens_ref = bf16[128,896]{1,0:T(8,128)(2,1)S(1)} collective-permute-done((bf16[128,896]{1,0:T(8,128)(2,1)}, bf16[128,896]{1,0:T(8,128)(2,1)S(1)}, u32[]{:S(2)}, u32[]{:S(2)}) %collective-permute-start) | collective-permute-done | bytes 229408 | tf_op jit(solution)/shard_map/ppermute | solution.py:113
  2.5 0.1 line_up.1
  2.6 4.0 %collective-permute-start.1 = (bf16[8,1792]{1,0:T(8,128)(2,1)S(1)}, bf16[8,1792]{1,0:T(8,128)(2,1)S(1)}, u32[]{:S(2)}, u32[]{:S(2)}) collective-permute-start(bf16[8,1792]{1,0:T(8,128)(2,1)S(1)} %get-tuple-element.35), channel_id=1, source_target_pairs={{0,8},{1,11},{2,10},{3,9},{4,12},{5,15},{6,14},{7,13},{8,0},{9,3},... | collective-permute-start | bytes 86024 | tf_op jit(solution)/shard_map/ppermute | solution.py:118
  6.7 1.3 %collective-permute-start.2 = (bf16[8,1792]{1,0:T(8,128)(2,1)S(1)}, bf16[8,1792]{1,0:T(8,128)(2,1)S(1)}, u32[]{:S(2)}, u32[]{:S(2)}) collective-permute-start(bf16[8,1792]{1,0:T(8,128)(2,1)S(1)} %get-tuple-element.36), channel_id=1, source_target_pairs={{0,12},{1,15},{2,14},{3,13},{4,8},{5,11},{6,10},{7,9},{8,4},{9,7},... | collective-permute-start | bytes 86024 | tf_op jit(solution)/shard_map/ppermute | solution.py:118
  8.0 0.2 collective-permute-start.3
  8.2 1.5 %collective-permute-start.5 = (bf16[8,1792]{1,0:T(8,128)(2,1)S(1)}, bf16[8,1792]{1,0:T(8,128)(2,1)S(1)}, u32[]{:S(2)}, u32[]{:S(2)}) collective-permute-start(bf16[8,1792]{1,0:T(8,128)(2,1)S(1)} %get-tuple-element.33.own_ref), channel_id=1, source_target_pairs={{0,2},{1,3},{2,0},{3,1},{4,6},{5,7},{6,4},{7,5},{8,10},{9,11},{10,... | collective-permute-start | bytes 86024 | tf_op jit(solution)/shard_map/ppermute | solution.py:122
  9.7 0.0 copy-done.4
  9.7 0.0 copy-done.5
  9.7 0.0 copy-done.6
  9.7 0.0 copy-done.7
  9.8 0.7 %prepare.1 = (f32[2,3584]{1,0:T(2,128)S(1)}, f32[2,3584]{1,0:T(2,128)S(1)}, f32[2,3584]{1,0:T(2,128)S(1)}, bf16[128,128]{1,0:T(8,128)(2,1)S(1)}) custom-call(f32[2,28]{1,0:T(2,128)S(1)} %bitcast.23, f32[2,28]{1,0:T(2,128)S(1)} %bitcast.24, f32[2,28]{1,0:T(2,128)S(1)} %bitcast.25, s32[8,128]{1,0:T(8,128)S(1)} %bitcast.21, f32[8,128]{1,0:T(8,128)S(1)} %bitcast.22, ...), custom_call_target="tpu_custom_call" | custom-call | tf_op jit(solution)/shard_map/prepare/pallas_call | solution.py:381
  10.4 0.0 collective-permute-done.1.two_ref
  10.5 2.1 %collective-permute-done.2.three_ref = bf16[8,1792]{1,0:T(8,128)(2,1)S(1)} collective-permute-done((bf16[8,1792]{1,0:T(8,128)(2,1)S(1)}, bf16[8,1792]{1,0:T(8,128)(2,1)S(1)}, u32[]{:S(2)}, u32[]{:S(2)}) %collective-permute-start.2) | collective-permute-done | bytes 28704 | tf_op jit(solution)/shard_map/ppermute | solution.py:118
  12.5 0.0 collective-permute-done.3.one_ref
  12.5 0.1 collect.1
  12.6 0.5 %collective-permute-start.4 = (bf16[32,1792]{1,0:T(8,128)(2,1)S(1)}, bf16[32,1792]{1,0:T(8,128)(2,1)S(1)}, u32[]{:S(2)}, u32[]{:S(2)}) collective-permute-start(bf16[32,1792]{1,0:T(8,128)(2,1)S(1)} %get-tuple-element.39.x_ref), channel_id=1, source_target_pairs={{0,1},{1,0},{2,3},{3,2},{4,5},{5,4},{6,7},{7,6},{8,9},{9,8},{10,11... | collective-permute-start | bytes 344072 | tf_op jit(solution)/shard_map/ppermute | solution.py:113
  13.1 0.0 collective-permute-done.5.crossed_ref
  13.1 0.0 copy-done
  13.1 0.0 copy-done.1
  13.1 0.0 copy-done.2
  13.1 0.5 %near.1 = (f32[64,256]{1,0:T(8,128)S(1)}, f32[64,256]{1,0:T(8,128)S(1)}) custom-call(bf16[32,1792]{1,0:T(8,128)(2,1)S(1)} %get-tuple-element.39.x_ref, bf16[8,1792]{1,0:T(8,128)(2,1)S(1)} %collective-permute-done.5.crossed_ref, bf16[3584,256]{1,0:T(8,128)(2,1)S(1)} %bitcast.16, bf16[3584,256]{1,0:T(8,128)(2,1)S(1)} %bitcast.18, ...), custom_call_target="tpu_custom_call" | custom-call | flops 10000000000 | tf_op jit(solution)/shard_map/near/pallas_call | solution.py:381
  13.6 0.5 %collective-permute-done.4.x_ref = bf16[32,1792]{1,0:T(8,128)(2,1)S(1)} collective-permute-done((bf16[32,1792]{1,0:T(8,128)(2,1)S(1)}, bf16[32,1792]{1,0:T(8,128)(2,1)S(1)}, u32[]{:S(2)}, u32[]{:S(2)}) %collective-permute-start.4) | collective-permute-done | bytes 114720 | tf_op jit(solution)/shard_map/ppermute | solution.py:113
  14.1 0.7 %hidden.1 = (bf16[32,2048]{1,0:T(8,128)(2,1)S(1)}, bf16[32,256]{1,0:T(8,128)(2,1)S(1)}) custom-call(bf16[32,1792]{1,0:T(8,128)(2,1)S(1)} %collective-permute-done.4.x_ref, bf16[8,1792]{1,0:T(8,128)(2,1)S(1)} %collective-permute-done.5.crossed_ref, f32[64,256]{1,0:T(8,128)S(1)} %get-tuple-element.41.near_gate_ref, ...), custom_call_target="tpu_custom_call" | custom-call | tf_op jit(solution)/shard_map/hidden/pallas_call | solution.py:381
  14.8 0.4 %collective-permute-start.6 = (bf16[32,2048]{1,0:T(8,128)(2,1)S(1)}, bf16[32,2048]{1,0:T(8,128)(2,1)S(1)}, u32[]{:S(2)}, u32[]{:S(2)}) collective-permute-start(bf16[32,2048]{1,0:T(8,128)(2,1)S(1)} %get-tuple-element.45.send_ref), channel_id=1, source_target_pairs={{0,1},{1,0},{2,3},{3,2},{4,5},{5,4},{6,7},{7,6},{8,9},{9,8},{10,11... | collective-permute-start | bytes 393224 | tf_op jit(solution)/shard_map/ppermute | solution.py:113
  15.2 0.3 %keep.1 = (bf16[32,1792]{1,0:T(8,128)(2,1)S(1)}, bf16[8,2816]{1,0:T(8,128)(2,1)S(1)}) custom-call(bf16[32,256]{1,0:T(8,128)(2,1)S(1)} %get-tuple-element.44.hidden_ref.own_ref, bf16[32,2048]{1,0:T(8,128)(2,1)S(1)} %get-tuple-element.45.send_ref, bf16[256,3584]{1,0:T(8,128)(2,1)S(1)} %bitcast.15, f32[2,3584]{1,0:T(2,128)S(1)} %get-tuple-element.43.down_scale_ref), custom_call_target="tpu_custom_call" | custom-call | tf_op jit(solution)/shard_map/keep/pallas_call | solution.py:381
  15.5 1.3 %collective-permute-start.7 = (bf16[8,2816]{1,0:T(8,128)(2,1)S(1)}, bf16[8,2816]{1,0:T(8,128)(2,1)S(1)}, u32[]{:S(2)}, u32[]{:S(2)}) collective-permute-start(bf16[8,2816]{1,0:T(8,128)(2,1)S(1)} %get-tuple-element.48), channel_id=1, source_target_pairs={{0,2},{1,3},{2,0},{3,1},{4,6},{5,7},{6,4},{7,5},{8,10},{9,11},{10,... | collective-permute-start | bytes 135176 | tf_op jit(solution)/shard_map/ppermute | solution.py:122
  16.8 0.0 collective-permute-done.6.sent_ref
  16.9 1.9 %collective-permute-start.8 = (bf16[8,1792]{1,0:T(8,128)(2,1)S(1)}, bf16[8,1792]{1,0:T(8,128)(2,1)S(1)}, u32[]{:S(2)}, u32[]{:S(2)}) collective-permute-start(bf16[8,1792]{1,0:T(8,128)(2,1)S(1)} %get-tuple-element.49), channel_id=1, source_target_pairs={{0,12},{1,15},{2,14},{3,13},{4,8},{5,11},{6,10},{7,9},{8,4},{9,7},... | collective-permute-start | bytes 86024 | tf_op jit(solution)/shard_map/ppermute | solution.py:118
  18.7 0.0 collective-permute-start.9
  18.7 2.6 %collective-permute-start.10 = (bf16[8,1792]{1,0:T(8,128)(2,1)S(1)}, bf16[8,1792]{1,0:T(8,128)(2,1)S(1)}, u32[]{:S(2)}, u32[]{:S(2)}) collective-permute-start(bf16[8,1792]{1,0:T(8,128)(2,1)S(1)} %get-tuple-element.51), channel_id=1, source_target_pairs={{0,8},{1,11},{2,10},{3,9},{4,12},{5,15},{6,14},{7,13},{8,0},{9,3},... | collective-permute-start | bytes 86024 | tf_op jit(solution)/shard_map/ppermute | solution.py:118
  21.3 0.0 collective-permute-done.7.crossed_ref
  21.3 1.3 %hessian.1 = (f32[256,1024]{1,0:T(8,128)}, bf16[32,256]{1,0:T(8,128)(2,1)S(1)}, bf16[256,32]{1,0:T(8,128)(2,1)S(1)}) custom-call(bf16[32,128]{1,0:T(8,128)(2,1)S(1)} %get-tuple-element.52.count_ref, bf16[32,256]{1,0:T(8,128)(2,1)S(1)} %get-tuple-element.44.hidden_ref.own_ref, bf16[32,2048]{1,0:T(8,128)(2,1)S(1)} %collective-permute-done.6.sent_ref, ...), custom_call_target="tpu_custom_call" | custom-call | tf_op jit(solution)/shard_map/hessian/pallas_call | solution.py:381
  22.6 0.1 collective-permute-done.8.three_ref
  22.7 0.3 %collective-permute-done.9.one_ref = bf16[8,1792]{1,0:T(8,128)(2,1)S(1)} collective-permute-done((bf16[8,1792]{1,0:T(8,128)(2,1)S(1)}, bf16[8,1792]{1,0:T(8,128)(2,1)S(1)}, u32[]{:S(2)}, u32[]{:S(2)}) %collective-permute-start.9) | collective-permute-done | bytes 28704 | tf_op jit(solution)/shard_map/ppermute | solution.py:118
  23.0 0.8 %collective-permute-done.10.two_ref = bf16[8,1792]{1,0:T(8,128)(2,1)S(1)} collective-permute-done((bf16[8,1792]{1,0:T(8,128)(2,1)S(1)}, bf16[8,1792]{1,0:T(8,128)(2,1)S(1)}, u32[]{:S(2)}, u32[]{:S(2)}) %collective-permute-start.10) | collective-permute-done | bytes 28704 | tf_op jit(solution)/shard_map/ppermute | solution.py:118
  23.8 0.4 %collective-permute-start.11 = (bf16[32,1152]{1,0:T(8,128)(2,1)S(1)}, bf16[32,1152]{1,0:T(8,128)(2,1)S(1)}, u32[]{:S(2)}, u32[]{:S(2)}) collective-permute-start(bf16[32,1152]{1,0:T(8,128)(2,1)S(1)} %get-tuple-element.55), channel_id=1, source_target_pairs={{0,1},{1,0},{2,3},{3,2},{4,5},{5,4},{6,7},{7,6},{8,9},{9,8},{10,11... | collective-permute-start | bytes 221192 | tf_op jit(solution)/shard_map/ppermute | solution.py:113
  24.1 1.0 %collective-permute-done.11.far_ref = bf16[32,1152]{1,0:T(8,128)(2,1)S(1)} collective-permute-done((bf16[32,1152]{1,0:T(8,128)(2,1)S(1)}, bf16[32,1152]{1,0:T(8,128)(2,1)S(1)}, u32[]{:S(2)}, u32[]{:S(2)}) %collective-permute-start.11) | collective-permute-done | bytes 73760 | tf_op jit(solution)/shard_map/ppermute | solution.py:113
  25.1 1.0 %combine.1 = (bf16[128,896]{1,0:T(8,128)(2,1)}, f32[256,1024]{1,0:T(8,128)}) custom-call(bf16[128,128]{1,0:T(8,128)(2,1)S(1)} %get-tuple-element.32.coef_ref, bf16[32,896]{1,0:T(8,128)(2,1)S(1)} %get-tuple-element.54.near_ref, bf16[32,1152]{1,0:T(8,128)(2,1)S(1)} %collective-permute-done.11.far_ref, ...), custom_call_target="tpu_custom_call", output_to_operand_aliasing={{1}: (5, {})} | custom-call | tf_op jit(solution)/shard_map/combine/pallas_call | solution.py:471
  (7 shorter events, 0.1 us)
Async XLA Ops:
  0.6 1.0 %copy-start.8 = (bf16[128,896]{1,0:T(8,128)(2,1)S(1)}, bf16[128,896]{1,0:T(8,128)(2,1)}, u32[]{:S(2)}) copy-start(bf16[128,896]{1,0:T(8,128)(2,1)} %tokens_ref.1) | copy-start | bytes 688132
  0.6 0.7 %copy-start.3 = (s32[128,8]{0,1:T(8,128)S(1)}, s32[128,8]{0,1:T(8,128)}, u32[]{:S(2)}) copy-start(s32[128,8]{0,1:T(8,128)} %param.10) | copy-start | bytes 12292
  0.6 1.8 %collective-permute-start = (bf16[128,896]{1,0:T(8,128)(2,1)}, bf16[128,896]{1,0:T(8,128)(2,1)S(1)}, u32[]{:S(2)}, u32[]{:S(2)}) collective-permute-start(bf16[128,896]{1,0:T(8,128)(2,1)} %tokens_ref.1), channel_id=1, source_target_pairs={{0,1},{1,0},{2,3},{3,2},{4,5},{5,4},{6,7},{7,6},{8,9},{9,8},{10,11... | collective-permute-start | bytes 688136 | tf_op jit(solution)/shard_map/ppermute | solution.py:113
  1.6 8.2 %copy-start.4 = (f32[128,8]{0,1:T(8,128)S(1)}, f32[128,8]{0,1:T(8,128)}, u32[]{:S(2)}) copy-start(f32[128,8]{0,1:T(8,128)} %param.11) | copy-start | bytes 12292
  1.6 8.2 %copy-start.5 = (f32[1,28,2]{1,2,0:T(2,128)S(1)}, f32[1,28,2]{1,2,0:T(2,128)}, u32[]{:S(2)}) copy-start(f32[1,28,2]{1,2,0:T(2,128)} %param.13) | copy-start | bytes 676
  1.6 8.2 %copy-start.6 = (f32[1,28,2]{1,2,0:T(2,128)S(1)}, f32[1,28,2]{1,2,0:T(2,128)}, u32[]{:S(2)}) copy-start(f32[1,28,2]{1,2,0:T(2,128)} %param.15) | copy-start | bytes 676
  1.6 8.2 %copy-start.7 = (f32[1,2,28]{2,1,0:T(2,128)S(1)}, f32[1,2,28]{2,1,0:T(2,128)}, u32[]{:S(2)}) copy-start(f32[1,2,28]{2,1,0:T(2,128)} %param.17) | copy-start | bytes 676
  1.6 11.5 %copy-start = (bf16[1,256,3584]{2,1,0:T(8,128)(2,1)S(1)}, bf16[1,256,3584]{2,1,0:T(8,128)(2,1)}, u32[]{:S(2)}) copy-start(bf16[1,256,3584]{2,1,0:T(8,128)(2,1)} %param.16) | copy-start | bytes 5505028
  1.6 11.5 %copy-start.1 = (bf16[1,3584,256]{2,1,0:T(8,128)(2,1)S(1)}, bf16[1,3584,256]{2,1,0:T(8,128)(2,1)}, u32[]{:S(2)}) copy-start(bf16[1,3584,256]{2,1,0:T(8,128)(2,1)} %param.12) | copy-start | bytes 5505028
  1.6 11.5 %copy-start.2 = (bf16[1,3584,256]{2,1,0:T(8,128)(2,1)S(1)}, bf16[1,3584,256]{2,1,0:T(8,128)(2,1)}, u32[]{:S(2)}) copy-start(bf16[1,3584,256]{2,1,0:T(8,128)(2,1)} %param.14) | copy-start | bytes 5505028
  2.6 7.8 %collective-permute-start.1 = (bf16[8,1792]{1,0:T(8,128)(2,1)S(1)}, bf16[8,1792]{1,0:T(8,128)(2,1)S(1)}, u32[]{:S(2)}, u32[]{:S(2)}) collective-permute-start(bf16[8,1792]{1,0:T(8,128)(2,1)S(1)} %get-tuple-element.35), channel_id=1, source_target_pairs={{0,8},{1,11},{2,10},{3,9},{4,12},{5,15},{6,14},{7,13},{8,0},{9,3},... | collective-permute-start | bytes 86024 | tf_op jit(solution)/shard_map/ppermute | solution.py:118
  6.7 5.9 %collective-permute-start.2 = (bf16[8,1792]{1,0:T(8,128)(2,1)S(1)}, bf16[8,1792]{1,0:T(8,128)(2,1)S(1)}, u32[]{:S(2)}, u32[]{:S(2)}) collective-permute-start(bf16[8,1792]{1,0:T(8,128)(2,1)S(1)} %get-tuple-element.36), channel_id=1, source_target_pairs={{0,12},{1,15},{2,14},{3,13},{4,8},{5,11},{6,10},{7,9},{8,4},{9,7},... | collective-permute-start | bytes 86024 | tf_op jit(solution)/shard_map/ppermute | solution.py:118
  8.0 4.5 %collective-permute-start.3 = (bf16[8,1792]{1,0:T(8,128)(2,1)S(1)}, bf16[8,1792]{1,0:T(8,128)(2,1)S(1)}, u32[]{:S(2)}, u32[]{:S(2)}) collective-permute-start(bf16[8,1792]{1,0:T(8,128)(2,1)S(1)} %get-tuple-element.37), channel_id=1, source_target_pairs={{0,4},{1,7},{2,6},{3,5},{4,0},{5,3},{6,2},{7,1},{8,12},{9,15},{10,... | collective-permute-start | bytes 86024 | tf_op jit(solution)/shard_map/ppermute | solution.py:118
  8.2 4.9 %collective-permute-start.5 = (bf16[8,1792]{1,0:T(8,128)(2,1)S(1)}, bf16[8,1792]{1,0:T(8,128)(2,1)S(1)}, u32[]{:S(2)}, u32[]{:S(2)}) collective-permute-start(bf16[8,1792]{1,0:T(8,128)(2,1)S(1)} %get-tuple-element.33.own_ref), channel_id=1, source_target_pairs={{0,2},{1,3},{2,0},{3,1},{4,6},{5,7},{6,4},{7,5},{8,10},{9,11},{10,... | collective-permute-start | bytes 86024 | tf_op jit(solution)/shard_map/ppermute | solution.py:122
  12.6 1.5 %collective-permute-start.4 = (bf16[32,1792]{1,0:T(8,128)(2,1)S(1)}, bf16[32,1792]{1,0:T(8,128)(2,1)S(1)}, u32[]{:S(2)}, u32[]{:S(2)}) collective-permute-start(bf16[32,1792]{1,0:T(8,128)(2,1)S(1)} %get-tuple-element.39.x_ref), channel_id=1, source_target_pairs={{0,1},{1,0},{2,3},{3,2},{4,5},{5,4},{6,7},{7,6},{8,9},{9,8},{10,11... | collective-permute-start | bytes 344072 | tf_op jit(solution)/shard_map/ppermute | solution.py:113
  14.8 2.0 %collective-permute-start.6 = (bf16[32,2048]{1,0:T(8,128)(2,1)S(1)}, bf16[32,2048]{1,0:T(8,128)(2,1)S(1)}, u32[]{:S(2)}, u32[]{:S(2)}) collective-permute-start(bf16[32,2048]{1,0:T(8,128)(2,1)S(1)} %get-tuple-element.45.send_ref), channel_id=1, source_target_pairs={{0,1},{1,0},{2,3},{3,2},{4,5},{5,4},{6,7},{7,6},{8,9},{9,8},{10,11... | collective-permute-start | bytes 393224 | tf_op jit(solution)/shard_map/ppermute | solution.py:113
  15.5 5.8 %collective-permute-start.7 = (bf16[8,2816]{1,0:T(8,128)(2,1)S(1)}, bf16[8,2816]{1,0:T(8,128)(2,1)S(1)}, u32[]{:S(2)}, u32[]{:S(2)}) collective-permute-start(bf16[8,2816]{1,0:T(8,128)(2,1)S(1)} %get-tuple-element.48), channel_id=1, source_target_pairs={{0,2},{1,3},{2,0},{3,1},{4,6},{5,7},{6,4},{7,5},{8,10},{9,11},{10,... | collective-permute-start | bytes 135176 | tf_op jit(solution)/shard_map/ppermute | solution.py:122
  16.9 5.8 %collective-permute-start.8 = (bf16[8,1792]{1,0:T(8,128)(2,1)S(1)}, bf16[8,1792]{1,0:T(8,128)(2,1)S(1)}, u32[]{:S(2)}, u32[]{:S(2)}) collective-permute-start(bf16[8,1792]{1,0:T(8,128)(2,1)S(1)} %get-tuple-element.49), channel_id=1, source_target_pairs={{0,12},{1,15},{2,14},{3,13},{4,8},{5,11},{6,10},{7,9},{8,4},{9,7},... | collective-permute-start | bytes 86024 | tf_op jit(solution)/shard_map/ppermute | solution.py:118
  18.7 4.3 %collective-permute-start.9 = (bf16[8,1792]{1,0:T(8,128)(2,1)S(1)}, bf16[8,1792]{1,0:T(8,128)(2,1)S(1)}, u32[]{:S(2)}, u32[]{:S(2)}) collective-permute-start(bf16[8,1792]{1,0:T(8,128)(2,1)S(1)} %get-tuple-element.50), channel_id=1, source_target_pairs={{0,4},{1,7},{2,6},{3,5},{4,0},{5,3},{6,2},{7,1},{8,12},{9,15},{10,... | collective-permute-start | bytes 86024 | tf_op jit(solution)/shard_map/ppermute | solution.py:118
  18.7 5.0 %collective-permute-start.10 = (bf16[8,1792]{1,0:T(8,128)(2,1)S(1)}, bf16[8,1792]{1,0:T(8,128)(2,1)S(1)}, u32[]{:S(2)}, u32[]{:S(2)}) collective-permute-start(bf16[8,1792]{1,0:T(8,128)(2,1)S(1)} %get-tuple-element.51), channel_id=1, source_target_pairs={{0,8},{1,11},{2,10},{3,9},{4,12},{5,15},{6,14},{7,13},{8,0},{9,3},... | collective-permute-start | bytes 86024 | tf_op jit(solution)/shard_map/ppermute | solution.py:118
  23.8 1.3 %collective-permute-start.11 = (bf16[32,1152]{1,0:T(8,128)(2,1)S(1)}, bf16[32,1152]{1,0:T(8,128)(2,1)S(1)}, u32[]{:S(2)}, u32[]{:S(2)}) collective-permute-start(bf16[32,1152]{1,0:T(8,128)(2,1)S(1)} %get-tuple-element.55), channel_id=1, source_target_pairs={{0,1},{1,0},{2,3},{3,2},{4,5},{5,4},{6,7},{7,6},{8,9},{9,8},{10,11... | collective-permute-start | bytes 221192 | tf_op jit(solution)/shard_map/ppermute | solution.py:113
